TPU v7x, 32 devices: a whole 2x2x4 slice. The times are simulated.
32 devices in a mesh: parts: 2 (over y), row: 4 (over z), col: 2 (over x), rhs: 2 (over core).
Axes of the slice: x: 2, y: 2, z: 4, core: 2. Of those that a mesh axis runs over, the one named last changes fastest.
Arguments:
- current: bfloat16 [32, 65536], P('rhs', ('parts', 'row', 'col')), parts along dimension 1, may hold values from -6 to 6
- charge: bfloat16 [32, 8192], P('rhs', ('parts', 'row', 'col')), parts along dimension 1, may hold values from -6 to 6
- rhs_scale: float32 [64], P(('parts', 'rhs')), parts along dimension 0, may hold values from 0.5 to 2
- induct_tiles: bfloat16 [3072, 128, 128], P(('parts', 'row', 'col')), parts along dimension 0, may hold values from -0.21875 to 0.21875
- induct_rows: int32 [3072], P(('parts', 'row', 'col')), parts along dimension 0, may hold values from 0 to 63
- induct_slots: int32 [3072], P(('parts', 'row', 'col')), parts along dimension 0, may hold values from 0 to 31, as said below
- induct_needs: int32 [64, 8], P(('parts', 'row', 'col')), parts along dimension 0, may hold values from 0 to 63
- coeff_tiles: bfloat16 [1536, 128, 128], P(('parts', 'row', 'col')), parts along dimension 0, may hold values from -0.109375 to 0.109375
- coeff_rows: int32 [1536], P(('parts', 'row', 'col')), parts along dimension 0, may hold values from 0 to 7
- coeff_slots: int32 [1536], P(('parts', 'row', 'col')), parts along dimension 0, may hold values from 0 to 15, as said below
- coeff_needs: int32 [64, 4], P(('parts', 'row', 'col')), parts along dimension 0, may hold values from 0 to 7
- link_needs: int32 [64, 16], P(('parts', 'row', 'col')), parts along dimension 0, may hold values from 0 to 7
- end_slots: int32 [512, 2], P(('parts', 'row', 'col')), parts along dimension 0, may hold values from 0 to 63, as said below
- end_offsets: int32 [65536, 2], P(('parts', 'row', 'col')), parts along dimension 0, may hold values from 0 to 127
Outputs:
- seg_out: bfloat16 [32, 65536], P('rhs', ('parts', 'row', 'col')), parts along dimension 1
- pan_out: bfloat16 [32, 8192], P('rhs', ('parts', 'row', 'col')), parts along dimension 1
- potential: bfloat16 [32, 8192], P('rhs', ('parts', 'row', 'col')), parts along dimension 1
There are 2 independent parts, one for each index of `parts`. A program takes and returns all parts, laid end to end along the dimension named above; each array names one. Nothing has to cross between parts.
Inputs may be any that keep to these rules, and one draw needn't show every extreme that they name: `induct_slots`: every slot 0 to 31 of a device is named by one or more of its tiles. `coeff_slots`: every slot 0 to 15 of a device is named by one or more of its tiles. `end_slots`: the 64 ends of a device's segment blocks take its link slots, each once.
All inputs are finite; a program needn't handle non-finite values.
Results may differ from a plain program's by a relative error of at most 0.0044.
Values may be sent and summed in bfloat16 or wider, within the bound.
No kernel may reach another device: no remote copies, remote signals or barrier semaphores. Data moves between devices by JAX's collectives and lax.ppermute only.
A program may use at most 64 MiB of HBM per device.

v0:
```python
import jax
import jax.numpy as jnp
from jax import lax
from jax.sharding import PartitionSpec as P


def one_hot(indices, count, dtype):
    return (
        indices[:, None] == lax.broadcasted_iota(jnp.int32, (indices.shape[0], count), 1)
    ).astype(dtype)


def tile_products(fetched, tile_set, sources, targets, group_count):
    picked = jnp.take(fetched, sources, axis=1)
    product = jnp.einsum("rta,tab->rtb", picked, tile_set, preferred_element_type=jnp.float32)
    landed = jnp.zeros((product.shape[0], group_count, product.shape[2]), jnp.float32)
    return landed.at[:, targets].add(product)


def shards(
    current,
    charge,
    rhs_scale,
    induct_tiles,
    induct_rows,
    induct_slots,
    induct_needs,
    coeff_tiles,
    coeff_rows,
    coeff_slots,
    coeff_needs,
    link_needs,
    end_slots,
    end_offsets,
):
    row_count = lax.axis_size("row")
    col_count = lax.axis_size("col")
    here_col = lax.axis_index("col")
    tile_width = induct_tiles.shape[1]
    rhs_local = current.shape[0]
    seg_own = current.shape[1] // tile_width
    pan_own = charge.shape[1] // tile_width
    seg_group = seg_own * col_count
    pan_group = pan_own * col_count
    link_count = 2 * seg_own
    cur_group, chg_group = (
        lax.all_gather(current, "col", axis=1, tiled=True),
        lax.all_gather(charge, "col", axis=1, tiled=True),
    )
    cur_blocks = cur_group.reshape(rhs_local, seg_group, tile_width)
    chg_blocks = chg_group.reshape(rhs_local, pan_group, tile_width)
    ind_asked, coe_asked, link_asked = (
        lax.all_to_all(induct_needs, "row", split_axis=0, concat_axis=0, tiled=True),
        lax.all_to_all(coeff_needs, "row", split_axis=0, concat_axis=0, tiled=True),
        lax.all_to_all(link_needs, "row", split_axis=0, concat_axis=0, tiled=True),
    )
    offsets = end_offsets.reshape(seg_own, tile_width, 2)
    levels = lax.broadcasted_iota(jnp.int32, (seg_own, tile_width, 2, tile_width), 3)
    end_signs = jnp.array([1.0, -1.0], jnp.float32)
    selector = jnp.where(offsets[..., None] == levels, end_signs[None, None, :, None], 0.0).astype(
        jnp.bfloat16
    )
    own_blocks = current.reshape(rhs_local, seg_own, tile_width)
    end_terms = jnp.einsum(
        "rki,kieo->rkeo", own_blocks, selector, preferred_element_type=jnp.float32
    )
    end_terms = end_terms.astype(jnp.bfloat16).reshape(rhs_local, link_count, tile_width)
    placing = one_hot(end_slots.reshape(-1), link_count, jnp.bfloat16)
    slot_terms = jnp.einsum(
        "rxo,xl->rlo", end_terms, placing, preferred_element_type=jnp.float32
    ).astype(jnp.bfloat16)
    cur_all, chg_all = (
        lax.all_gather(cur_blocks, "row", axis=1, tiled=True),
        lax.all_gather(chg_blocks, "row", axis=1, tiled=True),
    )
    peer_row = lax.broadcasted_iota(jnp.int32, (row_count, 1), 0)
    ind_global = (peer_row * seg_group + induct_needs).reshape(-1)
    coe_global = (peer_row * pan_group + coeff_needs).reshape(-1)
    ind_got = jnp.take(cur_all, ind_global, axis=1)
    coe_got = jnp.take(chg_all, coe_global, axis=1)
    end_got = lax.all_to_all(slot_terms, "row", split_axis=1, concat_axis=1, tiled=True)
    seg_part = tile_products(ind_got, induct_tiles, induct_slots, induct_rows, seg_group).reshape(
        rhs_local, -1
    )
    pot_part = tile_products(coe_got, coeff_tiles, coeff_slots, coeff_rows, pan_group).reshape(
        rhs_local, -1
    )
    arrivals = one_hot(link_asked.reshape(-1), pan_group, jnp.bfloat16)
    pan_part = jnp.einsum(
        "rlo,lg->rgo", end_got, arrivals, preferred_element_type=jnp.float32
    ).reshape(rhs_local, -1)
    seg_span = seg_own * tile_width
    pan_span = pan_own * tile_width
    seg_sum, end_sum, pot_sum = lax.psum((seg_part, pan_part, pot_part), "col")
    pot_group = pot_sum.astype(jnp.bfloat16)
    seg_mine = lax.dynamic_slice_in_dim(seg_sum, here_col * seg_span, seg_span, 1)
    end_mine = lax.dynamic_slice_in_dim(end_sum, here_col * pan_span, pan_span, 1)
    pot_own = lax.dynamic_slice_in_dim(pot_group, here_col * pan_span, pan_span, 1)
    pan_out = (rhs_scale[:, None] * charge.astype(jnp.float32) + end_mine).astype(jnp.bfloat16)
    pot_blocks = pot_group.reshape(rhs_local, pan_group, tile_width)
    pot_send = jnp.take(pot_blocks, link_asked.reshape(-1), axis=1)
    pot_got = lax.all_to_all(pot_send, "row", split_axis=1, concat_axis=1, tiled=True)
    at_ends = jnp.einsum(
        "rlo,xl->rxo", pot_got, placing, preferred_element_type=jnp.float32
    ).astype(jnp.bfloat16)
    at_ends = at_ends.reshape(rhs_local, seg_own, 2, tile_width)
    end_drops = jnp.einsum("rkeo,kieo->rki", at_ends, selector, preferred_element_type=jnp.float32)
    seg_out = (seg_mine + end_drops.reshape(rhs_local, -1)).astype(jnp.bfloat16)
    return (seg_out, pan_out, pot_own)


def solution(mesh):
    return jax.shard_map(
        shards,
        mesh=mesh,
        in_specs=(
            P("rhs", ("parts", "row", "col")),
            P("rhs", ("parts", "row", "col")),
            P(("parts", "rhs")),
            P(("parts", "row", "col"), None, None),
            P(("parts", "row", "col")),
            P(("parts", "row", "col")),
            P(("parts", "row", "col"), None),
            P(("parts", "row", "col"), None, None),
            P(("parts", "row", "col")),
            P(("parts", "row", "col")),
            P(("parts", "row", "col"), None),
            P(("parts", "row", "col"), None),
            P(("parts", "row", "col"), None),
            P(("parts", "row", "col"), None),
        ),
        out_specs=(
            P("rhs", ("parts", "row", "col")),
            P("rhs", ("parts", "row", "col")),
            P("rhs", ("parts", "row", "col")),
        ),
        check_vma=False,
    )
```

profile of v0, /device:TPU:0, one launch (start us, length us, event | category | flops | bytes accessed | tf_op | source)
XLA Modules:
  0.0 169.4 jit_solution(2511694011303648130)
XLA Ops:
  7.2 6.6 %all-to-all-start = ((s32[4,1,16]{2,1,0:T(1,128)}), s32[4,1,16]{2,1,0:T(1,128)S(1)}, u32[]{:S(2)}, u32[]{:S(2)}) async-start(s32[4,1,16]{2,1,0:T(1,128)} %bitcast.92), calls=%async_computation | async-start | bytes 4096 | tf_op jit(solution)/shard_map/all_to_all | solution.py:55
  13.8 5.8 %all_gather.12 = bf16[16,8192]{1,0:T(8,128)(2,1)S(1)} all-gather(bf16[16,4096]{1,0:T(8,128)(2,1)} %param.15), channel_id=1, replica_groups=mesh['parts'=2,'row'=4,'col'=2,'rhs'=2] {'col'}, dimensions={1}, use_global_device_ids=true | all-gather | bytes 393216 | tf_op jit(solution)/shard_map/all_gather | solution.py:47
  19.6 0.7 copy_bitcast_fusion.1
  20.4 0.8 broadcast_add_fusion
  22.7 0.8 broadcast_add_fusion.1
  23.6 0.7 compare_select_fusion
  24.3 1.2 compare_and_fusion.4
  25.5 4.6 %all_gather.14 = bf16[16,1024]{1,0:T(8,128)(2,1)S(1)} all-gather(bf16[16,512]{1,0:T(8,128)(2,1)} %param.16), channel_id=1, replica_groups=mesh['parts'=2,'row'=4,'col'=2,'rhs'=2] {'col'}, dimensions={1}, use_global_device_ids=true | all-gather | bytes 49152 | tf_op jit(solution)/shard_map/all_gather | solution.py:48
  30.1 15.0 %all_gather.15 = bf16[16,32,128]{2,0,1:T(8,128)(2,1)S(1)} all-gather(bf16[16,8,128]{2,0,1:T(8,128)(2,1)S(1)} %copy_bitcast_fusion.5), channel_id=1, replica_groups=mesh['parts'=2,'row'=4,'col'=2,'rhs'=2] {'row'}, dimensions={1}, use_global_device_ids=true | all-gather | bytes 163840 | tf_op jit(solution)/shard_map/all_gather | solution.py:74
  46.4 1.4 gather_fusion.3
  47.8 2.9 %fusion.15 = f32[96,16,128]{2,1,0:T(8,128)} fusion(bf16[96,128,128]{2,1,0:T(8,128)(2,1)S(1)} %copy-done, bf16[96,16,128]{2,1,0:T(8,128)(2,1)} %gather_fusion.3, pred[96]{0:T(512)(128)(4,1)S(1)} %compare_and_fusion.1), kind=kOutput, calls=%fused_computation.27 | convolution fusion | flops 50528256 | bytes 4325472 | tf_op jit(solution)/shard_map/rta,tab->rtb/dot_general | solution.py:15
  50.8 8.1 %scatter_fusion.1 = f32[16,8,128]{2,0,1:T(8,128)S(1)} fusion(f32[16,8,128]{2,0,1:T(8,128)S(1)} %broadcast_in_dim.90, s32[96]{0:T(128)S(1)} %compare_select_fusion.6, f32[96,16,128]{2,1,0:T(8,128)} %fusion.15), kind=kCustom, calls=%fused_computation.6 | custom fusion | flops 196608 | bytes 2359680 | tf_op jit(solution)/shard_map/scatter-add | solution.py:17
  58.9 8.9 %psum.22 = bf16[16,1024]{1,0:T(8,128)(2,1)S(1)} all-reduce(f32[16,1024]{1,0:T(8,128)S(1)} %copy_bitcast_fusion.3), channel_id=1, replica_groups=mesh['parts'=2,'row'=4,'col'=2,'rhs'=2] {'col'}, use_global_device_ids=true, to_apply=%region_3.4 | all-reduce | flops 16384 | bytes 98304 | tf_op jit(solution)/shard_map/psum | solution.py:94
  68.1 1.8 %fusion.8 = bf16[32,2,128,16]{2,3,1,0:T(8,128)(2,1)S(1)} fusion(bf16[2]{0:T(256)(128)(2,1)S(1)} %copy-done.10, s32[32,128,2]{1,2,0:T(2,128)S(1)} %bitcast.94, bf16[16,32,128,1]{2,1,0,3:T(8,128)(2,1)S(1)} %bitcast.90), kind=kOutput, calls=%fused_computation.19 | convolution fusion | flops 35782656 | bytes 425988 | tf_op jit(solution)/shard_map/rki,kieo->rkeo/dot_general | solution.py:64
  70.2 0.9 copy.57
  71.7 4.4 %all-to-all-start.2 = ((bf16[16,64,128]{2,0,1:T(8,128)(2,1)}), bf16[16,64,128]{2,0,1:T(8,128)(2,1)}, u32[]{:S(2)}, u32[]{:S(2)}) async-start(bf16[16,64,128]{2,0,1:T(8,128)(2,1)} %copy.57), calls=%async_computation.2 | async-start | bytes 524288 | tf_op jit(solution)/shard_map/all_to_all | solution.py:81
  76.7 0.7 reduce.5
  78.2 0.8 select_bitcast_fusion
  79.0 6.1 %all-to-all-done.2 = bf16[16,64,128]{2,0,1:T(8,128)(2,1)} async-done(((bf16[16,64,128]{2,0,1:T(8,128)(2,1)}), bf16[16,64,128]{2,0,1:T(8,128)(2,1)}, u32[]{:S(2)}, u32[]{:S(2)}) %all-to-all-start.2) | async-done | bytes 262176 | tf_op jit(solution)/shard_map/all_to_all | solution.py:81
  85.1 3.8 %all-to-all-start.1 = ((bf16[16,64,128]{2,0,1:T(8,128)(2,1)}), bf16[16,64,128]{2,0,1:T(8,128)(2,1)S(1)}, u32[]{:S(2)}, u32[]{:S(2)}) async-start(bf16[16,64,128]{2,0,1:T(8,128)(2,1)} %select_bitcast_fusion), calls=%async_computation.1 | async-start | bytes 524288 | tf_op jit(solution)/shard_map/all_to_all | solution.py:102
  89.0 1.1 fusion.21
  90.7 2.5 %gather_fusion = bf16[32,16,128]{2,1,0:T(8,128)(2,1)} fusion(bf16[16,256,128]{2,0,1:T(8,128)(2,1)} %all-gather.2.cloned.1.call-done, s32[1024]{0:T(1024)S(1)} %pad_clamp_fusion.4), kind=kCustom, calls=%fused_computation | custom fusion | bytes 262272 | tf_op jit(solution)/shard_map/jit(_take)/gather | solution.py:79
  93.2 1.0 select_bitcast_fusion.1
  94.2 1.7 gather_fusion.1
  95.9 6.0 %fusion.11 = f32[192,16,128]{2,1,0:T(8,128)} fusion(bf16[192,128,128]{2,1,0:T(8,128)(2,1)} %param.18, bf16[192,16,128]{2,1,0:T(8,128)(2,1)} %gather_fusion.1, pred[192]{0:T(512)(128)(4,1)} %compare_and_fusion.4), kind=kOutput, calls=%fused_computation.22 | convolution fusion | flops 101056512 | bytes 8650944 | tf_op jit(solution)/shard_map/rta,tab->rtb/dot_general | solution.py:15
  101.9 0.8 broadcast_in_dim.80
  102.7 23.9 %scatter_fusion = f32[16,64,128]{2,0,1:T(8,128)} fusion(f32[16,64,128]{2,0,1:T(8,128)} %broadcast_in_dim.80, s32[192]{0:T(256)S(1)} %compare_select_fusion.1, f32[192,16,128]{2,1,0:T(8,128)} %fusion.11), kind=kCustom, calls=%fused_computation.5 | custom fusion | flops 393216 | bytes 4719360 | tf_op jit(solution)/shard_map/scatter-add | solution.py:17
  126.7 1.9 %copy_bitcast_fusion = f32[16,8192]{1,0:T(8,128)} fusion(f32[16,64,128]{2,0,1:T(8,128)} %scatter_fusion), kind=kLoop, calls=%fused_computation.26 | loop fusion | bytes 1048576 | tf_op jit(solution)/shard_map/reshape | solution.py:82
  129.5 2.0 %fusion.9 = f32[32,2,8,128]{3,2,1,0:T(8,128)S(1)} fusion(bf16[2]{0:T(256)(128)(2,1)} %constant.170, s32[32,128,2]{1,2,0:T(2,128)} %bitcast.93, bf16[16,32,2,128]{3,2,1,0:T(2,128)(2,1)S(1)} %bitcast.86), kind=kOutput, calls=%fused_computation.20 | convolution fusion | flops 35651584 | bytes 557060 | tf_op jit(solution)/shard_map/rkeo,kieo->rki/dot_general | solution.py:107
  131.5 27.9 %all-reduce.3.cloned.1.call-done = (f32[16,8192]{1,0:T(8,128)}, f32[16,1024]{1,0:T(8,128)}) async-done(((f32[16,8192]{1,0:T(8,128)}, f32[16,1024]{1,0:T(8,128)}), (f32[16,8192]{1,0:T(8,128)}, f32[16,1024]{1,0:T(8,128)})) %all-reduce.3.cloned.1.call-update) | async-done | bytes 589840 | tf_op jit(solution)/shard_map/psum | solution.py:94
  159.5 1.4 add_convert_fusion
  160.9 1.6 fusion.20
  (67 shorter events, 7.0 us)
Async XLA Ops:
  7.2 40.6 %copy-start = (bf16[96,128,128]{2,1,0:T(8,128)(2,1)S(1)}, bf16[96,128,128]{2,1,0:T(8,128)(2,1)}, u32[]{:S(2)}) copy-start(bf16[96,128,128]{2,1,0:T(8,128)(2,1)} %param.22) | copy-start | bytes 9437188
  7.2 64.5 %all-to-all-start = ((s32[4,1,16]{2,1,0:T(1,128)}), s32[4,1,16]{2,1,0:T(1,128)S(1)}, u32[]{:S(2)}, u32[]{:S(2)}) async-start(s32[4,1,16]{2,1,0:T(1,128)} %bitcast.92), calls=%async_computation | async-start | bytes 4096 | tf_op jit(solution)/shard_map/all_to_all | solution.py:55
  13.8 77.0 %all-gather.2.cloned.1.call-start = ((), (), s32[]{:S(2)}) async-start(), calls=%async_computation.3 | async-start | bytes 1310720 | tf_op jit(solution)/shard_map/all_gather | solution.py:73
  47.8 20.0 %copy-start.7 = (s32[32,2]{0,1:T(2,128)S(1)}, s32[32,2]{0,1:T(2,128)}, u32[]{:S(2)}) copy-start(s32[32,2]{0,1:T(2,128)} %param.27) | copy-start | bytes 772
  47.8 20.2 %copy-start.1 = (bf16[16,4096]{1,0:T(8,128)(2,1)S(1)}, bf16[16,4096]{1,0:T(8,128)(2,1)}, u32[]{:S(2)}) copy-start(bf16[16,4096]{1,0:T(8,128)(2,1)} %param.15) | copy-start | bytes 393220
  47.8 20.3 %copy-start.9 = (s32[4096,2]{0,1:T(2,128)S(1)}, s32[4096,2]{0,1:T(2,128)}, u32[]{:S(2)}) copy-start(s32[4096,2]{0,1:T(2,128)} %param.28) | copy-start | bytes 98308
  47.8 20.3 %copy-start.10 = (bf16[2]{0:T(256)(128)(2,1)S(1)}, bf16[2]{0:T(256)(128)(2,1)}, u32[]{:S(2)}) copy-start(bf16[2]{0:T(256)(128)(2,1)} %constant.170) | copy-start | bytes 16
  58.9 12.8 %copy-start.8 = (s32[192]{0:T(256)S(1)}, s32[192]{0:T(256)}, u32[]{:S(2)}) copy-start(s32[192]{0:T(256)} %param.19) | copy-start | bytes 2308
  67.8 9.7 %copy-start.2 = (bf16[16,1024]{1,0:T(8,128)(2,1)}, bf16[16,1024]{1,0:T(8,128)(2,1)S(1)}, u32[]{:S(2)}) copy-start(bf16[16,1024]{1,0:T(8,128)(2,1)S(1)} %psum.22) | copy-start | bytes 98308
  68.0 3.6 %copy-start.5 = (s32[64]{0:T(128)}, s32[64]{0:T(128)S(1)}, u32[]{:S(2)}) copy-start(s32[64]{0:T(128)S(1)} %eq.31) | copy-start | bytes 772
  71.7 13.4 %all-to-all-start.2 = ((bf16[16,64,128]{2,0,1:T(8,128)(2,1)}), bf16[16,64,128]{2,0,1:T(8,128)(2,1)}, u32[]{:S(2)}, u32[]{:S(2)}) async-start(bf16[16,64,128]{2,0,1:T(8,128)(2,1)} %copy.57), calls=%async_computation.2 | async-start | bytes 524288 | tf_op jit(solution)/shard_map/all_to_all | solution.py:81
  85.1 44.1 %all-to-all-start.1 = ((bf16[16,64,128]{2,0,1:T(8,128)(2,1)}), bf16[16,64,128]{2,0,1:T(8,128)(2,1)S(1)}, u32[]{:S(2)}, u32[]{:S(2)}) async-start(bf16[16,64,128]{2,0,1:T(8,128)(2,1)} %select_bitcast_fusion), calls=%async_computation.1 | async-start | bytes 524288 | tf_op jit(solution)/shard_map/all_to_all | solution.py:102
  89.0 70.5 %all-reduce.3.cloned.1.call-start = ((), (), s32[]{:S(2)}) async-start(), calls=%async_computation.4 | async-start | bytes 1179648 | tf_op jit(solution)/shard_map/psum | solution.py:94
  102.7 25.8 %copy-start.3 = (bf16[16,1024]{1,0:T(8,128)(2,1)S(1)}, bf16[16,1024]{1,0:T(8,128)(2,1)}, u32[]{:S(2)}) copy-start(bf16[16,1024]{1,0:T(8,128)(2,1)} %copy-done.2) | copy-start | bytes 98308
  102.7 26.5 %copy-start.6 = (s32[64]{0:T(128)S(1)}, s32[64]{0:T(128)}, u32[]{:S(2)}) copy-start(s32[64]{0:T(128)} %copy-done.5) | copy-start | bytes 772
  128.6 30.9 %copy-start.4 = (bf16[16,512]{1,0:T(8,128)(2,1)S(1)}, bf16[16,512]{1,0:T(8,128)(2,1)}, u32[]{:S(2)}) copy-start(bf16[16,512]{1,0:T(8,128)(2,1)} %param.16) | copy-start | bytes 49156
Sparse Core Ops, SparseCore 0:
  20.5 31.1 all-gather.1
  128.7 30.7 all-reduce.2
where the time goes:
time: 171 us; the launch traced here: 169 us
  other arithmetic  43.7 us (26%)
  blocking collectives  34.3 us (20%)
  waiting for transfers between devices  34.1 us (20%)
  starting transfers between devices  14.9 us (9%)
  matrix products  14.5 us (8%)
  between operations  14.3 us (8%)
  local copies, waits for them, and re-layouts  13.6 us (8%)
    scatter-add x2, other arithmetic, tile_products(): return landed.at[:, targets].add(product)  32 us
    psum x1, waiting for transfers between devices, shards(): seg_sum, end_sum, pot_sum = lax.psum((seg_part, pan_part, pot_part), 'col')  27.9 us
    all_gather x1, blocking collectives, shards(): lax.all_gather(chg_blocks, 'row', axis=1, tiled=True)  15 us
    dot_general x2, matrix products, tile_products(): jnp.einsum('rta,tab->rtb', picked, tile_set, preferred_element_type=jnp.f...  8.96 us
    psum x1, blocking collectives, shards(): seg_sum, end_sum, pot_sum = lax.psum((seg_part, pan_part, pot_part), 'col')  8.89 us
    all_to_all x1, starting transfers between devices, shards(): lax.all_to_all(link_needs, 'row', split_axis=0, concat_axis=0, tiled=True)  6.59 us
    all_to_all x1, waiting for transfers between devices, shards(): lax.all_to_all(slot_terms, 'row', split_axis=1, concat_axis=1, tiled=True)  6.14 us
    all_gather x1, blocking collectives, shards(): lax.all_gather(current, 'col', axis=1, tiled=True)  5.84 us
  transfers between devices with their start and end apart: 5, of which 2 were waited for; matrix products, arithmetic and copies ran while one was open for 41% of the time, Pallas kernels for 0%

commit v1 on v0

v1 whole, which is shorter than its diff:
```python
import functools

import jax
import jax.numpy as jnp
from jax import lax
from jax.experimental import pallas as pl
from jax.experimental.pallas import tpu as pltpu
from jax.sharding import PartitionSpec as P

F32 = jnp.float32
BF16 = jnp.bfloat16
VMEM = pl.BlockSpec(memory_space=pltpu.VMEM)
SMEM = pl.BlockSpec(memory_space=pltpu.SMEM)
ANY = pl.BlockSpec(memory_space=pl.ANY)


def shift(x, axis, k):
    n = lax.axis_size(axis)
    if k % n == 0:
        return x
    return lax.ppermute(x, axis, [(i, (i + k) % n) for i in range(n)])


def call(body, name, out_shape, in_specs, scratch=(), limit=16, flops=0, moved=0):
    return pl.pallas_call(
        body,
        out_shape=out_shape,
        in_specs=in_specs,
        out_specs=[VMEM] * len(out_shape),
        scratch_shapes=list(scratch),
        compiler_params=pltpu.CompilerParams(vmem_limit_bytes=limit * 2**20),
        cost_estimate=pl.CostEstimate(flops=flops, bytes_accessed=moved, transcendentals=0),
        name=name,
    )


def wrapped(x, n):
    return lax.rem(x + n, n)


def one_hot_rows(off_ref, k, width):
    levels = lax.broadcasted_iota(jnp.int32, (width, width), 0)
    span = pl.ds(pl.multiple_of(k * width, width), width)
    to_hot = jnp.where(levels == off_ref[0:1, span], 1.0, 0.0).astype(BF16)
    from_hot = jnp.where(levels == off_ref[1:2, span], -1.0, 0.0).astype(BF16)
    return jnp.concatenate([to_hot, from_hot], axis=0)


def ends_body(n_row, n_col, seg_own, pan_own, cap, slots, links, cur, off, own, *rest):
    sends, acc = rest[:-1], rest[-1]
    width = cur.shape[1] // seg_own
    pan_group = pan_own * n_col
    r, c = lax.axis_index("row"), lax.axis_index("col")
    acc[...] = jnp.zeros_like(acc)

    def block(k):
        span = pl.ds(pl.multiple_of(k * width, width), width)
        hot = one_hot_rows(off, k, width)
        sums = lax.dot_general(cur[:, span], hot, (((1,), (1,)), ((), ())), preferred_element_type=F32)
        return sums.astype(BF16).astype(F32)

    unroll = 4

    def step(i, carry):
        got = [block(i * unroll + u) for u in range(unroll)]
        for u in range(unroll):
            for e in range(2):
                slot = slots[e, i * unroll + u]
                p = lax.div(slot, cap)
                b = links[p, slot - p * cap]
                place = wrapped(p - r, n_row) * pan_group + b
                acc[place] += got[u][:, e * width : (e + 1) * width]
        return carry

    lax.fori_loop(0, seg_own // unroll, step, 0)
    for k in range(n_row):
        own[k] = acc[pl.ds(k * pan_group + c * pan_own, pan_own)]
        for j in range(1, n_col):
            there = lax.rem(c + j, n_col)
            sends[j - 1][k] = acc[pl.ds(k * pan_group + there * pan_own, pan_own)].astype(BF16)


def pick_body(n_row, n_col, seg_own, pan_own, cap_l, cap_p, *refs):
    asked = refs[:n_row]
    cur = refs[n_row : n_row + n_col]
    chg = refs[n_row + n_col : n_row + 2 * n_col]
    outs = refs[n_row + 2 * n_col :]
    width = cur[0].shape[1] // seg_own
    r, c = lax.axis_index("row"), lax.axis_index("col")

    def block(parts, own_blocks, b):
        owner = lax.div(b, own_blocks)
        j = wrapped(owner - c, n_col)
        span = pl.ds(pl.multiple_of((b - owner * own_blocks) * width, width), width)
        value = parts[0][:, span]
        for q in range(1, n_col):
            value = jnp.where(j == q, parts[q][:, span], value)
        return value

    for k in range(n_row):
        for s in range(cap_l):
            outs[k][s] = block(cur, seg_own, asked[k][r, s])
        for s in range(cap_p):
            outs[k][cap_l + s] = block(chg, pan_own, asked[k][r, cap_l + s])


def tile_copies(tiles, held, sems):
    chunks = sems.shape[0]
    size = tiles.shape[0] // chunks
    spans = [pl.ds(q * size, size) for q in range(chunks)]
    return [pltpu.make_async_copy(tiles.at[s], held.at[s], sems.at[q]) for q, s in enumerate(spans)]


def multiply(copies, held, src, slots, rows, acc, unroll):
    size = held.shape[0] // len(copies)
    for q, copy in enumerate(copies):
        copy.wait()

        def step(i, carry):
            at = [q * size + i * unroll + u for u in range(unroll)]
            got = [jnp.dot(src[slots[t]], held[t], preferred_element_type=F32) for t in at]
            for t, value in zip(at, got):
                acc[rows[t]] += value
            return carry

        lax.fori_loop(0, size // unroll, step, 0)


def coeff_body(n_row, n_col, cap_l, cap_p, slots, rows, *refs):
    got = refs[:n_row]
    ends_own = refs[n_row]
    ends_in = refs[n_row + 1 : n_row + n_col]
    tiles = refs[n_row + n_col]
    part, end_keep, *end_sends = refs[n_row + n_col + 1 : -3]
    src, held, sems = refs[-3:]
    r = lax.axis_index("row")
    copies = tile_copies(tiles, held, sems)
    for copy in copies:
        copy.start()
    for k in range(n_row):
        src[pl.ds(lax.rem(r + k, n_row) * cap_p, cap_p)] = got[k][pl.ds(cap_l, cap_p)]
        total = ends_own[k]
        for more in ends_in:
            total += more[k].astype(F32)
        if k == 0:
            end_keep[...] = total
        else:
            end_sends[k - 1][...] = total.astype(BF16)
    part[...] = jnp.zeros_like(part)
    multiply(copies, held, src, slots, rows, part, 8)


def induct_body(n_row, n_col, seg_own, cap_l, slots, rows, *refs):
    got = refs[:n_row]
    tiles = refs[n_row]
    own, *sends = refs[n_row + 1 : -4]
    src, held, acc, sems = refs[-4:]
    r, c = lax.axis_index("row"), lax.axis_index("col")
    copies = tile_copies(tiles, held, sems)
    for copy in copies:
        copy.start()
    for k in range(n_row):
        src[pl.ds(lax.rem(r + k, n_row) * cap_l, cap_l)] = got[k][pl.ds(0, cap_l)]
    acc[...] = jnp.zeros_like(acc)
    multiply(copies, held, src, slots, rows, acc, 8)
    own[...] = acc[pl.ds(c * seg_own, seg_own)]
    for j in range(1, n_col):
        sends[j - 1][...] = acc[pl.ds(lax.rem(c + j, n_col) * seg_own, seg_own)].astype(BF16)


def final_body(n_row, n_col, seg_own, pan_own, cap, slots, links, off, charge, scale, *refs):
    field_own, end_own = refs[0], refs[1]
    field_in = refs[2 : 1 + n_col]
    end_in = refs[1 + n_col : n_col + n_row]
    pots = refs[n_col + n_row : n_col + 2 * n_row]
    seg_out, pan_out, pot_out, held = refs[n_col + 2 * n_row :]
    width = charge.shape[1] // pan_own
    pan_group = pan_own * n_col
    r, c = lax.axis_index("row"), lax.axis_index("col")
    for k in range(n_row):
        held[pl.ds(lax.rem(r + k, n_row) * pan_group, pan_group)] = pots[k][...]
    for q in range(pan_own):
        span = slice(q * width, (q + 1) * width)
        total = end_own[q]
        for more in end_in:
            total += more[q].astype(F32)
        pan_out[:, span] = (scale[...] * charge[:, span].astype(F32) + total).astype(BF16)
        pot_out[:, span] = pots[0][c * pan_own + q]

    def block(k):
        ends = []
        for e in range(2):
            slot = slots[e, k]
            p = lax.div(slot, cap)
            ends.append(held[p * pan_group + links[p, slot - p * cap]])
        drops = jnp.dot(
            jnp.concatenate(ends, axis=1), one_hot_rows(off, k, width), preferred_element_type=F32
        )
        total = field_own[k]
        for more in field_in:
            total += more[k].astype(F32)
        return (total + drops).astype(BF16)

    unroll = 4

    def step(i, carry):
        for u in range(unroll):
            k = i * unroll + u
            seg_out[:, pl.ds(pl.multiple_of(k * width, width), width)] = block(k)
        return carry

    lax.fori_loop(0, seg_own // unroll, step, 0)


def shards(
    current,
    charge,
    rhs_scale,
    induct_tiles,
    induct_rows,
    induct_slots,
    induct_needs,
    coeff_tiles,
    coeff_rows,
    coeff_slots,
    coeff_needs,
    link_needs,
    end_slots,
    end_offsets,
):
    n_row = lax.axis_size("row")
    n_col = lax.axis_size("col")
    width = induct_tiles.shape[1]
    rhs = current.shape[0]
    seg_own = current.shape[1] // width
    pan_own = charge.shape[1] // width
    seg_group, pan_group = seg_own * n_col, pan_own * n_col
    cap_l, cap_p, cap_k = induct_needs.shape[1], coeff_needs.shape[1], link_needs.shape[1]
    slots_t, off_t = end_slots.T, end_offsets.T

    def like(blocks, dtype):
        return jax.ShapeDtypeStruct((*blocks, rhs, width), dtype)

    needs = jnp.concatenate([induct_needs, coeff_needs], axis=1)
    asked = [shift(needs, "row", k) for k in range(n_row)]
    cur = [shift(current, "col", -j) for j in range(n_col)]
    chg = [shift(charge, "col", -j) for j in range(n_col)]

    ends_own, *ends_out = call(
        functools.partial(ends_body, n_row, n_col, seg_own, pan_own, cap_k),
        "end_sums",
        [like((n_row, pan_own), F32)] + [like((n_row, pan_own), BF16)] * (n_col - 1),
        [SMEM, SMEM, VMEM, VMEM],
        [pltpu.VMEM((n_row * pan_group, rhs, width), F32)],
        flops=2 * 10**9,
        moved=2**18,
    )(slots_t, link_needs, current, off_t)

    picked = call(
        functools.partial(pick_body, n_row, n_col, seg_own, pan_own, cap_l, cap_p),
        "pick_blocks",
        [like((cap_l + cap_p,), BF16)] * n_row,
        [SMEM] * n_row + [VMEM] * (2 * n_col),
        moved=2**20,
    )(*asked, *cur, *chg)
    got = [shift(x, "row", -k) for k, x in enumerate(picked)]
    ends_in = [shift(x, "col", j + 1) for j, x in enumerate(ends_out)]

    pt = coeff_tiles.shape[0]
    part, end_keep, *end_sends = call(
        functools.partial(coeff_body, n_row, n_col, cap_l, cap_p),
        "coeff_tiles",
        [like((pan_group,), F32), like((pan_own,), F32)] + [like((pan_own,), BF16)] * (n_row - 1),
        [SMEM, SMEM] + [VMEM] * (n_row + n_col) + [ANY],
        [
            pltpu.VMEM((n_row * cap_p, rhs, width), BF16),
            pltpu.VMEM(coeff_tiles.shape, BF16),
            pltpu.SemaphoreType.DMA((4,)),
        ],
        flops=2 * 10**9,
        moved=coeff_tiles.size * 2,
    )(coeff_slots, coeff_rows, *got, ends_own, *ends_in, coeff_tiles)
    parts = [shift(part, "col", j) for j in range(n_col)]
    end_in = [shift(x, "row", k + 1) for k, x in enumerate(end_sends)]

    field_own, *field_out = call(
        functools.partial(induct_body, n_row, n_col, seg_own, cap_l),
        "induct_tiles",
        [like((seg_own,), F32)] + [like((seg_own,), BF16)] * (n_col - 1),
        [SMEM, SMEM] + [VMEM] * n_row + [ANY],
        [
            pltpu.VMEM((n_row * cap_l, rhs, width), BF16),
            pltpu.VMEM(induct_tiles.shape, BF16),
            pltpu.VMEM((seg_group, rhs, width), F32),
            pltpu.SemaphoreType.DMA((8,)),
        ],
        flops=4 * 10**9,
        moved=induct_tiles.size * 2,
    )(induct_slots, induct_rows, *got, induct_tiles)
    field_in = [shift(x, "col", j + 1) for j, x in enumerate(field_out)]

    potential = parts[0]
    for more in parts[1:]:
        potential = potential + more
    potential = potential.astype(BF16)
    pots = [shift(potential, "row", -k) for k in range(n_row)]

    return tuple(
        call(
            functools.partial(final_body, n_row, n_col, seg_own, pan_own, cap_k),
            "outputs",
            [jax.ShapeDtypeStruct(x.shape, BF16) for x in (current, charge, charge)],
            [SMEM, SMEM] + [VMEM] * (3 + n_col + 2 * n_row),
            [pltpu.VMEM((n_row * pan_group, rhs, width), BF16)],
            flops=2 * 10**9,
            moved=2**20,
        )(
            slots_t,
            link_needs,
            off_t,
            charge,
            rhs_scale[:, None],
            field_own,
            end_keep,
            *field_in,
            *end_in,
            *pots,
        )
    )


def solution(mesh):
    blocks = P(("parts", "row", "col"))
    matrix = P(("parts", "row", "col"), None)
    tiles = P(("parts", "row", "col"), None, None)
    values = P("rhs", ("parts", "row", "col"))
    return jax.shard_map(
        shards,
        mesh=mesh,
        in_specs=(
            values,
            values,
            P(("parts", "rhs")),
            tiles,
            blocks,
            blocks,
            matrix,
            tiles,
            blocks,
            blocks,
            matrix,
            matrix,
            matrix,
            matrix,
        ),
        out_specs=(values, values, values),
        check_vma=False,
    )
```

time: 171 us -> 57.1 us (0.33)
  other arithmetic: 43.7 us -> 0.77 us
  blocking collectives: 34.3 us -> 0 us
  waiting for transfers between devices: 34.1 us -> 10.1 us
  Pallas kernels: 0 us -> 14.7 us
  matrix products: 14.5 us -> 0 us
  between operations: 14.3 us -> 0.79 us
  starting transfers between devices: 14.9 us -> 27.3 us
  local copies, waits for them, and re-layouts: 13.6 us -> 3.16 us
    scatter-add x2 -> x0, other arithmetic: 32 us -> none  [tile_products(): return landed.at[:, targets].add(product)]
    psum x1 -> x0, waiting for transfers between devices: 27.9 us -> none  [shards(): seg_sum, end_sum, pot_sum = lax.psum((seg_part, pan_part, pot_part), 'col')]
    ppermute x0 -> x17, starting transfers between devices: none -> 27.3 us  [shift(): return lax.ppermute(x, axis, [(i, (i + k) % n) for i in range(n)])]
    all_gather x3 -> x0, blocking collectives: 25.4 us -> none  [the longest x1 15 us: shards(): lax.all_gather(chg_blocks, 'row', axis=1, tiled=True)]
    all_to_all x3 -> x0, starting transfers between devices: 14.9 us -> none  [the longest x1 6.59 us: shards(): lax.all_to_all(link_needs, 'row', split_axis=0, concat_axis=0, tiled=True)]
    pallas_call x0 -> x5, Pallas kernels: none -> 14.7 us  [the longest x1 5.67 us: shards(): call(functools.partial(induct_body, n_row, n_col, seg_own, cap_l), 'induc...]
    dot_general x7 -> x0, matrix products: 14.5 us -> none  [the longest x2 8.96 us: tile_products(): jnp.einsum('rta,tab->rtb', picked, tile_set, preferred_element_type=jnp.f...]
    ppermute x0 -> x17, waiting for transfers between devices: none -> 10.1 us  [shift(): return lax.ppermute(x, axis, [(i, (i + k) % n) for i in range(n)])]
  transfers between devices with their start and end apart: 5 -> 17, of which waited for: 2 -> 7; matrix products, arithmetic and copies ran while one was open for 41% -> 1% of each run, Pallas kernels for 0% -> 16%
where the time goes in v1:
time: 57.1 us; the launch traced here: 56.8 us
  starting transfers between devices  27.3 us (48%)
  Pallas kernels  14.7 us (26%)
  waiting for transfers between devices  10.1 us (18%)
  local copies, waits for them, and re-layouts  3.16 us (6%)
  between operations  0.79 us (1%)
  other arithmetic  0.77 us (1%)
    ppermute x17, starting transfers between devices, shift(): return lax.ppermute(x, axis, [(i, (i + k) % n) for i in range(n)])  27.3 us
    ppermute x17, waiting for transfers between devices, shift(): return lax.ppermute(x, axis, [(i, (i + k) % n) for i in range(n)])  10.1 us
    pallas_call x1, Pallas kernels, shards(): call(functools.partial(induct_body, n_row, n_col, seg_own, cap_l), 'induc...  5.67 us
    pallas_call x1, Pallas kernels, shards(): call(functools.partial(coeff_body, n_row, n_col, cap_l, cap_p), 'coeff_ti...  3.1 us
    unnamed x36, local copies, waits for them, and re-layouts  3.08 us
    pallas_call x1, Pallas kernels, shards(): call(functools.partial(final_body, n_row, n_col, seg_own, pan_own, cap_k)...  2.7 us
    pallas_call x1, Pallas kernels, shards(): call(functools.partial(ends_body, n_row, n_col, seg_own, pan_own, cap_k),...  2.26 us
  transfers between devices with their start and end apart: 17, of which 7 were waited for; matrix products, arithmetic and copies ran while one was open for 1% of the time, Pallas kernels for 16%

profile of v1, /device:TPU:0, one launch (start us, length us, event | category | flops | bytes accessed | tf_op | source)
XLA Modules:
  0.0 56.8 jit_solution(9026057769151552594)
XLA Ops:
  0.7 3.0 %collective-permute-start.3 = (bf16[16,4096]{1,0:T(8,128)(2,1)}, bf16[16,4096]{1,0:T(8,128)(2,1)S(1)}, u32[]{:S(2)}, u32[]{:S(2)}) collective-permute-start(bf16[16,4096]{1,0:T(8,128)(2,1)} %cur.1), channel_id=1, source_target_pairs={{0,2},{2,0},{1,3},{3,1},{4,6},{6,4},{5,7},{7,5},{8,10},{10,8},{9,1... | collective-permute-start | bytes 393224 | tf_op jit(solution)/shard_map/ppermute | solution.py:21
  3.7 0.1 collective-permute-start.4
  3.7 0.9 %copy-done = bf16[16,4096]{1,0:T(8,128)(2,1)S(1)} copy-done((bf16[16,4096]{1,0:T(8,128)(2,1)S(1)}, bf16[16,4096]{1,0:T(8,128)(2,1)}, u32[]{:S(2)}) %copy-start) | copy-done | bytes 131096
  4.7 0.8 %copy-done.4 = s32[4096,2]{0,1:T(2,128)S(1)} copy-done((s32[4096,2]{0,1:T(2,128)S(1)}, s32[4096,2]{0,1:T(2,128)}, u32[]{:S(2)}) %copy-start.4) | copy-done | bytes 32792
  5.4 0.7 %copy-done.6 = s32[4,16]{1,0:T(4,128)S(1)} copy-done((s32[4,16]{1,0:T(4,128)S(1)}, s32[4,16]{1,0:T(4,128)}, u32[]{:S(2)}) %copy-start.6) | copy-done | bytes 280
  6.1 0.7 %copy-done.10 = s32[32,2]{0,1:T(2,128)S(1)} copy-done((s32[32,2]{0,1:T(2,128)S(1)}, s32[32,2]{0,1:T(2,128)}, u32[]{:S(2)}) %copy-start.10) | copy-done | bytes 280
  6.8 2.3 %end_sums.1 = (f32[4,4,16,128]{3,2,1,0:T(8,128)S(1)}, bf16[4,4,16,128]{3,2,1,0:T(8,128)(2,1)S(1)}) custom-call(s32[2,32]{1,0:T(2,128)S(1)} %bitcast.7, s32[4,16]{1,0:T(4,128)S(1)} %copy-done.6, bf16[16,4096]{1,0:T(8,128)(2,1)S(1)} %copy-done, s32[2,4096]{1,0:T(2,128)S(1)} %bitcast.5), custom_call_target="tpu_custom_call" | custom-call | flops 2000000000 | bytes 262144 | tf_op jit(solution)/shard_map/end_sums/pallas_call | solution.py:249
  9.1 2.0 %collective-permute-start.8 = (bf16[4,4,16,128]{3,2,1,0:T(8,128)(2,1)S(1)}, bf16[4,4,16,128]{3,2,1,0:T(8,128)(2,1)S(1)}, u32[]{:S(2)}, u32[]{:S(2)}) collective-permute-start(bf16[4,4,16,128]{3,2,1,0:T(8,128)(2,1)S(1)} %get-tuple-element.22), channel_id=1, source_target_pairs={{0,2},{2,0},{1,3},{3,1},{4,6},{6,4},{5,7},{7,5},{8,10},{10,8},{9,1... | collective-permute-start | bytes 196616 | tf_op jit(solution)/shard_map/ppermute | solution.py:21
  11.1 0.8 %pad_add_fusion.refs_0_ = s32[4,12]{1,0:T(4,128)S(1)} fusion(s32[4,4]{1,0:T(4,128)S(1)} %copy-done.14, s32[4,8]{1,0:T(4,128)} %param.20), kind=kLoop, calls=%fused_computation.1 | loop fusion | flops 48 | bytes 384 | tf_op jit(solution)/shard_map/concatenate | solution.py:244
  11.8 1.6 %collective-permute-start = (s32[4,12]{1,0:T(4,128)S(1)}, s32[4,12]{1,0:T(4,128)S(1)}, u32[]{:S(2)}, u32[]{:S(2)}) collective-permute-start(s32[4,12]{1,0:T(4,128)S(1)} %pad_add_fusion.refs_0_), channel_id=1, source_target_pairs={{0,4},{4,8},{8,12},{12,0},{1,5},{5,9},{9,13},{13,1},{2,6},{6,10},{... | collective-permute-start | bytes 584 | tf_op jit(solution)/shard_map/ppermute | solution.py:21
  13.4 2.6 %collective-permute-start.1 = (s32[4,12]{1,0:T(4,128)S(1)}, s32[4,12]{1,0:T(4,128)S(1)}, u32[]{:S(2)}, u32[]{:S(2)}) collective-permute-start(s32[4,12]{1,0:T(4,128)S(1)} %pad_add_fusion.refs_0_), channel_id=1, source_target_pairs={{0,8},{4,12},{8,0},{12,4},{1,9},{5,13},{9,1},{13,5},{2,10},{6,14},... | collective-permute-start | bytes 584 | tf_op jit(solution)/shard_map/ppermute | solution.py:21
  16.0 1.2 %collective-permute-done.refs_1_ = s32[4,12]{1,0:T(4,128)S(1)} collective-permute-done((s32[4,12]{1,0:T(4,128)S(1)}, s32[4,12]{1,0:T(4,128)S(1)}, u32[]{:S(2)}, u32[]{:S(2)}) %collective-permute-start) | collective-permute-done | bytes 224 | tf_op jit(solution)/shard_map/ppermute | solution.py:21
  17.2 1.8 %collective-permute-start.2 = (s32[4,12]{1,0:T(4,128)S(1)}, s32[4,12]{1,0:T(4,128)S(1)}, u32[]{:S(2)}, u32[]{:S(2)}) collective-permute-start(s32[4,12]{1,0:T(4,128)S(1)} %pad_add_fusion.refs_0_), channel_id=1, source_target_pairs={{0,12},{4,0},{8,4},{12,8},{1,13},{5,1},{9,5},{13,9},{2,14},{6,2},{... | collective-permute-start | bytes 584 | tf_op jit(solution)/shard_map/ppermute | solution.py:21
  19.0 1.8 %collective-permute-done.2.refs_3_ = s32[4,12]{1,0:T(4,128)S(1)} collective-permute-done((s32[4,12]{1,0:T(4,128)S(1)}, s32[4,12]{1,0:T(4,128)S(1)}, u32[]{:S(2)}, u32[]{:S(2)}) %collective-permute-start.2) | collective-permute-done | bytes 224 | tf_op jit(solution)/shard_map/ppermute | solution.py:21
  20.8 1.0 %pick_blocks.1 = (bf16[12,16,128]{2,1,0:T(8,128)(2,1)S(1)}, bf16[12,16,128]{2,1,0:T(8,128)(2,1)S(1)}, bf16[12,16,128]{2,1,0:T(8,128)(2,1)S(1)}, bf16[12,16,128]{2,1,0:T(8,128)(2,1)S(1)}) custom-call(s32[4,12]{1,0:T(4,128)S(1)} %pad_add_fusion.refs_0_, s32[4,12]{1,0:T(4,128)S(1)} %collective-permute-done.refs_1_, s32[4,12]{1,0:T(4,128)S(1)} %collective-permute-done.1.refs_2_, ...), custom_call_target="tpu_custom_call" | custom-call | bytes 1048576 | tf_op jit(solution)/shard_map/pick_blocks/pallas_call | solution.py:259
  21.8 3.6 %collective-permute-start.5 = (bf16[12,16,128]{2,1,0:T(8,128)(2,1)S(1)}, bf16[12,16,128]{2,1,0:T(8,128)(2,1)S(1)}, u32[]{:S(2)}, u32[]{:S(2)}) collective-permute-start(bf16[12,16,128]{2,1,0:T(8,128)(2,1)S(1)} %get-tuple-element.17), channel_id=1, source_target_pairs={{0,12},{4,0},{8,4},{12,8},{1,13},{5,1},{9,5},{13,9},{2,14},{6,2},{... | collective-permute-start | bytes 147464 | tf_op jit(solution)/shard_map/ppermute | solution.py:21
  25.5 0.6 %collective-permute-start.7 = (bf16[12,16,128]{2,1,0:T(8,128)(2,1)S(1)}, bf16[12,16,128]{2,1,0:T(8,128)(2,1)S(1)}, u32[]{:S(2)}, u32[]{:S(2)}) collective-permute-start(bf16[12,16,128]{2,1,0:T(8,128)(2,1)S(1)} %get-tuple-element.19), channel_id=1, source_target_pairs={{0,4},{4,8},{8,12},{12,0},{1,5},{5,9},{9,13},{13,1},{2,6},{6,10},{... | collective-permute-start | bytes 147464 | tf_op jit(solution)/shard_map/ppermute | solution.py:21
  26.1 1.1 %collective-permute-done.5.refs_1_ = bf16[12,16,128]{2,1,0:T(8,128)(2,1)S(1)} collective-permute-done((bf16[12,16,128]{2,1,0:T(8,128)(2,1)S(1)}, bf16[12,16,128]{2,1,0:T(8,128)(2,1)S(1)}, u32[]{:S(2)}, u32[]{:S(2)}) %collective-permute-start.5) | collective-permute-done | bytes 49184 | tf_op jit(solution)/shard_map/ppermute | solution.py:21
  27.2 3.2 %collective-permute-done.6.refs_2_ = bf16[12,16,128]{2,1,0:T(8,128)(2,1)S(1)} collective-permute-done((bf16[12,16,128]{2,1,0:T(8,128)(2,1)S(1)}, bf16[12,16,128]{2,1,0:T(8,128)(2,1)S(1)}, u32[]{:S(2)}, u32[]{:S(2)}) %collective-permute-start.6) | collective-permute-done | bytes 49184 | tf_op jit(solution)/shard_map/ppermute | solution.py:21
  30.5 0.9 %collective-permute-done.7.refs_3_ = bf16[12,16,128]{2,1,0:T(8,128)(2,1)S(1)} collective-permute-done((bf16[12,16,128]{2,1,0:T(8,128)(2,1)S(1)}, bf16[12,16,128]{2,1,0:T(8,128)(2,1)S(1)}, u32[]{:S(2)}, u32[]{:S(2)}) %collective-permute-start.7) | collective-permute-done | bytes 49184 | tf_op jit(solution)/shard_map/ppermute | solution.py:21
  31.4 3.1 %coeff_tiles.1 = (f32[8,16,128]{2,1,0:T(8,128)S(1)}, f32[4,16,128]{2,1,0:T(8,128)S(1)}, bf16[4,16,128]{2,1,0:T(8,128)(2,1)S(1)}, bf16[4,16,128]{2,1,0:T(8,128)(2,1)S(1)}, bf16[4,16,128]{2,1,0:T(8,128)(2,1)S(1)}) custom-call(s32[96]{0:T(128)S(1)} %copy-done.12, s32[96]{0:T(128)S(1)} %copy-done.13, bf16[12,16,128]{2,1,0:T(8,128)(2,1)S(1)} %get-tuple-element.16.refs_0_, ...), custom_call_target="tpu_custom_call" | custom-call | flops 2000000000 | bytes 3145728 | tf_op jit(solution)/shard_map/coeff_tiles/pallas_call | solution.py:270
  34.5 0.6 %collective-permute-start.13 = (f32[8,16,128]{2,1,0:T(8,128)S(1)}, f32[8,16,128]{2,1,0:T(8,128)S(1)}, u32[]{:S(2)}, u32[]{:S(2)}) collective-permute-start(f32[8,16,128]{2,1,0:T(8,128)S(1)} %get-tuple-element.28), channel_id=1, source_target_pairs={{0,2},{2,0},{1,3},{3,1},{4,6},{6,4},{5,7},{7,5},{8,10},{10,8},{9,1... | collective-permute-start | bytes 196616 | tf_op jit(solution)/shard_map/ppermute | solution.py:21
  35.1 1.2 %collective-permute-start.11 = (bf16[4,16,128]{2,1,0:T(8,128)(2,1)S(1)}, bf16[4,16,128]{2,1,0:T(8,128)(2,1)S(1)}, u32[]{:S(2)}, u32[]{:S(2)}) collective-permute-start(bf16[4,16,128]{2,1,0:T(8,128)(2,1)S(1)} %get-tuple-element.26), channel_id=1, source_target_pairs={{0,8},{4,12},{8,0},{12,4},{1,9},{5,13},{9,1},{13,5},{2,10},{6,14},... | collective-permute-start | bytes 49160 | tf_op jit(solution)/shard_map/ppermute | solution.py:21
  36.4 5.7 %induct_tiles.1 = (f32[32,16,128]{2,1,0:T(8,128)S(1)}, bf16[32,16,128]{2,1,0:T(8,128)(2,1)S(1)}) custom-call(s32[192]{0:T(256)S(1)} %copy-done.8, s32[192]{0:T(256)S(1)} %copy-done.9, bf16[12,16,128]{2,1,0:T(8,128)(2,1)S(1)} %get-tuple-element.16.refs_0_, bf16[12,16,128]{2,1,0:T(8,128)(2,1)S(1)} %collective-permute-done.5.refs_1_, ...), custom_call_target="tpu_custom_call" | custom-call | flops 4000000000 | bytes 6291456 | tf_op jit(solution)/shard_map/induct_tiles/pallas_call | solution.py:286
  42.0 1.5 %collective-permute-start.9 = (bf16[32,16,128]{2,1,0:T(8,128)(2,1)S(1)}, bf16[32,16,128]{2,1,0:T(8,128)(2,1)S(1)}, u32[]{:S(2)}, u32[]{:S(2)}) collective-permute-start(bf16[32,16,128]{2,1,0:T(8,128)(2,1)S(1)} %get-tuple-element.24), channel_id=1, source_target_pairs={{0,2},{2,0},{1,3},{3,1},{4,6},{6,4},{5,7},{7,5},{8,10},{10,8},{9,1... | collective-permute-start | bytes 393224 | tf_op jit(solution)/shard_map/ppermute | solution.py:21
  43.6 3.0 %collective-permute-start.14 = (bf16[8,16,128]{2,1,0:T(8,128)(2,1)S(1)}, bf16[8,16,128]{2,1,0:T(8,128)(2,1)S(1)}, u32[]{:S(2)}, u32[]{:S(2)}) collective-permute-start(bf16[8,16,128]{2,1,0:T(8,128)(2,1)S(1)} %add_convert_fusion.refs_6_), channel_id=1, source_target_pairs={{0,12},{4,0},{8,4},{12,8},{1,13},{5,1},{9,5},{13,9},{2,14},{6,2},{... | collective-permute-start | bytes 98312 | tf_op jit(solution)/shard_map/ppermute | solution.py:21
  46.6 1.8 %collective-permute-start.15 = (bf16[8,16,128]{2,1,0:T(8,128)(2,1)S(1)}, bf16[8,16,128]{2,1,0:T(8,128)(2,1)S(1)}, u32[]{:S(2)}, u32[]{:S(2)}) collective-permute-start(bf16[8,16,128]{2,1,0:T(8,128)(2,1)S(1)} %add_convert_fusion.refs_6_), channel_id=1, source_target_pairs={{0,8},{4,12},{8,0},{12,4},{1,9},{5,13},{9,1},{13,5},{2,10},{6,14},... | collective-permute-start | bytes 98312 | tf_op jit(solution)/shard_map/ppermute | solution.py:21
  48.4 3.8 %collective-permute-start.12 = (bf16[4,16,128]{2,1,0:T(8,128)(2,1)S(1)}, bf16[4,16,128]{2,1,0:T(8,128)(2,1)S(1)}, u32[]{:S(2)}, u32[]{:S(2)}) collective-permute-start(bf16[4,16,128]{2,1,0:T(8,128)(2,1)S(1)} %get-tuple-element.27), channel_id=1, source_target_pairs={{0,12},{4,0},{8,4},{12,8},{1,13},{5,1},{9,5},{13,9},{2,14},{6,2},{... | collective-permute-start | bytes 49160 | tf_op jit(solution)/shard_map/ppermute | solution.py:21
  52.2 0.1 copy.17.scale
  52.3 1.4 %collective-permute-done.12.refs_5_ = bf16[4,16,128]{2,1,0:T(8,128)(2,1)S(1)} collective-permute-done((bf16[4,16,128]{2,1,0:T(8,128)(2,1)S(1)}, bf16[4,16,128]{2,1,0:T(8,128)(2,1)S(1)}, u32[]{:S(2)}, u32[]{:S(2)}) %collective-permute-start.12) | collective-permute-done | bytes 16416 | tf_op jit(solution)/shard_map/ppermute | solution.py:21
  53.6 0.4 collective-permute-done.16.refs_9_
  54.1 2.7 %outputs.1 = (bf16[16,4096]{1,0:T(8,128)(2,1)}, bf16[16,512]{1,0:T(8,128)(2,1)}, bf16[16,512]{1,0:T(8,128)(2,1)}) custom-call(s32[2,32]{1,0:T(2,128)S(1)} %bitcast.8, s32[4,16]{1,0:T(4,128)S(1)} %copy-done.7, s32[2,4096]{1,0:T(2,128)S(1)} %bitcast.6, bf16[16,512]{1,0:T(8,128)(2,1)S(1)} %copy-done.2, f32[16,1]{1,0:T(8,128)S(1)} %copy.17.scale, ...), custom_call_target="tpu_custom_call" | custom-call | flops 2000000000 | bytes 1048576 | tf_op jit(solution)/shard_map/outputs/pallas_call | solution.py:309
  (47 shorter events, 0.1 us)
Async XLA Ops:
  0.6 10.4 %copy-start.14 = (s32[4,4]{1,0:T(4,128)S(1)}, s32[4,4]{1,0:T(4,128)}, u32[]{:S(2)}) copy-start(s32[4,4]{1,0:T(4,128)} %param.24) | copy-start | bytes 196
  0.6 30.7 %copy-start.13 = (s32[96]{0:T(128)S(1)}, s32[96]{0:T(128)}, u32[]{:S(2)}) copy-start(s32[96]{0:T(128)} %rows.3) | copy-start | bytes 1156
  0.7 30.7 %copy-start.12 = (s32[96]{0:T(128)S(1)}, s32[96]{0:T(128)}, u32[]{:S(2)}) copy-start(s32[96]{0:T(128)} %slots.3) | copy-start | bytes 1156
  0.7 20.2 %collective-permute-start.3 = (bf16[16,4096]{1,0:T(8,128)(2,1)}, bf16[16,4096]{1,0:T(8,128)(2,1)S(1)}, u32[]{:S(2)}, u32[]{:S(2)}) collective-permute-start(bf16[16,4096]{1,0:T(8,128)(2,1)} %cur.1), channel_id=1, source_target_pairs={{0,2},{2,0},{1,3},{3,1},{4,6},{6,4},{5,7},{7,5},{8,10},{10,8},{9,1... | collective-permute-start | bytes 393224 | tf_op jit(solution)/shard_map/ppermute | solution.py:21
  3.7 17.1 %collective-permute-start.4 = (bf16[16,512]{1,0:T(8,128)(2,1)}, bf16[16,512]{1,0:T(8,128)(2,1)S(1)}, u32[]{:S(2)}, u32[]{:S(2)}) collective-permute-start(bf16[16,512]{1,0:T(8,128)(2,1)} %charge.1), channel_id=1, source_target_pairs={{0,2},{2,0},{1,3},{3,1},{4,6},{6,4},{5,7},{7,5},{8,10},{10,8},{9,1... | collective-permute-start | bytes 49160 | tf_op jit(solution)/shard_map/ppermute | solution.py:21
  3.7 0.9 %copy-start = (bf16[16,4096]{1,0:T(8,128)(2,1)S(1)}, bf16[16,4096]{1,0:T(8,128)(2,1)}, u32[]{:S(2)}) copy-start(bf16[16,4096]{1,0:T(8,128)(2,1)} %cur.1) | copy-start | bytes 393220
  6.8 14.0 %copy-start.1 = (bf16[16,4096]{1,0:T(8,128)(2,1)S(1)}, bf16[16,4096]{1,0:T(8,128)(2,1)}, u32[]{:S(2)}) copy-start(bf16[16,4096]{1,0:T(8,128)(2,1)} %cur.1) | copy-start | bytes 393220
  6.8 14.1 %copy-start.2 = (bf16[16,512]{1,0:T(8,128)(2,1)S(1)}, bf16[16,512]{1,0:T(8,128)(2,1)}, u32[]{:S(2)}) copy-start(bf16[16,512]{1,0:T(8,128)(2,1)} %charge.1) | copy-start | bytes 49156
  6.8 24.6 %copy-start.3 = (bf16[96,128,128]{2,1,0:T(8,128)(2,1)S(1)}, bf16[96,128,128]{2,1,0:T(8,128)(2,1)}, u32[]{:S(2)}) copy-start(bf16[96,128,128]{2,1,0:T(8,128)(2,1)} %refs_6_.3) | copy-start | bytes 9437188
  6.8 29.6 %slice-start = ((s8[6291456]{0:T(1024)(128)(4,1)}), s8[4194304]{0:T(1024)(128)(4,1)S(1)}, s32[]{:S(2)}) async-start(s8[6291456]{0:T(1024)(128)(4,1)} %bitcast.3), calls=%async_computation | async-start | bytes 8388608
  6.8 29.6 %copy-start.8 = (s32[192]{0:T(256)S(1)}, s32[192]{0:T(256)}, u32[]{:S(2)}) copy-start(s32[192]{0:T(256)} %slots.2) | copy-start | bytes 2308
  6.8 29.6 %copy-start.9 = (s32[192]{0:T(256)S(1)}, s32[192]{0:T(256)}, u32[]{:S(2)}) copy-start(s32[192]{0:T(256)} %rows.2) | copy-start | bytes 2308
  9.1 17.1 %collective-permute-start.8 = (bf16[4,4,16,128]{3,2,1,0:T(8,128)(2,1)S(1)}, bf16[4,4,16,128]{3,2,1,0:T(8,128)(2,1)S(1)}, u32[]{:S(2)}, u32[]{:S(2)}) collective-permute-start(bf16[4,4,16,128]{3,2,1,0:T(8,128)(2,1)S(1)} %get-tuple-element.22), channel_id=1, source_target_pairs={{0,2},{2,0},{1,3},{3,1},{4,6},{6,4},{5,7},{7,5},{8,10},{10,8},{9,1... | collective-permute-start | bytes 196616 | tf_op jit(solution)/shard_map/ppermute | solution.py:21
  11.8 24.5 %slice-start.1 = ((s8[6291456]{0:T(1024)(128)(4,1)}), s8[2097152]{0:T(1024)(128)(4,1)S(1)}, s32[]{:S(2)}) async-start(s8[6291456]{0:T(1024)(128)(4,1)} %bitcast.3), calls=%async_computation.1 | async-start | bytes 4194304
  11.8 5.4 %collective-permute-start = (s32[4,12]{1,0:T(4,128)S(1)}, s32[4,12]{1,0:T(4,128)S(1)}, u32[]{:S(2)}, u32[]{:S(2)}) collective-permute-start(s32[4,12]{1,0:T(4,128)S(1)} %pad_add_fusion.refs_0_), channel_id=1, source_target_pairs={{0,4},{4,8},{8,12},{12,0},{1,5},{5,9},{9,13},{13,1},{2,6},{6,10},{... | collective-permute-start | bytes 584 | tf_op jit(solution)/shard_map/ppermute | solution.py:21
  13.4 5.6 %collective-permute-start.1 = (s32[4,12]{1,0:T(4,128)S(1)}, s32[4,12]{1,0:T(4,128)S(1)}, u32[]{:S(2)}, u32[]{:S(2)}) collective-permute-start(s32[4,12]{1,0:T(4,128)S(1)} %pad_add_fusion.refs_0_), channel_id=1, source_target_pairs={{0,8},{4,12},{8,0},{12,4},{1,9},{5,13},{9,1},{13,5},{2,10},{6,14},... | collective-permute-start | bytes 584 | tf_op jit(solution)/shard_map/ppermute | solution.py:21
  17.2 3.6 %collective-permute-start.2 = (s32[4,12]{1,0:T(4,128)S(1)}, s32[4,12]{1,0:T(4,128)S(1)}, u32[]{:S(2)}, u32[]{:S(2)}) collective-permute-start(s32[4,12]{1,0:T(4,128)S(1)} %pad_add_fusion.refs_0_), channel_id=1, source_target_pairs={{0,12},{4,0},{8,4},{12,8},{1,13},{5,1},{9,5},{13,9},{2,14},{6,2},{... | collective-permute-start | bytes 584 | tf_op jit(solution)/shard_map/ppermute | solution.py:21
  21.8 5.4 %collective-permute-start.5 = (bf16[12,16,128]{2,1,0:T(8,128)(2,1)S(1)}, bf16[12,16,128]{2,1,0:T(8,128)(2,1)S(1)}, u32[]{:S(2)}, u32[]{:S(2)}) collective-permute-start(bf16[12,16,128]{2,1,0:T(8,128)(2,1)S(1)} %get-tuple-element.17), channel_id=1, source_target_pairs={{0,12},{4,0},{8,4},{12,8},{1,13},{5,1},{9,5},{13,9},{2,14},{6,2},{... | collective-permute-start | bytes 147464 | tf_op jit(solution)/shard_map/ppermute | solution.py:21
  25.5 5.0 %collective-permute-start.6 = (bf16[12,16,128]{2,1,0:T(8,128)(2,1)S(1)}, bf16[12,16,128]{2,1,0:T(8,128)(2,1)S(1)}, u32[]{:S(2)}, u32[]{:S(2)}) collective-permute-start(bf16[12,16,128]{2,1,0:T(8,128)(2,1)S(1)} %get-tuple-element.18), channel_id=1, source_target_pairs={{0,8},{4,12},{8,0},{12,4},{1,9},{5,13},{9,1},{13,5},{2,10},{6,14},... | collective-permute-start | bytes 147464 | tf_op jit(solution)/shard_map/ppermute | solution.py:21
  25.5 5.9 %collective-permute-start.7 = (bf16[12,16,128]{2,1,0:T(8,128)(2,1)S(1)}, bf16[12,16,128]{2,1,0:T(8,128)(2,1)S(1)}, u32[]{:S(2)}, u32[]{:S(2)}) collective-permute-start(bf16[12,16,128]{2,1,0:T(8,128)(2,1)S(1)} %get-tuple-element.19), channel_id=1, source_target_pairs={{0,4},{4,8},{8,12},{12,0},{1,5},{5,9},{9,13},{13,1},{2,6},{6,10},{... | collective-permute-start | bytes 147464 | tf_op jit(solution)/shard_map/ppermute | solution.py:21
  34.5 9.1 %collective-permute-start.13 = (f32[8,16,128]{2,1,0:T(8,128)S(1)}, f32[8,16,128]{2,1,0:T(8,128)S(1)}, u32[]{:S(2)}, u32[]{:S(2)}) collective-permute-start(f32[8,16,128]{2,1,0:T(8,128)S(1)} %get-tuple-element.28), channel_id=1, source_target_pairs={{0,2},{2,0},{1,3},{3,1},{4,6},{6,4},{5,7},{7,5},{8,10},{10,8},{9,1... | collective-permute-start | bytes 196616 | tf_op jit(solution)/shard_map/ppermute | solution.py:21
  35.1 13.3 %collective-permute-start.10 = (bf16[4,16,128]{2,1,0:T(8,128)(2,1)S(1)}, bf16[4,16,128]{2,1,0:T(8,128)(2,1)S(1)}, u32[]{:S(2)}, u32[]{:S(2)}) collective-permute-start(bf16[4,16,128]{2,1,0:T(8,128)(2,1)S(1)} %get-tuple-element.25), channel_id=1, source_target_pairs={{0,4},{4,8},{8,12},{12,0},{1,5},{5,9},{9,13},{13,1},{2,6},{6,10},{... | collective-permute-start | bytes 49160 | tf_op jit(solution)/shard_map/ppermute | solution.py:21
  35.1 17.1 %copy-start.15 = (f32[16]{0:T(128)S(1)}, f32[16]{0:T(128)}, u32[]{:S(2)}) copy-start(f32[16]{0:T(128)} %param.16) | copy-start | bytes 196
  35.1 19.0 %copy-start.5 = (s32[4096,2]{0,1:T(2,128)S(1)}, s32[4096,2]{0,1:T(2,128)}, u32[]{:S(2)}) copy-start(s32[4096,2]{0,1:T(2,128)} %param.27) | copy-start | bytes 98308
  35.1 19.0 %copy-start.7 = (s32[4,16]{1,0:T(4,128)S(1)}, s32[4,16]{1,0:T(4,128)}, u32[]{:S(2)}) copy-start(s32[4,16]{1,0:T(4,128)} %links.3) | copy-start | bytes 772
  35.1 19.0 %copy-start.11 = (s32[32,2]{0,1:T(2,128)S(1)}, s32[32,2]{0,1:T(2,128)}, u32[]{:S(2)}) copy-start(s32[32,2]{0,1:T(2,128)} %param.26) | copy-start | bytes 772
  35.1 13.2 %collective-permute-start.11 = (bf16[4,16,128]{2,1,0:T(8,128)(2,1)S(1)}, bf16[4,16,128]{2,1,0:T(8,128)(2,1)S(1)}, u32[]{:S(2)}, u32[]{:S(2)}) collective-permute-start(bf16[4,16,128]{2,1,0:T(8,128)(2,1)S(1)} %get-tuple-element.26), channel_id=1, source_target_pairs={{0,8},{4,12},{8,0},{12,4},{1,9},{5,13},{9,1},{13,5},{2,10},{6,14},... | collective-permute-start | bytes 49160 | tf_op jit(solution)/shard_map/ppermute | solution.py:21
  42.0 12.0 %collective-permute-start.9 = (bf16[32,16,128]{2,1,0:T(8,128)(2,1)S(1)}, bf16[32,16,128]{2,1,0:T(8,128)(2,1)S(1)}, u32[]{:S(2)}, u32[]{:S(2)}) collective-permute-start(bf16[32,16,128]{2,1,0:T(8,128)(2,1)S(1)} %get-tuple-element.24), channel_id=1, source_target_pairs={{0,2},{2,0},{1,3},{3,1},{4,6},{6,4},{5,7},{7,5},{8,10},{10,8},{9,1... | collective-permute-start | bytes 393224 | tf_op jit(solution)/shard_map/ppermute | solution.py:21
  43.6 10.0 %collective-permute-start.14 = (bf16[8,16,128]{2,1,0:T(8,128)(2,1)S(1)}, bf16[8,16,128]{2,1,0:T(8,128)(2,1)S(1)}, u32[]{:S(2)}, u32[]{:S(2)}) collective-permute-start(bf16[8,16,128]{2,1,0:T(8,128)(2,1)S(1)} %add_convert_fusion.refs_6_), channel_id=1, source_target_pairs={{0,12},{4,0},{8,4},{12,8},{1,13},{5,1},{9,5},{13,9},{2,14},{6,2},{... | collective-permute-start | bytes 98312 | tf_op jit(solution)/shard_map/ppermute | solution.py:21
  46.6 7.1 %collective-permute-start.15 = (bf16[8,16,128]{2,1,0:T(8,128)(2,1)S(1)}, bf16[8,16,128]{2,1,0:T(8,128)(2,1)S(1)}, u32[]{:S(2)}, u32[]{:S(2)}) collective-permute-start(bf16[8,16,128]{2,1,0:T(8,128)(2,1)S(1)} %add_convert_fusion.refs_6_), channel_id=1, source_target_pairs={{0,8},{4,12},{8,0},{12,4},{1,9},{5,13},{9,1},{13,5},{2,10},{6,14},... | collective-permute-start | bytes 98312 | tf_op jit(solution)/shard_map/ppermute | solution.py:21
  48.4 5.7 %collective-permute-start.16 = (bf16[8,16,128]{2,1,0:T(8,128)(2,1)S(1)}, bf16[8,16,128]{2,1,0:T(8,128)(2,1)S(1)}, u32[]{:S(2)}, u32[]{:S(2)}) collective-permute-start(bf16[8,16,128]{2,1,0:T(8,128)(2,1)S(1)} %add_convert_fusion.refs_6_), channel_id=1, source_target_pairs={{0,4},{4,8},{8,12},{12,0},{1,5},{5,9},{9,13},{13,1},{2,6},{6,10},{... | collective-permute-start | bytes 98312 | tf_op jit(solution)/shard_map/ppermute | solution.py:21
  48.4 5.3 %collective-permute-start.12 = (bf16[4,16,128]{2,1,0:T(8,128)(2,1)S(1)}, bf16[4,16,128]{2,1,0:T(8,128)(2,1)S(1)}, u32[]{:S(2)}, u32[]{:S(2)}) collective-permute-start(bf16[4,16,128]{2,1,0:T(8,128)(2,1)S(1)} %get-tuple-element.27), channel_id=1, source_target_pairs={{0,12},{4,0},{8,4},{12,8},{1,13},{5,1},{9,5},{13,9},{2,14},{6,2},{... | collective-permute-start | bytes 49160 | tf_op jit(solution)/shard_map/ppermute | solution.py:21
  (3 other events, 2.1 us)

commit v2 on v1

--- a/solution.py
+++ b/solution.py
@@ -34,6 +34,10 @@
     )
 
 
+def in_hbm(*arrays):
+    return [pltpu.with_memory_space_constraint(x, pltpu.HBM) for x in arrays]
+
+
 def wrapped(x, n):
     return lax.rem(x + n, n)
 
@@ -74,10 +78,11 @@
 
     lax.fori_loop(0, seg_own // unroll, step, 0)
     for k in range(n_row):
-        own[k] = acc[pl.ds(k * pan_group + c * pan_own, pan_own)]
+        here = pl.ds(k * pan_own, pan_own)
+        own[here] = acc[pl.ds(k * pan_group + c * pan_own, pan_own)]
         for j in range(1, n_col):
             there = lax.rem(c + j, n_col)
-            sends[j - 1][k] = acc[pl.ds(k * pan_group + there * pan_own, pan_own)].astype(BF16)
+            sends[j - 1][here] = acc[pl.ds(k * pan_group + there * pan_own, pan_own)].astype(BF16)
 
 
 def pick_body(n_row, n_col, seg_own, pan_own, cap_l, cap_p, *refs):
@@ -111,43 +116,69 @@
     return [pltpu.make_async_copy(tiles.at[s], held.at[s], sems.at[q]) for q, s in enumerate(spans)]
 
 
-def multiply(copies, held, src, slots, rows, acc, unroll):
-    size = held.shape[0] // len(copies)
-    for q, copy in enumerate(copies):
-        copy.wait()
-
-        def step(i, carry):
-            at = [q * size + i * unroll + u for u in range(unroll)]
-            got = [jnp.dot(src[slots[t]], held[t], preferred_element_type=F32) for t in at]
-            for t, value in zip(at, got):
-                acc[rows[t]] += value
-            return carry
-
-        lax.fori_loop(0, size // unroll, step, 0)
+def multiply(held, first, count, src, slots, rows, acc, unroll, paired):
+    def products(t):
+        if not paired:
+            return [jnp.dot(src[slots[t]], held[t], preferred_element_type=F32)]
+        left = jnp.concatenate([src[slots[t]], src[slots[t + 1]]], axis=0)
+        both = jnp.dot(left, jnp.concatenate([held[t], held[t + 1]], axis=1), preferred_element_type=F32)
+        rhs, width = src.shape[1:]
+        return [both[:rhs, :width], both[rhs:, width:]]
+
+    def step(i, carry):
+        start = first + i * unroll
+        got = []
+        for u in range(0, unroll, 2 if paired else 1):
+            got += products(start + u)
+        for u, value in enumerate(got):
+            acc[rows[start + u]] += value
+        return carry
+
+    lax.fori_loop(0, count // unroll, step, 0)
 
 
 def coeff_body(n_row, n_col, cap_l, cap_p, slots, rows, *refs):
     got = refs[:n_row]
-    ends_own = refs[n_row]
-    ends_in = refs[n_row + 1 : n_row + n_col]
-    tiles = refs[n_row + n_col]
-    part, end_keep, *end_sends = refs[n_row + n_col + 1 : -3]
-    src, held, sems = refs[-3:]
+    ends_out = refs[n_row : n_row + n_col - 1]
+    tiles = refs[n_row + n_col - 1]
+    part, *messages = refs[n_row + n_col : -1]
+    src = refs[-1]
     r = lax.axis_index("row")
-    copies = tile_copies(tiles, held, sems)
-    for copy in copies:
-        copy.start()
     for k in range(n_row):
         src[pl.ds(lax.rem(r + k, n_row) * cap_p, cap_p)] = got[k][pl.ds(cap_l, cap_p)]
-        total = ends_own[k]
-        for more in ends_in:
-            total += more[k].astype(F32)
+    part[...] = jnp.zeros_like(part)
+    multiply(tiles, 0, tiles.shape[0], src, slots, rows, part, 8, False)
+    high = part[...].astype(BF16)
+    low = (part[...] - high.astype(F32)).astype(BF16)
+    pan_group = part.shape[0]
+    for message, ends in zip(messages, ends_out):
+        count = ends.shape[0]
+        message[pl.ds(0, count)] = ends[...]
+        message[pl.ds(count, pan_group)] = high
+        message[pl.ds(count + pan_group, pan_group)] = low
+
+
+def panels_body(n_row, n_col, pan_own, part, ends_own, *refs):
+    arrived = refs[: n_col - 1]
+    pot, end_keep, *messages = refs[n_col - 1 :]
+    pan_group = part.shape[0]
+    count = n_row * pan_own
+    total = part[...]
+    for x in arrived:
+        high, low = x[pl.ds(count, pan_group)], x[pl.ds(count + pan_group, pan_group)]
+        total += high.astype(F32) + low.astype(F32)
+    rounded = total.astype(BF16)
+    pot[...] = rounded
+    for k in range(n_row):
+        here = pl.ds(k * pan_own, pan_own)
+        sums = ends_own[here]
+        for x in arrived:
+            sums += x[here].astype(F32)
         if k == 0:
-            end_keep[...] = total
+            end_keep[...] = sums
         else:
-            end_sends[k - 1][...] = total.astype(BF16)
-    part[...] = jnp.zeros_like(part)
-    multiply(copies, held, src, slots, rows, part, 8)
+            messages[k - 1][pl.ds(0, pan_own)] = sums.astype(BF16)
+            messages[k - 1][pl.ds(pan_own, pan_group)] = rounded
 
 
 def induct_body(n_row, n_col, seg_own, cap_l, slots, rows, *refs):
@@ -162,30 +193,34 @@
     for k in range(n_row):
         src[pl.ds(lax.rem(r + k, n_row) * cap_l, cap_l)] = got[k][pl.ds(0, cap_l)]
     acc[...] = jnp.zeros_like(acc)
-    multiply(copies, held, src, slots, rows, acc, 8)
+    size = tiles.shape[0] // len(copies)
+    for q, copy in enumerate(copies):
+        copy.wait()
+        multiply(held, q * size, size, src, slots, rows, acc, 8, True)
     own[...] = acc[pl.ds(c * seg_own, seg_own)]
     for j in range(1, n_col):
         sends[j - 1][...] = acc[pl.ds(lax.rem(c + j, n_col) * seg_own, seg_own)].astype(BF16)
 
 
 def final_body(n_row, n_col, seg_own, pan_own, cap, slots, links, off, charge, scale, *refs):
-    field_own, end_own = refs[0], refs[1]
-    field_in = refs[2 : 1 + n_col]
-    end_in = refs[1 + n_col : n_col + n_row]
-    pots = refs[n_col + n_row : n_col + 2 * n_row]
-    seg_out, pan_out, pot_out, held = refs[n_col + 2 * n_row :]
+    field_own, end_own, pot = refs[:3]
+    field_in = refs[3 : 2 + n_col]
+    arrived = refs[2 + n_col : 1 + n_col + n_row]
+    seg_out, pan_out, pot_out, held = refs[1 + n_col + n_row :]
     width = charge.shape[1] // pan_own
     pan_group = pan_own * n_col
     r, c = lax.axis_index("row"), lax.axis_index("col")
-    for k in range(n_row):
-        held[pl.ds(lax.rem(r + k, n_row) * pan_group, pan_group)] = pots[k][...]
+    held[pl.ds(r * pan_group, pan_group)] = pot[...]
+    for k, x in enumerate(arrived):
+        sender = wrapped(r - (k + 1), n_row)
+        held[pl.ds(sender * pan_group, pan_group)] = x[pl.ds(pan_own, pan_group)]
     for q in range(pan_own):
         span = slice(q * width, (q + 1) * width)
         total = end_own[q]
-        for more in end_in:
-            total += more[q].astype(F32)
+        for x in arrived:
+            total += x[q].astype(F32)
         pan_out[:, span] = (scale[...] * charge[:, span].astype(F32) + total).astype(BF16)
-        pot_out[:, span] = pots[0][c * pan_own + q]
+        pot_out[:, span] = pot[c * pan_own + q]
 
     def block(k):
         ends = []
@@ -249,12 +284,12 @@
     ends_own, *ends_out = call(
         functools.partial(ends_body, n_row, n_col, seg_own, pan_own, cap_k),
         "end_sums",
-        [like((n_row, pan_own), F32)] + [like((n_row, pan_own), BF16)] * (n_col - 1),
+        [like((n_row * pan_own,), F32)] + [like((n_row * pan_own,), BF16)] * (n_col - 1),
         [SMEM, SMEM, VMEM, VMEM],
         [pltpu.VMEM((n_row * pan_group, rhs, width), F32)],
         flops=2 * 10**9,
         moved=2**18,
-    )(slots_t, link_needs, current, off_t)
+    )(*in_hbm(slots_t, link_needs, current, off_t))
 
     picked = call(
         functools.partial(pick_body, n_row, n_col, seg_own, pan_own, cap_l, cap_p),
@@ -262,26 +297,20 @@
         [like((cap_l + cap_p,), BF16)] * n_row,
         [SMEM] * n_row + [VMEM] * (2 * n_col),
         moved=2**20,
-    )(*asked, *cur, *chg)
+    )(*asked, *in_hbm(cur[0]), *cur[1:], *in_hbm(chg[0]), *chg[1:])
     got = [shift(x, "row", -k) for k, x in enumerate(picked)]
-    ends_in = [shift(x, "col", j + 1) for j, x in enumerate(ends_out)]
-
-    pt = coeff_tiles.shape[0]
-    part, end_keep, *end_sends = call(
+
+    message = like((n_row * pan_own + 2 * pan_group,), BF16)
+    part, *col_messages = call(
         functools.partial(coeff_body, n_row, n_col, cap_l, cap_p),
         "coeff_tiles",
-        [like((pan_group,), F32), like((pan_own,), F32)] + [like((pan_own,), BF16)] * (n_row - 1),
-        [SMEM, SMEM] + [VMEM] * (n_row + n_col) + [ANY],
-        [
-            pltpu.VMEM((n_row * cap_p, rhs, width), BF16),
-            pltpu.VMEM(coeff_tiles.shape, BF16),
-            pltpu.SemaphoreType.DMA((4,)),
-        ],
+        [like((pan_group,), F32)] + [message] * (n_col - 1),
+        [SMEM, SMEM] + [VMEM] * (n_row + n_col),
+        [pltpu.VMEM((n_row * cap_p, rhs, width), BF16)],
         flops=2 * 10**9,
         moved=coeff_tiles.size * 2,
-    )(coeff_slots, coeff_rows, *got, ends_own, *ends_in, coeff_tiles)
-    parts = [shift(part, "col", j) for j in range(n_col)]
-    end_in = [shift(x, "row", k + 1) for k, x in enumerate(end_sends)]
+    )(coeff_slots, coeff_rows, *got, *ends_out, coeff_tiles)
+    from_col = [shift(x, "col", j + 1) for j, x in enumerate(col_messages)]
 
     field_own, *field_out = call(
         functools.partial(induct_body, n_row, n_col, seg_own, cap_l),
@@ -299,18 +328,21 @@
     )(induct_slots, induct_rows, *got, induct_tiles)
     field_in = [shift(x, "col", j + 1) for j, x in enumerate(field_out)]
 
-    potential = parts[0]
-    for more in parts[1:]:
-        potential = potential + more
-    potential = potential.astype(BF16)
-    pots = [shift(potential, "row", -k) for k in range(n_row)]
+    pot, end_keep, *row_messages = call(
+        functools.partial(panels_body, n_row, n_col, pan_own),
+        "panel_sums",
+        [like((pan_group,), BF16), like((pan_own,), F32)] + [like((pan_own + pan_group,), BF16)] * (n_row - 1),
+        [VMEM] * (1 + n_col),
+        moved=2**18,
+    )(part, ends_own, *from_col)
+    from_row = [shift(x, "row", k + 1) for k, x in enumerate(row_messages)]
 
     return tuple(
         call(
             functools.partial(final_body, n_row, n_col, seg_own, pan_own, cap_k),
             "outputs",
             [jax.ShapeDtypeStruct(x.shape, BF16) for x in (current, charge, charge)],
-            [SMEM, SMEM] + [VMEM] * (3 + n_col + 2 * n_row),
+            [SMEM, SMEM] + [VMEM] * (4 + n_col + n_row),
             [pltpu.VMEM((n_row * pan_group, rhs, width), BF16)],
             flops=2 * 10**9,
             moved=2**20,
@@ -322,9 +354,9 @@
             rhs_scale[:, None],
             field_own,
             end_keep,
+            pot,
             *field_in,
-            *end_in,
-            *pots,
+            *from_row,
         )
     )
 

time: 57.1 us -> 43 us (0.75)
  starting transfers between devices: 27.3 us -> 19.2 us
  waiting for transfers between devices: 10.1 us -> 6.84 us
  local copies, waits for them, and re-layouts: 3.16 us -> 0.14 us
    ppermute x17 -> x13, starting transfers between devices: 27.3 us -> 19.2 us  [shift(): return lax.ppermute(x, axis, [(i, (i + k) % n) for i in range(n)])]
    ppermute x17 -> x13, waiting for transfers between devices: 10.1 us -> 6.84 us  [shift(): return lax.ppermute(x, axis, [(i, (i + k) % n) for i in range(n)])]
    unnamed x36 -> x24, local copies, waits for them, and re-layouts: 3.08 us -> 0.06 us
    pallas_call x1, Pallas kernels: 2.26 us -> 2.94 us  [shards(): call(functools.partial(ends_body, n_row, n_col, seg_own, pan_own, cap_k),...]
  transfers between devices with their start and end apart: 17 -> 13, of which waited for: 7 -> 7; matrix products, arithmetic and copies ran while one was open for 1% -> 2% of each run, Pallas kernels for 16% -> 19%
where the time goes in v2:
time: 43 us; the launch traced here: 42.8 us
  starting transfers between devices  19.2 us (45%)
  Pallas kernels  15.1 us (35%)
  waiting for transfers between devices  6.84 us (16%)
  between operations  0.78 us (2%)
  other arithmetic  0.77 us (2%)
    ppermute x13, starting transfers between devices, shift(): return lax.ppermute(x, axis, [(i, (i + k) % n) for i in range(n)])  19.2 us
    ppermute x13, waiting for transfers between devices, shift(): return lax.ppermute(x, axis, [(i, (i + k) % n) for i in range(n)])  6.84 us
    pallas_call x1, Pallas kernels, shards(): call(functools.partial(induct_body, n_row, n_col, seg_own, cap_l), 'induc...  5.35 us
    pallas_call x1, Pallas kernels, shards(): call(functools.partial(ends_body, n_row, n_col, seg_own, pan_own, cap_k),...  2.94 us
    pallas_call x1, Pallas kernels, shards(): call(functools.partial(coeff_body, n_row, n_col, cap_l, cap_p), 'coeff_ti...  2.85 us
    pallas_call x1, Pallas kernels, shards(): call(functools.partial(final_body, n_row, n_col, seg_own, pan_own, cap_k)...  2.68 us
    pallas_call x1, Pallas kernels, shards(): call(functools.partial(pick_body, n_row, n_col, seg_own, pan_own, cap_l,...  1.26 us
  transfers between devices with their start and end apart: 13, of which 7 were waited for; matrix products, arithmetic and copies ran while one was open for 2% of the time, Pallas kernels for 19%

profile of v2, /device:TPU:0, one launch (start us, length us, event | category | flops | bytes accessed | tf_op | source)
XLA Modules:
  0.0 42.8 jit_solution(3181069478249835798)
XLA Ops:
  0.7 3.0 %collective-permute-start.3 = (bf16[16,4096]{1,0:T(8,128)(2,1)}, bf16[16,4096]{1,0:T(8,128)(2,1)S(1)}, u32[]{:S(2)}, u32[]{:S(2)}) collective-permute-start(bf16[16,4096]{1,0:T(8,128)(2,1)} %cur.1), channel_id=1, source_target_pairs={{0,2},{2,0},{1,3},{3,1},{4,6},{6,4},{5,7},{7,5},{8,10},{10,8},{9,1... | collective-permute-start | bytes 393224 | tf_op jit(solution)/shard_map/ppermute | solution.py:21
  3.7 0.1 collective-permute-start.4
  3.7 0.8 %pad_add_fusion.refs_0_ = s32[4,12]{1,0:T(4,128)S(1)} fusion(s32[4,4]{1,0:T(4,128)} %param.24, s32[4,8]{1,0:T(4,128)} %param.20), kind=kLoop, calls=%fused_computation | loop fusion | flops 48 | bytes 384 | tf_op jit(solution)/shard_map/concatenate | solution.py:279
  4.5 2.0 %collective-permute-start = (s32[4,12]{1,0:T(4,128)S(1)}, s32[4,12]{1,0:T(4,128)S(1)}, u32[]{:S(2)}, u32[]{:S(2)}) collective-permute-start(s32[4,12]{1,0:T(4,128)S(1)} %pad_add_fusion.refs_0_), channel_id=1, source_target_pairs={{0,4},{4,8},{8,12},{12,0},{1,5},{5,9},{9,13},{13,1},{2,6},{6,10},{... | collective-permute-start | bytes 584 | tf_op jit(solution)/shard_map/ppermute | solution.py:21
  6.5 2.6 %collective-permute-start.1 = (s32[4,12]{1,0:T(4,128)S(1)}, s32[4,12]{1,0:T(4,128)S(1)}, u32[]{:S(2)}, u32[]{:S(2)}) collective-permute-start(s32[4,12]{1,0:T(4,128)S(1)} %pad_add_fusion.refs_0_), channel_id=1, source_target_pairs={{0,8},{4,12},{8,0},{12,4},{1,9},{5,13},{9,1},{13,5},{2,10},{6,14},... | collective-permute-start | bytes 584 | tf_op jit(solution)/shard_map/ppermute | solution.py:21
  9.1 1.3 %collective-permute-start.2 = (s32[4,12]{1,0:T(4,128)S(1)}, s32[4,12]{1,0:T(4,128)S(1)}, u32[]{:S(2)}, u32[]{:S(2)}) collective-permute-start(s32[4,12]{1,0:T(4,128)S(1)} %pad_add_fusion.refs_0_), channel_id=1, source_target_pairs={{0,12},{4,0},{8,4},{12,8},{1,13},{5,1},{9,5},{13,9},{2,14},{6,2},{... | collective-permute-start | bytes 584 | tf_op jit(solution)/shard_map/ppermute | solution.py:21
  10.5 0.5 %collective-permute-done.1.refs_2_ = s32[4,12]{1,0:T(4,128)S(1)} collective-permute-done((s32[4,12]{1,0:T(4,128)S(1)}, s32[4,12]{1,0:T(4,128)S(1)}, u32[]{:S(2)}, u32[]{:S(2)}) %collective-permute-start.1) | collective-permute-done | bytes 224 | tf_op jit(solution)/shard_map/ppermute | solution.py:21
  11.0 1.7 %collective-permute-done.2.refs_3_ = s32[4,12]{1,0:T(4,128)S(1)} collective-permute-done((s32[4,12]{1,0:T(4,128)S(1)}, s32[4,12]{1,0:T(4,128)S(1)}, u32[]{:S(2)}, u32[]{:S(2)}) %collective-permute-start.2) | collective-permute-done | bytes 224 | tf_op jit(solution)/shard_map/ppermute | solution.py:21
  12.7 1.3 %pick_blocks.1 = (bf16[12,16,128]{2,1,0:T(8,128)(2,1)S(1)}, bf16[12,16,128]{2,1,0:T(8,128)(2,1)S(1)}, bf16[12,16,128]{2,1,0:T(8,128)(2,1)S(1)}, bf16[12,16,128]{2,1,0:T(8,128)(2,1)S(1)}) custom-call(s32[4,12]{1,0:T(4,128)S(1)} %pad_add_fusion.refs_0_, s32[4,12]{1,0:T(4,128)S(1)} %collective-permute-done.refs_1_, s32[4,12]{1,0:T(4,128)S(1)} %collective-permute-done.1.refs_2_, ...), custom_call_target="tpu_custom_call" | custom-call | bytes 1048576 | tf_op jit(solution)/shard_map/pick_blocks/pallas_call | solution.py:294
  14.0 3.2 %collective-permute-start.5 = (bf16[12,16,128]{2,1,0:T(8,128)(2,1)S(1)}, bf16[12,16,128]{2,1,0:T(8,128)(2,1)S(1)}, u32[]{:S(2)}, u32[]{:S(2)}) collective-permute-start(bf16[12,16,128]{2,1,0:T(8,128)(2,1)S(1)} %get-tuple-element.19), channel_id=1, source_target_pairs={{0,12},{4,0},{8,4},{12,8},{1,13},{5,1},{9,5},{13,9},{2,14},{6,2},{... | collective-permute-start | bytes 147464 | tf_op jit(solution)/shard_map/ppermute | solution.py:21
  17.2 0.7 %collective-permute-start.7 = (bf16[12,16,128]{2,1,0:T(8,128)(2,1)S(1)}, bf16[12,16,128]{2,1,0:T(8,128)(2,1)S(1)}, u32[]{:S(2)}, u32[]{:S(2)}) collective-permute-start(bf16[12,16,128]{2,1,0:T(8,128)(2,1)S(1)} %get-tuple-element.21), channel_id=1, source_target_pairs={{0,4},{4,8},{8,12},{12,0},{1,5},{5,9},{9,13},{13,1},{2,6},{6,10},{... | collective-permute-start | bytes 147464 | tf_op jit(solution)/shard_map/ppermute | solution.py:21
  17.9 2.9 %end_sums.1 = (f32[16,16,128]{2,1,0:T(8,128)S(1)}, bf16[16,16,128]{2,1,0:T(8,128)(2,1)S(1)}) custom-call(s32[2,32]{1,0:T(2,128)} %bitcast.7, s32[4,16]{1,0:T(4,128)} %links.3, bf16[16,4096]{1,0:T(8,128)(2,1)} %cur.1, s32[2,4096]{1,0:T(2,128)} %bitcast.5), custom_call_target="tpu_custom_call" | custom-call | flops 2000000000 | bytes 262144 | tf_op jit(solution)/shard_map/end_sums/pallas_call | solution.py:284
  20.8 0.0 collective-permute-done.5.refs_1_
  20.8 1.4 %collective-permute-done.6.refs_2_ = bf16[12,16,128]{2,1,0:T(8,128)(2,1)S(1)} collective-permute-done((bf16[12,16,128]{2,1,0:T(8,128)(2,1)S(1)}, bf16[12,16,128]{2,1,0:T(8,128)(2,1)S(1)}, u32[]{:S(2)}, u32[]{:S(2)}) %collective-permute-start.6) | collective-permute-done | bytes 49184 | tf_op jit(solution)/shard_map/ppermute | solution.py:21
  22.2 0.9 %collective-permute-done.7.refs_3_ = bf16[12,16,128]{2,1,0:T(8,128)(2,1)S(1)} collective-permute-done((bf16[12,16,128]{2,1,0:T(8,128)(2,1)S(1)}, bf16[12,16,128]{2,1,0:T(8,128)(2,1)S(1)}, u32[]{:S(2)}, u32[]{:S(2)}) %collective-permute-start.7) | collective-permute-done | bytes 49184 | tf_op jit(solution)/shard_map/ppermute | solution.py:21
  23.1 2.8 %coeff_tiles.1 = (f32[8,16,128]{2,1,0:T(8,128)S(1)}, bf16[32,16,128]{2,1,0:T(8,128)(2,1)S(1)}) custom-call(s32[96]{0:T(128)S(1)} %copy-done.7, s32[96]{0:T(128)S(1)} %copy-done.8, bf16[12,16,128]{2,1,0:T(8,128)(2,1)S(1)} %get-tuple-element.18.refs_0_, bf16[12,16,128]{2,1,0:T(8,128)(2,1)S(1)} %collective-permute-done.5.refs_1_, ...), custom_call_target="tpu_custom_call" | custom-call | flops 2000000000 | bytes 3145728 | tf_op jit(solution)/shard_map/coeff_tiles/pallas_call | solution.py:304
  26.0 0.0 copy-start.9
  26.0 0.0 copy-start
  26.0 0.0 copy-start.2
  26.0 0.0 copy-start.3
  26.0 0.0 copy-start.6
  26.0 1.6 %collective-permute-start.8 = (bf16[32,16,128]{2,1,0:T(8,128)(2,1)S(1)}, bf16[32,16,128]{2,1,0:T(8,128)(2,1)S(1)}, u32[]{:S(2)}, u32[]{:S(2)}) collective-permute-start(bf16[32,16,128]{2,1,0:T(8,128)(2,1)S(1)} %get-tuple-element.26), channel_id=1, source_target_pairs={{0,2},{2,0},{1,3},{3,1},{4,6},{6,4},{5,7},{7,5},{8,10},{10,8},{9,1... | collective-permute-start | bytes 393224 | tf_op jit(solution)/shard_map/ppermute | solution.py:21
  27.6 5.4 %induct_tiles.1 = (f32[32,16,128]{2,1,0:T(8,128)S(1)}, bf16[32,16,128]{2,1,0:T(8,128)(2,1)S(1)}) custom-call(s32[192]{0:T(256)S(1)} %copy-done.4, s32[192]{0:T(256)S(1)} %copy-done.5, bf16[12,16,128]{2,1,0:T(8,128)(2,1)S(1)} %get-tuple-element.18.refs_0_, bf16[12,16,128]{2,1,0:T(8,128)(2,1)S(1)} %collective-permute-done.5.refs_1_, ...), custom_call_target="tpu_custom_call" | custom-call | flops 4000000000 | bytes 6291456 | tf_op jit(solution)/shard_map/induct_tiles/pallas_call | solution.py:315
  33.0 0.6 %collective-permute-start.9 = (bf16[32,16,128]{2,1,0:T(8,128)(2,1)S(1)}, bf16[32,16,128]{2,1,0:T(8,128)(2,1)S(1)}, u32[]{:S(2)}, u32[]{:S(2)}) collective-permute-start(bf16[32,16,128]{2,1,0:T(8,128)(2,1)S(1)} %get-tuple-element.29), channel_id=1, source_target_pairs={{0,2},{2,0},{1,3},{3,1},{4,6},{6,4},{5,7},{7,5},{8,10},{10,8},{9,1... | collective-permute-start | bytes 393224 | tf_op jit(solution)/shard_map/ppermute | solution.py:21
  33.6 0.5 %collective-permute-start.10 = (bf16[12,16,128]{2,1,0:T(8,128)(2,1)S(1)}, bf16[12,16,128]{2,1,0:T(8,128)(2,1)S(1)}, u32[]{:S(2)}, u32[]{:S(2)}) collective-permute-start(bf16[12,16,128]{2,1,0:T(8,128)(2,1)S(1)} %get-tuple-element.30), channel_id=1, source_target_pairs={{0,4},{4,8},{8,12},{12,0},{1,5},{5,9},{9,13},{13,1},{2,6},{6,10},{... | collective-permute-start | bytes 147464 | tf_op jit(solution)/shard_map/ppermute | solution.py:21
  34.1 0.9 %collective-permute-start.11 = (bf16[12,16,128]{2,1,0:T(8,128)(2,1)S(1)}, bf16[12,16,128]{2,1,0:T(8,128)(2,1)S(1)}, u32[]{:S(2)}, u32[]{:S(2)}) collective-permute-start(bf16[12,16,128]{2,1,0:T(8,128)(2,1)S(1)} %get-tuple-element.31), channel_id=1, source_target_pairs={{0,8},{4,12},{8,0},{12,4},{1,9},{5,13},{9,1},{13,5},{2,10},{6,14},... | collective-permute-start | bytes 147464 | tf_op jit(solution)/shard_map/ppermute | solution.py:21
  35.0 2.7 %collective-permute-start.12 = (bf16[12,16,128]{2,1,0:T(8,128)(2,1)S(1)}, bf16[12,16,128]{2,1,0:T(8,128)(2,1)S(1)}, u32[]{:S(2)}, u32[]{:S(2)}) collective-permute-start(bf16[12,16,128]{2,1,0:T(8,128)(2,1)S(1)} %get-tuple-element.32), channel_id=1, source_target_pairs={{0,12},{4,0},{8,4},{12,8},{1,13},{5,1},{9,5},{13,9},{2,14},{6,2},{... | collective-permute-start | bytes 147464 | tf_op jit(solution)/shard_map/ppermute | solution.py:21
  37.7 0.1 copy.17.scale
  37.8 0.2 collective-permute-done.9.refs_3_
  38.0 1.6 %collective-permute-done.10.refs_4_ = bf16[12,16,128]{2,1,0:T(8,128)(2,1)S(1)} collective-permute-done((bf16[12,16,128]{2,1,0:T(8,128)(2,1)S(1)}, bf16[12,16,128]{2,1,0:T(8,128)(2,1)S(1)}, u32[]{:S(2)}, u32[]{:S(2)}) %collective-permute-start.10) | collective-permute-done | bytes 49184 | tf_op jit(solution)/shard_map/ppermute | solution.py:21
  39.6 0.5 %collective-permute-done.12.refs_6_ = bf16[12,16,128]{2,1,0:T(8,128)(2,1)S(1)} collective-permute-done((bf16[12,16,128]{2,1,0:T(8,128)(2,1)S(1)}, bf16[12,16,128]{2,1,0:T(8,128)(2,1)S(1)}, u32[]{:S(2)}, u32[]{:S(2)}) %collective-permute-start.12) | collective-permute-done | bytes 49184 | tf_op jit(solution)/shard_map/ppermute | solution.py:21
  40.1 2.7 %outputs.1 = (bf16[16,4096]{1,0:T(8,128)(2,1)}, bf16[16,512]{1,0:T(8,128)(2,1)}, bf16[16,512]{1,0:T(8,128)(2,1)}) custom-call(s32[2,32]{1,0:T(2,128)S(1)} %bitcast.8, s32[4,16]{1,0:T(4,128)S(1)} %copy-done.3, s32[2,4096]{1,0:T(2,128)S(1)} %bitcast.6, bf16[16,512]{1,0:T(8,128)(2,1)S(1)} %copy-done, f32[16,1]{1,0:T(8,128)S(1)} %copy.17.scale, ...), custom_call_target="tpu_custom_call" | custom-call | flops 2000000000 | bytes 1048576 | tf_op jit(solution)/shard_map/outputs/pallas_call | solution.py:341
  (27 shorter events, 0.1 us)
Async XLA Ops:
  0.6 22.5 %copy-start.1 = (bf16[96,128,128]{2,1,0:T(8,128)(2,1)S(1)}, bf16[96,128,128]{2,1,0:T(8,128)(2,1)}, u32[]{:S(2)}) copy-start(bf16[96,128,128]{2,1,0:T(8,128)(2,1)} %refs_5_.1) | copy-start | bytes 9437188
  0.6 22.5 %copy-start.8 = (s32[96]{0:T(128)S(1)}, s32[96]{0:T(128)}, u32[]{:S(2)}) copy-start(s32[96]{0:T(128)} %rows.3) | copy-start | bytes 1156
  0.7 22.4 %copy-start.7 = (s32[96]{0:T(128)S(1)}, s32[96]{0:T(128)}, u32[]{:S(2)}) copy-start(s32[96]{0:T(128)} %slots.3) | copy-start | bytes 1156
  0.7 12.1 %collective-permute-start.3 = (bf16[16,4096]{1,0:T(8,128)(2,1)}, bf16[16,4096]{1,0:T(8,128)(2,1)S(1)}, u32[]{:S(2)}, u32[]{:S(2)}) collective-permute-start(bf16[16,4096]{1,0:T(8,128)(2,1)} %cur.1), channel_id=1, source_target_pairs={{0,2},{2,0},{1,3},{3,1},{4,6},{6,4},{5,7},{7,5},{8,10},{10,8},{9,1... | collective-permute-start | bytes 393224 | tf_op jit(solution)/shard_map/ppermute | solution.py:21
  3.7 9.1 %collective-permute-start.4 = (bf16[16,512]{1,0:T(8,128)(2,1)}, bf16[16,512]{1,0:T(8,128)(2,1)S(1)}, u32[]{:S(2)}, u32[]{:S(2)}) collective-permute-start(bf16[16,512]{1,0:T(8,128)(2,1)} %charge.1), channel_id=1, source_target_pairs={{0,2},{2,0},{1,3},{3,1},{4,6},{6,4},{5,7},{7,5},{8,10},{10,8},{9,1... | collective-permute-start | bytes 49160 | tf_op jit(solution)/shard_map/ppermute | solution.py:21
  4.5 6.0 %collective-permute-start = (s32[4,12]{1,0:T(4,128)S(1)}, s32[4,12]{1,0:T(4,128)S(1)}, u32[]{:S(2)}, u32[]{:S(2)}) collective-permute-start(s32[4,12]{1,0:T(4,128)S(1)} %pad_add_fusion.refs_0_), channel_id=1, source_target_pairs={{0,4},{4,8},{8,12},{12,0},{1,5},{5,9},{9,13},{13,1},{2,6},{6,10},{... | collective-permute-start | bytes 584 | tf_op jit(solution)/shard_map/ppermute | solution.py:21
  6.5 4.5 %collective-permute-start.1 = (s32[4,12]{1,0:T(4,128)S(1)}, s32[4,12]{1,0:T(4,128)S(1)}, u32[]{:S(2)}, u32[]{:S(2)}) collective-permute-start(s32[4,12]{1,0:T(4,128)S(1)} %pad_add_fusion.refs_0_), channel_id=1, source_target_pairs={{0,8},{4,12},{8,0},{12,4},{1,9},{5,13},{9,1},{13,5},{2,10},{6,14},... | collective-permute-start | bytes 584 | tf_op jit(solution)/shard_map/ppermute | solution.py:21
  9.1 3.6 %collective-permute-start.2 = (s32[4,12]{1,0:T(4,128)S(1)}, s32[4,12]{1,0:T(4,128)S(1)}, u32[]{:S(2)}, u32[]{:S(2)}) collective-permute-start(s32[4,12]{1,0:T(4,128)S(1)} %pad_add_fusion.refs_0_), channel_id=1, source_target_pairs={{0,12},{4,0},{8,4},{12,8},{1,13},{5,1},{9,5},{13,9},{2,14},{6,2},{... | collective-permute-start | bytes 584 | tf_op jit(solution)/shard_map/ppermute | solution.py:21
  14.0 6.8 %collective-permute-start.5 = (bf16[12,16,128]{2,1,0:T(8,128)(2,1)S(1)}, bf16[12,16,128]{2,1,0:T(8,128)(2,1)S(1)}, u32[]{:S(2)}, u32[]{:S(2)}) collective-permute-start(bf16[12,16,128]{2,1,0:T(8,128)(2,1)S(1)} %get-tuple-element.19), channel_id=1, source_target_pairs={{0,12},{4,0},{8,4},{12,8},{1,13},{5,1},{9,5},{13,9},{2,14},{6,2},{... | collective-permute-start | bytes 147464 | tf_op jit(solution)/shard_map/ppermute | solution.py:21
  17.2 10.4 %slice-start = ((s8[6291456]{0:T(1024)(128)(4,1)}), s8[4194304]{0:T(1024)(128)(4,1)S(1)}, s32[]{:S(2)}) async-start(s8[6291456]{0:T(1024)(128)(4,1)} %bitcast.3), calls=%async_computation | async-start | bytes 8388608
  17.2 5.0 %collective-permute-start.6 = (bf16[12,16,128]{2,1,0:T(8,128)(2,1)S(1)}, bf16[12,16,128]{2,1,0:T(8,128)(2,1)S(1)}, u32[]{:S(2)}, u32[]{:S(2)}) collective-permute-start(bf16[12,16,128]{2,1,0:T(8,128)(2,1)S(1)} %get-tuple-element.20), channel_id=1, source_target_pairs={{0,8},{4,12},{8,0},{12,4},{1,9},{5,13},{9,1},{13,5},{2,10},{6,14},... | collective-permute-start | bytes 147464 | tf_op jit(solution)/shard_map/ppermute | solution.py:21
  17.2 5.9 %collective-permute-start.7 = (bf16[12,16,128]{2,1,0:T(8,128)(2,1)S(1)}, bf16[12,16,128]{2,1,0:T(8,128)(2,1)S(1)}, u32[]{:S(2)}, u32[]{:S(2)}) collective-permute-start(bf16[12,16,128]{2,1,0:T(8,128)(2,1)S(1)} %get-tuple-element.21), channel_id=1, source_target_pairs={{0,4},{4,8},{8,12},{12,0},{1,5},{5,9},{9,13},{13,1},{2,6},{6,10},{... | collective-permute-start | bytes 147464 | tf_op jit(solution)/shard_map/ppermute | solution.py:21
  17.9 9.7 %slice-start.1 = ((s8[6291456]{0:T(1024)(128)(4,1)}), s8[2097152]{0:T(1024)(128)(4,1)S(1)}, s32[]{:S(2)}) async-start(s8[6291456]{0:T(1024)(128)(4,1)} %bitcast.3), calls=%async_computation.1 | async-start | bytes 4194304
  17.9 9.7 %copy-start.4 = (s32[192]{0:T(256)S(1)}, s32[192]{0:T(256)}, u32[]{:S(2)}) copy-start(s32[192]{0:T(256)} %slots.2) | copy-start | bytes 2308
  17.9 9.7 %copy-start.5 = (s32[192]{0:T(256)S(1)}, s32[192]{0:T(256)}, u32[]{:S(2)}) copy-start(s32[192]{0:T(256)} %rows.2) | copy-start | bytes 2308
  26.0 11.7 %copy-start.9 = (f32[16]{0:T(128)S(1)}, f32[16]{0:T(128)}, u32[]{:S(2)}) copy-start(f32[16]{0:T(128)} %param.16) | copy-start | bytes 196
  26.0 14.1 %copy-start = (bf16[16,512]{1,0:T(8,128)(2,1)S(1)}, bf16[16,512]{1,0:T(8,128)(2,1)}, u32[]{:S(2)}) copy-start(bf16[16,512]{1,0:T(8,128)(2,1)} %charge.1) | copy-start | bytes 49156
  26.0 14.1 %copy-start.2 = (s32[4096,2]{0,1:T(2,128)S(1)}, s32[4096,2]{0,1:T(2,128)}, u32[]{:S(2)}) copy-start(s32[4096,2]{0,1:T(2,128)} %param.27) | copy-start | bytes 98308
  26.0 14.1 %copy-start.3 = (s32[4,16]{1,0:T(4,128)S(1)}, s32[4,16]{1,0:T(4,128)}, u32[]{:S(2)}) copy-start(s32[4,16]{1,0:T(4,128)} %links.3) | copy-start | bytes 772
  26.0 14.1 %copy-start.6 = (s32[32,2]{0,1:T(2,128)S(1)}, s32[32,2]{0,1:T(2,128)}, u32[]{:S(2)}) copy-start(s32[32,2]{0,1:T(2,128)} %param.26) | copy-start | bytes 772
  26.0 7.5 %collective-permute-start.8 = (bf16[32,16,128]{2,1,0:T(8,128)(2,1)S(1)}, bf16[32,16,128]{2,1,0:T(8,128)(2,1)S(1)}, u32[]{:S(2)}, u32[]{:S(2)}) collective-permute-start(bf16[32,16,128]{2,1,0:T(8,128)(2,1)S(1)} %get-tuple-element.26), channel_id=1, source_target_pairs={{0,2},{2,0},{1,3},{3,1},{4,6},{6,4},{5,7},{7,5},{8,10},{10,8},{9,1... | collective-permute-start | bytes 393224 | tf_op jit(solution)/shard_map/ppermute | solution.py:21
  33.0 5.0 %collective-permute-start.9 = (bf16[32,16,128]{2,1,0:T(8,128)(2,1)S(1)}, bf16[32,16,128]{2,1,0:T(8,128)(2,1)S(1)}, u32[]{:S(2)}, u32[]{:S(2)}) collective-permute-start(bf16[32,16,128]{2,1,0:T(8,128)(2,1)S(1)} %get-tuple-element.29), channel_id=1, source_target_pairs={{0,2},{2,0},{1,3},{3,1},{4,6},{6,4},{5,7},{7,5},{8,10},{10,8},{9,1... | collective-permute-start | bytes 393224 | tf_op jit(solution)/shard_map/ppermute | solution.py:21
  33.6 6.0 %collective-permute-start.10 = (bf16[12,16,128]{2,1,0:T(8,128)(2,1)S(1)}, bf16[12,16,128]{2,1,0:T(8,128)(2,1)S(1)}, u32[]{:S(2)}, u32[]{:S(2)}) collective-permute-start(bf16[12,16,128]{2,1,0:T(8,128)(2,1)S(1)} %get-tuple-element.30), channel_id=1, source_target_pairs={{0,4},{4,8},{8,12},{12,0},{1,5},{5,9},{9,13},{13,1},{2,6},{6,10},{... | collective-permute-start | bytes 147464 | tf_op jit(solution)/shard_map/ppermute | solution.py:21
  34.1 5.5 %collective-permute-start.11 = (bf16[12,16,128]{2,1,0:T(8,128)(2,1)S(1)}, bf16[12,16,128]{2,1,0:T(8,128)(2,1)S(1)}, u32[]{:S(2)}, u32[]{:S(2)}) collective-permute-start(bf16[12,16,128]{2,1,0:T(8,128)(2,1)S(1)} %get-tuple-element.31), channel_id=1, source_target_pairs={{0,8},{4,12},{8,0},{12,4},{1,9},{5,13},{9,1},{13,5},{2,10},{6,14},... | collective-permute-start | bytes 147464 | tf_op jit(solution)/shard_map/ppermute | solution.py:21
  35.0 5.1 %collective-permute-start.12 = (bf16[12,16,128]{2,1,0:T(8,128)(2,1)S(1)}, bf16[12,16,128]{2,1,0:T(8,128)(2,1)S(1)}, u32[]{:S(2)}, u32[]{:S(2)}) collective-permute-start(bf16[12,16,128]{2,1,0:T(8,128)(2,1)S(1)} %get-tuple-element.32), channel_id=1, source_target_pairs={{0,12},{4,0},{8,4},{12,8},{1,13},{5,1},{9,5},{13,9},{2,14},{6,2},{... | collective-permute-start | bytes 147464 | tf_op jit(solution)/shard_map/ppermute | solution.py:21

commit v3 on v2

v3 whole, which is shorter than its diff:
```python
import functools

import jax
import jax.numpy as jnp
from jax import lax
from jax.experimental import pallas as pl
from jax.experimental.pallas import tpu as pltpu
from jax.sharding import PartitionSpec as P

F32 = jnp.float32
BF16 = jnp.bfloat16
VMEM = pl.BlockSpec(memory_space=pltpu.VMEM)
SMEM = pl.BlockSpec(memory_space=pltpu.SMEM)
ANY = pl.BlockSpec(memory_space=pl.ANY)


def exchange(x, axis, k):
    if k == 0:
        return x
    return lax.ppermute(x, axis, [(i, i ^ k) for i in range(lax.axis_size(axis))])


def exchange_all(first, others, axis):
    n = lax.axis_size(axis)
    got = {0: first}
    for k in reversed(range(1, n)):
        got[k] = exchange(others[k - 1], axis, k)
    return [got[k] for k in range(n)]


def call(body, name, out_shape, in_specs, scratch=(), flops=0, moved=0):
    return pl.pallas_call(
        body,
        out_shape=out_shape,
        in_specs=in_specs,
        out_specs=[VMEM] * len(out_shape),
        scratch_shapes=list(scratch),
        compiler_params=pltpu.CompilerParams(vmem_limit_bytes=16 * 2**20),
        cost_estimate=pl.CostEstimate(flops=flops, bytes_accessed=moved, transcendentals=0),
        name=name,
    )


def in_hbm(*arrays):
    return [pltpu.with_memory_space_constraint(x, pltpu.HBM) for x in arrays]


def pack_body(pan_own, charge, needs, message, wide):
    width = charge.shape[1] // pan_own
    for q in range(pan_own):
        message[q] = charge[:, q * width : (q + 1) * width]
    wide[...] = jnp.zeros_like(wide)
    wide[: needs.shape[0], : needs.shape[1]] = needs[...]
    message[pan_own] = wide[...].astype(F32).astype(BF16)


def ends_body(n_row, n_col, seg_own, pan_own, cap, slots, links, cur, off, own, *rest):
    sends, (blocks, hots, acc) = rest[: n_col - 1], rest[n_col - 1 :]
    width = cur.shape[1] // seg_own
    pan_group = pan_own * n_col
    r, c = lax.axis_index("row"), lax.axis_index("col")
    acc[...] = jnp.zeros_like(acc)
    levels = lax.broadcasted_iota(jnp.int32, (width, width), 0)

    def block(k):
        span = pl.ds(pl.multiple_of(k * width, width), width)
        value = cur[:, span]
        blocks[k] = value
        to_hot = jnp.where(levels == off[0:1, span], 1.0, 0.0).astype(BF16)
        from_hot = jnp.where(levels == off[1:2, span], -1.0, 0.0).astype(BF16)
        hot = jnp.concatenate([to_hot, from_hot], axis=0)
        hots[k] = hot
        sums = lax.dot_general(value, hot, (((1,), (1,)), ((), ())), preferred_element_type=F32)
        return sums.astype(BF16).astype(F32)

    unroll = 8

    def step(i, carry):
        got = [block(i * unroll + u) for u in range(unroll)]
        for u in range(unroll):
            for e in range(2):
                slot = slots[e, i * unroll + u]
                p = lax.div(slot, cap)
                b = links[p, slot - p * cap]
                acc[lax.bitwise_xor(p, r) * pan_group + b] += got[u][:, e * width : (e + 1) * width]
        return carry

    lax.fori_loop(0, seg_own // unroll, step, 0)
    for k in range(n_row):
        here = pl.ds(k * pan_own, pan_own)
        own[here] = acc[pl.ds(k * pan_group + c * pan_own, pan_own)]
        for j in range(1, n_col):
            there = lax.bitwise_xor(c, j)
            sends[j - 1][here] = acc[pl.ds(k * pan_group + there * pan_own, pan_own)].astype(BF16)


def relay_body(n_row, n_col, pan_own, *refs):
    packs = refs[:n_row][::-1]
    ends = refs[n_row : n_row + n_col - 1]
    asked, *messages = refs[n_row + n_col - 1 :]
    r = lax.axis_index("row")
    rhs, width = packs[0].shape[1:]
    mine = lax.broadcasted_iota(jnp.int32, (rhs, width), 0) == r
    for k in range(n_row):
        needs = packs[k][pan_own].astype(F32)
        asked[k : k + 1, :] = jnp.sum(jnp.where(mine, needs, 0.0), axis=0, keepdims=True).astype(jnp.int32)
        for message in messages:
            message[pl.ds(k * pan_own, pan_own)] = packs[k][pl.ds(0, pan_own)]
    for message, sums in zip(messages, ends):
        message[pl.ds(n_row * pan_own, n_row * pan_own)] = sums[...]


def pick_body(n_row, n_col, cap, asked, own, *refs):
    peers, outs = refs[: n_col - 1], refs[n_col - 1 :]
    seg_own, _, width = own.shape
    c = lax.axis_index("col")
    for k in range(n_row):
        for s in range(cap):
            b = asked[k, s]
            holder = lax.div(b, seg_own)
            b = b - holder * seg_own
            j = lax.bitwise_xor(holder, c)
            value = own[b]
            span = pl.ds(pl.multiple_of(b * width, width), width)
            for q, peer in enumerate(peers):
                value = jnp.where(j == q + 1, peer[:, span], value)
            outs[n_row - 1 - k][s] = value


def multiply(tiles, src, source, rows, acc):
    rhs, width = src.shape[1:]
    unroll = min(32, tiles.shape[0])

    def step(i, carry):
        start = i * unroll
        got = []
        for u in range(0, unroll, 2):
            t = start + u
            left = jnp.concatenate([src[source(t)], src[source(t + 1)]], axis=0)
            right = jnp.concatenate([tiles[t], tiles[t + 1]], axis=1)
            both = jnp.dot(left, right, preferred_element_type=F32)
            got += [both[:rhs, :width], both[rhs:, width:]]
        for u, value in enumerate(got):
            acc[rows[start + u]] += value
        return carry

    lax.fori_loop(0, tiles.shape[0] // unroll, step, 0)


def coeff_body(n_row, n_col, pan_own, slots, rows, needs, *refs):
    packs = refs[:n_row][::-1]
    from_col = refs[n_row : n_row + n_col - 1]
    tiles, part, message, src, named = refs[n_row + n_col - 1 :]
    r, c = lax.axis_index("row"), lax.axis_index("col")
    pan_group = pan_own * n_col
    cap = needs.shape[1]
    for k in range(n_row):
        first = lax.bitwise_xor(r, k) * pan_group
        src[pl.ds(first + c * pan_own, pan_own)] = packs[k][pl.ds(0, pan_own)]
        for j, x in enumerate(from_col):
            there = first + lax.bitwise_xor(c, j + 1) * pan_own
            src[pl.ds(there, pan_own)] = x[pl.ds(k * pan_own, pan_own)]
    for p in range(n_row):
        for s in range(cap):
            named[p * cap + s] = p * pan_group + needs[p, s]
    part[...] = jnp.zeros_like(part)
    multiply(tiles, src, lambda t: named[slots[t]], rows, part)
    high = part[...].astype(BF16)
    message[pl.ds(0, pan_group)] = high
    message[pl.ds(pan_group, pan_group)] = (part[...] - high.astype(F32)).astype(BF16)


def induct_body(n_row, n_col, seg_own, slots, rows, _after, *refs):
    got = refs[:n_row][::-1]
    tiles = refs[n_row]
    own, *sends = refs[n_row + 1 : -2]
    src, acc = refs[-2:]
    cap = got[0].shape[0]
    r, c = lax.axis_index("row"), lax.axis_index("col")
    for k in range(n_row):
        src[pl.ds(lax.bitwise_xor(r, k) * cap, cap)] = got[k][...]
    acc[...] = jnp.zeros_like(acc)
    multiply(tiles, src, lambda t: slots[t], rows, acc)
    own[...] = acc[pl.ds(c * seg_own, seg_own)]
    for j in range(1, n_col):
        sends[j - 1][...] = acc[pl.ds(lax.bitwise_xor(c, j) * seg_own, seg_own)].astype(BF16)


def panels_body(n_row, n_col, pan_own, part, ends_own, *refs):
    parts = refs[: n_col - 1]
    relayed = refs[n_col - 1 : 2 * n_col - 2]
    pot, end_keep, *messages = refs[2 * n_col - 2 :]
    pan_group = part.shape[0]
    total = part[...]
    for x in parts:
        total += x[pl.ds(0, pan_group)].astype(F32) + x[pl.ds(pan_group, pan_group)].astype(F32)
    rounded = total.astype(BF16)
    pot[...] = rounded
    for k in range(n_row):
        sums = ends_own[pl.ds(k * pan_own, pan_own)]
        for x in relayed:
            sums += x[pl.ds((n_row + k) * pan_own, pan_own)].astype(F32)
        if k == 0:
            end_keep[...] = sums
        else:
            messages[n_row - 1 - k][pl.ds(0, pan_own)] = sums.astype(BF16)
            messages[n_row - 1 - k][pl.ds(pan_own, pan_group)] = rounded


def final_body(n_row, n_col, pan_own, cap, slots, links, hots, charge, scale, *refs):
    field_own, end_own, pot = refs[:3]
    field_in = refs[3 : 2 + n_col]
    arrived = refs[2 + n_col : 1 + n_col + n_row][::-1]
    seg_out, pan_out, pot_out, held = refs[1 + n_col + n_row :]
    width = charge.shape[1] // pan_own
    pan_group = pan_own * n_col
    r, c = lax.axis_index("row"), lax.axis_index("col")
    held[pl.ds(r * pan_group, pan_group)] = pot[...]
    for k, x in enumerate(arrived):
        sender = lax.bitwise_xor(r, k + 1)
        held[pl.ds(sender * pan_group, pan_group)] = x[pl.ds(pan_own, pan_group)]
    for q in range(pan_own):
        span = slice(q * width, (q + 1) * width)
        total = end_own[q]
        for x in arrived:
            total += x[q].astype(F32)
        pan_out[:, span] = (scale[...] * charge[:, span].astype(F32) + total).astype(BF16)
        pot_out[:, span] = pot[c * pan_own + q]

    def block(k):
        ends = []
        for e in range(2):
            slot = slots[e, k]
            p = lax.div(slot, cap)
            ends.append(held[p * pan_group + links[p, slot - p * cap]])
        drops = jnp.dot(jnp.concatenate(ends, axis=1), hots[k], preferred_element_type=F32)
        total = field_own[k]
        for x in field_in:
            total += x[k].astype(F32)
        return (total + drops).astype(BF16)

    unroll = 16

    def step(i, carry):
        got = [block(i * unroll + u) for u in range(unroll)]
        for u, value in enumerate(got):
            first = pl.multiple_of((i * unroll + u) * width, width)
            seg_out[:, pl.ds(first, width)] = value
        return carry

    lax.fori_loop(0, hots.shape[0] // unroll, step, 0)


def shards(
    current,
    charge,
    rhs_scale,
    induct_tiles,
    induct_rows,
    induct_slots,
    induct_needs,
    coeff_tiles,
    coeff_rows,
    coeff_slots,
    coeff_needs,
    link_needs,
    end_slots,
    end_offsets,
):
    n_row = lax.axis_size("row")
    n_col = lax.axis_size("col")
    width = induct_tiles.shape[1]
    rhs = current.shape[0]
    seg_own = current.shape[1] // width
    pan_own = charge.shape[1] // width
    seg_group, pan_group = seg_own * n_col, pan_own * n_col
    cap_l, cap_p, cap_k = induct_needs.shape[1], coeff_needs.shape[1], link_needs.shape[1]
    slots_t, off_t = end_slots.T, end_offsets.T

    def like(blocks, dtype):
        return jax.ShapeDtypeStruct((blocks, rhs, width), dtype)

    cur = exchange_all(current, [current] * (n_col - 1), "col")
    (pack,) = call(
        functools.partial(pack_body, pan_own),
        "pack_charges",
        [like(pan_own + 1, BF16)],
        [VMEM] * 2,
        [pltpu.VMEM((rhs, width), jnp.int32)],
        moved=2**16,
    )(*in_hbm(charge, induct_needs))
    packs = exchange_all(pack, [pack] * (n_row - 1), "row")

    rows_own = n_row * pan_own
    ends_own, *rest = call(
        functools.partial(ends_body, n_row, n_col, seg_own, pan_own, cap_k),
        "end_sums",
        [like(rows_own, F32)]
        + [like(rows_own, BF16)] * (n_col - 1)
        + [like(seg_own, BF16), jax.ShapeDtypeStruct((seg_own, 2 * width, width), BF16)],
        [SMEM, SMEM, VMEM, VMEM],
        [pltpu.VMEM((n_row * pan_group, rhs, width), F32)],
        flops=2 * 10**9,
        moved=2**18,
    )(*in_hbm(slots_t, link_needs, current, off_t))
    ends_out, (own_blocks, hots) = rest[: n_col - 1], rest[n_col - 1 :]

    asked, *relays = call(
        functools.partial(relay_body, n_row, n_col, pan_own),
        "relay_charges",
        [jax.ShapeDtypeStruct((n_row, width), jnp.int32)] + [like(2 * rows_own, BF16)] * (n_col - 1),
        [VMEM] * (n_row + n_col - 1),
        moved=2**16,
    )(*packs[::-1], *ends_out)
    relayed = exchange_all(None, relays, "col")[1:]

    *picks, own_picks = call(
        functools.partial(pick_body, n_row, n_col, cap_l),
        "pick_blocks",
        [like(cap_l, BF16)] * n_row,
        [SMEM] + [VMEM] * n_col,
        moved=2**18,
    )(asked, own_blocks, *cur[1:])
    got = exchange_all(own_picks, picks[::-1], "row")

    part, message = call(
        functools.partial(coeff_body, n_row, n_col, pan_own),
        "coeff_tiles",
        [like(pan_group, F32), like(2 * pan_group, BF16)],
        [SMEM] * 3 + [VMEM] * (n_row + n_col),
        [
            pltpu.VMEM((n_row * pan_group, rhs, width), BF16),
            pltpu.SMEM((n_row * cap_p,), jnp.int32),
        ],
        flops=2 * 10**9,
        moved=coeff_tiles.size * 2,
    )(coeff_slots, coeff_rows, coeff_needs, *packs[::-1], *relayed, coeff_tiles)
    parts = exchange_all(None, [message] * (n_col - 1), "col")[1:]

    field_own, *field_out = call(
        functools.partial(induct_body, n_row, n_col, seg_own),
        "induct_tiles",
        [like(seg_own, F32)] + [like(seg_own, BF16)] * (n_col - 1),
        [SMEM, SMEM, ANY] + [VMEM] * (n_row + 1),
        [
            pltpu.VMEM((n_row * cap_l, rhs, width), BF16),
            pltpu.VMEM((seg_group, rhs, width), F32),
        ],
        flops=4 * 10**9,
        moved=induct_tiles.size * 2,
    )(induct_slots, induct_rows, part, *got[::-1], induct_tiles)
    field_in = exchange_all(None, field_out, "col")[1:]

    pot, end_keep, *row_messages = call(
        functools.partial(panels_body, n_row, n_col, pan_own),
        "panel_sums",
        [like(pan_group, BF16), like(pan_own, F32)] + [like(pan_own + pan_group, BF16)] * (n_row - 1),
        [VMEM] * (2 * n_col),
        flops=5 * 10**9,
        moved=2**18,
    )(part, ends_own, *parts, *relayed)
    arrived = exchange_all(None, row_messages[::-1], "row")[1:]

    return tuple(
        call(
            functools.partial(final_body, n_row, n_col, pan_own, cap_k),
            "outputs",
            [jax.ShapeDtypeStruct(x.shape, BF16) for x in (current, charge, charge)],
            [SMEM, SMEM] + [VMEM] * (4 + n_col + n_row),
            [pltpu.VMEM((n_row * pan_group, rhs, width), BF16)],
            flops=2 * 10**9,
            moved=2**20,
        )(
            slots_t,
            link_needs,
            hots,
            charge,
            rhs_scale[:, None],
            field_own,
            end_keep,
            pot,
            *field_in,
            *arrived[::-1],
        )
    )


def solution(mesh):
    blocks = P(("parts", "row", "col"))
    matrix = P(("parts", "row", "col"), None)
    tiles = P(("parts", "row", "col"), None, None)
    values = P("rhs", ("parts", "row", "col"))
    return jax.shard_map(
        shards,
        mesh=mesh,
        in_specs=(
            values,
            values,
            P(("parts", "rhs")),
            tiles,
            blocks,
            blocks,
            matrix,
            tiles,
            blocks,
            blocks,
            matrix,
            matrix,
            matrix,
            matrix,
        ),
        out_specs=(values, values, values),
        check_vma=False,
    )
```

time: 43 us -> 35.8 us (0.83)
  Pallas kernels: 15.1 us -> 9.9 us
  waiting for transfers between devices: 6.84 us -> 2.86 us
  starting transfers between devices: 19.2 us -> 21.7 us
  other arithmetic: 0.77 us -> 0.01 us
    pallas_call x4 -> x6, Pallas kernels: 12.1 us -> 7.38 us  [the longest x1 2.42 us: shards(): call(functools.partial(induct_body, n_row, n_col, seg_own), 'induct_tiles...]
    ppermute x13, waiting for transfers between devices: 6.84 us -> 2.86 us  [exchange(): lax.ppermute(x, axis, [(i, i ^ k) for i in range(lax.axis_size(axis))])]
    ppermute x13, starting transfers between devices: 19.2 us -> 21.7 us  [exchange(): lax.ppermute(x, axis, [(i, i ^ k) for i in range(lax.axis_size(axis))])]
    concatenate x1 -> x0, other arithmetic: 0.77 us -> none  [shards(): needs = jnp.concatenate([induct_needs, coeff_needs], axis=1)]
    pallas_call x1, Pallas kernels: 2.94 us -> 2.49 us  [shards(): call(functools.partial(ends_body, n_row, n_col, seg_own, pan_own, cap_k),...]
  transfers between devices with their start and end apart: 13 -> 13, of which waited for: 7 -> 4; matrix products, arithmetic and copies ran while one was open for 2% -> 0% of each run, Pallas kernels for 19% -> 20%
where the time goes in v3:
time: 35.8 us; the launch traced here: 35.4 us
  starting transfers between devices  21.7 us (61%)
  Pallas kernels  9.9 us (28%)
  waiting for transfers between devices  2.86 us (8%)
  between operations  0.8 us (2%)
    ppermute x13, starting transfers between devices, exchange(): lax.ppermute(x, axis, [(i, i ^ k) for i in range(lax.axis_size(axis))])  21.7 us
    ppermute x13, waiting for transfers between devices, exchange(): lax.ppermute(x, axis, [(i, i ^ k) for i in range(lax.axis_size(axis))])  2.86 us
    pallas_call x1, Pallas kernels, shards(): call(functools.partial(ends_body, n_row, n_col, seg_own, pan_own, cap_k),...  2.49 us
    pallas_call x1, Pallas kernels, shards(): call(functools.partial(induct_body, n_row, n_col, seg_own), 'induct_tiles...  2.42 us
    pallas_call x1, Pallas kernels, shards(): call(functools.partial(final_body, n_row, n_col, pan_own, cap_k), 'output...  1.94 us
    pallas_call x1, Pallas kernels, shards(): call(functools.partial(coeff_body, n_row, n_col, pan_own), 'coeff_tiles',...  1.52 us
    pallas_call x1, Pallas kernels, shards(): call(functools.partial(pick_body, n_row, n_col, cap_l), 'pick_blocks', [l...  0.73 us
    pallas_call x1, Pallas kernels, shards(): call(functools.partial(pack_body, pan_own), 'pack_charges', [like(pan_own...  0.73 us
  transfers between devices with their start and end apart: 13, of which 4 were waited for; matrix products, arithmetic and copies ran while one was open for 0% of the time, Pallas kernels for 20%

profile of v3, /device:TPU:0, one launch (start us, length us, event | category | flops | bytes accessed | tf_op | source)
XLA Modules:
  0.0 35.4 jit_solution(828645618457660842)
XLA Ops:
  0.6 0.7 %pack_charges.1.refs_3_ = bf16[5,16,128]{2,1,0:T(8,128)(2,1)S(1)} custom-call(bf16[16,512]{1,0:T(8,128)(2,1)} %charge.3, s32[4,8]{1,0:T(4,128)} %needs.2), custom_call_target="tpu_custom_call" | custom-call | bytes 65536 | tf_op jit(solution)/shard_map/pack_charges/pallas_call | solution.py:284
  1.4 5.0 %collective-permute-start = (bf16[5,16,128]{2,1,0:T(8,128)(2,1)S(1)}, bf16[5,16,128]{2,1,0:T(8,128)(2,1)S(1)}, u32[]{:S(2)}, u32[]{:S(2)}) collective-permute-start(bf16[5,16,128]{2,1,0:T(8,128)(2,1)S(1)} %pack_charges.1.refs_3_), channel_id=1, source_target_pairs={{0,12},{4,8},{8,4},{12,0},{1,13},{5,9},{9,5},{13,1},{2,14},{6,10},... | collective-permute-start | bytes 61448 | tf_op jit(solution)/shard_map/ppermute | solution.py:20
  6.4 0.0 collective-permute-start.1
  6.4 0.6 %collective-permute-start.2 = (bf16[5,16,128]{2,1,0:T(8,128)(2,1)S(1)}, bf16[5,16,128]{2,1,0:T(8,128)(2,1)S(1)}, u32[]{:S(2)}, u32[]{:S(2)}) collective-permute-start(bf16[5,16,128]{2,1,0:T(8,128)(2,1)S(1)} %pack_charges.1.refs_3_), channel_id=1, source_target_pairs={{0,4},{4,0},{8,12},{12,8},{1,5},{5,1},{9,13},{13,9},{2,6},{6,2},{1... | collective-permute-start | bytes 61448 | tf_op jit(solution)/shard_map/ppermute | solution.py:20
  7.0 1.6 %collective-permute-start.4 = (bf16[16,4096]{1,0:T(8,128)(2,1)}, bf16[16,4096]{1,0:T(8,128)(2,1)S(1)}, u32[]{:S(2)}, u32[]{:S(2)}) collective-permute-start(bf16[16,4096]{1,0:T(8,128)(2,1)} %cur.1), channel_id=1, source_target_pairs={{0,2},{2,0},{1,3},{3,1},{4,6},{6,4},{5,7},{7,5},{8,10},{10,8},{9,1... | collective-permute-start | bytes 393224 | tf_op jit(solution)/shard_map/ppermute | solution.py:20
  8.7 0.0 slice-start
  8.7 2.5 %end_sums.1 = (f32[16,16,128]{2,1,0:T(8,128)S(1)}, bf16[16,16,128]{2,1,0:T(8,128)(2,1)S(1)}, bf16[32,16,128]{2,1,0:T(8,128)(2,1)S(1)}, bf16[32,256,128]{2,1,0:T(8,128)(2,1)S(1)}) custom-call(s32[2,32]{1,0:T(2,128)} %bitcast.5, s32[4,16]{1,0:T(4,128)} %links.3, bf16[16,4096]{1,0:T(8,128)(2,1)} %cur.1, s32[2,4096]{1,0:T(2,128)} %bitcast.8), custom_call_target="tpu_custom_call" | custom-call | flops 2000000000 | bytes 262144 | tf_op jit(solution)/shard_map/end_sums/pallas_call | solution.py:295
  11.2 0.0 collective-permute-done.refs_0_
  11.2 0.0 collective-permute-done.1.refs_1_
  11.2 0.0 collective-permute-done.2.refs_2_
  11.3 1.4 %collective-permute-start.3 = (bf16[32,16,128]{2,1,0:T(8,128)(2,1)S(1)}, bf16[32,16,128]{2,1,0:T(8,128)(2,1)S(1)}, u32[]{:S(2)}, u32[]{:S(2)}) collective-permute-start(bf16[32,16,128]{2,1,0:T(8,128)(2,1)S(1)} %get-tuple-element.24), channel_id=1, source_target_pairs={{0,2},{2,0},{1,3},{3,1},{4,6},{6,4},{5,7},{7,5},{8,10},{10,8},{9,1... | collective-permute-start | bytes 393224 | tf_op jit(solution)/shard_map/ppermute | solution.py:20
  12.7 0.7 %pick_blocks.1 = (bf16[8,16,128]{2,1,0:T(8,128)(2,1)S(1)}, bf16[8,16,128]{2,1,0:T(8,128)(2,1)S(1)}, bf16[8,16,128]{2,1,0:T(8,128)(2,1)S(1)}, bf16[8,16,128]{2,1,0:T(8,128)(2,1)S(1)}) custom-call(s32[4,128]{1,0:T(4,128)S(1)} %get-tuple-element.26.asked, bf16[32,16,128]{2,1,0:T(8,128)(2,1)S(1)} %get-tuple-element.27.own, ...), custom_call_target="tpu_custom_call" | custom-call | bytes 262144 | tf_op jit(solution)/shard_map/pick_blocks/pallas_call | solution.py:317
  13.4 3.4 %collective-permute-start.5 = (bf16[8,16,128]{2,1,0:T(8,128)(2,1)S(1)}, bf16[8,16,128]{2,1,0:T(8,128)(2,1)S(1)}, u32[]{:S(2)}, u32[]{:S(2)}) collective-permute-start(bf16[8,16,128]{2,1,0:T(8,128)(2,1)S(1)} %get-tuple-element.28), channel_id=1, source_target_pairs={{0,12},{4,8},{8,4},{12,0},{1,13},{5,9},{9,5},{13,1},{2,14},{6,10},... | collective-permute-start | bytes 98312 | tf_op jit(solution)/shard_map/ppermute | solution.py:20
  16.8 1.1 %collective-permute-start.7 = (bf16[8,16,128]{2,1,0:T(8,128)(2,1)S(1)}, bf16[8,16,128]{2,1,0:T(8,128)(2,1)S(1)}, u32[]{:S(2)}, u32[]{:S(2)}) collective-permute-start(bf16[8,16,128]{2,1,0:T(8,128)(2,1)S(1)} %get-tuple-element.30), channel_id=1, source_target_pairs={{0,4},{4,0},{8,12},{12,8},{1,5},{5,1},{9,13},{13,9},{2,6},{6,2},{1... | collective-permute-start | bytes 98312 | tf_op jit(solution)/shard_map/ppermute | solution.py:20
  17.9 0.0 collective-permute-done.3.refs_4_.refs_1_
  17.9 1.5 %coeff_tiles.1 = (f32[8,16,128]{2,1,0:T(8,128)S(1)}, bf16[16,16,128]{2,1,0:T(8,128)(2,1)S(1)}) custom-call(s32[96]{0:T(128)S(1)} %copy-done.7, s32[96]{0:T(128)S(1)} %copy-done.8, s32[4,4]{1,0:T(4,128)S(1)} %copy-done.2, bf16[5,16,128]{2,1,0:T(8,128)(2,1)S(1)} %collective-permute-done.refs_0_, bf16[5,16,128]{2,1,0:T(8,128)(2,1)S(1)} %collective-permute-done.1.refs_1_, ...), custom_call_target="tpu_custom_call" | custom-call | flops 2000000000 | bytes 3145728 | tf_op jit(solution)/shard_map/coeff_tiles/pallas_call | solution.py:326
  19.4 1.8 %collective-permute-start.8 = (bf16[16,16,128]{2,1,0:T(8,128)(2,1)S(1)}, bf16[16,16,128]{2,1,0:T(8,128)(2,1)S(1)}, u32[]{:S(2)}, u32[]{:S(2)}) collective-permute-start(bf16[16,16,128]{2,1,0:T(8,128)(2,1)S(1)} %get-tuple-element.34), channel_id=1, source_target_pairs={{0,2},{2,0},{1,3},{3,1},{4,6},{6,4},{5,7},{7,5},{8,10},{10,8},{9,1... | collective-permute-start | bytes 196616 | tf_op jit(solution)/shard_map/ppermute | solution.py:20
  21.3 0.3 collective-permute-done.6.refs_1_
  21.6 0.0 collective-permute-done.7.refs_2_
  21.6 2.4 %induct_tiles.1 = (f32[32,16,128]{2,1,0:T(8,128)S(1)}, bf16[32,16,128]{2,1,0:T(8,128)(2,1)S(1)}) custom-call(s32[192]{0:T(256)S(1)} %copy-done.4, s32[192]{0:T(256)S(1)} %copy-done.5, f32[8,16,128]{2,1,0:T(8,128)S(1)} %get-tuple-element.25._after.part, bf16[8,16,128]{2,1,0:T(8,128)(2,1)S(1)} %collective-permute-done.5.refs_0_, ...), custom_call_target="tpu_custom_call" | custom-call | flops 4000000000 | bytes 6291456 | tf_op jit(solution)/shard_map/induct_tiles/pallas_call | solution.py:340
  24.1 2.3 %collective-permute-start.9 = (bf16[32,16,128]{2,1,0:T(8,128)(2,1)S(1)}, bf16[32,16,128]{2,1,0:T(8,128)(2,1)S(1)}, u32[]{:S(2)}, u32[]{:S(2)}) collective-permute-start(bf16[32,16,128]{2,1,0:T(8,128)(2,1)S(1)} %get-tuple-element.37), channel_id=1, source_target_pairs={{0,2},{2,0},{1,3},{3,1},{4,6},{6,4},{5,7},{7,5},{8,10},{10,8},{9,1... | collective-permute-start | bytes 393224 | tf_op jit(solution)/shard_map/ppermute | solution.py:20
  26.3 0.0 collective-permute-done.8.refs_0_
  26.4 0.0 copy-start.6
  26.4 1.7 %collective-permute-start.10 = (bf16[12,16,128]{2,1,0:T(8,128)(2,1)S(1)}, bf16[12,16,128]{2,1,0:T(8,128)(2,1)S(1)}, u32[]{:S(2)}, u32[]{:S(2)}) collective-permute-start(bf16[12,16,128]{2,1,0:T(8,128)(2,1)S(1)} %get-tuple-element.38), channel_id=1, source_target_pairs={{0,12},{4,8},{8,4},{12,0},{1,13},{5,9},{9,5},{13,1},{2,14},{6,10},... | collective-permute-start | bytes 147464 | tf_op jit(solution)/shard_map/ppermute | solution.py:20
  28.1 0.5 %collective-permute-start.11 = (bf16[12,16,128]{2,1,0:T(8,128)(2,1)S(1)}, bf16[12,16,128]{2,1,0:T(8,128)(2,1)S(1)}, u32[]{:S(2)}, u32[]{:S(2)}) collective-permute-start(bf16[12,16,128]{2,1,0:T(8,128)(2,1)S(1)} %get-tuple-element.39), channel_id=1, source_target_pairs={{0,8},{4,12},{8,0},{12,4},{1,9},{5,13},{9,1},{13,5},{2,10},{6,14},... | collective-permute-start | bytes 147464 | tf_op jit(solution)/shard_map/ppermute | solution.py:20
  28.6 2.3 %collective-permute-start.12 = (bf16[12,16,128]{2,1,0:T(8,128)(2,1)S(1)}, bf16[12,16,128]{2,1,0:T(8,128)(2,1)S(1)}, u32[]{:S(2)}, u32[]{:S(2)}) collective-permute-start(bf16[12,16,128]{2,1,0:T(8,128)(2,1)S(1)} %get-tuple-element.40), channel_id=1, source_target_pairs={{0,4},{4,0},{8,12},{12,8},{1,5},{5,1},{9,13},{13,9},{2,6},{6,2},{1... | collective-permute-start | bytes 147464 | tf_op jit(solution)/shard_map/ppermute | solution.py:20
  30.9 0.1 copy.17.scale
  30.9 1.4 %collective-permute-done.10.refs_4_ = bf16[12,16,128]{2,1,0:T(8,128)(2,1)S(1)} collective-permute-done((bf16[12,16,128]{2,1,0:T(8,128)(2,1)S(1)}, bf16[12,16,128]{2,1,0:T(8,128)(2,1)S(1)}, u32[]{:S(2)}, u32[]{:S(2)}) %collective-permute-start.10) | collective-permute-done | bytes 49184 | tf_op jit(solution)/shard_map/ppermute | solution.py:20
  32.4 0.8 %collective-permute-done.11.refs_5_ = bf16[12,16,128]{2,1,0:T(8,128)(2,1)S(1)} collective-permute-done((bf16[12,16,128]{2,1,0:T(8,128)(2,1)S(1)}, bf16[12,16,128]{2,1,0:T(8,128)(2,1)S(1)}, u32[]{:S(2)}, u32[]{:S(2)}) %collective-permute-start.11) | collective-permute-done | bytes 49184 | tf_op jit(solution)/shard_map/ppermute | solution.py:20
  33.2 0.3 collective-permute-done.12.refs_6_
  33.4 0.0 collective-permute-done.9.refs_3_
  33.5 1.9 %outputs.1 = (bf16[16,4096]{1,0:T(8,128)(2,1)}, bf16[16,512]{1,0:T(8,128)(2,1)}, bf16[16,512]{1,0:T(8,128)(2,1)}) custom-call(s32[2,32]{1,0:T(2,128)S(1)} %bitcast.6, s32[4,16]{1,0:T(4,128)S(1)} %copy-done.3, bf16[32,256,128]{2,1,0:T(8,128)(2,1)S(1)} %get-tuple-element.22.hots, bf16[16,512]{1,0:T(8,128)(2,1)S(1)} %copy-done, f32[16,1]{1,0:T(8,128)S(1)} %copy.17.scale, ...), custom_call_target="tpu_custom_call" | custom-call | flops 2000000000 | bytes 1048576 | tf_op jit(solution)/shard_map/outputs/pallas_call | solution.py:365
  (28 shorter events, 0.1 us)
Async XLA Ops:
  1.4 9.9 %collective-permute-start = (bf16[5,16,128]{2,1,0:T(8,128)(2,1)S(1)}, bf16[5,16,128]{2,1,0:T(8,128)(2,1)S(1)}, u32[]{:S(2)}, u32[]{:S(2)}) collective-permute-start(bf16[5,16,128]{2,1,0:T(8,128)(2,1)S(1)} %pack_charges.1.refs_3_), channel_id=1, source_target_pairs={{0,12},{4,8},{8,4},{12,0},{1,13},{5,9},{9,5},{13,1},{2,14},{6,10},... | collective-permute-start | bytes 61448 | tf_op jit(solution)/shard_map/ppermute | solution.py:20
  6.4 4.8 %collective-permute-start.1 = (bf16[5,16,128]{2,1,0:T(8,128)(2,1)S(1)}, bf16[5,16,128]{2,1,0:T(8,128)(2,1)S(1)}, u32[]{:S(2)}, u32[]{:S(2)}) collective-permute-start(bf16[5,16,128]{2,1,0:T(8,128)(2,1)S(1)} %pack_charges.1.refs_3_), channel_id=1, source_target_pairs={{0,8},{4,12},{8,0},{12,4},{1,9},{5,13},{9,1},{13,5},{2,10},{6,14},... | collective-permute-start | bytes 61448 | tf_op jit(solution)/shard_map/ppermute | solution.py:20
  6.4 4.8 %collective-permute-start.2 = (bf16[5,16,128]{2,1,0:T(8,128)(2,1)S(1)}, bf16[5,16,128]{2,1,0:T(8,128)(2,1)S(1)}, u32[]{:S(2)}, u32[]{:S(2)}) collective-permute-start(bf16[5,16,128]{2,1,0:T(8,128)(2,1)S(1)} %pack_charges.1.refs_3_), channel_id=1, source_target_pairs={{0,4},{4,0},{8,12},{12,8},{1,5},{5,1},{9,13},{13,9},{2,6},{6,2},{1... | collective-permute-start | bytes 61448 | tf_op jit(solution)/shard_map/ppermute | solution.py:20
  7.0 5.6 %collective-permute-start.4 = (bf16[16,4096]{1,0:T(8,128)(2,1)}, bf16[16,4096]{1,0:T(8,128)(2,1)S(1)}, u32[]{:S(2)}, u32[]{:S(2)}) collective-permute-start(bf16[16,4096]{1,0:T(8,128)(2,1)} %cur.1), channel_id=1, source_target_pairs={{0,2},{2,0},{1,3},{3,1},{4,6},{6,4},{5,7},{7,5},{8,10},{10,8},{9,1... | collective-permute-start | bytes 393224 | tf_op jit(solution)/shard_map/ppermute | solution.py:20
  8.7 9.2 %copy-start.1 = (bf16[96,128,128]{2,1,0:T(8,128)(2,1)S(1)}, bf16[96,128,128]{2,1,0:T(8,128)(2,1)}, u32[]{:S(2)}) copy-start(bf16[96,128,128]{2,1,0:T(8,128)(2,1)} %refs_5_.1) | copy-start | bytes 9437188
  8.7 9.2 %copy-start.2 = (s32[4,4]{1,0:T(4,128)S(1)}, s32[4,4]{1,0:T(4,128)}, u32[]{:S(2)}) copy-start(s32[4,4]{1,0:T(4,128)} %needs.3) | copy-start | bytes 196
  8.7 9.2 %copy-start.7 = (s32[96]{0:T(128)S(1)}, s32[96]{0:T(128)}, u32[]{:S(2)}) copy-start(s32[96]{0:T(128)} %slots.2) | copy-start | bytes 1156
  8.7 9.2 %copy-start.8 = (s32[96]{0:T(128)S(1)}, s32[96]{0:T(128)}, u32[]{:S(2)}) copy-start(s32[96]{0:T(128)} %rows.2) | copy-start | bytes 1156
  8.7 12.9 %slice-start = ((s8[6291456]{0:T(1024)(128)(4,1)}), s8[4194304]{0:T(1024)(128)(4,1)S(1)}, s32[]{:S(2)}) async-start(s8[6291456]{0:T(1024)(128)(4,1)} %bitcast.3), calls=%async_computation | async-start | bytes 8388608
  11.3 6.6 %collective-permute-start.3 = (bf16[32,16,128]{2,1,0:T(8,128)(2,1)S(1)}, bf16[32,16,128]{2,1,0:T(8,128)(2,1)S(1)}, u32[]{:S(2)}, u32[]{:S(2)}) collective-permute-start(bf16[32,16,128]{2,1,0:T(8,128)(2,1)S(1)} %get-tuple-element.24), channel_id=1, source_target_pairs={{0,2},{2,0},{1,3},{3,1},{4,6},{6,4},{5,7},{7,5},{8,10},{10,8},{9,1... | collective-permute-start | bytes 393224 | tf_op jit(solution)/shard_map/ppermute | solution.py:20
  12.7 8.9 %slice-start.1 = ((s8[6291456]{0:T(1024)(128)(4,1)}), s8[2097152]{0:T(1024)(128)(4,1)S(1)}, s32[]{:S(2)}) async-start(s8[6291456]{0:T(1024)(128)(4,1)} %bitcast.3), calls=%async_computation.1 | async-start | bytes 4194304
  13.4 7.8 %collective-permute-start.5 = (bf16[8,16,128]{2,1,0:T(8,128)(2,1)S(1)}, bf16[8,16,128]{2,1,0:T(8,128)(2,1)S(1)}, u32[]{:S(2)}, u32[]{:S(2)}) collective-permute-start(bf16[8,16,128]{2,1,0:T(8,128)(2,1)S(1)} %get-tuple-element.28), channel_id=1, source_target_pairs={{0,12},{4,8},{8,4},{12,0},{1,13},{5,9},{9,5},{13,1},{2,14},{6,10},... | collective-permute-start | bytes 98312 | tf_op jit(solution)/shard_map/ppermute | solution.py:20
  16.8 4.8 %collective-permute-start.6 = (bf16[8,16,128]{2,1,0:T(8,128)(2,1)S(1)}, bf16[8,16,128]{2,1,0:T(8,128)(2,1)S(1)}, u32[]{:S(2)}, u32[]{:S(2)}) collective-permute-start(bf16[8,16,128]{2,1,0:T(8,128)(2,1)S(1)} %get-tuple-element.29), channel_id=1, source_target_pairs={{0,8},{4,12},{8,0},{12,4},{1,9},{5,13},{9,1},{13,5},{2,10},{6,14},... | collective-permute-start | bytes 98312 | tf_op jit(solution)/shard_map/ppermute | solution.py:20
  16.8 4.8 %copy-start.4 = (s32[192]{0:T(256)S(1)}, s32[192]{0:T(256)}, u32[]{:S(2)}) copy-start(s32[192]{0:T(256)} %slots.3) | copy-start | bytes 2308
  16.8 4.8 %copy-start.5 = (s32[192]{0:T(256)S(1)}, s32[192]{0:T(256)}, u32[]{:S(2)}) copy-start(s32[192]{0:T(256)} %rows.3) | copy-start | bytes 2308
  16.8 4.8 %collective-permute-start.7 = (bf16[8,16,128]{2,1,0:T(8,128)(2,1)S(1)}, bf16[8,16,128]{2,1,0:T(8,128)(2,1)S(1)}, u32[]{:S(2)}, u32[]{:S(2)}) collective-permute-start(bf16[8,16,128]{2,1,0:T(8,128)(2,1)S(1)} %get-tuple-element.30), channel_id=1, source_target_pairs={{0,4},{4,0},{8,12},{12,8},{1,5},{5,1},{9,13},{13,9},{2,6},{6,2},{1... | collective-permute-start | bytes 98312 | tf_op jit(solution)/shard_map/ppermute | solution.py:20
  19.4 6.9 %collective-permute-start.8 = (bf16[16,16,128]{2,1,0:T(8,128)(2,1)S(1)}, bf16[16,16,128]{2,1,0:T(8,128)(2,1)S(1)}, u32[]{:S(2)}, u32[]{:S(2)}) collective-permute-start(bf16[16,16,128]{2,1,0:T(8,128)(2,1)S(1)} %get-tuple-element.34), channel_id=1, source_target_pairs={{0,2},{2,0},{1,3},{3,1},{4,6},{6,4},{5,7},{7,5},{8,10},{10,8},{9,1... | collective-permute-start | bytes 196616 | tf_op jit(solution)/shard_map/ppermute | solution.py:20
  24.1 9.4 %collective-permute-start.9 = (bf16[32,16,128]{2,1,0:T(8,128)(2,1)S(1)}, bf16[32,16,128]{2,1,0:T(8,128)(2,1)S(1)}, u32[]{:S(2)}, u32[]{:S(2)}) collective-permute-start(bf16[32,16,128]{2,1,0:T(8,128)(2,1)S(1)} %get-tuple-element.37), channel_id=1, source_target_pairs={{0,2},{2,0},{1,3},{3,1},{4,6},{6,4},{5,7},{7,5},{8,10},{10,8},{9,1... | collective-permute-start | bytes 393224 | tf_op jit(solution)/shard_map/ppermute | solution.py:20
  26.3 4.5 %copy-start.9 = (f32[16]{0:T(128)S(1)}, f32[16]{0:T(128)}, u32[]{:S(2)}) copy-start(f32[16]{0:T(128)} %param.16) | copy-start | bytes 196
  26.3 7.1 %copy-start = (bf16[16,512]{1,0:T(8,128)(2,1)S(1)}, bf16[16,512]{1,0:T(8,128)(2,1)}, u32[]{:S(2)}) copy-start(bf16[16,512]{1,0:T(8,128)(2,1)} %charge.3) | copy-start | bytes 49156
  26.3 7.1 %copy-start.3 = (s32[4,16]{1,0:T(4,128)S(1)}, s32[4,16]{1,0:T(4,128)}, u32[]{:S(2)}) copy-start(s32[4,16]{1,0:T(4,128)} %links.3) | copy-start | bytes 772
  26.4 7.1 %copy-start.6 = (s32[32,2]{0,1:T(2,128)S(1)}, s32[32,2]{0,1:T(2,128)}, u32[]{:S(2)}) copy-start(s32[32,2]{0,1:T(2,128)} %param.26) | copy-start | bytes 772
  26.4 6.0 %collective-permute-start.10 = (bf16[12,16,128]{2,1,0:T(8,128)(2,1)S(1)}, bf16[12,16,128]{2,1,0:T(8,128)(2,1)S(1)}, u32[]{:S(2)}, u32[]{:S(2)}) collective-permute-start(bf16[12,16,128]{2,1,0:T(8,128)(2,1)S(1)} %get-tuple-element.38), channel_id=1, source_target_pairs={{0,12},{4,8},{8,4},{12,0},{1,13},{5,9},{9,5},{13,1},{2,14},{6,10},... | collective-permute-start | bytes 147464 | tf_op jit(solution)/shard_map/ppermute | solution.py:20
  28.1 5.1 %collective-permute-start.11 = (bf16[12,16,128]{2,1,0:T(8,128)(2,1)S(1)}, bf16[12,16,128]{2,1,0:T(8,128)(2,1)S(1)}, u32[]{:S(2)}, u32[]{:S(2)}) collective-permute-start(bf16[12,16,128]{2,1,0:T(8,128)(2,1)S(1)} %get-tuple-element.39), channel_id=1, source_target_pairs={{0,8},{4,12},{8,0},{12,4},{1,9},{5,13},{9,1},{13,5},{2,10},{6,14},... | collective-permute-start | bytes 147464 | tf_op jit(solution)/shard_map/ppermute | solution.py:20
  28.6 4.9 %collective-permute-start.12 = (bf16[12,16,128]{2,1,0:T(8,128)(2,1)S(1)}, bf16[12,16,128]{2,1,0:T(8,128)(2,1)S(1)}, u32[]{:S(2)}, u32[]{:S(2)}) collective-permute-start(bf16[12,16,128]{2,1,0:T(8,128)(2,1)S(1)} %get-tuple-element.40), channel_id=1, source_target_pairs={{0,4},{4,0},{8,12},{12,8},{1,5},{5,1},{9,13},{13,9},{2,6},{6,2},{1... | collective-permute-start | bytes 147464 | tf_op jit(solution)/shard_map/ppermute | solution.py:20

commit v4 on v3

v4 whole, which is shorter than its diff:
```python
import functools

import jax
import jax.numpy as jnp
from jax import lax
from jax.experimental import pallas as pl
from jax.experimental.pallas import tpu as pltpu
from jax.sharding import PartitionSpec as P

F32 = jnp.float32
BF16 = jnp.bfloat16
VMEM = pl.BlockSpec(memory_space=pltpu.VMEM)
SMEM = pl.BlockSpec(memory_space=pltpu.SMEM)
ANY = pl.BlockSpec(memory_space=pl.ANY)


def exchange(x, axis, k):
    if k == 0:
        return x
    return lax.ppermute(x, axis, [(i, i ^ k) for i in range(lax.axis_size(axis))])


def exchange_all(others, axis):
    return [exchange(x, axis, k + 1) for k, x in enumerate(others)]


def bits_of(n):
    return [1 << i for i in range(n.bit_length() - 1)]


def gather_plan(bits):
    known = [[0]]
    for bit in bits:
        known.append(known[-1] + [s ^ bit for s in known[-1]])
    return known


def scatter_plan(n, bits):
    left, plan = list(range(n)), []
    for bit in bits:
        plan.append(([k for k in left if not k & bit], [k for k in left if k & bit]))
        left = plan[-1][0]
    return plan


def swap_plan(n, bits):
    at = {(k, 0): (0, k) for k in range(n)}
    hops = []
    for i, bit in enumerate(bits):
        sent = sorted(pair for pair in at if pair[0] & bit)
        hops.append([at.pop(pair) for pair in sent])
        for place, (k, s) in enumerate(sent):
            at[(k ^ bit, s ^ bit)] = (i + 1, place)
    return hops, [at[(0, s)] for s in range(n)]


def call(body, name, out_shape, in_specs, scratch=(), flops=0, moved=0):
    return pl.pallas_call(
        body,
        out_shape=out_shape,
        in_specs=in_specs,
        out_specs=[VMEM] * len(out_shape),
        scratch_shapes=list(scratch),
        compiler_params=pltpu.CompilerParams(vmem_limit_bytes=16 * 2**20),
        cost_estimate=pl.CostEstimate(flops=flops, bytes_accessed=moved, transcendentals=0),
        name=name,
    )


def in_hbm(*arrays):
    return [pltpu.with_memory_space_constraint(x, pltpu.HBM) for x in arrays]


def stage_body(pan_own, seg_own, charge, needs, cur, off, slots, links, message, blocks, off_out, slots_out, links_out, wide):
    width = charge.shape[1] // pan_own
    for q in range(pan_own):
        message[q] = charge[:, q * width : (q + 1) * width]
    wide[...] = jnp.zeros_like(wide)
    wide[: needs.shape[0], : needs.shape[1]] = needs[...]
    message[pan_own] = wide[...].astype(F32).astype(BF16)
    for k in range(seg_own):
        blocks[k] = cur[:, k * width : (k + 1) * width]
    off_out[...] = off[...]
    slots_out[...] = slots[...]
    links_out[...] = links[...]


def join_body(*refs):
    out, first = refs[-1], 0
    for x in refs[:-1]:
        out[pl.ds(first, x.shape[0])] = x[...]
        first += x.shape[0]


def ends_body(n_row, n_col, pan_own, cap, slots, links, blocks, off, own, *rest):
    sends, (hots, acc) = rest[: n_col - 1], rest[n_col - 1 :]
    seg_own, _, width = blocks.shape
    pan_group = pan_own * n_col
    r, c = lax.axis_index("row"), lax.axis_index("col")
    acc[...] = jnp.zeros_like(acc)
    levels = lax.broadcasted_iota(jnp.int32, (width, width), 0)

    def block(k):
        span = pl.ds(pl.multiple_of(k * width, width), width)
        to_hot = jnp.where(levels == off[0:1, span], 1.0, 0.0).astype(BF16)
        from_hot = jnp.where(levels == off[1:2, span], -1.0, 0.0).astype(BF16)
        hot = jnp.concatenate([to_hot, from_hot], axis=0)
        hots[k] = hot
        sums = lax.dot_general(blocks[k], hot, (((1,), (1,)), ((), ())), preferred_element_type=F32)
        return sums.astype(BF16).astype(F32)

    unroll = 16

    def step(i, carry):
        got = [block(i * unroll + u) for u in range(unroll)]
        for u in range(unroll):
            for e in range(2):
                slot = slots[e, i * unroll + u]
                p = lax.div(slot, cap)
                b = links[p, slot - p * cap]
                acc[lax.bitwise_xor(p, r) * pan_group + b] += got[u][:, e * width : (e + 1) * width]
        return carry

    lax.fori_loop(0, seg_own // unroll, step, 0)
    for k in range(n_row):
        here = pl.ds(k * pan_own, pan_own)
        own[here] = acc[pl.ds(k * pan_group + c * pan_own, pan_own)]
        for j in range(1, n_col):
            there = lax.bitwise_xor(c, j)
            sends[j - 1][here] = acc[pl.ds(k * pan_group + there * pan_own, pan_own)].astype(BF16)


def pack_of(packs, size, k):
    own, *arrived = packs
    if k == 0:
        return own, 0
    hop = k.bit_length() - 1
    return arrived[hop], (k - (1 << hop)) * size


def relay_body(n_row, n_col, pan_own, *refs):
    hops = n_row.bit_length()
    packs = refs[:hops]
    ends = refs[hops : hops + n_col - 1]
    asked, *messages = refs[hops + n_col - 1 :]
    r = lax.axis_index("row")
    rhs, width = packs[0].shape[1:]
    mine = lax.broadcasted_iota(jnp.int32, (rhs, width), 0) == r
    for k in range(n_row):
        pack, first = pack_of(packs, pan_own + 1, k)
        needs = pack[first + pan_own].astype(F32)
        asked[k : k + 1, :] = jnp.sum(jnp.where(mine, needs, 0.0), axis=0, keepdims=True).astype(jnp.int32)
        for message in messages:
            message[pl.ds(k * pan_own, pan_own)] = pack[pl.ds(first, pan_own)]
    for message, sums in zip(messages, ends):
        message[pl.ds(n_row * pan_own, n_row * pan_own)] = sums[...]


def pick_body(n_row, n_col, cap, asked, own, *refs):
    peers, (keep, send) = refs[: n_col - 1], refs[n_col - 1 :]
    seg_own, _, width = own.shape
    c = lax.axis_index("col")
    for k in range(n_row):
        out = keep if k < n_row // 2 else send
        for s in range(cap):
            b = asked[k, s]
            holder = lax.div(b, seg_own)
            b = b - holder * seg_own
            j = lax.bitwise_xor(holder, c)
            value = own[b]
            span = pl.ds(pl.multiple_of(b * width, width), width)
            for q, peer in enumerate(peers):
                value = jnp.where(j == q + 1, peer[:, span], value)
            out[k % (n_row // 2) * cap + s] = value


def forward_body(cap, places, _after, *refs):
    held, out = refs[:-1], refs[-1]
    for i, (holder, place) in enumerate(places):
        out[pl.ds(i * cap, cap)] = held[holder][pl.ds(place * cap, cap)]


def multiply(tiles, src, source, rows, acc):
    rhs, width = src.shape[1:]
    unroll = min(32, tiles.shape[0])

    def step(i, carry):
        start = i * unroll
        got = []
        for u in range(0, unroll, 2):
            t = start + u
            left = jnp.concatenate([src[source(t)], src[source(t + 1)]], axis=0)
            right = jnp.concatenate([tiles[t], tiles[t + 1]], axis=1)
            both = jnp.dot(left, right, preferred_element_type=F32)
            got += [both[:rhs, :width], both[rhs:, width:]]
        for u, value in enumerate(got):
            acc[rows[start + u]] += value
        return carry

    lax.fori_loop(0, tiles.shape[0] // unroll, step, 0)


def coeff_body(n_row, n_col, pan_own, slots, rows, needs, _after, *refs):
    hops = n_row.bit_length()
    packs = refs[:hops]
    from_col = refs[hops : hops + n_col - 1]
    tiles, part, message, src, named = refs[hops + n_col - 1 :]
    r, c = lax.axis_index("row"), lax.axis_index("col")
    pan_group = pan_own * n_col
    cap = needs.shape[1]
    for k in range(n_row):
        first = lax.bitwise_xor(r, k) * pan_group
        pack, at = pack_of(packs, pan_own + 1, k)
        src[pl.ds(first + c * pan_own, pan_own)] = pack[pl.ds(at, pan_own)]
        for j, x in enumerate(from_col):
            there = first + lax.bitwise_xor(c, j + 1) * pan_own
            src[pl.ds(there, pan_own)] = x[pl.ds(k * pan_own, pan_own)]
    for p in range(n_row):
        for s in range(cap):
            named[p * cap + s] = p * pan_group + needs[p, s]
    part[...] = jnp.zeros_like(part)
    multiply(tiles, src, lambda t: named[slots[t]], rows, part)
    high = part[...].astype(BF16)
    message[pl.ds(0, pan_group)] = high
    message[pl.ds(pan_group, pan_group)] = (part[...] - high.astype(F32)).astype(BF16)


def induct_body(n_row, n_col, seg_own, places, cap, slots, rows, _after, *refs):
    hops = n_row.bit_length()
    held = refs[:hops]
    tiles = refs[hops]
    own, *sends = refs[hops + 1 : -2]
    src, acc = refs[-2:]
    r, c = lax.axis_index("row"), lax.axis_index("col")
    for k, (holder, place) in enumerate(places):
        src[pl.ds(lax.bitwise_xor(r, k) * cap, cap)] = held[holder][pl.ds(place * cap, cap)]
    acc[...] = jnp.zeros_like(acc)
    multiply(tiles, src, lambda t: slots[t], rows, acc)
    own[...] = acc[pl.ds(c * seg_own, seg_own)]
    for j in range(1, n_col):
        sends[j - 1][...] = acc[pl.ds(lax.bitwise_xor(c, j) * seg_own, seg_own)].astype(BF16)


def panels_body(n_row, n_col, pan_own, _after, part, ends_own, *refs):
    parts = refs[: n_col - 1]
    relayed = refs[n_col - 1 : 2 * n_col - 2]
    pot, keep, message = refs[2 * n_col - 2 :]
    pan_group = part.shape[0]
    total = part[...]
    for x in parts:
        total += x[pl.ds(0, pan_group)].astype(F32) + x[pl.ds(pan_group, pan_group)].astype(F32)
    rounded = total.astype(BF16)
    pot[...] = rounded
    half = n_row // 2
    for k in range(n_row):
        sums = ends_own[pl.ds(k * pan_own, pan_own)]
        for x in relayed:
            sums += x[pl.ds((n_row + k) * pan_own, pan_own)].astype(F32)
        here = pl.ds(k % half * pan_own, pan_own)
        if k < half:
            keep[here] = sums
        else:
            message[here] = sums.astype(BF16)
    message[pl.ds(half * pan_own, pan_group)] = rounded


def pass_body(stay, go, pan_own, _after, sums, pot, *refs):
    arrived, (keep, message) = refs[:-2], refs[-2:]
    pan_group = pot.shape[0]

    def total(k):
        here = pl.ds(k * pan_own, pan_own)
        return sums[here] + arrived[-1][here].astype(F32)

    for i, k in enumerate(stay):
        keep[pl.ds(i * pan_own, pan_own)] = total(k)
    for i, k in enumerate(go):
        message[pl.ds(i * pan_own, pan_own)] = total(k).astype(BF16)
    first = len(go) * pan_own
    message[pl.ds(first, pan_group)] = pot[...]
    first += pan_group
    for i, x in enumerate(arrived):
        count = pan_group << i
        message[pl.ds(first, count)] = x[pl.ds(x.shape[0] - count, count)]
        first += count


def final_body(n_row, n_col, pan_own, cap, slots, links, hots, charge, scale, *refs):
    field_own, end_own, pot = refs[:3]
    field_in = refs[3 : 2 + n_col]
    arrived, (seg_out, pan_out, pot_out, held) = refs[2 + n_col : -4], refs[-4:]
    width = charge.shape[1] // pan_own
    pan_group = pan_own * n_col
    r, c = lax.axis_index("row"), lax.axis_index("col")
    known = gather_plan(bits_of(n_row)[::-1])
    held[pl.ds(r * pan_group, pan_group)] = pot[...]
    for i, x in enumerate(arrived):
        first = x.shape[0] - (pan_group << i)
        for k in known[i + 1][1 << i :]:
            sender = lax.bitwise_xor(r, k)
            held[pl.ds(sender * pan_group, pan_group)] = x[pl.ds(first, pan_group)]
            first += pan_group
    for q in range(pan_own):
        span = slice(q * width, (q + 1) * width)
        total = end_own[q] + arrived[-1][q].astype(F32)
        pan_out[:, span] = (scale[...] * charge[:, span].astype(F32) + total).astype(BF16)
        pot_out[:, span] = pot[c * pan_own + q]

    def block(k):
        ends = []
        for e in range(2):
            slot = slots[e, k]
            p = lax.div(slot, cap)
            ends.append(held[p * pan_group + links[p, slot - p * cap]])
        drops = jnp.dot(jnp.concatenate(ends, axis=1), hots[k], preferred_element_type=F32)
        total = field_own[k]
        for x in field_in:
            total += x[k].astype(F32)
        return (total + drops).astype(BF16)

    unroll = min(32, hots.shape[0])

    def step(i, carry):
        got = [block(i * unroll + u) for u in range(unroll)]
        for u, value in enumerate(got):
            first = pl.multiple_of((i * unroll + u) * width, width)
            seg_out[:, pl.ds(first, width)] = value
        return carry

    lax.fori_loop(0, hots.shape[0] // unroll, step, 0)


def shards(
    current,
    charge,
    rhs_scale,
    induct_tiles,
    induct_rows,
    induct_slots,
    induct_needs,
    coeff_tiles,
    coeff_rows,
    coeff_slots,
    coeff_needs,
    link_needs,
    end_slots,
    end_offsets,
):
    n_row = lax.axis_size("row")
    n_col = lax.axis_size("col")
    width = induct_tiles.shape[1]
    rhs = current.shape[0]
    seg_own = current.shape[1] // width
    pan_own = charge.shape[1] // width
    seg_group, pan_group = seg_own * n_col, pan_own * n_col
    cap_l, cap_p, cap_k = induct_needs.shape[1], coeff_needs.shape[1], link_needs.shape[1]
    slots_t, off_t = end_slots.T, end_offsets.T

    def like(blocks, dtype):
        return jax.ShapeDtypeStruct((blocks, rhs, width), dtype)

    bits = bits_of(n_row)
    half = n_row // 2

    message, own_blocks, off_v, slots_v, links_v = call(
        functools.partial(stage_body, pan_own, seg_own),
        "stage_inputs",
        [like(pan_own + 1, BF16), like(seg_own, BF16)]
        + [jax.ShapeDtypeStruct(x.shape, jnp.int32) for x in (off_t, slots_t, link_needs)],
        [VMEM] * 6,
        [pltpu.VMEM((rhs, width), jnp.int32)],
        moved=2**18,
    )(*in_hbm(charge, induct_needs, current, off_t, slots_t, link_needs))
    packs = [message]
    for i, bit in enumerate(bits):
        packs.append(exchange(message, "row", bit))
        if i < len(bits) - 1:
            (message,) = call(
                join_body,
                "join_packs",
                [like(message.shape[0] * 2, BF16)],
                [VMEM] * len(packs),
                moved=2**16,
            )(*packs)
    cur = exchange_all([current] * (n_col - 1), "col")

    rows_own = n_row * pan_own
    ends_own, *rest = call(
        functools.partial(ends_body, n_row, n_col, pan_own, cap_k),
        "end_sums",
        [like(rows_own, F32)]
        + [like(rows_own, BF16)] * (n_col - 1)
        + [jax.ShapeDtypeStruct((seg_own, 2 * width, width), BF16)],
        [SMEM, SMEM, VMEM, VMEM],
        [pltpu.VMEM((n_row * pan_group, rhs, width), F32)],
        flops=2 * 10**9,
        moved=2**18,
    )(slots_v, links_v, own_blocks, off_v)
    ends_out, (hots,) = rest[: n_col - 1], rest[n_col - 1 :]

    asked, *relays = call(
        functools.partial(relay_body, n_row, n_col, pan_own),
        "relay_charges",
        [jax.ShapeDtypeStruct((n_row, width), jnp.int32)] + [like(2 * rows_own, BF16)] * (n_col - 1),
        [VMEM] * (len(packs) + n_col - 1),
        moved=2**16,
    )(*packs, *ends_out)
    relayed = exchange_all(relays, "col")

    picks, message = call(
        functools.partial(pick_body, n_row, n_col, cap_l),
        "pick_blocks",
        [like(half * cap_l, BF16)] * 2,
        [SMEM] + [VMEM] * n_col,
        moved=2**18,
    )(asked, own_blocks, *cur)

    part, part_message = call(
        functools.partial(coeff_body, n_row, n_col, pan_own),
        "coeff_tiles",
        [like(pan_group, F32), like(2 * pan_group, BF16)],
        [SMEM] * 3 + [ANY] + [VMEM] * (len(packs) + n_col),
        [
            pltpu.VMEM((n_row * pan_group, rhs, width), BF16),
            pltpu.SMEM((n_row * cap_p,), jnp.int32),
        ],
        flops=2 * 10**9,
        moved=coeff_tiles.size * 2,
    )(coeff_slots, coeff_rows, coeff_needs, picks, *packs, *relayed, coeff_tiles)
    parts = exchange_all([part_message] * (n_col - 1), "col")

    hops, places = swap_plan(n_row, bits[::-1])
    held = [picks, exchange(message, "row", bits[-1])]
    for bit, hop in zip(bits[-2::-1], hops[1:]):
        (message,) = call(
            functools.partial(forward_body, cap_l, hop),
            "forward_blocks",
            [like(half * cap_l, BF16)],
            [ANY] + [VMEM] * len(held),
            moved=2**16,
        )(part, *held)
        held.append(exchange(message, "row", bit))

    plan = scatter_plan(n_row, bits[::-1])
    pot, sums, end_message = call(
        functools.partial(panels_body, n_row, n_col, pan_own),
        "panel_sums",
        [like(pan_group, BF16), like(half * pan_own, F32), like(half * pan_own + pan_group, BF16)],
        [ANY] + [VMEM] * (2 * n_col),
        flops=10**9,
        moved=2**18,
    )(message, part, ends_own, *parts, *relayed)

    field_own, *field_out = call(
        functools.partial(induct_body, n_row, n_col, seg_own, places, cap_l),
        "induct_tiles",
        [like(seg_own, F32)] + [like(seg_own, BF16)] * (n_col - 1),
        [SMEM, SMEM, ANY] + [VMEM] * (len(held) + 1),
        [
            pltpu.VMEM((n_row * cap_l, rhs, width), BF16),
            pltpu.VMEM((seg_group, rhs, width), F32),
        ],
        flops=4 * 10**9,
        moved=induct_tiles.size * 2,
    )(induct_slots, induct_rows, pot, *held, induct_tiles)
    field_in = exchange_all(field_out, "col")

    arrived = [exchange(end_message, "row", bits[-1])]
    for i, bit in enumerate(bits[-2::-1]):
        stay, go = plan[i + 1]
        known = 2 << i
        sums, end_message = call(
            functools.partial(pass_body, stay, go, pan_own),
            "pass_sums",
            [like(len(stay) * pan_own, F32), like(len(go) * pan_own + known * pan_group, BF16)],
            [ANY] + [VMEM] * (2 + len(arrived)),
            moved=2**18,
        )(field_own, sums, pot, *arrived)
        arrived.append(exchange(end_message, "row", bit))

    return tuple(
        call(
            functools.partial(final_body, n_row, n_col, pan_own, cap_k),
            "outputs",
            [jax.ShapeDtypeStruct(x.shape, BF16) for x in (current, charge, charge)],
            [SMEM, SMEM] + [VMEM] * (5 + n_col + len(arrived)),
            [pltpu.VMEM((n_row * pan_group, rhs, width), BF16)],
            flops=2 * 10**9,
            moved=2**20,
        )(
            slots_v,
            links_v,
            hots,
            charge,
            rhs_scale[:, None],
            field_own,
            sums,
            pot,
            *field_in,
            *arrived,
        )
    )


def solution(mesh):
    blocks = P(("parts", "row", "col"))
    matrix = P(("parts", "row", "col"), None)
    tiles = P(("parts", "row", "col"), None, None)
    values = P("rhs", ("parts", "row", "col"))
    return jax.shard_map(
        shards,
        mesh=mesh,
        in_specs=(
            values,
            values,
            P(("parts", "rhs")),
            tiles,
            blocks,
            blocks,
            matrix,
            tiles,
            blocks,
            blocks,
            matrix,
            matrix,
            matrix,
            matrix,
        ),
        out_specs=(values, values, values),
        check_vma=False,
    )
```

time: 35.8 us -> 35.9 us (level)
  waiting for transfers between devices: 2.86 us -> 4.07 us
  Pallas kernels: 9.9 us -> 9.15 us
    ppermute x13 -> x10, waiting for transfers between devices: 2.86 us -> 4.07 us  [exchange(): lax.ppermute(x, axis, [(i, i ^ k) for i in range(lax.axis_size(axis))])]
    pallas_call x3 -> x6, Pallas kernels: 5.65 us -> 5.16 us  [the longest x1 2.42 us: shards(): call(functools.partial(induct_body, n_row, n_col, seg_own, places, cap_l)...]
    ppermute x13 -> x10, starting transfers between devices: 21.7 us -> 21.7 us  [exchange(): lax.ppermute(x, axis, [(i, i ^ k) for i in range(lax.axis_size(axis))])]
  transfers between devices with their start and end apart: 13 -> 10, of which waited for: 4 -> 5; matrix products, arithmetic and copies ran while one was open for 0% -> 0% of each run, Pallas kernels for 20% -> 18%
where the time goes in v4:
time: 35.9 us; the launch traced here: 35.8 us
  starting transfers between devices  21.7 us (60%)
  Pallas kernels  9.15 us (25%)
  waiting for transfers between devices  4.07 us (11%)
  between operations  0.78 us (2%)
    ppermute x10, starting transfers between devices, exchange(): lax.ppermute(x, axis, [(i, i ^ k) for i in range(lax.axis_size(axis))])  21.7 us
    ppermute x10, waiting for transfers between devices, exchange(): lax.ppermute(x, axis, [(i, i ^ k) for i in range(lax.axis_size(axis))])  4.07 us
    pallas_call x1, Pallas kernels, shards(): call(functools.partial(induct_body, n_row, n_col, seg_own, places, cap_l)...  2.42 us
    pallas_call x1, Pallas kernels, shards(): call(functools.partial(ends_body, n_row, n_col, pan_own, cap_k), 'end_sum...  1.73 us
    pallas_call x1, Pallas kernels, shards(): call(functools.partial(final_body, n_row, n_col, pan_own, cap_k), 'output...  1.69 us
    pallas_call x1, Pallas kernels, shards(): call(functools.partial(coeff_body, n_row, n_col, pan_own), 'coeff_tiles',...  1.52 us
    pallas_call x1, Pallas kernels, shards(): call(functools.partial(stage_body, pan_own, seg_own), 'stage_inputs', [li...  0.99 us
    pallas_call x1, Pallas kernels, shards(): call(functools.partial(pick_body, n_row, n_col, cap_l), 'pick_blocks', [l...  0.73 us
  transfers between devices with their start and end apart: 10, of which 5 were waited for; matrix products, arithmetic and copies ran while one was open for 0% of the time, Pallas kernels for 18%

profile of v4, /device:TPU:0, one launch (start us, length us, event | category | flops | bytes accessed | tf_op | source)
XLA Modules:
  0.0 35.8 jit_solution(15395881834196774199)
XLA Ops:
  0.6 1.0 %stage_inputs.1 = (bf16[5,16,128]{2,1,0:T(8,128)(2,1)S(1)}, bf16[32,16,128]{2,1,0:T(8,128)(2,1)S(1)}, s32[2,4096]{1,0:T(2,128)S(1)}, s32[2,32]{1,0:T(2,128)S(1)}, s32[4,16]{1,0:T(4,128)S(1)}) custom-call(bf16[16,512]{1,0:T(8,128)(2,1)} %charge.3, s32[4,8]{1,0:T(4,128)} %needs.2, bf16[16,4096]{1,0:T(8,128)(2,1)} %cur.1, s32[2,4096]{1,0:T(2,128)} %bitcast.5, ...), custom_call_target="tpu_custom_call" | custom-call | bytes 262144 | tf_op jit(solution)/shard_map/stage_inputs/pallas_call | solution.py:365
  1.6 3.1 %collective-permute-start = (bf16[5,16,128]{2,1,0:T(8,128)(2,1)S(1)}, bf16[5,16,128]{2,1,0:T(8,128)(2,1)S(1)}, u32[]{:S(2)}, u32[]{:S(2)}) collective-permute-start(bf16[5,16,128]{2,1,0:T(8,128)(2,1)S(1)} %get-tuple-element.29.refs_0_), channel_id=1, source_target_pairs={{0,4},{4,0},{8,12},{12,8},{1,5},{5,1},{9,13},{13,9},{2,6},{6,2},{1... | collective-permute-start | bytes 61448 | tf_op jit(solution)/shard_map/ppermute | solution.py:20
  4.7 1.5 %collective-permute-start.2 = (bf16[16,4096]{1,0:T(8,128)(2,1)}, bf16[16,4096]{1,0:T(8,128)(2,1)S(1)}, u32[]{:S(2)}, u32[]{:S(2)}) collective-permute-start(bf16[16,4096]{1,0:T(8,128)(2,1)} %cur.1), channel_id=1, source_target_pairs={{0,2},{2,0},{1,3},{3,1},{4,6},{6,4},{5,7},{7,5},{8,10},{10,8},{9,1... | collective-permute-start | bytes 393224 | tf_op jit(solution)/shard_map/ppermute | solution.py:20
  6.2 0.3 collective-permute-done.refs_1_
  6.5 3.0 %collective-permute-start.1 = (bf16[10,16,128]{2,1,0:T(8,128)(2,1)S(1)}, bf16[10,16,128]{2,1,0:T(8,128)(2,1)S(1)}, u32[]{:S(2)}, u32[]{:S(2)}) collective-permute-start(bf16[10,16,128]{2,1,0:T(8,128)(2,1)S(1)} %join_packs.1), channel_id=1, source_target_pairs={{0,8},{4,12},{8,0},{12,4},{1,9},{5,13},{9,1},{13,5},{2,10},{6,14},... | collective-permute-start | bytes 122888 | tf_op jit(solution)/shard_map/ppermute | solution.py:20
  9.5 1.7 %end_sums.1 = (f32[16,16,128]{2,1,0:T(8,128)S(1)}, bf16[16,16,128]{2,1,0:T(8,128)(2,1)S(1)}, bf16[32,256,128]{2,1,0:T(8,128)(2,1)S(1)}) custom-call(s32[2,32]{1,0:T(2,128)S(1)} %get-tuple-element.24.slots, s32[4,16]{1,0:T(4,128)S(1)} %get-tuple-element.25.links, bf16[32,16,128]{2,1,0:T(8,128)(2,1)S(1)} %get-tuple-element.26.blocks.own, ...), custom_call_target="tpu_custom_call" | custom-call | flops 2000000000 | bytes 262144 | tf_op jit(solution)/shard_map/end_sums/pallas_call | solution.py:388
  11.3 0.2 collective-permute-done.1.refs_2_
  11.5 1.9 %collective-permute-start.3 = (bf16[32,16,128]{2,1,0:T(8,128)(2,1)S(1)}, bf16[32,16,128]{2,1,0:T(8,128)(2,1)S(1)}, u32[]{:S(2)}, u32[]{:S(2)}) collective-permute-start(bf16[32,16,128]{2,1,0:T(8,128)(2,1)S(1)} %get-tuple-element.33), channel_id=1, source_target_pairs={{0,2},{2,0},{1,3},{3,1},{4,6},{6,4},{5,7},{7,5},{8,10},{10,8},{9,1... | collective-permute-start | bytes 393224 | tf_op jit(solution)/shard_map/ppermute | solution.py:20
  13.4 0.0 collective-permute-done.2.refs_0_
  13.4 0.7 %pick_blocks.1 = (bf16[16,16,128]{2,1,0:T(8,128)(2,1)S(1)}, bf16[16,16,128]{2,1,0:T(8,128)(2,1)S(1)}) custom-call(s32[4,128]{1,0:T(4,128)S(1)} %get-tuple-element.31.asked, bf16[32,16,128]{2,1,0:T(8,128)(2,1)S(1)} %get-tuple-element.26.blocks.own, bf16[16,4096]{1,0:T(8,128)(2,1)S(1)} %collective-permute-done.2.refs_0_), custom_call_target="tpu_custom_call" | custom-call | bytes 262144 | tf_op jit(solution)/shard_map/pick_blocks/pallas_call | solution.py:410
  14.2 2.7 %collective-permute-start.4 = (bf16[16,16,128]{2,1,0:T(8,128)(2,1)S(1)}, bf16[16,16,128]{2,1,0:T(8,128)(2,1)S(1)}, u32[]{:S(2)}, u32[]{:S(2)}) collective-permute-start(bf16[16,16,128]{2,1,0:T(8,128)(2,1)S(1)} %get-tuple-element.35), channel_id=1, source_target_pairs={{0,8},{4,12},{8,0},{12,4},{1,9},{5,13},{9,1},{13,5},{2,10},{6,14},... | collective-permute-start | bytes 196616 | tf_op jit(solution)/shard_map/ppermute | solution.py:20
  16.8 0.0 collective-permute-done.3.refs_3_.refs_1_
  16.9 0.0 slice-start.1
  16.9 1.5 %coeff_tiles.1 = (f32[8,16,128]{2,1,0:T(8,128)S(1)}, bf16[16,16,128]{2,1,0:T(8,128)(2,1)S(1)}) custom-call(s32[96]{0:T(128)S(1)} %copy-done.5, s32[96]{0:T(128)S(1)} %copy-done.6, s32[4,4]{1,0:T(4,128)S(1)} %copy-done.2, bf16[16,16,128]{2,1,0:T(8,128)(2,1)S(1)} %get-tuple-element.32._after.refs_0_, bf16[5,16,128]{2,1,0:T(8,128)(2,1)S(1)} %get-tuple-element.29.refs_0_, ...), custom_call_target="tpu_custom_call" | custom-call | flops 2000000000 | bytes 3145728 | tf_op jit(solution)/shard_map/coeff_tiles/pallas_call | solution.py:418
  18.4 0.0 copy-start.3
  18.4 0.0 copy-start.4
  18.4 1.6 %collective-permute-start.5 = (bf16[16,16,128]{2,1,0:T(8,128)(2,1)S(1)}, bf16[16,16,128]{2,1,0:T(8,128)(2,1)S(1)}, u32[]{:S(2)}, u32[]{:S(2)}) collective-permute-start(bf16[16,16,128]{2,1,0:T(8,128)(2,1)S(1)} %get-tuple-element.37), channel_id=1, source_target_pairs={{0,2},{2,0},{1,3},{3,1},{4,6},{6,4},{5,7},{7,5},{8,10},{10,8},{9,1... | collective-permute-start | bytes 196616 | tf_op jit(solution)/shard_map/ppermute | solution.py:20
  20.0 0.0 collective-permute-done.4.refs_1_
  20.0 1.6 %collective-permute-start.6 = (bf16[16,16,128]{2,1,0:T(8,128)(2,1)S(1)}, bf16[16,16,128]{2,1,0:T(8,128)(2,1)S(1)}, u32[]{:S(2)}, u32[]{:S(2)}) collective-permute-start(bf16[16,16,128]{2,1,0:T(8,128)(2,1)S(1)} %forward_blocks.1._after), channel_id=1, source_target_pairs={{0,4},{4,0},{8,12},{12,8},{1,5},{5,1},{9,13},{13,9},{2,6},{6,2},{1... | collective-permute-start | bytes 196616 | tf_op jit(solution)/shard_map/ppermute | solution.py:20
  21.7 1.1 %collective-permute-done.5.refs_0_ = bf16[16,16,128]{2,1,0:T(8,128)(2,1)S(1)} collective-permute-done((bf16[16,16,128]{2,1,0:T(8,128)(2,1)S(1)}, bf16[16,16,128]{2,1,0:T(8,128)(2,1)S(1)}, u32[]{:S(2)}, u32[]{:S(2)}) %collective-permute-start.5) | collective-permute-done | bytes 65568 | tf_op jit(solution)/shard_map/ppermute | solution.py:20
  22.8 2.7 %collective-permute-start.7 = (bf16[16,16,128]{2,1,0:T(8,128)(2,1)S(1)}, bf16[16,16,128]{2,1,0:T(8,128)(2,1)S(1)}, u32[]{:S(2)}, u32[]{:S(2)}) collective-permute-start(bf16[16,16,128]{2,1,0:T(8,128)(2,1)S(1)} %get-tuple-element.41), channel_id=1, source_target_pairs={{0,8},{4,12},{8,0},{12,4},{1,9},{5,13},{9,1},{13,5},{2,10},{6,14},... | collective-permute-start | bytes 196616 | tf_op jit(solution)/shard_map/ppermute | solution.py:20
  25.5 0.0 collective-permute-done.6.refs_2_
  25.6 0.0 copy-start.7
  25.6 0.0 copy-start
  25.6 2.4 %induct_tiles.1 = (f32[32,16,128]{2,1,0:T(8,128)S(1)}, bf16[32,16,128]{2,1,0:T(8,128)(2,1)S(1)}) custom-call(s32[192]{0:T(256)S(1)} %copy-done.3, s32[192]{0:T(256)S(1)} %copy-done.4, bf16[8,16,128]{2,1,0:T(8,128)(2,1)S(1)} %get-tuple-element.38._after.pot.refs_2_, bf16[16,16,128]{2,1,0:T(8,128)(2,1)S(1)} %get-tuple-element.32._after.refs_0_, ...), custom_call_target="tpu_custom_call" | custom-call | flops 4000000000 | bytes 6291456 | tf_op jit(solution)/shard_map/induct_tiles/pallas_call | solution.py:454
  28.0 1.6 %collective-permute-start.8 = (bf16[32,16,128]{2,1,0:T(8,128)(2,1)S(1)}, bf16[32,16,128]{2,1,0:T(8,128)(2,1)S(1)}, u32[]{:S(2)}, u32[]{:S(2)}) collective-permute-start(bf16[32,16,128]{2,1,0:T(8,128)(2,1)S(1)} %get-tuple-element.43), channel_id=1, source_target_pairs={{0,2},{2,0},{1,3},{3,1},{4,6},{6,4},{5,7},{7,5},{8,10},{10,8},{9,1... | collective-permute-start | bytes 393224 | tf_op jit(solution)/shard_map/ppermute | solution.py:20
  29.6 0.0 collective-permute-done.7.refs_0_.refs_4_
  29.6 1.9 %collective-permute-start.9 = (bf16[20,16,128]{2,1,0:T(8,128)(2,1)S(1)}, bf16[20,16,128]{2,1,0:T(8,128)(2,1)S(1)}, u32[]{:S(2)}, u32[]{:S(2)}) collective-permute-start(bf16[20,16,128]{2,1,0:T(8,128)(2,1)S(1)} %get-tuple-element.44), channel_id=1, source_target_pairs={{0,4},{4,0},{8,12},{12,8},{1,5},{5,1},{9,13},{13,9},{2,6},{6,2},{1... | collective-permute-start | bytes 245768 | tf_op jit(solution)/shard_map/ppermute | solution.py:20
  31.5 0.1 copy.17.scale
  31.6 1.4 %collective-permute-done.8.refs_3_ = bf16[32,16,128]{2,1,0:T(8,128)(2,1)S(1)} collective-permute-done((bf16[32,16,128]{2,1,0:T(8,128)(2,1)S(1)}, bf16[32,16,128]{2,1,0:T(8,128)(2,1)S(1)}, u32[]{:S(2)}, u32[]{:S(2)}) %collective-permute-start.8) | collective-permute-done | bytes 131104 | tf_op jit(solution)/shard_map/ppermute | solution.py:20
  33.0 1.1 %collective-permute-done.9.refs_5_ = bf16[20,16,128]{2,1,0:T(8,128)(2,1)S(1)} collective-permute-done((bf16[20,16,128]{2,1,0:T(8,128)(2,1)S(1)}, bf16[20,16,128]{2,1,0:T(8,128)(2,1)S(1)}, u32[]{:S(2)}, u32[]{:S(2)}) %collective-permute-start.9) | collective-permute-done | bytes 81952 | tf_op jit(solution)/shard_map/ppermute | solution.py:20
  34.1 1.7 %outputs.1 = (bf16[16,4096]{1,0:T(8,128)(2,1)}, bf16[16,512]{1,0:T(8,128)(2,1)}, bf16[16,512]{1,0:T(8,128)(2,1)}) custom-call(s32[2,32]{1,0:T(2,128)S(1)} %get-tuple-element.24.slots, s32[4,16]{1,0:T(4,128)S(1)} %get-tuple-element.25.links, bf16[32,256,128]{2,1,0:T(8,128)(2,1)S(1)} %get-tuple-element.28.hots, bf16[16,512]{1,0:T(8,128)(2,1)S(1)} %copy-done, ...), custom_call_target="tpu_custom_call" | custom-call | flops 2000000000 | bytes 1048576 | tf_op jit(solution)/shard_map/outputs/pallas_call | solution.py:482
  (21 shorter events, 0.1 us)
Async XLA Ops:
  1.6 4.9 %collective-permute-start = (bf16[5,16,128]{2,1,0:T(8,128)(2,1)S(1)}, bf16[5,16,128]{2,1,0:T(8,128)(2,1)S(1)}, u32[]{:S(2)}, u32[]{:S(2)}) collective-permute-start(bf16[5,16,128]{2,1,0:T(8,128)(2,1)S(1)} %get-tuple-element.29.refs_0_), channel_id=1, source_target_pairs={{0,4},{4,0},{8,12},{12,8},{1,5},{5,1},{9,13},{13,9},{2,6},{6,2},{1... | collective-permute-start | bytes 61448 | tf_op jit(solution)/shard_map/ppermute | solution.py:20
  4.7 8.7 %collective-permute-start.2 = (bf16[16,4096]{1,0:T(8,128)(2,1)}, bf16[16,4096]{1,0:T(8,128)(2,1)S(1)}, u32[]{:S(2)}, u32[]{:S(2)}) collective-permute-start(bf16[16,4096]{1,0:T(8,128)(2,1)} %cur.1), channel_id=1, source_target_pairs={{0,2},{2,0},{1,3},{3,1},{4,6},{6,4},{5,7},{7,5},{8,10},{10,8},{9,1... | collective-permute-start | bytes 393224 | tf_op jit(solution)/shard_map/ppermute | solution.py:20
  6.5 5.0 %collective-permute-start.1 = (bf16[10,16,128]{2,1,0:T(8,128)(2,1)S(1)}, bf16[10,16,128]{2,1,0:T(8,128)(2,1)S(1)}, u32[]{:S(2)}, u32[]{:S(2)}) collective-permute-start(bf16[10,16,128]{2,1,0:T(8,128)(2,1)S(1)} %join_packs.1), channel_id=1, source_target_pairs={{0,8},{4,12},{8,0},{12,4},{1,9},{5,13},{9,1},{13,5},{2,10},{6,14},... | collective-permute-start | bytes 122888 | tf_op jit(solution)/shard_map/ppermute | solution.py:20
  9.5 7.3 %copy-start.1 = (bf16[96,128,128]{2,1,0:T(8,128)(2,1)S(1)}, bf16[96,128,128]{2,1,0:T(8,128)(2,1)}, u32[]{:S(2)}) copy-start(bf16[96,128,128]{2,1,0:T(8,128)(2,1)} %refs_4_.1) | copy-start | bytes 9437188
  9.5 7.3 %copy-start.2 = (s32[4,4]{1,0:T(4,128)S(1)}, s32[4,4]{1,0:T(4,128)}, u32[]{:S(2)}) copy-start(s32[4,4]{1,0:T(4,128)} %needs.3) | copy-start | bytes 196
  9.5 7.3 %copy-start.5 = (s32[96]{0:T(128)S(1)}, s32[96]{0:T(128)}, u32[]{:S(2)}) copy-start(s32[96]{0:T(128)} %slots.2) | copy-start | bytes 1156
  9.5 7.3 %copy-start.6 = (s32[96]{0:T(128)S(1)}, s32[96]{0:T(128)}, u32[]{:S(2)}) copy-start(s32[96]{0:T(128)} %rows.2) | copy-start | bytes 1156
  11.5 5.3 %collective-permute-start.3 = (bf16[32,16,128]{2,1,0:T(8,128)(2,1)S(1)}, bf16[32,16,128]{2,1,0:T(8,128)(2,1)S(1)}, u32[]{:S(2)}, u32[]{:S(2)}) collective-permute-start(bf16[32,16,128]{2,1,0:T(8,128)(2,1)S(1)} %get-tuple-element.33), channel_id=1, source_target_pairs={{0,2},{2,0},{1,3},{3,1},{4,6},{6,4},{5,7},{7,5},{8,10},{10,8},{9,1... | collective-permute-start | bytes 393224 | tf_op jit(solution)/shard_map/ppermute | solution.py:20
  14.2 5.9 %collective-permute-start.4 = (bf16[16,16,128]{2,1,0:T(8,128)(2,1)S(1)}, bf16[16,16,128]{2,1,0:T(8,128)(2,1)S(1)}, u32[]{:S(2)}, u32[]{:S(2)}) collective-permute-start(bf16[16,16,128]{2,1,0:T(8,128)(2,1)S(1)} %get-tuple-element.35), channel_id=1, source_target_pairs={{0,8},{4,12},{8,0},{12,4},{1,9},{5,13},{9,1},{13,5},{2,10},{6,14},... | collective-permute-start | bytes 196616 | tf_op jit(solution)/shard_map/ppermute | solution.py:20
  16.8 8.7 %slice-start = ((s8[6291456]{0:T(1024)(128)(4,1)}), s8[4194304]{0:T(1024)(128)(4,1)S(1)}, s32[]{:S(2)}) async-start(s8[6291456]{0:T(1024)(128)(4,1)} %bitcast.3), calls=%async_computation | async-start | bytes 8388608
  16.9 8.6 %slice-start.1 = ((s8[6291456]{0:T(1024)(128)(4,1)}), s8[2097152]{0:T(1024)(128)(4,1)S(1)}, s32[]{:S(2)}) async-start(s8[6291456]{0:T(1024)(128)(4,1)} %bitcast.3), calls=%async_computation.1 | async-start | bytes 4194304
  18.4 7.1 %copy-start.3 = (s32[192]{0:T(256)S(1)}, s32[192]{0:T(256)}, u32[]{:S(2)}) copy-start(s32[192]{0:T(256)} %slots.3) | copy-start | bytes 2308
  18.4 7.1 %copy-start.4 = (s32[192]{0:T(256)S(1)}, s32[192]{0:T(256)}, u32[]{:S(2)}) copy-start(s32[192]{0:T(256)} %rows.3) | copy-start | bytes 2308
  18.4 4.3 %collective-permute-start.5 = (bf16[16,16,128]{2,1,0:T(8,128)(2,1)S(1)}, bf16[16,16,128]{2,1,0:T(8,128)(2,1)S(1)}, u32[]{:S(2)}, u32[]{:S(2)}) collective-permute-start(bf16[16,16,128]{2,1,0:T(8,128)(2,1)S(1)} %get-tuple-element.37), channel_id=1, source_target_pairs={{0,2},{2,0},{1,3},{3,1},{4,6},{6,4},{5,7},{7,5},{8,10},{10,8},{9,1... | collective-permute-start | bytes 196616 | tf_op jit(solution)/shard_map/ppermute | solution.py:20
  20.0 5.5 %collective-permute-start.6 = (bf16[16,16,128]{2,1,0:T(8,128)(2,1)S(1)}, bf16[16,16,128]{2,1,0:T(8,128)(2,1)S(1)}, u32[]{:S(2)}, u32[]{:S(2)}) collective-permute-start(bf16[16,16,128]{2,1,0:T(8,128)(2,1)S(1)} %forward_blocks.1._after), channel_id=1, source_target_pairs={{0,4},{4,0},{8,12},{12,8},{1,5},{5,1},{9,13},{13,9},{2,6},{6,2},{1... | collective-permute-start | bytes 196616 | tf_op jit(solution)/shard_map/ppermute | solution.py:20
  22.8 6.8 %collective-permute-start.7 = (bf16[16,16,128]{2,1,0:T(8,128)(2,1)S(1)}, bf16[16,16,128]{2,1,0:T(8,128)(2,1)S(1)}, u32[]{:S(2)}, u32[]{:S(2)}) collective-permute-start(bf16[16,16,128]{2,1,0:T(8,128)(2,1)S(1)} %get-tuple-element.41), channel_id=1, source_target_pairs={{0,8},{4,12},{8,0},{12,4},{1,9},{5,13},{9,1},{13,5},{2,10},{6,14},... | collective-permute-start | bytes 196616 | tf_op jit(solution)/shard_map/ppermute | solution.py:20
  25.6 6.0 %copy-start.7 = (f32[16]{0:T(128)S(1)}, f32[16]{0:T(128)}, u32[]{:S(2)}) copy-start(f32[16]{0:T(128)} %param.16) | copy-start | bytes 196
  25.6 8.5 %copy-start = (bf16[16,512]{1,0:T(8,128)(2,1)S(1)}, bf16[16,512]{1,0:T(8,128)(2,1)}, u32[]{:S(2)}) copy-start(bf16[16,512]{1,0:T(8,128)(2,1)} %charge.3) | copy-start | bytes 49156
  28.0 5.0 %collective-permute-start.8 = (bf16[32,16,128]{2,1,0:T(8,128)(2,1)S(1)}, bf16[32,16,128]{2,1,0:T(8,128)(2,1)S(1)}, u32[]{:S(2)}, u32[]{:S(2)}) collective-permute-start(bf16[32,16,128]{2,1,0:T(8,128)(2,1)S(1)} %get-tuple-element.43), channel_id=1, source_target_pairs={{0,2},{2,0},{1,3},{3,1},{4,6},{6,4},{5,7},{7,5},{8,10},{10,8},{9,1... | collective-permute-start | bytes 393224 | tf_op jit(solution)/shard_map/ppermute | solution.py:20
  29.6 4.5 %collective-permute-start.9 = (bf16[20,16,128]{2,1,0:T(8,128)(2,1)S(1)}, bf16[20,16,128]{2,1,0:T(8,128)(2,1)S(1)}, u32[]{:S(2)}, u32[]{:S(2)}) collective-permute-start(bf16[20,16,128]{2,1,0:T(8,128)(2,1)S(1)} %get-tuple-element.44), channel_id=1, source_target_pairs={{0,4},{4,0},{8,12},{12,8},{1,5},{5,1},{9,13},{13,9},{2,6},{6,2},{1... | collective-permute-start | bytes 245768 | tf_op jit(solution)/shard_map/ppermute | solution.py:20

commit v5 on v3

--- a/solution.py
+++ b/solution.py
@@ -45,18 +45,23 @@
     return [pltpu.with_memory_space_constraint(x, pltpu.HBM) for x in arrays]
 
 
-def pack_body(pan_own, charge, needs, message, wide):
+def stage_body(pan_own, seg_own, charge, needs, cur, off, slots, links, message, blocks, off_out, slots_out, links_out, wide):
     width = charge.shape[1] // pan_own
     for q in range(pan_own):
         message[q] = charge[:, q * width : (q + 1) * width]
     wide[...] = jnp.zeros_like(wide)
     wide[: needs.shape[0], : needs.shape[1]] = needs[...]
     message[pan_own] = wide[...].astype(F32).astype(BF16)
-
-
-def ends_body(n_row, n_col, seg_own, pan_own, cap, slots, links, cur, off, own, *rest):
-    sends, (blocks, hots, acc) = rest[: n_col - 1], rest[n_col - 1 :]
-    width = cur.shape[1] // seg_own
+    for k in range(seg_own):
+        blocks[k] = cur[:, k * width : (k + 1) * width]
+    off_out[...] = off[...]
+    slots_out[...] = slots[...]
+    links_out[...] = links[...]
+
+
+def ends_body(n_row, n_col, pan_own, cap, slots, links, blocks, off, own, *rest):
+    sends, acc = rest[:-1], rest[-1]
+    seg_own, _, width = blocks.shape
     pan_group = pan_own * n_col
     r, c = lax.axis_index("row"), lax.axis_index("col")
     acc[...] = jnp.zeros_like(acc)
@@ -64,16 +69,13 @@
 
     def block(k):
         span = pl.ds(pl.multiple_of(k * width, width), width)
-        value = cur[:, span]
-        blocks[k] = value
         to_hot = jnp.where(levels == off[0:1, span], 1.0, 0.0).astype(BF16)
         from_hot = jnp.where(levels == off[1:2, span], -1.0, 0.0).astype(BF16)
         hot = jnp.concatenate([to_hot, from_hot], axis=0)
-        hots[k] = hot
-        sums = lax.dot_general(value, hot, (((1,), (1,)), ((), ())), preferred_element_type=F32)
+        sums = lax.dot_general(blocks[k], hot, (((1,), (1,)), ((), ())), preferred_element_type=F32)
         return sums.astype(BF16).astype(F32)
 
-    unroll = 8
+    unroll = 16
 
     def step(i, carry):
         got = [block(i * unroll + u) for u in range(unroll)]
@@ -95,9 +97,9 @@
 
 
 def relay_body(n_row, n_col, pan_own, *refs):
-    packs = refs[:n_row][::-1]
+    packs = refs[:n_row]
     ends = refs[n_row : n_row + n_col - 1]
-    asked, *messages = refs[n_row + n_col - 1 :]
+    asked, *messages = refs[n_row + 2 * n_col - 2 :]
     r = lax.axis_index("row")
     rhs, width = packs[0].shape[1:]
     mine = lax.broadcasted_iota(jnp.int32, (rhs, width), 0) == r
@@ -148,7 +150,7 @@
 
 
 def coeff_body(n_row, n_col, pan_own, slots, rows, needs, *refs):
-    packs = refs[:n_row][::-1]
+    packs = refs[:n_row]
     from_col = refs[n_row : n_row + n_col - 1]
     tiles, part, message, src, named = refs[n_row + n_col - 1 :]
     r, c = lax.axis_index("row"), lax.axis_index("col")
@@ -207,18 +209,18 @@
             messages[n_row - 1 - k][pl.ds(pan_own, pan_group)] = rounded
 
 
-def final_body(n_row, n_col, pan_own, cap, slots, links, hots, charge, scale, *refs):
+def final_body(n_row, n_col, pan_own, cap, slots, links, off, charge, scale, *refs):
     field_own, end_own, pot = refs[:3]
     field_in = refs[3 : 2 + n_col]
     arrived = refs[2 + n_col : 1 + n_col + n_row][::-1]
     seg_out, pan_out, pot_out, held = refs[1 + n_col + n_row :]
-    width = charge.shape[1] // pan_own
+    seg_own, rhs, width = field_own.shape
     pan_group = pan_own * n_col
     r, c = lax.axis_index("row"), lax.axis_index("col")
-    held[pl.ds(r * pan_group, pan_group)] = pot[...]
+    held[pl.ds(r * pan_group, pan_group)] = pot[...].astype(F32)
     for k, x in enumerate(arrived):
         sender = lax.bitwise_xor(r, k + 1)
-        held[pl.ds(sender * pan_group, pan_group)] = x[pl.ds(pan_own, pan_group)]
+        held[pl.ds(sender * pan_group, pan_group)] = x[pl.ds(pan_own, pan_group)].astype(F32)
     for q in range(pan_own):
         span = slice(q * width, (q + 1) * width)
         total = end_own[q]
@@ -227,28 +229,26 @@
         pan_out[:, span] = (scale[...] * charge[:, span].astype(F32) + total).astype(BF16)
         pot_out[:, span] = pot[c * pan_own + q]
 
-    def block(k):
-        ends = []
-        for e in range(2):
-            slot = slots[e, k]
-            p = lax.div(slot, cap)
-            ends.append(held[p * pan_group + links[p, slot - p * cap]])
-        drops = jnp.dot(jnp.concatenate(ends, axis=1), hots[k], preferred_element_type=F32)
-        total = field_own[k]
-        for x in field_in:
-            total += x[k].astype(F32)
-        return (total + drops).astype(BF16)
-
-    unroll = 16
+    def at_end(e, k, span):
+        slot = slots[e, k]
+        p = lax.div(slot, cap)
+        values = held[p * pan_group + links[p, slot - p * cap]]
+        lanes = jnp.broadcast_to(off[e : e + 1, span], (rhs, width))
+        return jnp.take_along_axis(values, lanes, axis=1, mode="promise_in_bounds")
+
+    unroll = 8
 
     def step(i, carry):
-        got = [block(i * unroll + u) for u in range(unroll)]
-        for u, value in enumerate(got):
-            first = pl.multiple_of((i * unroll + u) * width, width)
-            seg_out[:, pl.ds(first, width)] = value
+        for u in range(unroll):
+            k = i * unroll + u
+            span = pl.ds(pl.multiple_of(k * width, width), width)
+            total = field_own[k]
+            for x in field_in:
+                total += x[k].astype(F32)
+            seg_out[:, span] = (total + at_end(0, k, span) - at_end(1, k, span)).astype(BF16)
         return carry
 
-    lax.fori_loop(0, hots.shape[0] // unroll, step, 0)
+    lax.fori_loop(0, seg_own // unroll, step, 0)
 
 
 def shards(
@@ -281,37 +281,35 @@
         return jax.ShapeDtypeStruct((blocks, rhs, width), dtype)
 
     cur = exchange_all(current, [current] * (n_col - 1), "col")
-    (pack,) = call(
-        functools.partial(pack_body, pan_own),
-        "pack_charges",
-        [like(pan_own + 1, BF16)],
-        [VMEM] * 2,
+    pack, own_blocks, off_v, slots_v, links_v = call(
+        functools.partial(stage_body, pan_own, seg_own),
+        "stage_inputs",
+        [like(pan_own + 1, BF16), like(seg_own, BF16)]
+        + [jax.ShapeDtypeStruct(x.shape, jnp.int32) for x in (off_t, slots_t, link_needs)],
+        [VMEM] * 6,
         [pltpu.VMEM((rhs, width), jnp.int32)],
-        moved=2**16,
-    )(*in_hbm(charge, induct_needs))
+        moved=2**18,
+    )(*in_hbm(charge, induct_needs, current, off_t, slots_t, link_needs))
     packs = exchange_all(pack, [pack] * (n_row - 1), "row")
 
     rows_own = n_row * pan_own
-    ends_own, *rest = call(
-        functools.partial(ends_body, n_row, n_col, seg_own, pan_own, cap_k),
+    ends_own, *ends_out = call(
+        functools.partial(ends_body, n_row, n_col, pan_own, cap_k),
         "end_sums",
-        [like(rows_own, F32)]
-        + [like(rows_own, BF16)] * (n_col - 1)
-        + [like(seg_own, BF16), jax.ShapeDtypeStruct((seg_own, 2 * width, width), BF16)],
+        [like(rows_own, F32)] + [like(rows_own, BF16)] * (n_col - 1),
         [SMEM, SMEM, VMEM, VMEM],
         [pltpu.VMEM((n_row * pan_group, rhs, width), F32)],
         flops=2 * 10**9,
         moved=2**18,
-    )(*in_hbm(slots_t, link_needs, current, off_t))
-    ends_out, (own_blocks, hots) = rest[: n_col - 1], rest[n_col - 1 :]
+    )(slots_v, links_v, own_blocks, off_v)
 
     asked, *relays = call(
         functools.partial(relay_body, n_row, n_col, pan_own),
         "relay_charges",
         [jax.ShapeDtypeStruct((n_row, width), jnp.int32)] + [like(2 * rows_own, BF16)] * (n_col - 1),
-        [VMEM] * (n_row + n_col - 1),
+        [VMEM] * (n_row + n_col - 1) + [ANY] * (n_col - 1),
         moved=2**16,
-    )(*packs[::-1], *ends_out)
+    )(*packs, *ends_out, *cur[1:])
     relayed = exchange_all(None, relays, "col")[1:]
 
     *picks, own_picks = call(
@@ -334,7 +332,7 @@
         ],
         flops=2 * 10**9,
         moved=coeff_tiles.size * 2,
-    )(coeff_slots, coeff_rows, coeff_needs, *packs[::-1], *relayed, coeff_tiles)
+    )(coeff_slots, coeff_rows, coeff_needs, *packs, *relayed, coeff_tiles)
     parts = exchange_all(None, [message] * (n_col - 1), "col")[1:]
 
     field_own, *field_out = call(
@@ -367,13 +365,13 @@
             "outputs",
             [jax.ShapeDtypeStruct(x.shape, BF16) for x in (current, charge, charge)],
             [SMEM, SMEM] + [VMEM] * (4 + n_col + n_row),
-            [pltpu.VMEM((n_row * pan_group, rhs, width), BF16)],
-            flops=2 * 10**9,
+            [pltpu.VMEM((n_row * pan_group, rhs, width), F32)],
+            flops=10**9,
             moved=2**20,
         )(
-            slots_t,
-            link_needs,
-            hots,
+            slots_v,
+            links_v,
+            off_v,
             charge,
             rhs_scale[:, None],
             field_own,

time: 35.8 us -> 35.2 us (0.983)
  waiting for transfers between devices: 2.86 us -> 5.5 us
  starting transfers between devices: 21.7 us -> 19.4 us
  Pallas kernels: 9.9 us -> 9.17 us
    ppermute x13, waiting for transfers between devices: 2.86 us -> 5.5 us  [exchange(): lax.ppermute(x, axis, [(i, i ^ k) for i in range(lax.axis_size(axis))])]
    ppermute x13, starting transfers between devices: 21.7 us -> 19.4 us  [exchange(): lax.ppermute(x, axis, [(i, i ^ k) for i in range(lax.axis_size(axis))])]
    pallas_call x2, Pallas kernels: 3.23 us -> 2.44 us  [the longest x1 1.43 us: shards(): call(functools.partial(ends_body, n_row, n_col, pan_own, cap_k), 'end_sum...]
  transfers between devices with their start and end apart: 13 -> 13, of which waited for: 4 -> 5; matrix products, arithmetic and copies ran while one was open for 0% -> 0% of each run, Pallas kernels for 20% -> 20%
where the time goes in v5:
time: 35.2 us; the launch traced here: 35 us
  starting transfers between devices  19.4 us (55%)
  Pallas kernels  9.17 us (26%)
  waiting for transfers between devices  5.5 us (16%)
  between operations  0.8 us (2%)
    ppermute x13, starting transfers between devices, exchange(): lax.ppermute(x, axis, [(i, i ^ k) for i in range(lax.axis_size(axis))])  19.4 us
    ppermute x13, waiting for transfers between devices, exchange(): lax.ppermute(x, axis, [(i, i ^ k) for i in range(lax.axis_size(axis))])  5.5 us
    pallas_call x1, Pallas kernels, shards(): call(functools.partial(induct_body, n_row, n_col, seg_own), 'induct_tiles...  2.41 us
    pallas_call x1, Pallas kernels, shards(): call(functools.partial(final_body, n_row, n_col, pan_own, cap_k), 'output...  2.01 us
    pallas_call x1, Pallas kernels, shards(): call(functools.partial(coeff_body, n_row, n_col, pan_own), 'coeff_tiles',...  1.52 us
    pallas_call x1, Pallas kernels, shards(): call(functools.partial(ends_body, n_row, n_col, pan_own, cap_k), 'end_sum...  1.43 us
    pallas_call x1, Pallas kernels, shards(): call(functools.partial(stage_body, pan_own, seg_own), 'stage_inputs', [li...  1.01 us
    pallas_call x1, Pallas kernels, shards(): call(functools.partial(pick_body, n_row, n_col, cap_l), 'pick_blocks', [l...  0.73 us
  transfers between devices with their start and end apart: 13, of which 5 were waited for; matrix products, arithmetic and copies ran while one was open for 0% of the time, Pallas kernels for 20%

profile of v5, /device:TPU:0, one launch (start us, length us, event | category | flops | bytes accessed | tf_op | source)
XLA Modules:
  0.0 35.0 jit_solution(5541148189843768225)
XLA Ops:
  0.7 3.0 %collective-permute-start.3 = (bf16[16,4096]{1,0:T(8,128)(2,1)}, bf16[16,4096]{1,0:T(8,128)(2,1)S(1)}, u32[]{:S(2)}, u32[]{:S(2)}) collective-permute-start(bf16[16,4096]{1,0:T(8,128)(2,1)} %cur.1), channel_id=1, source_target_pairs={{0,2},{2,0},{1,3},{3,1},{4,6},{6,4},{5,7},{7,5},{8,10},{10,8},{9,1... | collective-permute-start | bytes 393224 | tf_op jit(solution)/shard_map/ppermute | solution.py:20
  3.7 1.0 %stage_inputs.1 = (bf16[5,16,128]{2,1,0:T(8,128)(2,1)S(1)}, bf16[32,16,128]{2,1,0:T(8,128)(2,1)S(1)}, s32[2,4096]{1,0:T(2,128)S(1)}, s32[2,32]{1,0:T(2,128)S(1)}, s32[4,16]{1,0:T(4,128)S(1)}) custom-call(bf16[16,512]{1,0:T(8,128)(2,1)} %charge.3, s32[4,8]{1,0:T(4,128)} %needs.2, bf16[16,4096]{1,0:T(8,128)(2,1)} %cur.1, s32[2,4096]{1,0:T(2,128)} %bitcast.5, ...), custom_call_target="tpu_custom_call" | custom-call | bytes 262144 | tf_op jit(solution)/shard_map/stage_inputs/pallas_call | solution.py:284
  4.7 3.7 %collective-permute-start.2 = (bf16[5,16,128]{2,1,0:T(8,128)(2,1)S(1)}, bf16[5,16,128]{2,1,0:T(8,128)(2,1)S(1)}, u32[]{:S(2)}, u32[]{:S(2)}) collective-permute-start(bf16[5,16,128]{2,1,0:T(8,128)(2,1)S(1)} %get-tuple-element.28.refs_0_), channel_id=1, source_target_pairs={{0,12},{4,8},{8,4},{12,0},{1,13},{5,9},{9,5},{13,1},{2,14},{6,10},... | collective-permute-start | bytes 61448 | tf_op jit(solution)/shard_map/ppermute | solution.py:20
  8.4 0.0 collective-permute-start.1
  8.4 0.8 %collective-permute-start = (bf16[5,16,128]{2,1,0:T(8,128)(2,1)S(1)}, bf16[5,16,128]{2,1,0:T(8,128)(2,1)S(1)}, u32[]{:S(2)}, u32[]{:S(2)}) collective-permute-start(bf16[5,16,128]{2,1,0:T(8,128)(2,1)S(1)} %get-tuple-element.28.refs_0_), channel_id=1, source_target_pairs={{0,4},{4,0},{8,12},{12,8},{1,5},{5,1},{9,13},{13,9},{2,6},{6,2},{1... | collective-permute-start | bytes 61448 | tf_op jit(solution)/shard_map/ppermute | solution.py:20
  9.2 1.4 %end_sums.1 = (f32[16,16,128]{2,1,0:T(8,128)S(1)}, bf16[16,16,128]{2,1,0:T(8,128)(2,1)S(1)}) custom-call(s32[2,32]{1,0:T(2,128)S(1)} %get-tuple-element.25.slots, s32[4,16]{1,0:T(4,128)S(1)} %get-tuple-element.26.links, bf16[32,16,128]{2,1,0:T(8,128)(2,1)S(1)} %get-tuple-element.29.blocks.own, s32[2,4096]{1,0:T(2,128)S(1)} %get-tuple-element.27.off), custom_call_target="tpu_custom_call" | custom-call | flops 2000000000 | bytes 262144 | tf_op jit(solution)/shard_map/end_sums/pallas_call | solution.py:296
  10.6 0.0 collective-permute-done.2.refs_3_
  10.6 2.4 %collective-permute-done.1.refs_2_ = bf16[5,16,128]{2,1,0:T(8,128)(2,1)S(1)} collective-permute-done((bf16[5,16,128]{2,1,0:T(8,128)(2,1)S(1)}, bf16[5,16,128]{2,1,0:T(8,128)(2,1)S(1)}, u32[]{:S(2)}, u32[]{:S(2)}) %collective-permute-start.1) | collective-permute-done | bytes 20512 | tf_op jit(solution)/shard_map/ppermute | solution.py:20
  13.0 0.0 collective-permute-done.3.refs_5_.refs_0_
  13.1 0.9 %collective-permute-start.4 = (bf16[32,16,128]{2,1,0:T(8,128)(2,1)S(1)}, bf16[32,16,128]{2,1,0:T(8,128)(2,1)S(1)}, u32[]{:S(2)}, u32[]{:S(2)}) collective-permute-start(bf16[32,16,128]{2,1,0:T(8,128)(2,1)S(1)} %get-tuple-element.31), channel_id=1, source_target_pairs={{0,2},{2,0},{1,3},{3,1},{4,6},{6,4},{5,7},{7,5},{8,10},{10,8},{9,1... | collective-permute-start | bytes 393224 | tf_op jit(solution)/shard_map/ppermute | solution.py:20
  14.0 0.7 %pick_blocks.1 = (bf16[8,16,128]{2,1,0:T(8,128)(2,1)S(1)}, bf16[8,16,128]{2,1,0:T(8,128)(2,1)S(1)}, bf16[8,16,128]{2,1,0:T(8,128)(2,1)S(1)}, bf16[8,16,128]{2,1,0:T(8,128)(2,1)S(1)}) custom-call(s32[4,128]{1,0:T(4,128)S(1)} %get-tuple-element.33.asked, bf16[32,16,128]{2,1,0:T(8,128)(2,1)S(1)} %get-tuple-element.29.blocks.own, ...), custom_call_target="tpu_custom_call" | custom-call | bytes 262144 | tf_op jit(solution)/shard_map/pick_blocks/pallas_call | solution.py:315
  14.7 1.5 %collective-permute-start.5 = (bf16[8,16,128]{2,1,0:T(8,128)(2,1)S(1)}, bf16[8,16,128]{2,1,0:T(8,128)(2,1)S(1)}, u32[]{:S(2)}, u32[]{:S(2)}) collective-permute-start(bf16[8,16,128]{2,1,0:T(8,128)(2,1)S(1)} %get-tuple-element.34), channel_id=1, source_target_pairs={{0,12},{4,8},{8,4},{12,0},{1,13},{5,9},{9,5},{13,1},{2,14},{6,10},... | collective-permute-start | bytes 98312 | tf_op jit(solution)/shard_map/ppermute | solution.py:20
  16.2 0.6 %collective-permute-start.6 = (bf16[8,16,128]{2,1,0:T(8,128)(2,1)S(1)}, bf16[8,16,128]{2,1,0:T(8,128)(2,1)S(1)}, u32[]{:S(2)}, u32[]{:S(2)}) collective-permute-start(bf16[8,16,128]{2,1,0:T(8,128)(2,1)S(1)} %get-tuple-element.35), channel_id=1, source_target_pairs={{0,8},{4,12},{8,0},{12,4},{1,9},{5,13},{9,1},{13,5},{2,10},{6,14},... | collective-permute-start | bytes 98312 | tf_op jit(solution)/shard_map/ppermute | solution.py:20
  16.9 2.3 %collective-permute-start.7 = (bf16[8,16,128]{2,1,0:T(8,128)(2,1)S(1)}, bf16[8,16,128]{2,1,0:T(8,128)(2,1)S(1)}, u32[]{:S(2)}, u32[]{:S(2)}) collective-permute-start(bf16[8,16,128]{2,1,0:T(8,128)(2,1)S(1)} %get-tuple-element.36), channel_id=1, source_target_pairs={{0,4},{4,0},{8,12},{12,8},{1,5},{5,1},{9,13},{13,9},{2,6},{6,2},{1... | collective-permute-start | bytes 98312 | tf_op jit(solution)/shard_map/ppermute | solution.py:20
  19.2 0.0 collective-permute-done.4.refs_4_.refs_1_
  19.2 1.5 %coeff_tiles.1 = (f32[8,16,128]{2,1,0:T(8,128)S(1)}, bf16[16,16,128]{2,1,0:T(8,128)(2,1)S(1)}) custom-call(s32[96]{0:T(128)S(1)} %copy-done.5, s32[96]{0:T(128)S(1)} %copy-done.6, s32[4,4]{1,0:T(4,128)S(1)} %copy-done.2, bf16[5,16,128]{2,1,0:T(8,128)(2,1)S(1)} %get-tuple-element.28.refs_0_, bf16[5,16,128]{2,1,0:T(8,128)(2,1)S(1)} %collective-permute-done.refs_1_, ...), custom_call_target="tpu_custom_call" | custom-call | flops 2000000000 | bytes 3145728 | tf_op jit(solution)/shard_map/coeff_tiles/pallas_call | solution.py:324
  20.7 1.3 %collective-permute-start.8 = (bf16[16,16,128]{2,1,0:T(8,128)(2,1)S(1)}, bf16[16,16,128]{2,1,0:T(8,128)(2,1)S(1)}, u32[]{:S(2)}, u32[]{:S(2)}) collective-permute-start(bf16[16,16,128]{2,1,0:T(8,128)(2,1)S(1)} %get-tuple-element.40), channel_id=1, source_target_pairs={{0,2},{2,0},{1,3},{3,1},{4,6},{6,4},{5,7},{7,5},{8,10},{10,8},{9,1... | collective-permute-start | bytes 196616 | tf_op jit(solution)/shard_map/ppermute | solution.py:20
  22.0 0.0 collective-permute-done.5.refs_0_
  22.0 0.0 collective-permute-done.6.refs_1_
  22.0 0.0 collective-permute-done.7.refs_2_
  22.1 2.4 %induct_tiles.1 = (f32[32,16,128]{2,1,0:T(8,128)S(1)}, bf16[32,16,128]{2,1,0:T(8,128)(2,1)S(1)}) custom-call(s32[192]{0:T(256)S(1)} %copy-done.3, s32[192]{0:T(256)S(1)} %copy-done.4, f32[8,16,128]{2,1,0:T(8,128)S(1)} %get-tuple-element.32._after.part, bf16[8,16,128]{2,1,0:T(8,128)(2,1)S(1)} %collective-permute-done.5.refs_0_, ...), custom_call_target="tpu_custom_call" | custom-call | flops 4000000000 | bytes 6291456 | tf_op jit(solution)/shard_map/induct_tiles/pallas_call | solution.py:338
  24.5 0.9 %collective-permute-start.9 = (bf16[32,16,128]{2,1,0:T(8,128)(2,1)S(1)}, bf16[32,16,128]{2,1,0:T(8,128)(2,1)S(1)}, u32[]{:S(2)}, u32[]{:S(2)}) collective-permute-start(bf16[32,16,128]{2,1,0:T(8,128)(2,1)S(1)} %get-tuple-element.43), channel_id=1, source_target_pairs={{0,2},{2,0},{1,3},{3,1},{4,6},{6,4},{5,7},{7,5},{8,10},{10,8},{9,1... | collective-permute-start | bytes 393224 | tf_op jit(solution)/shard_map/ppermute | solution.py:20
  25.4 0.3 collective-permute-done.8.refs_0_
  25.7 1.9 %collective-permute-start.10 = (bf16[12,16,128]{2,1,0:T(8,128)(2,1)S(1)}, bf16[12,16,128]{2,1,0:T(8,128)(2,1)S(1)}, u32[]{:S(2)}, u32[]{:S(2)}) collective-permute-start(bf16[12,16,128]{2,1,0:T(8,128)(2,1)S(1)} %get-tuple-element.44), channel_id=1, source_target_pairs={{0,12},{4,8},{8,4},{12,0},{1,13},{5,9},{9,5},{13,1},{2,14},{6,10},... | collective-permute-start | bytes 147464 | tf_op jit(solution)/shard_map/ppermute | solution.py:20
  27.6 0.8 %collective-permute-start.11 = (bf16[12,16,128]{2,1,0:T(8,128)(2,1)S(1)}, bf16[12,16,128]{2,1,0:T(8,128)(2,1)S(1)}, u32[]{:S(2)}, u32[]{:S(2)}) collective-permute-start(bf16[12,16,128]{2,1,0:T(8,128)(2,1)S(1)} %get-tuple-element.45), channel_id=1, source_target_pairs={{0,8},{4,12},{8,0},{12,4},{1,9},{5,13},{9,1},{13,5},{2,10},{6,14},... | collective-permute-start | bytes 147464 | tf_op jit(solution)/shard_map/ppermute | solution.py:20
  28.4 1.8 %collective-permute-start.12 = (bf16[12,16,128]{2,1,0:T(8,128)(2,1)S(1)}, bf16[12,16,128]{2,1,0:T(8,128)(2,1)S(1)}, u32[]{:S(2)}, u32[]{:S(2)}) collective-permute-start(bf16[12,16,128]{2,1,0:T(8,128)(2,1)S(1)} %get-tuple-element.46), channel_id=1, source_target_pairs={{0,4},{4,0},{8,12},{12,8},{1,5},{5,1},{9,13},{13,9},{2,6},{6,2},{1... | collective-permute-start | bytes 147464 | tf_op jit(solution)/shard_map/ppermute | solution.py:20
  30.2 0.1 copy.17.scale
  30.3 1.4 %collective-permute-done.10.refs_4_ = bf16[12,16,128]{2,1,0:T(8,128)(2,1)S(1)} collective-permute-done((bf16[12,16,128]{2,1,0:T(8,128)(2,1)S(1)}, bf16[12,16,128]{2,1,0:T(8,128)(2,1)S(1)}, u32[]{:S(2)}, u32[]{:S(2)}) %collective-permute-start.10) | collective-permute-done | bytes 49184 | tf_op jit(solution)/shard_map/ppermute | solution.py:20
  31.7 1.2 %collective-permute-done.11.refs_5_ = bf16[12,16,128]{2,1,0:T(8,128)(2,1)S(1)} collective-permute-done((bf16[12,16,128]{2,1,0:T(8,128)(2,1)S(1)}, bf16[12,16,128]{2,1,0:T(8,128)(2,1)S(1)}, u32[]{:S(2)}, u32[]{:S(2)}) %collective-permute-start.11) | collective-permute-done | bytes 49184 | tf_op jit(solution)/shard_map/ppermute | solution.py:20
  32.8 0.1 collective-permute-done.12.refs_6_
  33.0 0.0 collective-permute-done.9.refs_3_
  33.0 2.0 %outputs.1 = (bf16[16,4096]{1,0:T(8,128)(2,1)}, bf16[16,512]{1,0:T(8,128)(2,1)}, bf16[16,512]{1,0:T(8,128)(2,1)}) custom-call(s32[2,32]{1,0:T(2,128)S(1)} %get-tuple-element.25.slots, s32[4,16]{1,0:T(4,128)S(1)} %get-tuple-element.26.links, s32[2,4096]{1,0:T(2,128)S(1)} %get-tuple-element.27.off, bf16[16,512]{1,0:T(8,128)(2,1)S(1)} %copy-done, ...), custom_call_target="tpu_custom_call" | custom-call | flops 1000000000 | bytes 1048576 | tf_op jit(solution)/shard_map/outputs/pallas_call | solution.py:363
  (24 shorter events, 0.1 us)
Async XLA Ops:
  0.6 18.5 %copy-start.2 = (s32[4,4]{1,0:T(4,128)S(1)}, s32[4,4]{1,0:T(4,128)}, u32[]{:S(2)}) copy-start(s32[4,4]{1,0:T(4,128)} %needs.3) | copy-start | bytes 196
  0.6 18.5 %copy-start.5 = (s32[96]{0:T(128)S(1)}, s32[96]{0:T(128)}, u32[]{:S(2)}) copy-start(s32[96]{0:T(128)} %slots.2) | copy-start | bytes 1156
  0.7 18.5 %copy-start.6 = (s32[96]{0:T(128)S(1)}, s32[96]{0:T(128)}, u32[]{:S(2)}) copy-start(s32[96]{0:T(128)} %rows.2) | copy-start | bytes 1156
  0.7 18.5 %copy-start.1 = (bf16[96,128,128]{2,1,0:T(8,128)(2,1)S(1)}, bf16[96,128,128]{2,1,0:T(8,128)(2,1)}, u32[]{:S(2)}) copy-start(bf16[96,128,128]{2,1,0:T(8,128)(2,1)} %refs_5_.1) | copy-start | bytes 9437188
  0.7 12.4 %collective-permute-start.3 = (bf16[16,4096]{1,0:T(8,128)(2,1)}, bf16[16,4096]{1,0:T(8,128)(2,1)S(1)}, u32[]{:S(2)}, u32[]{:S(2)}) collective-permute-start(bf16[16,4096]{1,0:T(8,128)(2,1)} %cur.1), channel_id=1, source_target_pairs={{0,2},{2,0},{1,3},{3,1},{4,6},{6,4},{5,7},{7,5},{8,10},{10,8},{9,1... | collective-permute-start | bytes 393224 | tf_op jit(solution)/shard_map/ppermute | solution.py:20
  4.7 5.9 %collective-permute-start.2 = (bf16[5,16,128]{2,1,0:T(8,128)(2,1)S(1)}, bf16[5,16,128]{2,1,0:T(8,128)(2,1)S(1)}, u32[]{:S(2)}, u32[]{:S(2)}) collective-permute-start(bf16[5,16,128]{2,1,0:T(8,128)(2,1)S(1)} %get-tuple-element.28.refs_0_), channel_id=1, source_target_pairs={{0,12},{4,8},{8,4},{12,0},{1,13},{5,9},{9,5},{13,1},{2,14},{6,10},... | collective-permute-start | bytes 61448 | tf_op jit(solution)/shard_map/ppermute | solution.py:20
  8.4 4.7 %collective-permute-start.1 = (bf16[5,16,128]{2,1,0:T(8,128)(2,1)S(1)}, bf16[5,16,128]{2,1,0:T(8,128)(2,1)S(1)}, u32[]{:S(2)}, u32[]{:S(2)}) collective-permute-start(bf16[5,16,128]{2,1,0:T(8,128)(2,1)S(1)} %get-tuple-element.28.refs_0_), channel_id=1, source_target_pairs={{0,8},{4,12},{8,0},{12,4},{1,9},{5,13},{9,1},{13,5},{2,10},{6,14},... | collective-permute-start | bytes 61448 | tf_op jit(solution)/shard_map/ppermute | solution.py:20
  8.4 4.7 %collective-permute-start = (bf16[5,16,128]{2,1,0:T(8,128)(2,1)S(1)}, bf16[5,16,128]{2,1,0:T(8,128)(2,1)S(1)}, u32[]{:S(2)}, u32[]{:S(2)}) collective-permute-start(bf16[5,16,128]{2,1,0:T(8,128)(2,1)S(1)} %get-tuple-element.28.refs_0_), channel_id=1, source_target_pairs={{0,4},{4,0},{8,12},{12,8},{1,5},{5,1},{9,13},{13,9},{2,6},{6,2},{1... | collective-permute-start | bytes 61448 | tf_op jit(solution)/shard_map/ppermute | solution.py:20
  9.1 12.9 %slice-start = ((s8[6291456]{0:T(1024)(128)(4,1)}), s8[4194304]{0:T(1024)(128)(4,1)S(1)}, s32[]{:S(2)}) async-start(s8[6291456]{0:T(1024)(128)(4,1)} %bitcast.3), calls=%async_computation | async-start | bytes 8388608
  9.2 12.9 %copy-start.3 = (s32[192]{0:T(256)S(1)}, s32[192]{0:T(256)}, u32[]{:S(2)}) copy-start(s32[192]{0:T(256)} %slots.3) | copy-start | bytes 2308
  9.2 12.9 %copy-start.4 = (s32[192]{0:T(256)S(1)}, s32[192]{0:T(256)}, u32[]{:S(2)}) copy-start(s32[192]{0:T(256)} %rows.3) | copy-start | bytes 2308
  13.1 9.0 %slice-start.1 = ((s8[6291456]{0:T(1024)(128)(4,1)}), s8[2097152]{0:T(1024)(128)(4,1)S(1)}, s32[]{:S(2)}) async-start(s8[6291456]{0:T(1024)(128)(4,1)} %bitcast.3), calls=%async_computation.1 | async-start | bytes 4194304
  13.1 6.1 %collective-permute-start.4 = (bf16[32,16,128]{2,1,0:T(8,128)(2,1)S(1)}, bf16[32,16,128]{2,1,0:T(8,128)(2,1)S(1)}, u32[]{:S(2)}, u32[]{:S(2)}) collective-permute-start(bf16[32,16,128]{2,1,0:T(8,128)(2,1)S(1)} %get-tuple-element.31), channel_id=1, source_target_pairs={{0,2},{2,0},{1,3},{3,1},{4,6},{6,4},{5,7},{7,5},{8,10},{10,8},{9,1... | collective-permute-start | bytes 393224 | tf_op jit(solution)/shard_map/ppermute | solution.py:20
  14.7 7.3 %collective-permute-start.5 = (bf16[8,16,128]{2,1,0:T(8,128)(2,1)S(1)}, bf16[8,16,128]{2,1,0:T(8,128)(2,1)S(1)}, u32[]{:S(2)}, u32[]{:S(2)}) collective-permute-start(bf16[8,16,128]{2,1,0:T(8,128)(2,1)S(1)} %get-tuple-element.34), channel_id=1, source_target_pairs={{0,12},{4,8},{8,4},{12,0},{1,13},{5,9},{9,5},{13,1},{2,14},{6,10},... | collective-permute-start | bytes 98312 | tf_op jit(solution)/shard_map/ppermute | solution.py:20
  16.2 5.8 %collective-permute-start.6 = (bf16[8,16,128]{2,1,0:T(8,128)(2,1)S(1)}, bf16[8,16,128]{2,1,0:T(8,128)(2,1)S(1)}, u32[]{:S(2)}, u32[]{:S(2)}) collective-permute-start(bf16[8,16,128]{2,1,0:T(8,128)(2,1)S(1)} %get-tuple-element.35), channel_id=1, source_target_pairs={{0,8},{4,12},{8,0},{12,4},{1,9},{5,13},{9,1},{13,5},{2,10},{6,14},... | collective-permute-start | bytes 98312 | tf_op jit(solution)/shard_map/ppermute | solution.py:20
  16.9 5.1 %collective-permute-start.7 = (bf16[8,16,128]{2,1,0:T(8,128)(2,1)S(1)}, bf16[8,16,128]{2,1,0:T(8,128)(2,1)S(1)}, u32[]{:S(2)}, u32[]{:S(2)}) collective-permute-start(bf16[8,16,128]{2,1,0:T(8,128)(2,1)S(1)} %get-tuple-element.36), channel_id=1, source_target_pairs={{0,4},{4,0},{8,12},{12,8},{1,5},{5,1},{9,13},{13,9},{2,6},{6,2},{1... | collective-permute-start | bytes 98312 | tf_op jit(solution)/shard_map/ppermute | solution.py:20
  20.7 5.0 %collective-permute-start.8 = (bf16[16,16,128]{2,1,0:T(8,128)(2,1)S(1)}, bf16[16,16,128]{2,1,0:T(8,128)(2,1)S(1)}, u32[]{:S(2)}, u32[]{:S(2)}) collective-permute-start(bf16[16,16,128]{2,1,0:T(8,128)(2,1)S(1)} %get-tuple-element.40), channel_id=1, source_target_pairs={{0,2},{2,0},{1,3},{3,1},{4,6},{6,4},{5,7},{7,5},{8,10},{10,8},{9,1... | collective-permute-start | bytes 196616 | tf_op jit(solution)/shard_map/ppermute | solution.py:20
  24.5 8.5 %collective-permute-start.9 = (bf16[32,16,128]{2,1,0:T(8,128)(2,1)S(1)}, bf16[32,16,128]{2,1,0:T(8,128)(2,1)S(1)}, u32[]{:S(2)}, u32[]{:S(2)}) collective-permute-start(bf16[32,16,128]{2,1,0:T(8,128)(2,1)S(1)} %get-tuple-element.43), channel_id=1, source_target_pairs={{0,2},{2,0},{1,3},{3,1},{4,6},{6,4},{5,7},{7,5},{8,10},{10,8},{9,1... | collective-permute-start | bytes 393224 | tf_op jit(solution)/shard_map/ppermute | solution.py:20
  25.7 4.5 %copy-start.7 = (f32[16]{0:T(128)S(1)}, f32[16]{0:T(128)}, u32[]{:S(2)}) copy-start(f32[16]{0:T(128)} %param.16) | copy-start | bytes 196
  25.7 7.3 %copy-start = (bf16[16,512]{1,0:T(8,128)(2,1)S(1)}, bf16[16,512]{1,0:T(8,128)(2,1)}, u32[]{:S(2)}) copy-start(bf16[16,512]{1,0:T(8,128)(2,1)} %charge.3) | copy-start | bytes 49156
  25.7 6.0 %collective-permute-start.10 = (bf16[12,16,128]{2,1,0:T(8,128)(2,1)S(1)}, bf16[12,16,128]{2,1,0:T(8,128)(2,1)S(1)}, u32[]{:S(2)}, u32[]{:S(2)}) collective-permute-start(bf16[12,16,128]{2,1,0:T(8,128)(2,1)S(1)} %get-tuple-element.44), channel_id=1, source_target_pairs={{0,12},{4,8},{8,4},{12,0},{1,13},{5,9},{9,5},{13,1},{2,14},{6,10},... | collective-permute-start | bytes 147464 | tf_op jit(solution)/shard_map/ppermute | solution.py:20
  27.6 5.2 %collective-permute-start.11 = (bf16[12,16,128]{2,1,0:T(8,128)(2,1)S(1)}, bf16[12,16,128]{2,1,0:T(8,128)(2,1)S(1)}, u32[]{:S(2)}, u32[]{:S(2)}) collective-permute-start(bf16[12,16,128]{2,1,0:T(8,128)(2,1)S(1)} %get-tuple-element.45), channel_id=1, source_target_pairs={{0,8},{4,12},{8,0},{12,4},{1,9},{5,13},{9,1},{13,5},{2,10},{6,14},... | collective-permute-start | bytes 147464 | tf_op jit(solution)/shard_map/ppermute | solution.py:20
  28.4 4.6 %collective-permute-start.12 = (bf16[12,16,128]{2,1,0:T(8,128)(2,1)S(1)}, bf16[12,16,128]{2,1,0:T(8,128)(2,1)S(1)}, u32[]{:S(2)}, u32[]{:S(2)}) collective-permute-start(bf16[12,16,128]{2,1,0:T(8,128)(2,1)S(1)} %get-tuple-element.46), channel_id=1, source_target_pairs={{0,4},{4,0},{8,12},{12,8},{1,5},{5,1},{9,13},{13,9},{2,6},{6,2},{1... | collective-permute-start | bytes 147464 | tf_op jit(solution)/shard_map/ppermute | solution.py:20

commit v6 on v5

--- a/solution.py
+++ b/solution.py
@@ -28,12 +28,12 @@
     return [got[k] for k in range(n)]
 
 
-def call(body, name, out_shape, in_specs, scratch=(), flops=0, moved=0):
+def call(body, name, out_shape, in_specs, scratch=(), flops=0, moved=0, out_specs=None):
     return pl.pallas_call(
         body,
         out_shape=out_shape,
         in_specs=in_specs,
-        out_specs=[VMEM] * len(out_shape),
+        out_specs=out_specs or [VMEM] * len(out_shape),
         scratch_shapes=list(scratch),
         compiler_params=pltpu.CompilerParams(vmem_limit_bytes=16 * 2**20),
         cost_estimate=pl.CostEstimate(flops=flops, bytes_accessed=moved, transcendentals=0),
@@ -45,34 +45,42 @@
     return [pltpu.with_memory_space_constraint(x, pltpu.HBM) for x in arrays]
 
 
-def stage_body(pan_own, seg_own, charge, needs, cur, off, slots, links, message, blocks, off_out, slots_out, links_out, wide):
+def pack_body(pan_own, charge, needs, message, wide):
     width = charge.shape[1] // pan_own
     for q in range(pan_own):
         message[q] = charge[:, q * width : (q + 1) * width]
     wide[...] = jnp.zeros_like(wide)
     wide[: needs.shape[0], : needs.shape[1]] = needs[...]
     message[pan_own] = wide[...].astype(F32).astype(BF16)
-    for k in range(seg_own):
-        blocks[k] = cur[:, k * width : (k + 1) * width]
-    off_out[...] = off[...]
-    slots_out[...] = slots[...]
-    links_out[...] = links[...]
-
-
-def ends_body(n_row, n_col, pan_own, cap, slots, links, blocks, off, own, *rest):
-    sends, acc = rest[:-1], rest[-1]
+
+
+def ends_body(n_row, n_col, pan_own, cap, n_tables, *refs):
+    sources, rest = refs[: n_tables + 2], refs[n_tables + 2 :]
+    tables, (off, blocks, own) = rest[:n_tables], rest[n_tables : n_tables + 3]
+    sends, (cur, acc, sems) = rest[n_tables + 3 : -3], rest[-3:]
+    copies = [
+        pltpu.make_async_copy(source, target, sems.at[i])
+        for i, (source, target) in enumerate(zip(sources, (*tables, off, cur)))
+    ]
+    for copy in copies[::-1]:
+        copy.start()
+    slots, links = tables[:2]
     seg_own, _, width = blocks.shape
     pan_group = pan_own * n_col
     r, c = lax.axis_index("row"), lax.axis_index("col")
     acc[...] = jnp.zeros_like(acc)
     levels = lax.broadcasted_iota(jnp.int32, (width, width), 0)
+    for copy in copies[::-1]:
+        copy.wait()
 
     def block(k):
         span = pl.ds(pl.multiple_of(k * width, width), width)
         to_hot = jnp.where(levels == off[0:1, span], 1.0, 0.0).astype(BF16)
         from_hot = jnp.where(levels == off[1:2, span], -1.0, 0.0).astype(BF16)
         hot = jnp.concatenate([to_hot, from_hot], axis=0)
-        sums = lax.dot_general(blocks[k], hot, (((1,), (1,)), ((), ())), preferred_element_type=F32)
+        value = cur[:, span]
+        blocks[k] = value
+        sums = lax.dot_general(value, hot, (((1,), (1,)), ((), ())), preferred_element_type=F32)
         return sums.astype(BF16).astype(F32)
 
     unroll = 16
@@ -209,25 +217,29 @@
             messages[n_row - 1 - k][pl.ds(pan_own, pan_group)] = rounded
 
 
-def final_body(n_row, n_col, pan_own, cap, slots, links, off, charge, scale, *refs):
-    field_own, end_own, pot = refs[:3]
-    field_in = refs[3 : 2 + n_col]
-    arrived = refs[2 + n_col : 1 + n_col + n_row][::-1]
-    seg_out, pan_out, pot_out, held = refs[1 + n_col + n_row :]
-    seg_own, rhs, width = field_own.shape
+def base_body(n_col, pan_own, charge, scale, field_own, end_own, pot, *refs):
+    field_in, (field, panels, pot_out) = refs[: n_col - 1], refs[n_col - 1 :]
+    width = pot.shape[2]
+    c = lax.axis_index("col")
+    total = field_own[...]
+    for x in field_in:
+        total += x[...].astype(F32)
+    field[...] = total
+    for q in range(pan_own):
+        span = slice(q * width, (q + 1) * width)
+        panels[q] = scale[...] * charge[:, span].astype(F32) + end_own[q]
+        pot_out[:, span] = pot[c * pan_own + q]
+
+
+def final_body(n_row, n_col, pan_own, cap, slots, links, off, field, panels, pot, *refs):
+    arrived, (seg_out, pan_out, held, seg, sems) = refs[: n_row - 1][::-1], refs[n_row - 1 :]
+    seg_own, rhs, width = field.shape
     pan_group = pan_own * n_col
-    r, c = lax.axis_index("row"), lax.axis_index("col")
+    r = lax.axis_index("row")
     held[pl.ds(r * pan_group, pan_group)] = pot[...].astype(F32)
     for k, x in enumerate(arrived):
         sender = lax.bitwise_xor(r, k + 1)
         held[pl.ds(sender * pan_group, pan_group)] = x[pl.ds(pan_own, pan_group)].astype(F32)
-    for q in range(pan_own):
-        span = slice(q * width, (q + 1) * width)
-        total = end_own[q]
-        for x in arrived:
-            total += x[q].astype(F32)
-        pan_out[:, span] = (scale[...] * charge[:, span].astype(F32) + total).astype(BF16)
-        pot_out[:, span] = pot[c * pan_own + q]
 
     def at_end(e, k, span):
         slot = slots[e, k]
@@ -236,19 +248,23 @@
         lanes = jnp.broadcast_to(off[e : e + 1, span], (rhs, width))
         return jnp.take_along_axis(values, lanes, axis=1, mode="promise_in_bounds")
 
-    unroll = 8
-
-    def step(i, carry):
-        for u in range(unroll):
-            k = i * unroll + u
-            span = pl.ds(pl.multiple_of(k * width, width), width)
-            total = field_own[k]
-            for x in field_in:
-                total += x[k].astype(F32)
-            seg_out[:, span] = (total + at_end(0, k, span) - at_end(1, k, span)).astype(BF16)
-        return carry
-
-    lax.fori_loop(0, seg_own // unroll, step, 0)
+    chunks = sems.shape[0]
+    size = seg_own // chunks
+    copies = []
+    for i in range(chunks):
+        for k in range(i * size, (i + 1) * size):
+            span = pl.ds(k * width, width)
+            seg[:, span] = (field[k] + at_end(0, k, span) - at_end(1, k, span)).astype(BF16)
+        part = pl.ds(i * size * width, size * width)
+        copies.append(pltpu.make_async_copy(seg.at[:, part], seg_out.at[:, part], sems.at[i]))
+        copies[i].start()
+    for q in range(pan_own):
+        total = panels[q]
+        for x in arrived:
+            total += x[q].astype(F32)
+        pan_out[:, q * width : (q + 1) * width] = total.astype(BF16)
+    for copy in copies:
+        copy.wait()
 
 
 def shards(
@@ -281,27 +297,37 @@
         return jax.ShapeDtypeStruct((blocks, rhs, width), dtype)
 
     cur = exchange_all(current, [current] * (n_col - 1), "col")
-    pack, own_blocks, off_v, slots_v, links_v = call(
-        functools.partial(stage_body, pan_own, seg_own),
-        "stage_inputs",
-        [like(pan_own + 1, BF16), like(seg_own, BF16)]
-        + [jax.ShapeDtypeStruct(x.shape, jnp.int32) for x in (off_t, slots_t, link_needs)],
-        [VMEM] * 6,
+    (pack,) = call(
+        functools.partial(pack_body, pan_own),
+        "pack_charges",
+        [like(pan_own + 1, BF16)],
+        [VMEM] * 2,
         [pltpu.VMEM((rhs, width), jnp.int32)],
+        moved=2**16,
+    )(*in_hbm(charge, induct_needs))
+    packs = exchange_all(pack, [pack] * (n_row - 1), "row")
+
+    rows_own = n_row * pan_own
+    scalars = [slots_t, link_needs, induct_slots, induct_rows, coeff_slots, coeff_rows, coeff_needs]
+    n_tables = len(scalars)
+    outs = call(
+        functools.partial(ends_body, n_row, n_col, pan_own, cap_k, n_tables),
+        "end_sums",
+        [pltpu.SMEM(x.shape, jnp.int32) for x in scalars]
+        + [jax.ShapeDtypeStruct(off_t.shape, jnp.int32), like(seg_own, BF16), like(rows_own, F32)]
+        + [like(rows_own, BF16)] * (n_col - 1),
+        [ANY] * (n_tables + 2),
+        [
+            pltpu.VMEM(current.shape, BF16),
+            pltpu.VMEM((n_row * pan_group, rhs, width), F32),
+            pltpu.SemaphoreType.DMA((n_tables + 2,)),
+        ],
+        flops=5 * 10**8,
         moved=2**18,
-    )(*in_hbm(charge, induct_needs, current, off_t, slots_t, link_needs))
-    packs = exchange_all(pack, [pack] * (n_row - 1), "row")
-
-    rows_own = n_row * pan_own
-    ends_own, *ends_out = call(
-        functools.partial(ends_body, n_row, n_col, pan_own, cap_k),
-        "end_sums",
-        [like(rows_own, F32)] + [like(rows_own, BF16)] * (n_col - 1),
-        [SMEM, SMEM, VMEM, VMEM],
-        [pltpu.VMEM((n_row * pan_group, rhs, width), F32)],
-        flops=2 * 10**9,
-        moved=2**18,
-    )(slots_v, links_v, own_blocks, off_v)
+        out_specs=[SMEM] * n_tables + [VMEM] * (2 + n_col),
+    )(*in_hbm(*scalars, off_t, current))
+    slots_s, links_s, induct_slots, induct_rows, coeff_slots, coeff_rows, coeff_needs = outs[:n_tables]
+    off_v, own_blocks, ends_own, *ends_out = outs[n_tables:]
 
     asked, *relays = call(
         functools.partial(relay_body, n_row, n_col, pan_own),
@@ -359,28 +385,30 @@
     )(part, ends_own, *parts, *relayed)
     arrived = exchange_all(None, row_messages[::-1], "row")[1:]
 
-    return tuple(
-        call(
-            functools.partial(final_body, n_row, n_col, pan_own, cap_k),
-            "outputs",
-            [jax.ShapeDtypeStruct(x.shape, BF16) for x in (current, charge, charge)],
-            [SMEM, SMEM] + [VMEM] * (4 + n_col + n_row),
-            [pltpu.VMEM((n_row * pan_group, rhs, width), F32)],
-            flops=10**9,
-            moved=2**20,
-        )(
-            slots_v,
-            links_v,
-            off_v,
-            charge,
-            rhs_scale[:, None],
-            field_own,
-            end_keep,
-            pot,
-            *field_in,
-            *arrived[::-1],
-        )
-    )
+    field, panels, pot_out = call(
+        functools.partial(base_body, n_col, pan_own),
+        "base_sums",
+        [like(seg_own, F32), like(pan_own, F32), jax.ShapeDtypeStruct(charge.shape, BF16)],
+        [VMEM] * (4 + n_col),
+        flops=10**9,
+        moved=2**20,
+    )(charge, rhs_scale[:, None], field_own, end_keep, pot, *field_in)
+
+    seg_out, pan_out = call(
+        functools.partial(final_body, n_row, n_col, pan_own, cap_k),
+        "outputs",
+        [jax.ShapeDtypeStruct(x.shape, BF16) for x in (current, charge)],
+        [SMEM, SMEM] + [VMEM] * (3 + n_row),
+        [
+            pltpu.VMEM((n_row * pan_group, rhs, width), F32),
+            pltpu.VMEM(current.shape, BF16),
+            pltpu.SemaphoreType.DMA((4,)),
+        ],
+        flops=10**9,
+        moved=2**20,
+        out_specs=[ANY, VMEM],
+    )(slots_s, links_s, off_v, field, panels, pot, *arrived[::-1])
+    return (seg_out, pan_out, pot_out)
 
 
 def solution(mesh):

time: 35.2 us -> 36 us (1.023)
  local copies, waits for them, and re-layouts: 0.12 us -> 2.63 us
  waiting for transfers between devices: 5.5 us -> 4.83 us
  Pallas kernels: 9.17 us -> 8.54 us
    unnamed x20 -> x6, local copies, waits for them, and re-layouts: 0.04 us -> 1.9 us
    pallas_call x2 -> x3, Pallas kernels: 2.44 us -> 3.25 us  [the longest x1 1.9 us: shards(): call(functools.partial(ends_body, n_row, n_col, pan_own, cap_k, n_tables)...]
    ppermute x13, waiting for transfers between devices: 5.5 us -> 4.83 us  [exchange(): lax.ppermute(x, axis, [(i, i ^ k) for i in range(lax.axis_size(axis))])]
    broadcast_in_dim x1, local copies, waits for them, and re-layouts: 0.08 us -> 0.73 us  [shards(): rhs_scale[:, None]]
    pallas_call x1, Pallas kernels: 1.52 us -> 0.95 us  [shards(): call(functools.partial(coeff_body, n_row, n_col, pan_own), 'coeff_tiles',...]
    pallas_call x1, Pallas kernels: 2.41 us -> 1.85 us  [shards(): call(functools.partial(induct_body, n_row, n_col, seg_own), 'induct_tiles...]
  transfers between devices with their start and end apart: 13 -> 13, of which waited for: 5 -> 4; matrix products, arithmetic and copies ran while one was open for 0% -> 2% of each run, Pallas kernels for 20% -> 19%
where the time goes in v6:
time: 36 us; the launch traced here: 35.8 us
  starting transfers between devices  19.1 us (53%)
  Pallas kernels  8.54 us (24%)
  waiting for transfers between devices  4.83 us (13%)
  local copies, waits for them, and re-layouts  2.63 us (7%)
  between operations  0.71 us (2%)
    ppermute x13, starting transfers between devices, exchange(): lax.ppermute(x, axis, [(i, i ^ k) for i in range(lax.axis_size(axis))])  19.1 us
    ppermute x13, waiting for transfers between devices, exchange(): lax.ppermute(x, axis, [(i, i ^ k) for i in range(lax.axis_size(axis))])  4.83 us
    pallas_call x1, Pallas kernels, shards(): call(functools.partial(ends_body, n_row, n_col, pan_own, cap_k, n_tables)...  1.9 us
    unnamed x6, local copies, waits for them, and re-layouts  1.9 us
    pallas_call x1, Pallas kernels, shards(): call(functools.partial(induct_body, n_row, n_col, seg_own), 'induct_tiles...  1.85 us
    pallas_call x1, Pallas kernels, shards(): call(functools.partial(final_body, n_row, n_col, pan_own, cap_k), 'output...  1.7 us
    pallas_call x1, Pallas kernels, shards(): call(functools.partial(coeff_body, n_row, n_col, pan_own), 'coeff_tiles',...  0.95 us
    pallas_call x1, Pallas kernels, shards(): call(functools.partial(pick_body, n_row, n_col, cap_l), 'pick_blocks', [l...  0.73 us
  transfers between devices with their start and end apart: 13, of which 4 were waited for; matrix products, arithmetic and copies ran while one was open for 2% of the time, Pallas kernels for 19%

profile of v6, /device:TPU:0, one launch (start us, length us, event | category | flops | bytes accessed | tf_op | source)
XLA Modules:
  0.0 35.8 jit_solution(7131153293199476600)
XLA Ops:
  0.6 3.0 %collective-permute-start.3 = (bf16[16,4096]{1,0:T(8,128)(2,1)}, bf16[16,4096]{1,0:T(8,128)(2,1)S(1)}, u32[]{:S(2)}, u32[]{:S(2)}) collective-permute-start(bf16[16,4096]{1,0:T(8,128)(2,1)} %refs_8_.1), channel_id=1, source_target_pairs={{0,2},{2,0},{1,3},{3,1},{4,6},{6,4},{5,7},{7,5},{8,10},{10,8},{9,1... | collective-permute-start | bytes 393224 | tf_op jit(solution)/shard_map/ppermute | solution.py:20
  3.6 0.7 %pack_charges.1.refs_0_ = bf16[5,16,128]{2,1,0:T(8,128)(2,1)S(1)} custom-call(bf16[16,512]{1,0:T(8,128)(2,1)} %charge.3, s32[4,8]{1,0:T(4,128)} %needs.1), custom_call_target="tpu_custom_call" | custom-call | bytes 65536 | tf_op jit(solution)/shard_map/pack_charges/pallas_call | solution.py:300
  4.4 3.6 %collective-permute-start.2 = (bf16[5,16,128]{2,1,0:T(8,128)(2,1)S(1)}, bf16[5,16,128]{2,1,0:T(8,128)(2,1)S(1)}, u32[]{:S(2)}, u32[]{:S(2)}) collective-permute-start(bf16[5,16,128]{2,1,0:T(8,128)(2,1)S(1)} %pack_charges.1.refs_0_), channel_id=1, source_target_pairs={{0,12},{4,8},{8,4},{12,0},{1,13},{5,9},{9,5},{13,1},{2,14},{6,10},... | collective-permute-start | bytes 61448 | tf_op jit(solution)/shard_map/ppermute | solution.py:20
  8.0 0.0 collective-permute-start.1
  8.0 0.8 %collective-permute-start = (bf16[5,16,128]{2,1,0:T(8,128)(2,1)S(1)}, bf16[5,16,128]{2,1,0:T(8,128)(2,1)S(1)}, u32[]{:S(2)}, u32[]{:S(2)}) collective-permute-start(bf16[5,16,128]{2,1,0:T(8,128)(2,1)S(1)} %pack_charges.1.refs_0_), channel_id=1, source_target_pairs={{0,4},{4,0},{8,12},{12,8},{1,5},{5,1},{9,13},{13,9},{2,6},{6,2},{1... | collective-permute-start | bytes 61448 | tf_op jit(solution)/shard_map/ppermute | solution.py:20
  8.8 1.9 %end_sums.1 = (s32[2,32]{1,0:T(2,128)S(4)}, s32[4,16]{1,0:T(4,128)S(4)}, s32[192]{0:T(256)S(4)}, s32[192]{0:T(256)S(4)}, s32[96]{0:T(128)S(4)}, /*index=5*/s32[9...) custom-call(s32[2,32]{1,0:T(2,128)} %bitcast.5, ...), custom_call_target="tpu_custom_call" | custom-call | flops 500000000 | bytes 262144 | tf_op jit(solution)/shard_map/end_sums/pallas_call | solution.py:313
  10.7 0.0 collective-permute-done.2.refs_3_
  10.7 2.0 %collective-permute-done.1.refs_2_ = bf16[5,16,128]{2,1,0:T(8,128)(2,1)S(1)} collective-permute-done((bf16[5,16,128]{2,1,0:T(8,128)(2,1)S(1)}, bf16[5,16,128]{2,1,0:T(8,128)(2,1)S(1)}, u32[]{:S(2)}, u32[]{:S(2)}) %collective-permute-start.1) | collective-permute-done | bytes 20512 | tf_op jit(solution)/shard_map/ppermute | solution.py:20
  12.6 0.0 collective-permute-done.refs_1_
  12.7 0.6 %collective-permute-start.4 = (bf16[32,16,128]{2,1,0:T(8,128)(2,1)S(1)}, bf16[32,16,128]{2,1,0:T(8,128)(2,1)S(1)}, u32[]{:S(2)}, u32[]{:S(2)}) collective-permute-start(bf16[32,16,128]{2,1,0:T(8,128)(2,1)S(1)} %get-tuple-element.43), channel_id=1, source_target_pairs={{0,2},{2,0},{1,3},{3,1},{4,6},{6,4},{5,7},{7,5},{8,10},{10,8},{9,1... | collective-permute-start | bytes 393224 | tf_op jit(solution)/shard_map/ppermute | solution.py:20
  13.3 0.7 %copy.17.scale = f32[16,1]{1,0:T(8,128)S(1)} copy(f32[16,1]{0,1:T(1,128)} %bitcast.3) | data formatting | bytes 128 | tf_op jit(solution)/shard_map/broadcast_in_dim | solution.py:395
  14.0 0.7 %pick_blocks.1 = (bf16[8,16,128]{2,1,0:T(8,128)(2,1)S(1)}, bf16[8,16,128]{2,1,0:T(8,128)(2,1)S(1)}, bf16[8,16,128]{2,1,0:T(8,128)(2,1)S(1)}, bf16[8,16,128]{2,1,0:T(8,128)(2,1)S(1)}) custom-call(s32[4,128]{1,0:T(4,128)S(1)} %get-tuple-element.45.asked, bf16[32,16,128]{2,1,0:T(8,128)(2,1)S(1)} %get-tuple-element.46.own, ...), custom_call_target="tpu_custom_call" | custom-call | bytes 262144 | tf_op jit(solution)/shard_map/pick_blocks/pallas_call | solution.py:341
  14.8 1.7 %collective-permute-start.5 = (bf16[8,16,128]{2,1,0:T(8,128)(2,1)S(1)}, bf16[8,16,128]{2,1,0:T(8,128)(2,1)S(1)}, u32[]{:S(2)}, u32[]{:S(2)}) collective-permute-start(bf16[8,16,128]{2,1,0:T(8,128)(2,1)S(1)} %get-tuple-element.47), channel_id=1, source_target_pairs={{0,12},{4,8},{8,4},{12,0},{1,13},{5,9},{9,5},{13,1},{2,14},{6,10},... | collective-permute-start | bytes 98312 | tf_op jit(solution)/shard_map/ppermute | solution.py:20
  16.5 0.4 %collective-permute-start.6 = (bf16[8,16,128]{2,1,0:T(8,128)(2,1)S(1)}, bf16[8,16,128]{2,1,0:T(8,128)(2,1)S(1)}, u32[]{:S(2)}, u32[]{:S(2)}) collective-permute-start(bf16[8,16,128]{2,1,0:T(8,128)(2,1)S(1)} %get-tuple-element.48), channel_id=1, source_target_pairs={{0,8},{4,12},{8,0},{12,4},{1,9},{5,13},{9,1},{13,5},{2,10},{6,14},... | collective-permute-start | bytes 98312 | tf_op jit(solution)/shard_map/ppermute | solution.py:20
  16.9 2.3 %collective-permute-start.7 = (bf16[8,16,128]{2,1,0:T(8,128)(2,1)S(1)}, bf16[8,16,128]{2,1,0:T(8,128)(2,1)S(1)}, u32[]{:S(2)}, u32[]{:S(2)}) collective-permute-start(bf16[8,16,128]{2,1,0:T(8,128)(2,1)S(1)} %get-tuple-element.49), channel_id=1, source_target_pairs={{0,4},{4,0},{8,12},{12,8},{1,5},{5,1},{9,13},{13,9},{2,6},{6,2},{1... | collective-permute-start | bytes 98312 | tf_op jit(solution)/shard_map/ppermute | solution.py:20
  19.2 1.9 %copy-done.2 = bf16[96,128,128]{2,1,0:T(8,128)(2,1)S(1)} copy-done((bf16[96,128,128]{2,1,0:T(8,128)(2,1)S(1)}, bf16[96,128,128]{2,1,0:T(8,128)(2,1)}, u32[]{:S(2)}) %copy-start.2) | copy-done | bytes 3145752
  21.1 0.9 %coeff_tiles.1 = (f32[8,16,128]{2,1,0:T(8,128)S(1)}, bf16[16,16,128]{2,1,0:T(8,128)(2,1)S(1)}) custom-call(s32[96]{0:T(128)S(4)} %get-tuple-element.39.slots, s32[96]{0:T(128)S(4)} %get-tuple-element.40.rows, s32[4,4]{1,0:T(4,128)S(4)} %get-tuple-element.41.needs, bf16[5,16,128]{2,1,0:T(8,128)(2,1)S(1)} %pack_charges.1.refs_0_, ...), custom_call_target="tpu_custom_call" | custom-call | flops 2000000000 | bytes 3145728 | tf_op jit(solution)/shard_map/coeff_tiles/pallas_call | solution.py:350
  22.1 1.5 %collective-permute-start.8 = (bf16[16,16,128]{2,1,0:T(8,128)(2,1)S(1)}, bf16[16,16,128]{2,1,0:T(8,128)(2,1)S(1)}, u32[]{:S(2)}, u32[]{:S(2)}) collective-permute-start(bf16[16,16,128]{2,1,0:T(8,128)(2,1)S(1)} %get-tuple-element.53), channel_id=1, source_target_pairs={{0,2},{2,0},{1,3},{3,1},{4,6},{6,4},{5,7},{7,5},{8,10},{10,8},{9,1... | collective-permute-start | bytes 196616 | tf_op jit(solution)/shard_map/ppermute | solution.py:20
  23.6 0.0 collective-permute-done.6.refs_1_
  23.6 0.0 collective-permute-done.7.refs_2_
  23.6 1.9 %induct_tiles.1 = (f32[32,16,128]{2,1,0:T(8,128)S(1)}, bf16[32,16,128]{2,1,0:T(8,128)(2,1)S(1)}) custom-call(s32[192]{0:T(256)S(4)} %get-tuple-element.37.slots, s32[192]{0:T(256)S(4)} %get-tuple-element.38.rows, f32[8,16,128]{2,1,0:T(8,128)S(1)} %get-tuple-element.44._after.part, bf16[8,16,128]{2,1,0:T(8,128)(2,1)S(1)} %collective-permute-done.5.refs_0_, ...), custom_call_target="tpu_custom_call" | custom-call | flops 4000000000 | bytes 6291456 | tf_op jit(solution)/shard_map/induct_tiles/pallas_call | solution.py:364
  25.5 0.6 %collective-permute-start.9 = (bf16[32,16,128]{2,1,0:T(8,128)(2,1)S(1)}, bf16[32,16,128]{2,1,0:T(8,128)(2,1)S(1)}, u32[]{:S(2)}, u32[]{:S(2)}) collective-permute-start(bf16[32,16,128]{2,1,0:T(8,128)(2,1)S(1)} %get-tuple-element.56), channel_id=1, source_target_pairs={{0,2},{2,0},{1,3},{3,1},{4,6},{6,4},{5,7},{7,5},{8,10},{10,8},{9,1... | collective-permute-start | bytes 393224 | tf_op jit(solution)/shard_map/ppermute | solution.py:20
  26.1 0.9 %collective-permute-done.8.refs_0_ = bf16[16,16,128]{2,1,0:T(8,128)(2,1)S(1)} collective-permute-done((bf16[16,16,128]{2,1,0:T(8,128)(2,1)S(1)}, bf16[16,16,128]{2,1,0:T(8,128)(2,1)S(1)}, u32[]{:S(2)}, u32[]{:S(2)}) %collective-permute-start.8) | collective-permute-done | bytes 65568 | tf_op jit(solution)/shard_map/ppermute | solution.py:20
  27.0 1.8 %collective-permute-start.10 = (bf16[12,16,128]{2,1,0:T(8,128)(2,1)S(1)}, bf16[12,16,128]{2,1,0:T(8,128)(2,1)S(1)}, u32[]{:S(2)}, u32[]{:S(2)}) collective-permute-start(bf16[12,16,128]{2,1,0:T(8,128)(2,1)S(1)} %get-tuple-element.59), channel_id=1, source_target_pairs={{0,12},{4,8},{8,4},{12,0},{1,13},{5,9},{9,5},{13,1},{2,14},{6,10},... | collective-permute-start | bytes 147464 | tf_op jit(solution)/shard_map/ppermute | solution.py:20
  28.8 0.0 collective-permute-start.11
  28.8 2.6 %collective-permute-start.12 = (bf16[12,16,128]{2,1,0:T(8,128)(2,1)S(1)}, bf16[12,16,128]{2,1,0:T(8,128)(2,1)S(1)}, u32[]{:S(2)}, u32[]{:S(2)}) collective-permute-start(bf16[12,16,128]{2,1,0:T(8,128)(2,1)S(1)} %get-tuple-element.61), channel_id=1, source_target_pairs={{0,4},{4,0},{8,12},{12,8},{1,5},{5,1},{9,13},{13,9},{2,6},{6,2},{1... | collective-permute-start | bytes 147464 | tf_op jit(solution)/shard_map/ppermute | solution.py:20
  31.5 0.0 collective-permute-done.9.refs_0_
  31.5 0.6 %base_sums.1 = (f32[32,16,128]{2,1,0:T(8,128)S(1)}, f32[4,16,128]{2,1,0:T(8,128)S(1)}, bf16[16,512]{1,0:T(8,128)(2,1)}) custom-call(bf16[16,512]{1,0:T(8,128)(2,1)S(1)} %copy-done, f32[16,1]{1,0:T(8,128)S(1)} %copy.17.scale, f32[32,16,128]{2,1,0:T(8,128)S(1)} %get-tuple-element.51.field_own, f32[4,16,128]{2,1,0:T(8,128)S(1)} %get-tuple-element.54.end_own, ...), custom_call_target="tpu_custom_call" | custom-call | flops 1000000000 | bytes 1048576 | tf_op jit(solution)/shard_map/base_sums/pallas_call | solution.py:388
  32.1 0.9 %collective-permute-done.10.refs_0_ = bf16[12,16,128]{2,1,0:T(8,128)(2,1)S(1)} collective-permute-done((bf16[12,16,128]{2,1,0:T(8,128)(2,1)S(1)}, bf16[12,16,128]{2,1,0:T(8,128)(2,1)S(1)}, u32[]{:S(2)}, u32[]{:S(2)}) %collective-permute-start.10) | collective-permute-done | bytes 49184 | tf_op jit(solution)/shard_map/ppermute | solution.py:20
  33.0 1.1 %collective-permute-done.11.refs_1_ = bf16[12,16,128]{2,1,0:T(8,128)(2,1)S(1)} collective-permute-done((bf16[12,16,128]{2,1,0:T(8,128)(2,1)S(1)}, bf16[12,16,128]{2,1,0:T(8,128)(2,1)S(1)}, u32[]{:S(2)}, u32[]{:S(2)}) %collective-permute-start.11) | collective-permute-done | bytes 49184 | tf_op jit(solution)/shard_map/ppermute | solution.py:20
  34.1 0.0 collective-permute-done.12.refs_2_
  34.1 1.7 %outputs.1 = (bf16[16,4096]{1,0:T(8,128)(2,1)}, bf16[16,512]{1,0:T(8,128)(2,1)}) custom-call(s32[2,32]{1,0:T(2,128)S(4)} %get-tuple-element.34.slots, s32[4,16]{1,0:T(4,128)S(4)} %get-tuple-element.35.links, s32[2,4096]{1,0:T(2,128)S(1)} %get-tuple-element.36.off, f32[32,16,128]{2,1,0:T(8,128)S(1)} %get-tuple-element.57.field, ...), custom_call_target="tpu_custom_call" | custom-call | flops 1000000000 | bytes 1048576 | tf_op jit(solution)/shard_map/outputs/pallas_call | solution.py:397
  (10 shorter events, 0.1 us)
Async XLA Ops:
  0.6 12.0 %collective-permute-start.3 = (bf16[16,4096]{1,0:T(8,128)(2,1)}, bf16[16,4096]{1,0:T(8,128)(2,1)S(1)}, u32[]{:S(2)}, u32[]{:S(2)}) collective-permute-start(bf16[16,4096]{1,0:T(8,128)(2,1)} %refs_8_.1), channel_id=1, source_target_pairs={{0,2},{2,0},{1,3},{3,1},{4,6},{6,4},{5,7},{7,5},{8,10},{10,8},{9,1... | collective-permute-start | bytes 393224 | tf_op jit(solution)/shard_map/ppermute | solution.py:20
  4.4 6.3 %collective-permute-start.2 = (bf16[5,16,128]{2,1,0:T(8,128)(2,1)S(1)}, bf16[5,16,128]{2,1,0:T(8,128)(2,1)S(1)}, u32[]{:S(2)}, u32[]{:S(2)}) collective-permute-start(bf16[5,16,128]{2,1,0:T(8,128)(2,1)S(1)} %pack_charges.1.refs_0_), channel_id=1, source_target_pairs={{0,12},{4,8},{8,4},{12,0},{1,13},{5,9},{9,5},{13,1},{2,14},{6,10},... | collective-permute-start | bytes 61448 | tf_op jit(solution)/shard_map/ppermute | solution.py:20
  8.0 4.7 %collective-permute-start.1 = (bf16[5,16,128]{2,1,0:T(8,128)(2,1)S(1)}, bf16[5,16,128]{2,1,0:T(8,128)(2,1)S(1)}, u32[]{:S(2)}, u32[]{:S(2)}) collective-permute-start(bf16[5,16,128]{2,1,0:T(8,128)(2,1)S(1)} %pack_charges.1.refs_0_), channel_id=1, source_target_pairs={{0,8},{4,12},{8,0},{12,4},{1,9},{5,13},{9,1},{13,5},{2,10},{6,14},... | collective-permute-start | bytes 61448 | tf_op jit(solution)/shard_map/ppermute | solution.py:20
  8.0 4.7 %collective-permute-start = (bf16[5,16,128]{2,1,0:T(8,128)(2,1)S(1)}, bf16[5,16,128]{2,1,0:T(8,128)(2,1)S(1)}, u32[]{:S(2)}, u32[]{:S(2)}) collective-permute-start(bf16[5,16,128]{2,1,0:T(8,128)(2,1)S(1)} %pack_charges.1.refs_0_), channel_id=1, source_target_pairs={{0,4},{4,0},{8,12},{12,8},{1,5},{5,1},{9,13},{13,9},{2,6},{6,2},{1... | collective-permute-start | bytes 61448 | tf_op jit(solution)/shard_map/ppermute | solution.py:20
  12.7 6.5 %collective-permute-start.4 = (bf16[32,16,128]{2,1,0:T(8,128)(2,1)S(1)}, bf16[32,16,128]{2,1,0:T(8,128)(2,1)S(1)}, u32[]{:S(2)}, u32[]{:S(2)}) collective-permute-start(bf16[32,16,128]{2,1,0:T(8,128)(2,1)S(1)} %get-tuple-element.43), channel_id=1, source_target_pairs={{0,2},{2,0},{1,3},{3,1},{4,6},{6,4},{5,7},{7,5},{8,10},{10,8},{9,1... | collective-permute-start | bytes 393224 | tf_op jit(solution)/shard_map/ppermute | solution.py:20
  14.0 9.6 %copy-start.1 = (bf16[192,128,128]{2,1,0:T(8,128)(2,1)S(1)}, bf16[192,128,128]{2,1,0:T(8,128)(2,1)}, u32[]{:S(2)}) copy-start(bf16[192,128,128]{2,1,0:T(8,128)(2,1)} %refs_4_.3) | copy-start | bytes 18874372
  14.8 8.8 %collective-permute-start.5 = (bf16[8,16,128]{2,1,0:T(8,128)(2,1)S(1)}, bf16[8,16,128]{2,1,0:T(8,128)(2,1)S(1)}, u32[]{:S(2)}, u32[]{:S(2)}) collective-permute-start(bf16[8,16,128]{2,1,0:T(8,128)(2,1)S(1)} %get-tuple-element.47), channel_id=1, source_target_pairs={{0,12},{4,8},{8,4},{12,0},{1,13},{5,9},{9,5},{13,1},{2,14},{6,10},... | collective-permute-start | bytes 98312 | tf_op jit(solution)/shard_map/ppermute | solution.py:20
  16.5 7.1 %collective-permute-start.6 = (bf16[8,16,128]{2,1,0:T(8,128)(2,1)S(1)}, bf16[8,16,128]{2,1,0:T(8,128)(2,1)S(1)}, u32[]{:S(2)}, u32[]{:S(2)}) collective-permute-start(bf16[8,16,128]{2,1,0:T(8,128)(2,1)S(1)} %get-tuple-element.48), channel_id=1, source_target_pairs={{0,8},{4,12},{8,0},{12,4},{1,9},{5,13},{9,1},{13,5},{2,10},{6,14},... | collective-permute-start | bytes 98312 | tf_op jit(solution)/shard_map/ppermute | solution.py:20
  16.9 6.7 %collective-permute-start.7 = (bf16[8,16,128]{2,1,0:T(8,128)(2,1)S(1)}, bf16[8,16,128]{2,1,0:T(8,128)(2,1)S(1)}, u32[]{:S(2)}, u32[]{:S(2)}) collective-permute-start(bf16[8,16,128]{2,1,0:T(8,128)(2,1)S(1)} %get-tuple-element.49), channel_id=1, source_target_pairs={{0,4},{4,0},{8,12},{12,8},{1,5},{5,1},{9,13},{13,9},{2,6},{6,2},{1... | collective-permute-start | bytes 98312 | tf_op jit(solution)/shard_map/ppermute | solution.py:20
  19.2 1.9 %copy-start.2 = (bf16[96,128,128]{2,1,0:T(8,128)(2,1)S(1)}, bf16[96,128,128]{2,1,0:T(8,128)(2,1)}, u32[]{:S(2)}) copy-start(bf16[96,128,128]{2,1,0:T(8,128)(2,1)} %refs_5_.3) | copy-start | bytes 9437188
  22.1 4.9 %collective-permute-start.8 = (bf16[16,16,128]{2,1,0:T(8,128)(2,1)S(1)}, bf16[16,16,128]{2,1,0:T(8,128)(2,1)S(1)}, u32[]{:S(2)}, u32[]{:S(2)}) collective-permute-start(bf16[16,16,128]{2,1,0:T(8,128)(2,1)S(1)} %get-tuple-element.53), channel_id=1, source_target_pairs={{0,2},{2,0},{1,3},{3,1},{4,6},{6,4},{5,7},{7,5},{8,10},{10,8},{9,1... | collective-permute-start | bytes 196616 | tf_op jit(solution)/shard_map/ppermute | solution.py:20
  25.5 6.0 %collective-permute-start.9 = (bf16[32,16,128]{2,1,0:T(8,128)(2,1)S(1)}, bf16[32,16,128]{2,1,0:T(8,128)(2,1)S(1)}, u32[]{:S(2)}, u32[]{:S(2)}) collective-permute-start(bf16[32,16,128]{2,1,0:T(8,128)(2,1)S(1)} %get-tuple-element.56), channel_id=1, source_target_pairs={{0,2},{2,0},{1,3},{3,1},{4,6},{6,4},{5,7},{7,5},{8,10},{10,8},{9,1... | collective-permute-start | bytes 393224 | tf_op jit(solution)/shard_map/ppermute | solution.py:20
  27.0 4.5 %copy-start = (bf16[16,512]{1,0:T(8,128)(2,1)S(1)}, bf16[16,512]{1,0:T(8,128)(2,1)}, u32[]{:S(2)}) copy-start(bf16[16,512]{1,0:T(8,128)(2,1)} %charge.3) | copy-start | bytes 49156
  27.0 6.0 %collective-permute-start.10 = (bf16[12,16,128]{2,1,0:T(8,128)(2,1)S(1)}, bf16[12,16,128]{2,1,0:T(8,128)(2,1)S(1)}, u32[]{:S(2)}, u32[]{:S(2)}) collective-permute-start(bf16[12,16,128]{2,1,0:T(8,128)(2,1)S(1)} %get-tuple-element.59), channel_id=1, source_target_pairs={{0,12},{4,8},{8,4},{12,0},{1,13},{5,9},{9,5},{13,1},{2,14},{6,10},... | collective-permute-start | bytes 147464 | tf_op jit(solution)/shard_map/ppermute | solution.py:20
  28.8 5.2 %collective-permute-start.11 = (bf16[12,16,128]{2,1,0:T(8,128)(2,1)S(1)}, bf16[12,16,128]{2,1,0:T(8,128)(2,1)S(1)}, u32[]{:S(2)}, u32[]{:S(2)}) collective-permute-start(bf16[12,16,128]{2,1,0:T(8,128)(2,1)S(1)} %get-tuple-element.60), channel_id=1, source_target_pairs={{0,8},{4,12},{8,0},{12,4},{1,9},{5,13},{9,1},{13,5},{2,10},{6,14},... | collective-permute-start | bytes 147464 | tf_op jit(solution)/shard_map/ppermute | solution.py:20
  28.8 5.2 %collective-permute-start.12 = (bf16[12,16,128]{2,1,0:T(8,128)(2,1)S(1)}, bf16[12,16,128]{2,1,0:T(8,128)(2,1)S(1)}, u32[]{:S(2)}, u32[]{:S(2)}) collective-permute-start(bf16[12,16,128]{2,1,0:T(8,128)(2,1)S(1)} %get-tuple-element.61), channel_id=1, source_target_pairs={{0,4},{4,0},{8,12},{12,8},{1,5},{5,1},{9,13},{13,9},{2,6},{6,2},{1... | collective-permute-start | bytes 147464 | tf_op jit(solution)/shard_map/ppermute | solution.py:20

commit v7 on v6

--- a/solution.py
+++ b/solution.py
@@ -54,27 +54,28 @@
     message[pan_own] = wide[...].astype(F32).astype(BF16)
 
 
-def ends_body(n_row, n_col, pan_own, cap, n_tables, *refs):
-    sources, rest = refs[: n_tables + 2], refs[n_tables + 2 :]
-    tables, (off, blocks, own) = rest[:n_tables], rest[n_tables : n_tables + 3]
-    sends, (cur, acc, sems) = rest[n_tables + 3 : -3], rest[-3:]
+def ends_body(n_row, n_col, pan_own, cap, n_moved, *refs):
+    sources, targets = refs[: n_moved + 2], refs[n_moved + 2 : 2 * n_moved + 2]
+    (holder, lanes, blocks, own, *sends), (cur, off, acc, sems) = refs[2 * n_moved + 2 : -4], refs[-4:]
     copies = [
         pltpu.make_async_copy(source, target, sems.at[i])
-        for i, (source, target) in enumerate(zip(sources, (*tables, off, cur)))
+        for i, (source, target) in enumerate(zip(sources, (cur, off, *targets)))
     ]
-    for copy in copies[::-1]:
+    for copy in copies:
         copy.start()
-    slots, links = tables[:2]
+    slots, links = targets[:2]
     seg_own, _, width = blocks.shape
     pan_group = pan_own * n_col
     r, c = lax.axis_index("row"), lax.axis_index("col")
     acc[...] = jnp.zeros_like(acc)
     levels = lax.broadcasted_iota(jnp.int32, (width, width), 0)
-    for copy in copies[::-1]:
+    for copy in copies[:4]:
         copy.wait()
 
     def block(k):
         span = pl.ds(pl.multiple_of(k * width, width), width)
+        for e in range(2):
+            lanes[pl.ds(2 * k + e, 1), :] = off[e : e + 1, span]
         to_hot = jnp.where(levels == off[0:1, span], 1.0, 0.0).astype(BF16)
         from_hot = jnp.where(levels == off[1:2, span], -1.0, 0.0).astype(BF16)
         hot = jnp.concatenate([to_hot, from_hot], axis=0)
@@ -90,6 +91,7 @@
         for u in range(unroll):
             for e in range(2):
                 slot = slots[e, i * unroll + u]
+                holder[slot] = 2 * (i * unroll + u) + e
                 p = lax.div(slot, cap)
                 b = links[p, slot - p * cap]
                 acc[lax.bitwise_xor(p, r) * pan_group + b] += got[u][:, e * width : (e + 1) * width]
@@ -102,6 +104,8 @@
         for j in range(1, n_col):
             there = lax.bitwise_xor(c, j)
             sends[j - 1][here] = acc[pl.ds(k * pan_group + there * pan_own, pan_own)].astype(BF16)
+    for copy in copies[4:]:
+        copy.wait()
 
 
 def relay_body(n_row, n_col, pan_own, *refs):
@@ -217,44 +221,57 @@
             messages[n_row - 1 - k][pl.ds(pan_own, pan_group)] = rounded
 
 
-def base_body(n_col, pan_own, charge, scale, field_own, end_own, pot, *refs):
+def add_drops(p, pots, first, links, holder, lanes, field):
+    cap = links.shape[1]
+    ends, drops = [], []
+    for s in range(cap):
+        j = holder[p * cap + s]
+        values = pots[first + links[p, s]].astype(F32)
+        at = jnp.broadcast_to(lanes[pl.ds(j, 1), :], values.shape)
+        drop = jnp.take_along_axis(values, at, axis=1, mode="promise_in_bounds")
+        k = lax.div(j, 2)
+        drops.append(drop * (1 - 2 * (j - 2 * k)).astype(F32))
+        ends.append(k)
+    for k, drop in zip(ends, drops):
+        field[k] += drop
+
+
+def base_body(n_col, pan_own, links, holder, scale, lanes, pack, field_own, end_own, pot, *refs):
     field_in, (field, panels, pot_out) = refs[: n_col - 1], refs[n_col - 1 :]
-    width = pot.shape[2]
-    c = lax.axis_index("col")
+    rhs, width = pot.shape[1:]
+    r, c = lax.axis_index("row"), lax.axis_index("col")
     total = field_own[...]
     for x in field_in:
         total += x[...].astype(F32)
     field[...] = total
+    row = lax.broadcasted_iota(jnp.int32, (rhs, width), 0)
+    factor = jnp.zeros((rhs, width), F32)
+    for i in range(rhs):
+        factor = jnp.where(row == i, scale[i], factor)
     for q in range(pan_own):
-        span = slice(q * width, (q + 1) * width)
-        panels[q] = scale[...] * charge[:, span].astype(F32) + end_own[q]
-        pot_out[:, span] = pot[c * pan_own + q]
-
-
-def final_body(n_row, n_col, pan_own, cap, slots, links, off, field, panels, pot, *refs):
-    arrived, (seg_out, pan_out, held, seg, sems) = refs[: n_row - 1][::-1], refs[n_row - 1 :]
-    seg_own, rhs, width = field.shape
-    pan_group = pan_own * n_col
-    r = lax.axis_index("row")
-    held[pl.ds(r * pan_group, pan_group)] = pot[...].astype(F32)
-    for k, x in enumerate(arrived):
-        sender = lax.bitwise_xor(r, k + 1)
-        held[pl.ds(sender * pan_group, pan_group)] = x[pl.ds(pan_own, pan_group)].astype(F32)
-
-    def at_end(e, k, span):
-        slot = slots[e, k]
-        p = lax.div(slot, cap)
-        values = held[p * pan_group + links[p, slot - p * cap]]
-        lanes = jnp.broadcast_to(off[e : e + 1, span], (rhs, width))
-        return jnp.take_along_axis(values, lanes, axis=1, mode="promise_in_bounds")
-
+        panels[q] = factor * pack[q].astype(F32) + end_own[q]
+        pot_out[:, q * width : (q + 1) * width] = pot[c * pan_own + q]
+    add_drops(r, pot, 0, links, holder, lanes, field)
+
+
+def drops_body(k, pan_own, links, holder, lanes, message, field_in, field):
+    field[...] = field_in[...]
+    p = lax.bitwise_xor(lax.axis_index("row"), k)
+    add_drops(p, message, pan_own, links, holder, lanes, field)
+
+
+def final_body(n_row, pan_own, links, holder, lanes, field_in, panels, *refs):
+    arrived, (seg_out, pan_out, field, seg, sems) = refs[: n_row - 1], refs[n_row - 1 :]
+    seg_own, _, width = field.shape
+    field[...] = field_in[...]
+    p = lax.bitwise_xor(lax.axis_index("row"), 1)
+    add_drops(p, arrived[0], pan_own, links, holder, lanes, field)
     chunks = sems.shape[0]
     size = seg_own // chunks
     copies = []
     for i in range(chunks):
         for k in range(i * size, (i + 1) * size):
-            span = pl.ds(k * width, width)
-            seg[:, span] = (field[k] + at_end(0, k, span) - at_end(1, k, span)).astype(BF16)
+            seg[:, k * width : (k + 1) * width] = field[k].astype(BF16)
         part = pl.ds(i * size * width, size * width)
         copies.append(pltpu.make_async_copy(seg.at[:, part], seg_out.at[:, part], sems.at[i]))
         copies[i].start()
@@ -308,26 +325,29 @@
     packs = exchange_all(pack, [pack] * (n_row - 1), "row")
 
     rows_own = n_row * pan_own
-    scalars = [slots_t, link_needs, induct_slots, induct_rows, coeff_slots, coeff_rows, coeff_needs]
-    n_tables = len(scalars)
+    scalars = [slots_t, link_needs, coeff_slots, coeff_rows, coeff_needs, induct_slots, induct_rows, rhs_scale]
+    moved = [*scalars, coeff_tiles]
     outs = call(
-        functools.partial(ends_body, n_row, n_col, pan_own, cap_k, n_tables),
+        functools.partial(ends_body, n_row, n_col, pan_own, cap_k, len(moved)),
         "end_sums",
-        [pltpu.SMEM(x.shape, jnp.int32) for x in scalars]
-        + [jax.ShapeDtypeStruct(off_t.shape, jnp.int32), like(seg_own, BF16), like(rows_own, F32)]
+        [pltpu.SMEM(x.shape, x.dtype) for x in scalars]
+        + [jax.ShapeDtypeStruct(coeff_tiles.shape, BF16)]
+        + [pltpu.SMEM((2 * seg_own,), jnp.int32), jax.ShapeDtypeStruct((2 * seg_own, width), jnp.int32)]
+        + [like(seg_own, BF16), like(rows_own, F32)]
         + [like(rows_own, BF16)] * (n_col - 1),
-        [ANY] * (n_tables + 2),
+        [ANY] * (len(moved) + 2),
         [
             pltpu.VMEM(current.shape, BF16),
+            pltpu.VMEM(off_t.shape, jnp.int32),
             pltpu.VMEM((n_row * pan_group, rhs, width), F32),
-            pltpu.SemaphoreType.DMA((n_tables + 2,)),
+            pltpu.SemaphoreType.DMA((len(moved) + 2,)),
         ],
         flops=5 * 10**8,
         moved=2**18,
-        out_specs=[SMEM] * n_tables + [VMEM] * (2 + n_col),
-    )(*in_hbm(*scalars, off_t, current))
-    slots_s, links_s, induct_slots, induct_rows, coeff_slots, coeff_rows, coeff_needs = outs[:n_tables]
-    off_v, own_blocks, ends_own, *ends_out = outs[n_tables:]
+        out_specs=[SMEM] * len(scalars) + [VMEM, SMEM] + [VMEM] * (2 + n_col),
+    )(*in_hbm(current, off_t, *moved))
+    _, links_s, coeff_slots, coeff_rows, coeff_needs, induct_slots, induct_rows, scale, coeff_tiles = outs[: len(moved)]
+    holder, lanes, own_blocks, ends_own, *ends_out = outs[len(moved) :]
 
     asked, *relays = call(
         functools.partial(relay_body, n_row, n_col, pan_own),
@@ -389,25 +409,35 @@
         functools.partial(base_body, n_col, pan_own),
         "base_sums",
         [like(seg_own, F32), like(pan_own, F32), jax.ShapeDtypeStruct(charge.shape, BF16)],
-        [VMEM] * (4 + n_col),
+        [SMEM] * 3 + [VMEM] * (4 + n_col),
         flops=10**9,
         moved=2**20,
-    )(charge, rhs_scale[:, None], field_own, end_keep, pot, *field_in)
+    )(links_s, holder, scale, lanes, pack, field_own, end_keep, pot, *field_in)
+
+    for k in reversed(range(2, n_row)):
+        (field,) = call(
+            functools.partial(drops_body, k, pan_own),
+            "add_drops",
+            [like(seg_own, F32)],
+            [SMEM] * 2 + [VMEM] * 3,
+            flops=10**8,
+            moved=2**20,
+        )(links_s, holder, lanes, arrived[k - 1], field)
 
     seg_out, pan_out = call(
-        functools.partial(final_body, n_row, n_col, pan_own, cap_k),
+        functools.partial(final_body, n_row, pan_own),
         "outputs",
         [jax.ShapeDtypeStruct(x.shape, BF16) for x in (current, charge)],
-        [SMEM, SMEM] + [VMEM] * (3 + n_row),
+        [SMEM] * 2 + [VMEM] * (2 + n_row),
         [
-            pltpu.VMEM((n_row * pan_group, rhs, width), F32),
+            pltpu.VMEM((seg_own, rhs, width), F32),
             pltpu.VMEM(current.shape, BF16),
             pltpu.SemaphoreType.DMA((4,)),
         ],
         flops=10**9,
         moved=2**20,
         out_specs=[ANY, VMEM],
-    )(slots_s, links_s, off_v, field, panels, pot, *arrived[::-1])
+    )(links_s, holder, lanes, field, panels, *arrived)
     return (seg_out, pan_out, pot_out)
 
 

time: 36 us -> 34.4 us (0.956)
  local copies, waits for them, and re-layouts: 2.63 us -> 0.17 us
  waiting for transfers between devices: 4.83 us -> 5.33 us
    unnamed x6 -> x2, local copies, waits for them, and re-layouts: 1.9 us -> 0.17 us
    broadcast_in_dim x1 -> x0, local copies, waits for them, and re-layouts: 0.73 us -> none  [shards(): rhs_scale[:, None]]
    ppermute x13, waiting for transfers between devices: 4.83 us -> 5.33 us  [exchange(): lax.ppermute(x, axis, [(i, i ^ k) for i in range(lax.axis_size(axis))])]
    pallas_call x2 -> x4, Pallas kernels: 3.6 us -> 3.83 us  [the longest x1 2.09 us: shards(): call(functools.partial(ends_body, n_row, n_col, pan_own, cap_k, len(moved...]
  transfers between devices with their start and end apart: 13 -> 13, of which waited for: 4 -> 4; matrix products, arithmetic and copies ran while one was open for 2% -> 0% of each run, Pallas kernels for 19% -> 22%
where the time goes in v7:
time: 34.4 us; the launch traced here: 34.1 us
  starting transfers between devices  19.1 us (56%)
  Pallas kernels  8.83 us (26%)
  waiting for transfers between devices  5.33 us (15%)
  between operations  0.71 us (2%)
    ppermute x13, starting transfers between devices, exchange(): lax.ppermute(x, axis, [(i, i ^ k) for i in range(lax.axis_size(axis))])  19.1 us
    ppermute x13, waiting for transfers between devices, exchange(): lax.ppermute(x, axis, [(i, i ^ k) for i in range(lax.axis_size(axis))])  5.33 us
    pallas_call x1, Pallas kernels, shards(): call(functools.partial(ends_body, n_row, n_col, pan_own, cap_k, len(moved...  2.09 us
    pallas_call x1, Pallas kernels, shards(): call(functools.partial(induct_body, n_row, n_col, seg_own), 'induct_tiles...  1.85 us
    pallas_call x1, Pallas kernels, shards(): call(functools.partial(final_body, n_row, pan_own), 'outputs', [jax.Shape...  1.44 us
    pallas_call x1, Pallas kernels, shards(): call(functools.partial(coeff_body, n_row, n_col, pan_own), 'coeff_tiles',...  0.93 us
    pallas_call x1, Pallas kernels, shards(): call(functools.partial(pick_body, n_row, n_col, cap_l), 'pick_blocks', [l...  0.73 us
    pallas_call x1, Pallas kernels, shards(): call(functools.partial(pack_body, pan_own), 'pack_charges', [like(pan_own...  0.73 us
  transfers between devices with their start and end apart: 13, of which 4 were waited for; matrix products, arithmetic and copies ran while one was open for 0% of the time, Pallas kernels for 22%

profile of v7, /device:TPU:0, one launch (start us, length us, event | category | flops | bytes accessed | tf_op | source)
XLA Modules:
  0.0 34.1 jit_solution(8529270364283425857)
XLA Ops:
  0.6 3.0 %collective-permute-start.3 = (bf16[16,4096]{1,0:T(8,128)(2,1)}, bf16[16,4096]{1,0:T(8,128)(2,1)S(1)}, u32[]{:S(2)}, u32[]{:S(2)}) collective-permute-start(bf16[16,4096]{1,0:T(8,128)(2,1)} %refs_0_.1), channel_id=1, source_target_pairs={{0,2},{2,0},{1,3},{3,1},{4,6},{6,4},{5,7},{7,5},{8,10},{10,8},{9,1... | collective-permute-start | bytes 393224 | tf_op jit(solution)/shard_map/ppermute | solution.py:20
  3.6 0.7 %pack_charges.1.refs_0_.pack = bf16[5,16,128]{2,1,0:T(8,128)(2,1)S(1)} custom-call(bf16[16,512]{1,0:T(8,128)(2,1)} %charge.1, s32[4,8]{1,0:T(4,128)} %needs.1), custom_call_target="tpu_custom_call" | custom-call | bytes 65536 | tf_op jit(solution)/shard_map/pack_charges/pallas_call | solution.py:317
  4.4 3.6 %collective-permute-start.2 = (bf16[5,16,128]{2,1,0:T(8,128)(2,1)S(1)}, bf16[5,16,128]{2,1,0:T(8,128)(2,1)S(1)}, u32[]{:S(2)}, u32[]{:S(2)}) collective-permute-start(bf16[5,16,128]{2,1,0:T(8,128)(2,1)S(1)} %pack_charges.1.refs_0_.pack), channel_id=1, source_target_pairs={{0,12},{4,8},{8,4},{12,0},{1,13},{5,9},{9,5},{13,1},{2,14},{6,10},... | collective-permute-start | bytes 61448 | tf_op jit(solution)/shard_map/ppermute | solution.py:20
  8.0 0.0 collective-permute-start.1
  8.0 0.8 %collective-permute-start = (bf16[5,16,128]{2,1,0:T(8,128)(2,1)S(1)}, bf16[5,16,128]{2,1,0:T(8,128)(2,1)S(1)}, u32[]{:S(2)}, u32[]{:S(2)}) collective-permute-start(bf16[5,16,128]{2,1,0:T(8,128)(2,1)S(1)} %pack_charges.1.refs_0_.pack), channel_id=1, source_target_pairs={{0,4},{4,0},{8,12},{12,8},{1,5},{5,1},{9,13},{13,9},{2,6},{6,2},{1... | collective-permute-start | bytes 61448 | tf_op jit(solution)/shard_map/ppermute | solution.py:20
  8.8 2.1 %end_sums.1 = (s32[2,32]{1,0:T(2,128)S(4)}, s32[4,16]{1,0:T(4,128)S(4)}, s32[96]{0:T(128)S(4)}, s32[96]{0:T(128)S(4)}, s32[4,4]{1,0:T(4,128)S(4)}, /*index=5*/s3...) custom-call(bf16[16,4096]{1,0:T(8,128)(2,1)} %refs_0_.1, ...), custom_call_target="tpu_custom_call" | custom-call | flops 500000000 | bytes 262144 | tf_op jit(solution)/shard_map/end_sums/pallas_call | solution.py:330
  10.9 1.8 %collective-permute-done.1.refs_2_ = bf16[5,16,128]{2,1,0:T(8,128)(2,1)S(1)} collective-permute-done((bf16[5,16,128]{2,1,0:T(8,128)(2,1)S(1)}, bf16[5,16,128]{2,1,0:T(8,128)(2,1)S(1)}, u32[]{:S(2)}, u32[]{:S(2)}) %collective-permute-start.1) | collective-permute-done | bytes 20512 | tf_op jit(solution)/shard_map/ppermute | solution.py:20
  12.6 0.0 collective-permute-done.refs_1_
  12.7 0.0 collective-permute-done.3.refs_5_.refs_0_
  12.7 0.6 %collective-permute-start.4 = (bf16[32,16,128]{2,1,0:T(8,128)(2,1)S(1)}, bf16[32,16,128]{2,1,0:T(8,128)(2,1)S(1)}, u32[]{:S(2)}, u32[]{:S(2)}) collective-permute-start(bf16[32,16,128]{2,1,0:T(8,128)(2,1)S(1)} %get-tuple-element.43), channel_id=1, source_target_pairs={{0,2},{2,0},{1,3},{3,1},{4,6},{6,4},{5,7},{7,5},{8,10},{10,8},{9,1... | collective-permute-start | bytes 393224 | tf_op jit(solution)/shard_map/ppermute | solution.py:20
  13.3 0.7 %pick_blocks.1 = (bf16[8,16,128]{2,1,0:T(8,128)(2,1)S(1)}, bf16[8,16,128]{2,1,0:T(8,128)(2,1)S(1)}, bf16[8,16,128]{2,1,0:T(8,128)(2,1)S(1)}, bf16[8,16,128]{2,1,0:T(8,128)(2,1)S(1)}) custom-call(s32[4,128]{1,0:T(4,128)S(1)} %get-tuple-element.53.asked, bf16[32,16,128]{2,1,0:T(8,128)(2,1)S(1)} %get-tuple-element.54.own, ...), custom_call_target="tpu_custom_call" | custom-call | bytes 262144 | tf_op jit(solution)/shard_map/pick_blocks/pallas_call | solution.py:361
  14.0 1.9 %collective-permute-start.8 = (bf16[8,16,128]{2,1,0:T(8,128)(2,1)S(1)}, bf16[8,16,128]{2,1,0:T(8,128)(2,1)S(1)}, u32[]{:S(2)}, u32[]{:S(2)}) collective-permute-start(bf16[8,16,128]{2,1,0:T(8,128)(2,1)S(1)} %get-tuple-element.55), channel_id=1, source_target_pairs={{0,12},{4,8},{8,4},{12,0},{1,13},{5,9},{9,5},{13,1},{2,14},{6,10},... | collective-permute-start | bytes 98312 | tf_op jit(solution)/shard_map/ppermute | solution.py:20
  15.9 0.3 collective-permute-start.9
  16.2 2.3 %collective-permute-start.10 = (bf16[8,16,128]{2,1,0:T(8,128)(2,1)S(1)}, bf16[8,16,128]{2,1,0:T(8,128)(2,1)S(1)}, u32[]{:S(2)}, u32[]{:S(2)}) collective-permute-start(bf16[8,16,128]{2,1,0:T(8,128)(2,1)S(1)} %get-tuple-element.57), channel_id=1, source_target_pairs={{0,4},{4,0},{8,12},{12,8},{1,5},{5,1},{9,13},{13,9},{2,6},{6,2},{1... | collective-permute-start | bytes 98312 | tf_op jit(solution)/shard_map/ppermute | solution.py:20
  18.5 0.0 collective-permute-done.4.refs_4_.refs_1_
  18.5 0.9 %coeff_tiles.1 = (f32[8,16,128]{2,1,0:T(8,128)S(1)}, bf16[16,16,128]{2,1,0:T(8,128)(2,1)S(1)}) custom-call(s32[96]{0:T(128)S(4)} %get-tuple-element.39.slots, s32[96]{0:T(128)S(4)} %get-tuple-element.40.rows, s32[4,4]{1,0:T(4,128)S(4)} %get-tuple-element.41.needs, bf16[5,16,128]{2,1,0:T(8,128)(2,1)S(1)} %pack_charges.1.refs_0_.pack, ...), custom_call_target="tpu_custom_call" | custom-call | flops 2000000000 | bytes 3145728 | tf_op jit(solution)/shard_map/coeff_tiles/pallas_call | solution.py:370
  19.4 1.6 %collective-permute-start.5 = (bf16[16,16,128]{2,1,0:T(8,128)(2,1)S(1)}, bf16[16,16,128]{2,1,0:T(8,128)(2,1)S(1)}, u32[]{:S(2)}, u32[]{:S(2)}) collective-permute-start(bf16[16,16,128]{2,1,0:T(8,128)(2,1)S(1)} %get-tuple-element.47), channel_id=1, source_target_pairs={{0,2},{2,0},{1,3},{3,1},{4,6},{6,4},{5,7},{7,5},{8,10},{10,8},{9,1... | collective-permute-start | bytes 196616 | tf_op jit(solution)/shard_map/ppermute | solution.py:20
  21.0 0.0 collective-permute-done.8.refs_0_
  21.0 0.1 collective-permute-done.9.refs_1_
  21.1 0.2 copy-done
  21.3 1.9 %induct_tiles.1 = (f32[32,16,128]{2,1,0:T(8,128)S(1)}, bf16[32,16,128]{2,1,0:T(8,128)(2,1)S(1)}) custom-call(s32[192]{0:T(256)S(4)} %get-tuple-element.51.slots, s32[192]{0:T(256)S(4)} %get-tuple-element.52.rows, f32[8,16,128]{2,1,0:T(8,128)S(1)} %get-tuple-element.45.part._after, bf16[8,16,128]{2,1,0:T(8,128)(2,1)S(1)} %collective-permute-done.8.refs_0_, ...), custom_call_target="tpu_custom_call" | custom-call | flops 4000000000 | bytes 6291456 | tf_op jit(solution)/shard_map/induct_tiles/pallas_call | solution.py:384
  23.1 1.6 %collective-permute-start.11 = (bf16[32,16,128]{2,1,0:T(8,128)(2,1)S(1)}, bf16[32,16,128]{2,1,0:T(8,128)(2,1)S(1)}, u32[]{:S(2)}, u32[]{:S(2)}) collective-permute-start(bf16[32,16,128]{2,1,0:T(8,128)(2,1)S(1)} %get-tuple-element.62), channel_id=1, source_target_pairs={{0,2},{2,0},{1,3},{3,1},{4,6},{6,4},{5,7},{7,5},{8,10},{10,8},{9,1... | collective-permute-start | bytes 393224 | tf_op jit(solution)/shard_map/ppermute | solution.py:20
  24.7 1.6 %collective-permute-start.6 = (bf16[12,16,128]{2,1,0:T(8,128)(2,1)S(1)}, bf16[12,16,128]{2,1,0:T(8,128)(2,1)S(1)}, u32[]{:S(2)}, u32[]{:S(2)}) collective-permute-start(bf16[12,16,128]{2,1,0:T(8,128)(2,1)S(1)} %get-tuple-element.48), channel_id=1, source_target_pairs={{0,8},{4,12},{8,0},{12,4},{1,9},{5,13},{9,1},{13,5},{2,10},{6,14},... | collective-permute-start | bytes 147464 | tf_op jit(solution)/shard_map/ppermute | solution.py:20
  26.3 2.0 %collective-permute-start.7 = (bf16[12,16,128]{2,1,0:T(8,128)(2,1)S(1)}, bf16[12,16,128]{2,1,0:T(8,128)(2,1)S(1)}, u32[]{:S(2)}, u32[]{:S(2)}) collective-permute-start(bf16[12,16,128]{2,1,0:T(8,128)(2,1)S(1)} %get-tuple-element.49), channel_id=1, source_target_pairs={{0,12},{4,8},{8,4},{12,0},{1,13},{5,9},{9,5},{13,1},{2,14},{6,10},... | collective-permute-start | bytes 147464 | tf_op jit(solution)/shard_map/ppermute | solution.py:20
  28.3 0.0 collective-permute-start.12
  28.3 0.7 %base_sums.1 = (f32[32,16,128]{2,1,0:T(8,128)S(1)}, f32[4,16,128]{2,1,0:T(8,128)S(1)}, bf16[16,512]{1,0:T(8,128)(2,1)}) custom-call(s32[4,16]{1,0:T(4,128)S(4)} %get-tuple-element.36.links, s32[64]{0:T(128)S(4)} %get-tuple-element.37.holder, f32[16]{0:T(128)S(4)} %get-tuple-element.50.scale, s32[64,128]{1,0:T(8,128)S(1)} %get-tuple-element.38.lanes, ...), custom_call_target="tpu_custom_call" | custom-call | flops 1000000000 | bytes 1048576 | tf_op jit(solution)/shard_map/base_sums/pallas_call | solution.py:408
  29.0 3.2 %collective-permute-done.7.message.refs_2_ = bf16[12,16,128]{2,1,0:T(8,128)(2,1)S(1)} collective-permute-done((bf16[12,16,128]{2,1,0:T(8,128)(2,1)S(1)}, bf16[12,16,128]{2,1,0:T(8,128)(2,1)S(1)}, u32[]{:S(2)}, u32[]{:S(2)}) %collective-permute-start.7) | collective-permute-done | bytes 49184 | tf_op jit(solution)/shard_map/ppermute | solution.py:20
  32.2 0.1 add_drops.2.field_in
  32.4 0.0 collective-permute-done.6.message.refs_1_
  32.4 0.1 add_drops.3.field_in
  32.5 0.2 collective-permute-done.12.refs_0_
  32.7 1.4 %outputs.1 = (bf16[16,4096]{1,0:T(8,128)(2,1)}, bf16[16,512]{1,0:T(8,128)(2,1)}) custom-call(s32[4,16]{1,0:T(4,128)S(4)} %get-tuple-element.36.links, s32[64]{0:T(128)S(4)} %get-tuple-element.37.holder, s32[64,128]{1,0:T(8,128)S(1)} %get-tuple-element.38.lanes, f32[32,16,128]{2,1,0:T(8,128)S(1)} %add_drops.3.field_in, ...), custom_call_target="tpu_custom_call" | custom-call | flops 1000000000 | bytes 1048576 | tf_op jit(solution)/shard_map/outputs/pallas_call | solution.py:427
  (7 shorter events, 0.1 us)
Async XLA Ops:
  0.6 12.0 %collective-permute-start.3 = (bf16[16,4096]{1,0:T(8,128)(2,1)}, bf16[16,4096]{1,0:T(8,128)(2,1)S(1)}, u32[]{:S(2)}, u32[]{:S(2)}) collective-permute-start(bf16[16,4096]{1,0:T(8,128)(2,1)} %refs_0_.1), channel_id=1, source_target_pairs={{0,2},{2,0},{1,3},{3,1},{4,6},{6,4},{5,7},{7,5},{8,10},{10,8},{9,1... | collective-permute-start | bytes 393224 | tf_op jit(solution)/shard_map/ppermute | solution.py:20
  4.4 6.5 %collective-permute-start.2 = (bf16[5,16,128]{2,1,0:T(8,128)(2,1)S(1)}, bf16[5,16,128]{2,1,0:T(8,128)(2,1)S(1)}, u32[]{:S(2)}, u32[]{:S(2)}) collective-permute-start(bf16[5,16,128]{2,1,0:T(8,128)(2,1)S(1)} %pack_charges.1.refs_0_.pack), channel_id=1, source_target_pairs={{0,12},{4,8},{8,4},{12,0},{1,13},{5,9},{9,5},{13,1},{2,14},{6,10},... | collective-permute-start | bytes 61448 | tf_op jit(solution)/shard_map/ppermute | solution.py:20
  8.0 4.7 %collective-permute-start.1 = (bf16[5,16,128]{2,1,0:T(8,128)(2,1)S(1)}, bf16[5,16,128]{2,1,0:T(8,128)(2,1)S(1)}, u32[]{:S(2)}, u32[]{:S(2)}) collective-permute-start(bf16[5,16,128]{2,1,0:T(8,128)(2,1)S(1)} %pack_charges.1.refs_0_.pack), channel_id=1, source_target_pairs={{0,8},{4,12},{8,0},{12,4},{1,9},{5,13},{9,1},{13,5},{2,10},{6,14},... | collective-permute-start | bytes 61448 | tf_op jit(solution)/shard_map/ppermute | solution.py:20
  8.0 4.7 %collective-permute-start = (bf16[5,16,128]{2,1,0:T(8,128)(2,1)S(1)}, bf16[5,16,128]{2,1,0:T(8,128)(2,1)S(1)}, u32[]{:S(2)}, u32[]{:S(2)}) collective-permute-start(bf16[5,16,128]{2,1,0:T(8,128)(2,1)S(1)} %pack_charges.1.refs_0_.pack), channel_id=1, source_target_pairs={{0,4},{4,0},{8,12},{12,8},{1,5},{5,1},{9,13},{13,9},{2,6},{6,2},{1... | collective-permute-start | bytes 61448 | tf_op jit(solution)/shard_map/ppermute | solution.py:20
  12.7 5.8 %collective-permute-start.4 = (bf16[32,16,128]{2,1,0:T(8,128)(2,1)S(1)}, bf16[32,16,128]{2,1,0:T(8,128)(2,1)S(1)}, u32[]{:S(2)}, u32[]{:S(2)}) collective-permute-start(bf16[32,16,128]{2,1,0:T(8,128)(2,1)S(1)} %get-tuple-element.43), channel_id=1, source_target_pairs={{0,2},{2,0},{1,3},{3,1},{4,6},{6,4},{5,7},{7,5},{8,10},{10,8},{9,1... | collective-permute-start | bytes 393224 | tf_op jit(solution)/shard_map/ppermute | solution.py:20
  14.0 7.0 %collective-permute-start.8 = (bf16[8,16,128]{2,1,0:T(8,128)(2,1)S(1)}, bf16[8,16,128]{2,1,0:T(8,128)(2,1)S(1)}, u32[]{:S(2)}, u32[]{:S(2)}) collective-permute-start(bf16[8,16,128]{2,1,0:T(8,128)(2,1)S(1)} %get-tuple-element.55), channel_id=1, source_target_pairs={{0,12},{4,8},{8,4},{12,0},{1,13},{5,9},{9,5},{13,1},{2,14},{6,10},... | collective-permute-start | bytes 98312 | tf_op jit(solution)/shard_map/ppermute | solution.py:20
  15.9 5.2 %collective-permute-start.9 = (bf16[8,16,128]{2,1,0:T(8,128)(2,1)S(1)}, bf16[8,16,128]{2,1,0:T(8,128)(2,1)S(1)}, u32[]{:S(2)}, u32[]{:S(2)}) collective-permute-start(bf16[8,16,128]{2,1,0:T(8,128)(2,1)S(1)} %get-tuple-element.56), channel_id=1, source_target_pairs={{0,8},{4,12},{8,0},{12,4},{1,9},{5,13},{9,1},{13,5},{2,10},{6,14},... | collective-permute-start | bytes 98312 | tf_op jit(solution)/shard_map/ppermute | solution.py:20
  16.2 4.9 %collective-permute-start.10 = (bf16[8,16,128]{2,1,0:T(8,128)(2,1)S(1)}, bf16[8,16,128]{2,1,0:T(8,128)(2,1)S(1)}, u32[]{:S(2)}, u32[]{:S(2)}) collective-permute-start(bf16[8,16,128]{2,1,0:T(8,128)(2,1)S(1)} %get-tuple-element.57), channel_id=1, source_target_pairs={{0,4},{4,0},{8,12},{12,8},{1,5},{5,1},{9,13},{13,9},{2,6},{6,2},{1... | collective-permute-start | bytes 98312 | tf_op jit(solution)/shard_map/ppermute | solution.py:20
  18.5 2.8 %copy-start = (bf16[192,128,128]{2,1,0:T(8,128)(2,1)S(1)}, bf16[192,128,128]{2,1,0:T(8,128)(2,1)}, u32[]{:S(2)}) copy-start(bf16[192,128,128]{2,1,0:T(8,128)(2,1)} %refs_4_.3) | copy-start | bytes 18874372
  19.4 5.3 %collective-permute-start.5 = (bf16[16,16,128]{2,1,0:T(8,128)(2,1)S(1)}, bf16[16,16,128]{2,1,0:T(8,128)(2,1)S(1)}, u32[]{:S(2)}, u32[]{:S(2)}) collective-permute-start(bf16[16,16,128]{2,1,0:T(8,128)(2,1)S(1)} %get-tuple-element.47), channel_id=1, source_target_pairs={{0,2},{2,0},{1,3},{3,1},{4,6},{6,4},{5,7},{7,5},{8,10},{10,8},{9,1... | collective-permute-start | bytes 196616 | tf_op jit(solution)/shard_map/ppermute | solution.py:20
  23.1 5.2 %collective-permute-start.11 = (bf16[32,16,128]{2,1,0:T(8,128)(2,1)S(1)}, bf16[32,16,128]{2,1,0:T(8,128)(2,1)S(1)}, u32[]{:S(2)}, u32[]{:S(2)}) collective-permute-start(bf16[32,16,128]{2,1,0:T(8,128)(2,1)S(1)} %get-tuple-element.62), channel_id=1, source_target_pairs={{0,2},{2,0},{1,3},{3,1},{4,6},{6,4},{5,7},{7,5},{8,10},{10,8},{9,1... | collective-permute-start | bytes 393224 | tf_op jit(solution)/shard_map/ppermute | solution.py:20
  24.7 7.6 %collective-permute-start.6 = (bf16[12,16,128]{2,1,0:T(8,128)(2,1)S(1)}, bf16[12,16,128]{2,1,0:T(8,128)(2,1)S(1)}, u32[]{:S(2)}, u32[]{:S(2)}) collective-permute-start(bf16[12,16,128]{2,1,0:T(8,128)(2,1)S(1)} %get-tuple-element.48), channel_id=1, source_target_pairs={{0,8},{4,12},{8,0},{12,4},{1,9},{5,13},{9,1},{13,5},{2,10},{6,14},... | collective-permute-start | bytes 147464 | tf_op jit(solution)/shard_map/ppermute | solution.py:20
  26.3 5.9 %collective-permute-start.7 = (bf16[12,16,128]{2,1,0:T(8,128)(2,1)S(1)}, bf16[12,16,128]{2,1,0:T(8,128)(2,1)S(1)}, u32[]{:S(2)}, u32[]{:S(2)}) collective-permute-start(bf16[12,16,128]{2,1,0:T(8,128)(2,1)S(1)} %get-tuple-element.49), channel_id=1, source_target_pairs={{0,12},{4,8},{8,4},{12,0},{1,13},{5,9},{9,5},{13,1},{2,14},{6,10},... | collective-permute-start | bytes 147464 | tf_op jit(solution)/shard_map/ppermute | solution.py:20
  28.3 4.4 %collective-permute-start.12 = (bf16[12,16,128]{2,1,0:T(8,128)(2,1)S(1)}, bf16[12,16,128]{2,1,0:T(8,128)(2,1)S(1)}, u32[]{:S(2)}, u32[]{:S(2)}) collective-permute-start(bf16[12,16,128]{2,1,0:T(8,128)(2,1)S(1)} %get-tuple-element.65), channel_id=1, source_target_pairs={{0,4},{4,0},{8,12},{12,8},{1,5},{5,1},{9,13},{13,9},{2,6},{6,2},{1... | collective-permute-start | bytes 147464 | tf_op jit(solution)/shard_map/ppermute | solution.py:20

commit v8 on v7

--- a/solution.py
+++ b/solution.py
@@ -261,25 +261,26 @@
 
 
 def final_body(n_row, pan_own, links, holder, lanes, field_in, panels, *refs):
-    arrived, (seg_out, pan_out, field, seg, sems) = refs[: n_row - 1], refs[n_row - 1 :]
+    arrived, (seg_out, pan_out, field, seg, pan, sems) = refs[: n_row - 1], refs[n_row - 1 :]
     seg_own, _, width = field.shape
     field[...] = field_in[...]
     p = lax.bitwise_xor(lax.axis_index("row"), 1)
     add_drops(p, arrived[0], pan_own, links, holder, lanes, field)
-    chunks = sems.shape[0]
+    for q in range(pan_own):
+        total = panels[q]
+        for x in arrived:
+            total += x[q].astype(F32)
+        pan[:, q * width : (q + 1) * width] = total.astype(BF16)
+    chunks = sems.shape[0] - 1
+    copies = [pltpu.make_async_copy(pan, pan_out, sems.at[chunks])]
+    copies[0].start()
     size = seg_own // chunks
-    copies = []
     for i in range(chunks):
         for k in range(i * size, (i + 1) * size):
             seg[:, k * width : (k + 1) * width] = field[k].astype(BF16)
         part = pl.ds(i * size * width, size * width)
         copies.append(pltpu.make_async_copy(seg.at[:, part], seg_out.at[:, part], sems.at[i]))
-        copies[i].start()
-    for q in range(pan_own):
-        total = panels[q]
-        for x in arrived:
-            total += x[q].astype(F32)
-        pan_out[:, q * width : (q + 1) * width] = total.astype(BF16)
+        copies[-1].start()
     for copy in copies:
         copy.wait()
 
@@ -362,7 +363,7 @@
         functools.partial(pick_body, n_row, n_col, cap_l),
         "pick_blocks",
         [like(cap_l, BF16)] * n_row,
-        [SMEM] + [VMEM] * n_col,
+        [VMEM] * (1 + n_col),
         moved=2**18,
     )(asked, own_blocks, *cur[1:])
     got = exchange_all(own_picks, picks[::-1], "row")
@@ -432,11 +433,12 @@
         [
             pltpu.VMEM((seg_own, rhs, width), F32),
             pltpu.VMEM(current.shape, BF16),
-            pltpu.SemaphoreType.DMA((4,)),
+            pltpu.VMEM(charge.shape, BF16),
+            pltpu.SemaphoreType.DMA((3,)),
         ],
         flops=10**9,
         moved=2**20,
-        out_specs=[ANY, VMEM],
+        out_specs=[ANY, ANY],
     )(links_s, holder, lanes, field, panels, *arrived)
     return (seg_out, pan_out, pot_out)
 

time: 34.4 us -> 33.3 us (0.968)
  Pallas kernels: 8.83 us -> 7.75 us
    pallas_call x1, Pallas kernels: 1.44 us -> 0.84 us  [shards(): call(functools.partial(final_body, n_row, pan_own), 'outputs', [jax.Shape...]
    pallas_call x1, Pallas kernels: 0.73 us -> 0.26 us  [shards(): call(functools.partial(pick_body, n_row, n_col, cap_l), 'pick_blocks', [l...]
  transfers between devices with their start and end apart: 13 -> 13, of which waited for: 4 -> 4; matrix products, arithmetic and copies ran while one was open for 0% -> 0% of each run, Pallas kernels for 22% -> 21%
where the time goes in v8:
time: 33.3 us; the launch traced here: 33.1 us
  starting transfers between devices  19.1 us (57%)
  Pallas kernels  7.75 us (23%)
  waiting for transfers between devices  5.32 us (16%)
  between operations  0.71 us (2%)
    ppermute x13, starting transfers between devices, exchange(): lax.ppermute(x, axis, [(i, i ^ k) for i in range(lax.axis_size(axis))])  19.1 us
    ppermute x13, waiting for transfers between devices, exchange(): lax.ppermute(x, axis, [(i, i ^ k) for i in range(lax.axis_size(axis))])  5.32 us
    pallas_call x1, Pallas kernels, shards(): call(functools.partial(ends_body, n_row, n_col, pan_own, cap_k, len(moved...  2.09 us
    pallas_call x1, Pallas kernels, shards(): call(functools.partial(induct_body, n_row, n_col, seg_own), 'induct_tiles...  1.84 us
    pallas_call x1, Pallas kernels, shards(): call(functools.partial(coeff_body, n_row, n_col, pan_own), 'coeff_tiles',...  0.94 us
    pallas_call x1, Pallas kernels, shards(): call(functools.partial(final_body, n_row, pan_own), 'outputs', [jax.Shape...  0.84 us
    pallas_call x1, Pallas kernels, shards(): call(functools.partial(pack_body, pan_own), 'pack_charges', [like(pan_own...  0.73 us
    pallas_call x1, Pallas kernels, shards(): call(functools.partial(base_body, n_col, pan_own), 'base_sums', [like(seg...  0.71 us
  transfers between devices with their start and end apart: 13, of which 4 were waited for; matrix products, arithmetic and copies ran while one was open for 0% of the time, Pallas kernels for 21%

profile of v8, /device:TPU:0, one launch (start us, length us, event | category | flops | bytes accessed | tf_op | source)
XLA Modules:
  0.0 33.1 jit_solution(12870913807685519473)
XLA Ops:
  0.6 3.0 %collective-permute-start.3 = (bf16[16,4096]{1,0:T(8,128)(2,1)}, bf16[16,4096]{1,0:T(8,128)(2,1)S(1)}, u32[]{:S(2)}, u32[]{:S(2)}) collective-permute-start(bf16[16,4096]{1,0:T(8,128)(2,1)} %refs_0_.1), channel_id=1, source_target_pairs={{0,2},{2,0},{1,3},{3,1},{4,6},{6,4},{5,7},{7,5},{8,10},{10,8},{9,1... | collective-permute-start | bytes 393224 | tf_op jit(solution)/shard_map/ppermute | solution.py:20
  3.6 0.7 %pack_charges.1.refs_0_.pack = bf16[5,16,128]{2,1,0:T(8,128)(2,1)S(1)} custom-call(bf16[16,512]{1,0:T(8,128)(2,1)} %charge.1, s32[4,8]{1,0:T(4,128)} %needs.1), custom_call_target="tpu_custom_call" | custom-call | bytes 65536 | tf_op jit(solution)/shard_map/pack_charges/pallas_call | solution.py:318
  4.4 3.6 %collective-permute-start.2 = (bf16[5,16,128]{2,1,0:T(8,128)(2,1)S(1)}, bf16[5,16,128]{2,1,0:T(8,128)(2,1)S(1)}, u32[]{:S(2)}, u32[]{:S(2)}) collective-permute-start(bf16[5,16,128]{2,1,0:T(8,128)(2,1)S(1)} %pack_charges.1.refs_0_.pack), channel_id=1, source_target_pairs={{0,12},{4,8},{8,4},{12,0},{1,13},{5,9},{9,5},{13,1},{2,14},{6,10},... | collective-permute-start | bytes 61448 | tf_op jit(solution)/shard_map/ppermute | solution.py:20
  8.0 0.0 collective-permute-start.1
  8.0 0.8 %collective-permute-start = (bf16[5,16,128]{2,1,0:T(8,128)(2,1)S(1)}, bf16[5,16,128]{2,1,0:T(8,128)(2,1)S(1)}, u32[]{:S(2)}, u32[]{:S(2)}) collective-permute-start(bf16[5,16,128]{2,1,0:T(8,128)(2,1)S(1)} %pack_charges.1.refs_0_.pack), channel_id=1, source_target_pairs={{0,4},{4,0},{8,12},{12,8},{1,5},{5,1},{9,13},{13,9},{2,6},{6,2},{1... | collective-permute-start | bytes 61448 | tf_op jit(solution)/shard_map/ppermute | solution.py:20
  8.8 2.1 %end_sums.1 = (s32[2,32]{1,0:T(2,128)S(4)}, s32[4,16]{1,0:T(4,128)S(4)}, s32[96]{0:T(128)S(4)}, s32[96]{0:T(128)S(4)}, s32[4,4]{1,0:T(4,128)S(4)}, /*index=5*/s3...) custom-call(bf16[16,4096]{1,0:T(8,128)(2,1)} %refs_0_.1, ...), custom_call_target="tpu_custom_call" | custom-call | flops 500000000 | bytes 262144 | tf_op jit(solution)/shard_map/end_sums/pallas_call | solution.py:331
  10.9 0.0 collective-permute-done.2.refs_3_
  10.9 1.8 %collective-permute-done.1.refs_2_ = bf16[5,16,128]{2,1,0:T(8,128)(2,1)S(1)} collective-permute-done((bf16[5,16,128]{2,1,0:T(8,128)(2,1)S(1)}, bf16[5,16,128]{2,1,0:T(8,128)(2,1)S(1)}, u32[]{:S(2)}, u32[]{:S(2)}) %collective-permute-start.1) | collective-permute-done | bytes 20512 | tf_op jit(solution)/shard_map/ppermute | solution.py:20
  12.6 0.0 collective-permute-done.refs_1_
  12.7 0.0 collective-permute-done.3.refs_5_.refs_0_
  12.7 0.6 %collective-permute-start.4 = (bf16[32,16,128]{2,1,0:T(8,128)(2,1)S(1)}, bf16[32,16,128]{2,1,0:T(8,128)(2,1)S(1)}, u32[]{:S(2)}, u32[]{:S(2)}) collective-permute-start(bf16[32,16,128]{2,1,0:T(8,128)(2,1)S(1)} %get-tuple-element.43), channel_id=1, source_target_pairs={{0,2},{2,0},{1,3},{3,1},{4,6},{6,4},{5,7},{7,5},{8,10},{10,8},{9,1... | collective-permute-start | bytes 393224 | tf_op jit(solution)/shard_map/ppermute | solution.py:20
  13.3 0.3 pick_blocks.1
  13.6 1.9 %collective-permute-start.8 = (bf16[8,16,128]{2,1,0:T(8,128)(2,1)S(1)}, bf16[8,16,128]{2,1,0:T(8,128)(2,1)S(1)}, u32[]{:S(2)}, u32[]{:S(2)}) collective-permute-start(bf16[8,16,128]{2,1,0:T(8,128)(2,1)S(1)} %get-tuple-element.55), channel_id=1, source_target_pairs={{0,12},{4,8},{8,4},{12,0},{1,13},{5,9},{9,5},{13,1},{2,14},{6,10},... | collective-permute-start | bytes 98312 | tf_op jit(solution)/shard_map/ppermute | solution.py:20
  15.5 0.3 collective-permute-start.9
  15.7 2.3 %collective-permute-start.10 = (bf16[8,16,128]{2,1,0:T(8,128)(2,1)S(1)}, bf16[8,16,128]{2,1,0:T(8,128)(2,1)S(1)}, u32[]{:S(2)}, u32[]{:S(2)}) collective-permute-start(bf16[8,16,128]{2,1,0:T(8,128)(2,1)S(1)} %get-tuple-element.57), channel_id=1, source_target_pairs={{0,4},{4,0},{8,12},{12,8},{1,5},{5,1},{9,13},{13,9},{2,6},{6,2},{1... | collective-permute-start | bytes 98312 | tf_op jit(solution)/shard_map/ppermute | solution.py:20
  18.0 0.0 collective-permute-done.4.refs_4_.refs_1_
  18.0 0.9 %coeff_tiles.1 = (f32[8,16,128]{2,1,0:T(8,128)S(1)}, bf16[16,16,128]{2,1,0:T(8,128)(2,1)S(1)}) custom-call(s32[96]{0:T(128)S(4)} %get-tuple-element.39.slots, s32[96]{0:T(128)S(4)} %get-tuple-element.40.rows, s32[4,4]{1,0:T(4,128)S(4)} %get-tuple-element.41.needs, bf16[5,16,128]{2,1,0:T(8,128)(2,1)S(1)} %pack_charges.1.refs_0_.pack, ...), custom_call_target="tpu_custom_call" | custom-call | flops 2000000000 | bytes 3145728 | tf_op jit(solution)/shard_map/coeff_tiles/pallas_call | solution.py:371
  19.0 1.6 %collective-permute-start.5 = (bf16[16,16,128]{2,1,0:T(8,128)(2,1)S(1)}, bf16[16,16,128]{2,1,0:T(8,128)(2,1)S(1)}, u32[]{:S(2)}, u32[]{:S(2)}) collective-permute-start(bf16[16,16,128]{2,1,0:T(8,128)(2,1)S(1)} %get-tuple-element.47), channel_id=1, source_target_pairs={{0,2},{2,0},{1,3},{3,1},{4,6},{6,4},{5,7},{7,5},{8,10},{10,8},{9,1... | collective-permute-start | bytes 196616 | tf_op jit(solution)/shard_map/ppermute | solution.py:20
  20.5 0.0 collective-permute-done.8.refs_0_
  20.5 0.1 collective-permute-done.9.refs_1_
  20.6 0.2 copy-done
  20.8 1.8 %induct_tiles.1 = (f32[32,16,128]{2,1,0:T(8,128)S(1)}, bf16[32,16,128]{2,1,0:T(8,128)(2,1)S(1)}) custom-call(s32[192]{0:T(256)S(4)} %get-tuple-element.51.slots, s32[192]{0:T(256)S(4)} %get-tuple-element.52.rows, f32[8,16,128]{2,1,0:T(8,128)S(1)} %get-tuple-element.45.part._after, bf16[8,16,128]{2,1,0:T(8,128)(2,1)S(1)} %collective-permute-done.8.refs_0_, ...), custom_call_target="tpu_custom_call" | custom-call | flops 4000000000 | bytes 6291456 | tf_op jit(solution)/shard_map/induct_tiles/pallas_call | solution.py:385
  22.6 1.6 %collective-permute-start.11 = (bf16[32,16,128]{2,1,0:T(8,128)(2,1)S(1)}, bf16[32,16,128]{2,1,0:T(8,128)(2,1)S(1)}, u32[]{:S(2)}, u32[]{:S(2)}) collective-permute-start(bf16[32,16,128]{2,1,0:T(8,128)(2,1)S(1)} %get-tuple-element.62), channel_id=1, source_target_pairs={{0,2},{2,0},{1,3},{3,1},{4,6},{6,4},{5,7},{7,5},{8,10},{10,8},{9,1... | collective-permute-start | bytes 393224 | tf_op jit(solution)/shard_map/ppermute | solution.py:20
  24.2 1.6 %collective-permute-start.6 = (bf16[12,16,128]{2,1,0:T(8,128)(2,1)S(1)}, bf16[12,16,128]{2,1,0:T(8,128)(2,1)S(1)}, u32[]{:S(2)}, u32[]{:S(2)}) collective-permute-start(bf16[12,16,128]{2,1,0:T(8,128)(2,1)S(1)} %get-tuple-element.48), channel_id=1, source_target_pairs={{0,8},{4,12},{8,0},{12,4},{1,9},{5,13},{9,1},{13,5},{2,10},{6,14},... | collective-permute-start | bytes 147464 | tf_op jit(solution)/shard_map/ppermute | solution.py:20
  25.8 2.0 %collective-permute-start.7 = (bf16[12,16,128]{2,1,0:T(8,128)(2,1)S(1)}, bf16[12,16,128]{2,1,0:T(8,128)(2,1)S(1)}, u32[]{:S(2)}, u32[]{:S(2)}) collective-permute-start(bf16[12,16,128]{2,1,0:T(8,128)(2,1)S(1)} %get-tuple-element.49), channel_id=1, source_target_pairs={{0,12},{4,8},{8,4},{12,0},{1,13},{5,9},{9,5},{13,1},{2,14},{6,10},... | collective-permute-start | bytes 147464 | tf_op jit(solution)/shard_map/ppermute | solution.py:20
  27.8 0.0 collective-permute-start.12
  27.8 0.7 %base_sums.1 = (f32[32,16,128]{2,1,0:T(8,128)S(1)}, f32[4,16,128]{2,1,0:T(8,128)S(1)}, bf16[16,512]{1,0:T(8,128)(2,1)}) custom-call(s32[4,16]{1,0:T(4,128)S(4)} %get-tuple-element.36.links, s32[64]{0:T(128)S(4)} %get-tuple-element.37.holder, f32[16]{0:T(128)S(4)} %get-tuple-element.50.scale, s32[64,128]{1,0:T(8,128)S(1)} %get-tuple-element.38.lanes, ...), custom_call_target="tpu_custom_call" | custom-call | flops 1000000000 | bytes 1048576 | tf_op jit(solution)/shard_map/base_sums/pallas_call | solution.py:409
  28.5 3.2 %collective-permute-done.7.message.refs_2_ = bf16[12,16,128]{2,1,0:T(8,128)(2,1)S(1)} collective-permute-done((bf16[12,16,128]{2,1,0:T(8,128)(2,1)S(1)}, bf16[12,16,128]{2,1,0:T(8,128)(2,1)S(1)}, u32[]{:S(2)}, u32[]{:S(2)}) %collective-permute-start.7) | collective-permute-done | bytes 49184 | tf_op jit(solution)/shard_map/ppermute | solution.py:20
  31.7 0.1 add_drops.2.field_in
  31.9 0.1 add_drops.3.field_in
  32.1 0.2 collective-permute-done.12.refs_0_
  32.2 0.8 %outputs.1 = (bf16[16,4096]{1,0:T(8,128)(2,1)}, bf16[16,512]{1,0:T(8,128)(2,1)}) custom-call(s32[4,16]{1,0:T(4,128)S(4)} %get-tuple-element.36.links, s32[64]{0:T(128)S(4)} %get-tuple-element.37.holder, s32[64,128]{1,0:T(8,128)S(1)} %get-tuple-element.38.lanes, f32[32,16,128]{2,1,0:T(8,128)S(1)} %add_drops.3.field_in, ...), custom_call_target="tpu_custom_call" | custom-call | flops 1000000000 | bytes 1048576 | tf_op jit(solution)/shard_map/outputs/pallas_call | solution.py:428
  (7 shorter events, 0.1 us)
Async XLA Ops:
  0.6 12.0 %collective-permute-start.3 = (bf16[16,4096]{1,0:T(8,128)(2,1)}, bf16[16,4096]{1,0:T(8,128)(2,1)S(1)}, u32[]{:S(2)}, u32[]{:S(2)}) collective-permute-start(bf16[16,4096]{1,0:T(8,128)(2,1)} %refs_0_.1), channel_id=1, source_target_pairs={{0,2},{2,0},{1,3},{3,1},{4,6},{6,4},{5,7},{7,5},{8,10},{10,8},{9,1... | collective-permute-start | bytes 393224 | tf_op jit(solution)/shard_map/ppermute | solution.py:20
  4.4 6.5 %collective-permute-start.2 = (bf16[5,16,128]{2,1,0:T(8,128)(2,1)S(1)}, bf16[5,16,128]{2,1,0:T(8,128)(2,1)S(1)}, u32[]{:S(2)}, u32[]{:S(2)}) collective-permute-start(bf16[5,16,128]{2,1,0:T(8,128)(2,1)S(1)} %pack_charges.1.refs_0_.pack), channel_id=1, source_target_pairs={{0,12},{4,8},{8,4},{12,0},{1,13},{5,9},{9,5},{13,1},{2,14},{6,10},... | collective-permute-start | bytes 61448 | tf_op jit(solution)/shard_map/ppermute | solution.py:20
  8.0 4.7 %collective-permute-start.1 = (bf16[5,16,128]{2,1,0:T(8,128)(2,1)S(1)}, bf16[5,16,128]{2,1,0:T(8,128)(2,1)S(1)}, u32[]{:S(2)}, u32[]{:S(2)}) collective-permute-start(bf16[5,16,128]{2,1,0:T(8,128)(2,1)S(1)} %pack_charges.1.refs_0_.pack), channel_id=1, source_target_pairs={{0,8},{4,12},{8,0},{12,4},{1,9},{5,13},{9,1},{13,5},{2,10},{6,14},... | collective-permute-start | bytes 61448 | tf_op jit(solution)/shard_map/ppermute | solution.py:20
  8.0 4.7 %collective-permute-start = (bf16[5,16,128]{2,1,0:T(8,128)(2,1)S(1)}, bf16[5,16,128]{2,1,0:T(8,128)(2,1)S(1)}, u32[]{:S(2)}, u32[]{:S(2)}) collective-permute-start(bf16[5,16,128]{2,1,0:T(8,128)(2,1)S(1)} %pack_charges.1.refs_0_.pack), channel_id=1, source_target_pairs={{0,4},{4,0},{8,12},{12,8},{1,5},{5,1},{9,13},{13,9},{2,6},{6,2},{1... | collective-permute-start | bytes 61448 | tf_op jit(solution)/shard_map/ppermute | solution.py:20
  12.7 5.3 %collective-permute-start.4 = (bf16[32,16,128]{2,1,0:T(8,128)(2,1)S(1)}, bf16[32,16,128]{2,1,0:T(8,128)(2,1)S(1)}, u32[]{:S(2)}, u32[]{:S(2)}) collective-permute-start(bf16[32,16,128]{2,1,0:T(8,128)(2,1)S(1)} %get-tuple-element.43), channel_id=1, source_target_pairs={{0,2},{2,0},{1,3},{3,1},{4,6},{6,4},{5,7},{7,5},{8,10},{10,8},{9,1... | collective-permute-start | bytes 393224 | tf_op jit(solution)/shard_map/ppermute | solution.py:20
  13.6 7.0 %collective-permute-start.8 = (bf16[8,16,128]{2,1,0:T(8,128)(2,1)S(1)}, bf16[8,16,128]{2,1,0:T(8,128)(2,1)S(1)}, u32[]{:S(2)}, u32[]{:S(2)}) collective-permute-start(bf16[8,16,128]{2,1,0:T(8,128)(2,1)S(1)} %get-tuple-element.55), channel_id=1, source_target_pairs={{0,12},{4,8},{8,4},{12,0},{1,13},{5,9},{9,5},{13,1},{2,14},{6,10},... | collective-permute-start | bytes 98312 | tf_op jit(solution)/shard_map/ppermute | solution.py:20
  15.5 5.2 %collective-permute-start.9 = (bf16[8,16,128]{2,1,0:T(8,128)(2,1)S(1)}, bf16[8,16,128]{2,1,0:T(8,128)(2,1)S(1)}, u32[]{:S(2)}, u32[]{:S(2)}) collective-permute-start(bf16[8,16,128]{2,1,0:T(8,128)(2,1)S(1)} %get-tuple-element.56), channel_id=1, source_target_pairs={{0,8},{4,12},{8,0},{12,4},{1,9},{5,13},{9,1},{13,5},{2,10},{6,14},... | collective-permute-start | bytes 98312 | tf_op jit(solution)/shard_map/ppermute | solution.py:20
  15.7 4.9 %collective-permute-start.10 = (bf16[8,16,128]{2,1,0:T(8,128)(2,1)S(1)}, bf16[8,16,128]{2,1,0:T(8,128)(2,1)S(1)}, u32[]{:S(2)}, u32[]{:S(2)}) collective-permute-start(bf16[8,16,128]{2,1,0:T(8,128)(2,1)S(1)} %get-tuple-element.57), channel_id=1, source_target_pairs={{0,4},{4,0},{8,12},{12,8},{1,5},{5,1},{9,13},{13,9},{2,6},{6,2},{1... | collective-permute-start | bytes 98312 | tf_op jit(solution)/shard_map/ppermute | solution.py:20
  18.0 2.8 %copy-start = (bf16[192,128,128]{2,1,0:T(8,128)(2,1)S(1)}, bf16[192,128,128]{2,1,0:T(8,128)(2,1)}, u32[]{:S(2)}) copy-start(bf16[192,128,128]{2,1,0:T(8,128)(2,1)} %refs_4_.3) | copy-start | bytes 18874372
  19.0 5.3 %collective-permute-start.5 = (bf16[16,16,128]{2,1,0:T(8,128)(2,1)S(1)}, bf16[16,16,128]{2,1,0:T(8,128)(2,1)S(1)}, u32[]{:S(2)}, u32[]{:S(2)}) collective-permute-start(bf16[16,16,128]{2,1,0:T(8,128)(2,1)S(1)} %get-tuple-element.47), channel_id=1, source_target_pairs={{0,2},{2,0},{1,3},{3,1},{4,6},{6,4},{5,7},{7,5},{8,10},{10,8},{9,1... | collective-permute-start | bytes 196616 | tf_op jit(solution)/shard_map/ppermute | solution.py:20
  22.6 5.2 %collective-permute-start.11 = (bf16[32,16,128]{2,1,0:T(8,128)(2,1)S(1)}, bf16[32,16,128]{2,1,0:T(8,128)(2,1)S(1)}, u32[]{:S(2)}, u32[]{:S(2)}) collective-permute-start(bf16[32,16,128]{2,1,0:T(8,128)(2,1)S(1)} %get-tuple-element.62), channel_id=1, source_target_pairs={{0,2},{2,0},{1,3},{3,1},{4,6},{6,4},{5,7},{7,5},{8,10},{10,8},{9,1... | collective-permute-start | bytes 393224 | tf_op jit(solution)/shard_map/ppermute | solution.py:20
  24.2 7.6 %collective-permute-start.6 = (bf16[12,16,128]{2,1,0:T(8,128)(2,1)S(1)}, bf16[12,16,128]{2,1,0:T(8,128)(2,1)S(1)}, u32[]{:S(2)}, u32[]{:S(2)}) collective-permute-start(bf16[12,16,128]{2,1,0:T(8,128)(2,1)S(1)} %get-tuple-element.48), channel_id=1, source_target_pairs={{0,8},{4,12},{8,0},{12,4},{1,9},{5,13},{9,1},{13,5},{2,10},{6,14},... | collective-permute-start | bytes 147464 | tf_op jit(solution)/shard_map/ppermute | solution.py:20
  25.8 5.9 %collective-permute-start.7 = (bf16[12,16,128]{2,1,0:T(8,128)(2,1)S(1)}, bf16[12,16,128]{2,1,0:T(8,128)(2,1)S(1)}, u32[]{:S(2)}, u32[]{:S(2)}) collective-permute-start(bf16[12,16,128]{2,1,0:T(8,128)(2,1)S(1)} %get-tuple-element.49), channel_id=1, source_target_pairs={{0,12},{4,8},{8,4},{12,0},{1,13},{5,9},{9,5},{13,1},{2,14},{6,10},... | collective-permute-start | bytes 147464 | tf_op jit(solution)/shard_map/ppermute | solution.py:20
  27.8 4.4 %collective-permute-start.12 = (bf16[12,16,128]{2,1,0:T(8,128)(2,1)S(1)}, bf16[12,16,128]{2,1,0:T(8,128)(2,1)S(1)}, u32[]{:S(2)}, u32[]{:S(2)}) collective-permute-start(bf16[12,16,128]{2,1,0:T(8,128)(2,1)S(1)} %get-tuple-element.65), channel_id=1, source_target_pairs={{0,4},{4,0},{8,12},{12,8},{1,5},{5,1},{9,13},{13,9},{2,6},{6,2},{1... | collective-permute-start | bytes 147464 | tf_op jit(solution)/shard_map/ppermute | solution.py:20

commit v9 on v8

--- a/solution.py
+++ b/solution.py
@@ -52,6 +52,18 @@
     wide[...] = jnp.zeros_like(wide)
     wide[: needs.shape[0], : needs.shape[1]] = needs[...]
     message[pan_own] = wide[...].astype(F32).astype(BF16)
+
+
+def join_body(pan_own, own, *refs):
+    others, message = refs[:-1], refs[-1]
+    c = lax.axis_index("col")
+    width = own.shape[2]
+    message[pl.ds(c * pan_own, pan_own)] = own[pl.ds(0, pan_own)]
+    for j, x in enumerate(others):
+        first = lax.bitwise_xor(c, j + 1) * pan_own
+        for q in range(pan_own):
+            message[first + q] = x[:, q * width : (q + 1) * width]
+    message[message.shape[0] - 1] = own[pan_own]
 
 
 def ends_body(n_row, n_col, pan_own, cap, n_moved, *refs):
@@ -108,26 +120,15 @@
         copy.wait()
 
 
-def relay_body(n_row, n_col, pan_own, *refs):
-    packs = refs[:n_row]
-    ends = refs[n_row : n_row + n_col - 1]
-    asked, *messages = refs[n_row + 2 * n_col - 2 :]
-    r = lax.axis_index("row")
-    rhs, width = packs[0].shape[1:]
+def pick_body(n_row, n_col, cap, _after, *refs):
+    packs, own, peers = refs[:n_row][::-1], refs[n_row], refs[n_row + 1 : n_row + n_col]
+    outs, asked = refs[n_row + n_col : -1], refs[-1]
+    seg_own, rhs, width = own.shape
+    r, c = lax.axis_index("row"), lax.axis_index("col")
     mine = lax.broadcasted_iota(jnp.int32, (rhs, width), 0) == r
     for k in range(n_row):
-        needs = packs[k][pan_own].astype(F32)
+        needs = packs[k][packs[k].shape[0] - 1].astype(F32)
         asked[k : k + 1, :] = jnp.sum(jnp.where(mine, needs, 0.0), axis=0, keepdims=True).astype(jnp.int32)
-        for message in messages:
-            message[pl.ds(k * pan_own, pan_own)] = packs[k][pl.ds(0, pan_own)]
-    for message, sums in zip(messages, ends):
-        message[pl.ds(n_row * pan_own, n_row * pan_own)] = sums[...]
-
-
-def pick_body(n_row, n_col, cap, asked, own, *refs):
-    peers, outs = refs[: n_col - 1], refs[n_col - 1 :]
-    seg_own, _, width = own.shape
-    c = lax.axis_index("col")
     for k in range(n_row):
         for s in range(cap):
             b = asked[k, s]
@@ -162,30 +163,30 @@
 
 
 def coeff_body(n_row, n_col, pan_own, slots, rows, needs, *refs):
-    packs = refs[:n_row]
-    from_col = refs[n_row : n_row + n_col - 1]
-    tiles, part, message, src, named = refs[n_row + n_col - 1 :]
-    r, c = lax.axis_index("row"), lax.axis_index("col")
+    packs = refs[:n_row][::-1]
+    ends = refs[n_row : n_row + n_col - 1]
+    tiles, part, *messages = refs[n_row + n_col - 1 : -2]
+    src, named = refs[-2:]
+    r = lax.axis_index("row")
     pan_group = pan_own * n_col
     cap = needs.shape[1]
     for k in range(n_row):
-        first = lax.bitwise_xor(r, k) * pan_group
-        src[pl.ds(first + c * pan_own, pan_own)] = packs[k][pl.ds(0, pan_own)]
-        for j, x in enumerate(from_col):
-            there = first + lax.bitwise_xor(c, j + 1) * pan_own
-            src[pl.ds(there, pan_own)] = x[pl.ds(k * pan_own, pan_own)]
+        src[pl.ds(lax.bitwise_xor(r, k) * pan_group, pan_group)] = packs[k][pl.ds(0, pan_group)]
     for p in range(n_row):
         for s in range(cap):
             named[p * cap + s] = p * pan_group + needs[p, s]
     part[...] = jnp.zeros_like(part)
     multiply(tiles, src, lambda t: named[slots[t]], rows, part)
     high = part[...].astype(BF16)
-    message[pl.ds(0, pan_group)] = high
-    message[pl.ds(pan_group, pan_group)] = (part[...] - high.astype(F32)).astype(BF16)
-
-
-def induct_body(n_row, n_col, seg_own, slots, rows, _after, *refs):
-    got = refs[:n_row][::-1]
+    low = (part[...] - high.astype(F32)).astype(BF16)
+    for message, sums in zip(messages, ends):
+        message[pl.ds(0, pan_group)] = high
+        message[pl.ds(pan_group, pan_group)] = low
+        message[pl.ds(2 * pan_group, sums.shape[0])] = sums[...]
+
+
+def induct_body(n_row, n_col, seg_own, order, slots, rows, _after, *refs):
+    got = {k: refs[i] for i, k in enumerate(order)}
     tiles = refs[n_row]
     own, *sends = refs[n_row + 1 : -2]
     src, acc = refs[-2:]
@@ -202,8 +203,7 @@
 
 def panels_body(n_row, n_col, pan_own, part, ends_own, *refs):
     parts = refs[: n_col - 1]
-    relayed = refs[n_col - 1 : 2 * n_col - 2]
-    pot, end_keep, *messages = refs[2 * n_col - 2 :]
+    pot, end_keep, *messages = refs[n_col - 1 :]
     pan_group = part.shape[0]
     total = part[...]
     for x in parts:
@@ -212,13 +212,17 @@
     pot[...] = rounded
     for k in range(n_row):
         sums = ends_own[pl.ds(k * pan_own, pan_own)]
-        for x in relayed:
-            sums += x[pl.ds((n_row + k) * pan_own, pan_own)].astype(F32)
+        for x in parts:
+            sums += x[pl.ds(2 * pan_group + k * pan_own, pan_own)].astype(F32)
         if k == 0:
             end_keep[...] = sums
         else:
             messages[n_row - 1 - k][pl.ds(0, pan_own)] = sums.astype(BF16)
             messages[n_row - 1 - k][pl.ds(pan_own, pan_group)] = rounded
+
+
+def hold_body(_after, message, out):
+    out[...] = message[...]
 
 
 def add_drops(p, pots, first, links, holder, lanes, field):
@@ -236,20 +240,16 @@
         field[k] += drop
 
 
-def base_body(n_col, pan_own, links, holder, scale, lanes, pack, field_own, end_own, pot, *refs):
-    field_in, (field, panels, pot_out) = refs[: n_col - 1], refs[n_col - 1 :]
+def base_body(pan_own, links, holder, scale, lanes, pack, field_own, end_own, pot, field, panels, pot_out):
     rhs, width = pot.shape[1:]
     r, c = lax.axis_index("row"), lax.axis_index("col")
-    total = field_own[...]
-    for x in field_in:
-        total += x[...].astype(F32)
-    field[...] = total
+    field[...] = field_own[...]
     row = lax.broadcasted_iota(jnp.int32, (rhs, width), 0)
     factor = jnp.zeros((rhs, width), F32)
     for i in range(rhs):
         factor = jnp.where(row == i, scale[i], factor)
     for q in range(pan_own):
-        panels[q] = factor * pack[q].astype(F32) + end_own[q]
+        panels[q] = factor * pack[c * pan_own + q].astype(F32) + end_own[q]
         pot_out[:, q * width : (q + 1) * width] = pot[c * pan_own + q]
     add_drops(r, pot, 0, links, holder, lanes, field)
 
@@ -260,10 +260,14 @@
     add_drops(p, message, pan_own, links, holder, lanes, field)
 
 
-def final_body(n_row, pan_own, links, holder, lanes, field_in, panels, *refs):
-    arrived, (seg_out, pan_out, field, seg, pan, sems) = refs[: n_row - 1], refs[n_row - 1 :]
+def final_body(n_row, n_col, pan_own, links, holder, lanes, field_own, panels, *refs):
+    arrived, field_in = refs[: n_row - 1], refs[n_row - 1 : n_row + n_col - 2]
+    seg_out, pan_out, field, seg, pan, sems = refs[n_row + n_col - 2 :]
     seg_own, _, width = field.shape
-    field[...] = field_in[...]
+    total = field_own[...]
+    for x in field_in:
+        total += x[...].astype(F32)
+    field[...] = total
     p = lax.bitwise_xor(lax.axis_index("row"), 1)
     add_drops(p, arrived[0], pan_own, links, holder, lanes, field)
     for q in range(pan_own):
@@ -314,6 +318,7 @@
     def like(blocks, dtype):
         return jax.ShapeDtypeStruct((blocks, rhs, width), dtype)
 
+    charges = exchange_all(charge, [charge] * (n_col - 1), "col")
     cur = exchange_all(current, [current] * (n_col - 1), "col")
     (pack,) = call(
         functools.partial(pack_body, pan_own),
@@ -323,6 +328,13 @@
         [pltpu.VMEM((rhs, width), jnp.int32)],
         moved=2**16,
     )(*in_hbm(charge, induct_needs))
+    (pack,) = call(
+        functools.partial(join_body, pan_own),
+        "join_charges",
+        [like(pan_group + 1, BF16)],
+        [VMEM] * n_col,
+        moved=2**16,
+    )(pack, *charges[1:])
     packs = exchange_all(pack, [pack] * (n_row - 1), "row")
 
     rows_own = n_row * pan_own
@@ -350,40 +362,42 @@
     _, links_s, coeff_slots, coeff_rows, coeff_needs, induct_slots, induct_rows, scale, coeff_tiles = outs[: len(moved)]
     holder, lanes, own_blocks, ends_own, *ends_out = outs[len(moved) :]
 
-    asked, *relays = call(
-        functools.partial(relay_body, n_row, n_col, pan_own),
-        "relay_charges",
-        [jax.ShapeDtypeStruct((n_row, width), jnp.int32)] + [like(2 * rows_own, BF16)] * (n_col - 1),
-        [VMEM] * (n_row + n_col - 1) + [ANY] * (n_col - 1),
-        moved=2**16,
-    )(*packs, *ends_out, *cur[1:])
-    relayed = exchange_all(None, relays, "col")[1:]
-
-    *picks, own_picks = call(
-        functools.partial(pick_body, n_row, n_col, cap_l),
-        "pick_blocks",
-        [like(cap_l, BF16)] * n_row,
-        [VMEM] * (1 + n_col),
-        moved=2**18,
-    )(asked, own_blocks, *cur[1:])
-    got = exchange_all(own_picks, picks[::-1], "row")
-
-    part, message = call(
+    part, *messages = call(
         functools.partial(coeff_body, n_row, n_col, pan_own),
         "coeff_tiles",
-        [like(pan_group, F32), like(2 * pan_group, BF16)],
+        [like(pan_group, F32)] + [like(2 * pan_group + rows_own, BF16)] * (n_col - 1),
         [SMEM] * 3 + [VMEM] * (n_row + n_col),
         [
             pltpu.VMEM((n_row * pan_group, rhs, width), BF16),
             pltpu.SMEM((n_row * cap_p,), jnp.int32),
         ],
-        flops=2 * 10**9,
+        flops=10**9,
         moved=coeff_tiles.size * 2,
-    )(coeff_slots, coeff_rows, coeff_needs, *packs, *relayed, coeff_tiles)
-    parts = exchange_all(None, [message] * (n_col - 1), "col")[1:]
-
+    )(coeff_slots, coeff_rows, coeff_needs, *packs[::-1], *ends_out, coeff_tiles)
+    parts = exchange_all(None, messages, "col")[1:]
+
+    *picks, own_picks = call(
+        functools.partial(pick_body, n_row, n_col, cap_l),
+        "pick_blocks",
+        [like(cap_l, BF16)] * n_row,
+        [ANY] + [VMEM] * (n_row + n_col),
+        [pltpu.VMEM((n_row, width), jnp.int32)],
+        moved=2**18,
+    )(part, *packs[::-1], own_blocks, *cur[1:])
+    got = exchange_all(own_picks, picks[::-1], "row")
+
+    pot, end_keep, *row_messages = call(
+        functools.partial(panels_body, n_row, n_col, pan_own),
+        "panel_sums",
+        [like(pan_group, BF16), like(pan_own, F32)] + [like(pan_own + pan_group, BF16)] * (n_row - 1),
+        [VMEM] * (1 + n_col),
+        flops=10**9,
+        moved=2**18,
+    )(part, ends_own, *parts)
+
+    order = [*range(n_row - 2, -1, -1), n_row - 1]
     field_own, *field_out = call(
-        functools.partial(induct_body, n_row, n_col, seg_own),
+        functools.partial(induct_body, n_row, n_col, seg_own, order),
         "induct_tiles",
         [like(seg_own, F32)] + [like(seg_own, BF16)] * (n_col - 1),
         [SMEM, SMEM, ANY] + [VMEM] * (n_row + 1),
@@ -391,29 +405,28 @@
             pltpu.VMEM((n_row * cap_l, rhs, width), BF16),
             pltpu.VMEM((seg_group, rhs, width), F32),
         ],
-        flops=4 * 10**9,
-        moved=induct_tiles.size * 2,
-    )(induct_slots, induct_rows, part, *got[::-1], induct_tiles)
+        flops=10**8,
+        moved=2**16,
+    )(induct_slots, induct_rows, pot, *[got[k] for k in order], induct_tiles)
     field_in = exchange_all(None, field_out, "col")[1:]
 
-    pot, end_keep, *row_messages = call(
-        functools.partial(panels_body, n_row, n_col, pan_own),
-        "panel_sums",
-        [like(pan_group, BF16), like(pan_own, F32)] + [like(pan_own + pan_group, BF16)] * (n_row - 1),
-        [VMEM] * (2 * n_col),
-        flops=5 * 10**9,
-        moved=2**18,
-    )(part, ends_own, *parts, *relayed)
+    (row_messages[-1],) = call(
+        hold_body,
+        "hold_near",
+        [like(pan_own + pan_group, BF16)],
+        [ANY, VMEM],
+        moved=2**16,
+    )(field_own, row_messages[-1])
     arrived = exchange_all(None, row_messages[::-1], "row")[1:]
 
     field, panels, pot_out = call(
-        functools.partial(base_body, n_col, pan_own),
+        functools.partial(base_body, pan_own),
         "base_sums",
         [like(seg_own, F32), like(pan_own, F32), jax.ShapeDtypeStruct(charge.shape, BF16)],
-        [SMEM] * 3 + [VMEM] * (4 + n_col),
-        flops=10**9,
-        moved=2**20,
-    )(links_s, holder, scale, lanes, pack, field_own, end_keep, pot, *field_in)
+        [SMEM] * 3 + [VMEM] * 5,
+        flops=0,
+        moved=0,
+    )(links_s, holder, scale, lanes, pack, field_own, end_keep, pot)
 
     for k in reversed(range(2, n_row)):
         (field,) = call(
@@ -421,15 +434,15 @@
             "add_drops",
             [like(seg_own, F32)],
             [SMEM] * 2 + [VMEM] * 3,
-            flops=10**8,
-            moved=2**20,
+            flops=11 * 10**8 if k == 2 else 0,
+            moved=0,
         )(links_s, holder, lanes, arrived[k - 1], field)
 
     seg_out, pan_out = call(
-        functools.partial(final_body, n_row, pan_own),
+        functools.partial(final_body, n_row, n_col, pan_own),
         "outputs",
         [jax.ShapeDtypeStruct(x.shape, BF16) for x in (current, charge)],
-        [SMEM] * 2 + [VMEM] * (2 + n_row),
+        [SMEM] * 2 + [VMEM] * (1 + n_row + n_col),
         [
             pltpu.VMEM((seg_own, rhs, width), F32),
             pltpu.VMEM(current.shape, BF16),
@@ -439,7 +452,7 @@
         flops=10**9,
         moved=2**20,
         out_specs=[ANY, ANY],
-    )(links_s, holder, lanes, field, panels, *arrived)
+    )(links_s, holder, lanes, field, panels, *arrived, *field_in)
     return (seg_out, pan_out, pot_out)
 
 

time: 33.3 us -> 33.3 us (level)
  waiting for transfers between devices: 5.32 us -> 6.95 us
  starting transfers between devices: 19.1 us -> 17.5 us
    ppermute x13, waiting for transfers between devices: 5.32 us -> 6.95 us  [exchange(): lax.ppermute(x, axis, [(i, i ^ k) for i in range(lax.axis_size(axis))])]
    ppermute x13, starting transfers between devices: 19.1 us -> 17.5 us  [exchange(): lax.ppermute(x, axis, [(i, i ^ k) for i in range(lax.axis_size(axis))])]
    pallas_call x4 -> x5, Pallas kernels: 3.42 us -> 3.42 us  [the longest x1 1.85 us: shards(): call(functools.partial(induct_body, n_row, n_col, seg_own, order), 'induc...]
  transfers between devices with their start and end apart: 13 -> 13, of which waited for: 4 -> 5; matrix products, arithmetic and copies ran while one was open for 0% -> 0% of each run, Pallas kernels for 21% -> 21%
where the time goes in v9:
time: 33.3 us; the launch traced here: 33.1 us
  starting transfers between devices  17.5 us (53%)
  Pallas kernels  7.92 us (24%)
  waiting for transfers between devices  6.95 us (21%)
  between operations  0.71 us (2%)
    ppermute x13, starting transfers between devices, exchange(): lax.ppermute(x, axis, [(i, i ^ k) for i in range(lax.axis_size(axis))])  17.5 us
    ppermute x13, waiting for transfers between devices, exchange(): lax.ppermute(x, axis, [(i, i ^ k) for i in range(lax.axis_size(axis))])  6.95 us
    pallas_call x1, Pallas kernels, shards(): call(functools.partial(ends_body, n_row, n_col, pan_own, cap_k, len(moved...  2.09 us
    pallas_call x1, Pallas kernels, shards(): call(functools.partial(induct_body, n_row, n_col, seg_own, order), 'induc...  1.85 us
    pallas_call x1, Pallas kernels, shards(): call(functools.partial(coeff_body, n_row, n_col, pan_own), 'coeff_tiles',...  0.93 us
    pallas_call x1, Pallas kernels, shards(): call(functools.partial(pack_body, pan_own), 'pack_charges', [like(pan_own...  0.88 us
    pallas_call x1, Pallas kernels, shards(): call(functools.partial(final_body, n_row, n_col, pan_own), 'outputs', [ja...  0.83 us
    pallas_call x1, Pallas kernels, shards(): call(functools.partial(base_body, pan_own), 'base_sums', [like(seg_own, F...  0.72 us
  transfers between devices with their start and end apart: 13, of which 5 were waited for; matrix products, arithmetic and copies ran while one was open for 0% of the time, Pallas kernels for 21%

profile of v9, /device:TPU:0, one launch (start us, length us, event | category | flops | bytes accessed | tf_op | source)
XLA Modules:
  0.0 33.1 jit_solution(2879202361496146815)
XLA Ops:
  0.6 3.0 %collective-permute-start = (bf16[16,512]{1,0:T(8,128)(2,1)}, bf16[16,512]{1,0:T(8,128)(2,1)S(1)}, u32[]{:S(2)}, u32[]{:S(2)}) collective-permute-start(bf16[16,512]{1,0:T(8,128)(2,1)} %charge.1), channel_id=1, source_target_pairs={{0,2},{2,0},{1,3},{3,1},{4,6},{6,4},{5,7},{7,5},{8,10},{10,8},{9,1... | collective-permute-start | bytes 49160 | tf_op jit(solution)/shard_map/ppermute | solution.py:20
  3.6 0.1 collective-permute-start.7
  3.7 0.9 %pack_charges.1.own = bf16[5,16,128]{2,1,0:T(8,128)(2,1)S(1)} custom-call(bf16[16,512]{1,0:T(8,128)(2,1)} %charge.1, s32[4,8]{1,0:T(4,128)} %needs.1), custom_call_target="tpu_custom_call" | custom-call | bytes 65536 | tf_op jit(solution)/shard_map/pack_charges/pallas_call | solution.py:323
  4.6 1.0 %collective-permute-done.refs_0_ = bf16[16,512]{1,0:T(8,128)(2,1)S(1)} collective-permute-done((bf16[16,512]{1,0:T(8,128)(2,1)}, bf16[16,512]{1,0:T(8,128)(2,1)S(1)}, u32[]{:S(2)}, u32[]{:S(2)}) %collective-permute-start) | collective-permute-done | bytes 16416 | tf_op jit(solution)/shard_map/ppermute | solution.py:20
  5.6 4.3 %collective-permute-start.1 = (bf16[9,16,128]{2,1,0:T(8,128)(2,1)S(1)}, bf16[9,16,128]{2,1,0:T(8,128)(2,1)S(1)}, u32[]{:S(2)}, u32[]{:S(2)}) collective-permute-start(bf16[9,16,128]{2,1,0:T(8,128)(2,1)S(1)} %join_charges.1.refs_3_.pack), channel_id=1, source_target_pairs={{0,12},{4,8},{8,4},{12,0},{1,13},{5,9},{9,5},{13,1},{2,14},{6,10},... | collective-permute-start | bytes 110600 | tf_op jit(solution)/shard_map/ppermute | solution.py:20
  9.9 0.6 %collective-permute-start.3 = (bf16[9,16,128]{2,1,0:T(8,128)(2,1)S(1)}, bf16[9,16,128]{2,1,0:T(8,128)(2,1)S(1)}, u32[]{:S(2)}, u32[]{:S(2)}) collective-permute-start(bf16[9,16,128]{2,1,0:T(8,128)(2,1)S(1)} %join_charges.1.refs_3_.pack), channel_id=1, source_target_pairs={{0,4},{4,0},{8,12},{12,8},{1,5},{5,1},{9,13},{13,9},{2,6},{6,2},{1... | collective-permute-start | bytes 110600 | tf_op jit(solution)/shard_map/ppermute | solution.py:20
  10.5 2.1 %end_sums.1 = (s32[2,32]{1,0:T(2,128)S(4)}, s32[4,16]{1,0:T(4,128)S(4)}, s32[96]{0:T(128)S(4)}, s32[96]{0:T(128)S(4)}, s32[4,4]{1,0:T(4,128)S(4)}, /*index=5*/s3...) custom-call(bf16[16,4096]{1,0:T(8,128)(2,1)} %refs_0_.1, ...), custom_call_target="tpu_custom_call" | custom-call | flops 500000000 | bytes 262144 | tf_op jit(solution)/shard_map/end_sums/pallas_call | solution.py:343
  12.6 0.0 collective-permute-done.1.refs_0_
  12.6 2.1 %collective-permute-done.2.refs_1_ = bf16[9,16,128]{2,1,0:T(8,128)(2,1)S(1)} collective-permute-done((bf16[9,16,128]{2,1,0:T(8,128)(2,1)S(1)}, bf16[9,16,128]{2,1,0:T(8,128)(2,1)S(1)}, u32[]{:S(2)}, u32[]{:S(2)}) %collective-permute-start.2) | collective-permute-done | bytes 36896 | tf_op jit(solution)/shard_map/ppermute | solution.py:20
  14.7 0.0 collective-permute-done.3.refs_2_
  14.7 0.9 %coeff_tiles.1 = (f32[8,16,128]{2,1,0:T(8,128)S(1)}, bf16[32,16,128]{2,1,0:T(8,128)(2,1)S(1)}) custom-call(s32[96]{0:T(128)S(4)} %get-tuple-element.37.slots, s32[96]{0:T(128)S(4)} %get-tuple-element.38.rows, s32[4,4]{1,0:T(4,128)S(4)} %get-tuple-element.39.needs, bf16[9,16,128]{2,1,0:T(8,128)(2,1)S(1)} %collective-permute-done.1.refs_0_, ...), custom_call_target="tpu_custom_call" | custom-call | flops 1000000000 | bytes 3145728 | tf_op jit(solution)/shard_map/coeff_tiles/pallas_call | solution.py:365
  15.7 1.6 %collective-permute-start.4 = (bf16[32,16,128]{2,1,0:T(8,128)(2,1)S(1)}, bf16[32,16,128]{2,1,0:T(8,128)(2,1)S(1)}, u32[]{:S(2)}, u32[]{:S(2)}) collective-permute-start(bf16[32,16,128]{2,1,0:T(8,128)(2,1)S(1)} %get-tuple-element.44), channel_id=1, source_target_pairs={{0,2},{2,0},{1,3},{3,1},{4,6},{6,4},{5,7},{7,5},{8,10},{10,8},{9,1... | collective-permute-start | bytes 393224 | tf_op jit(solution)/shard_map/ppermute | solution.py:20
  17.3 0.0 collective-permute-done.7.refs_5_
  17.3 0.3 pick_blocks.1
  17.6 1.7 %collective-permute-start.10 = (bf16[8,16,128]{2,1,0:T(8,128)(2,1)S(1)}, bf16[8,16,128]{2,1,0:T(8,128)(2,1)S(1)}, u32[]{:S(2)}, u32[]{:S(2)}) collective-permute-start(bf16[8,16,128]{2,1,0:T(8,128)(2,1)S(1)} %get-tuple-element.55), channel_id=1, source_target_pairs={{0,12},{4,8},{8,4},{12,0},{1,13},{5,9},{9,5},{13,1},{2,14},{6,10},... | collective-permute-start | bytes 98312 | tf_op jit(solution)/shard_map/ppermute | solution.py:20
  19.3 0.4 %collective-permute-start.8 = (bf16[8,16,128]{2,1,0:T(8,128)(2,1)S(1)}, bf16[8,16,128]{2,1,0:T(8,128)(2,1)S(1)}, u32[]{:S(2)}, u32[]{:S(2)}) collective-permute-start(bf16[8,16,128]{2,1,0:T(8,128)(2,1)S(1)} %get-tuple-element.52), channel_id=1, source_target_pairs={{0,8},{4,12},{8,0},{12,4},{1,9},{5,13},{9,1},{13,5},{2,10},{6,14},... | collective-permute-start | bytes 98312 | tf_op jit(solution)/shard_map/ppermute | solution.py:20
  19.7 2.3 %collective-permute-start.9 = (bf16[8,16,128]{2,1,0:T(8,128)(2,1)S(1)}, bf16[8,16,128]{2,1,0:T(8,128)(2,1)S(1)}, u32[]{:S(2)}, u32[]{:S(2)}) collective-permute-start(bf16[8,16,128]{2,1,0:T(8,128)(2,1)S(1)} %get-tuple-element.53), channel_id=1, source_target_pairs={{0,4},{4,0},{8,12},{12,8},{1,5},{5,1},{9,13},{13,9},{2,6},{6,2},{1... | collective-permute-start | bytes 98312 | tf_op jit(solution)/shard_map/ppermute | solution.py:20
  22.1 1.7 %collective-permute-start.6 = (bf16[12,16,128]{2,1,0:T(8,128)(2,1)S(1)}, bf16[12,16,128]{2,1,0:T(8,128)(2,1)S(1)}, u32[]{:S(2)}, u32[]{:S(2)}) collective-permute-start(bf16[12,16,128]{2,1,0:T(8,128)(2,1)S(1)} %get-tuple-element.46), channel_id=1, source_target_pairs={{0,12},{4,8},{8,4},{12,0},{1,13},{5,9},{9,5},{13,1},{2,14},{6,10},... | collective-permute-start | bytes 147464 | tf_op jit(solution)/shard_map/ppermute | solution.py:20
  23.8 0.0 collective-permute-start.5
  23.8 0.0 collective-permute-done.10.refs_3_
  23.8 1.6 %collective-permute-done.8.refs_0_ = bf16[8,16,128]{2,1,0:T(8,128)(2,1)S(1)} collective-permute-done((bf16[8,16,128]{2,1,0:T(8,128)(2,1)S(1)}, bf16[8,16,128]{2,1,0:T(8,128)(2,1)S(1)}, u32[]{:S(2)}, u32[]{:S(2)}) %collective-permute-start.8) | collective-permute-done | bytes 32800 | tf_op jit(solution)/shard_map/ppermute | solution.py:20
  25.4 0.0 collective-permute-done.9.refs_1_
  25.4 1.9 %induct_tiles.1 = (f32[32,16,128]{2,1,0:T(8,128)S(1)}, bf16[32,16,128]{2,1,0:T(8,128)(2,1)S(1)}) custom-call(s32[192]{0:T(256)S(4)} %get-tuple-element.48.slots, s32[192]{0:T(256)S(4)} %get-tuple-element.49.rows, bf16[8,16,128]{2,1,0:T(8,128)(2,1)S(1)} %get-tuple-element.50._after.pot, bf16[8,16,128]{2,1,0:T(8,128)(2,1)S(1)} %collective-permute-done.8.refs_0_, ...), custom_call_target="tpu_custom_call" | custom-call | flops 100000000 | bytes 65536 | tf_op jit(solution)/shard_map/induct_tiles/pallas_call | solution.py:399
  27.3 0.4 %collective-permute-start.12 = (bf16[32,16,128]{2,1,0:T(8,128)(2,1)S(1)}, bf16[32,16,128]{2,1,0:T(8,128)(2,1)S(1)}, u32[]{:S(2)}, u32[]{:S(2)}) collective-permute-start(bf16[32,16,128]{2,1,0:T(8,128)(2,1)S(1)} %get-tuple-element.61), channel_id=1, source_target_pairs={{0,2},{2,0},{1,3},{3,1},{4,6},{6,4},{5,7},{7,5},{8,10},{10,8},{9,1... | collective-permute-start | bytes 393224 | tf_op jit(solution)/shard_map/ppermute | solution.py:20
  27.6 1.3 %collective-permute-start.11 = (bf16[12,16,128]{2,1,0:T(8,128)(2,1)S(1)}, bf16[12,16,128]{2,1,0:T(8,128)(2,1)S(1)}, u32[]{:S(2)}, u32[]{:S(2)}) collective-permute-start(bf16[12,16,128]{2,1,0:T(8,128)(2,1)S(1)} %hold_near.1), channel_id=1, source_target_pairs={{0,4},{4,0},{8,12},{12,8},{1,5},{5,1},{9,13},{13,9},{2,6},{6,2},{1... | collective-permute-start | bytes 147464 | tf_op jit(solution)/shard_map/ppermute | solution.py:20
  29.0 0.7 %base_sums.1 = (f32[32,16,128]{2,1,0:T(8,128)S(1)}, f32[4,16,128]{2,1,0:T(8,128)S(1)}, bf16[16,512]{1,0:T(8,128)(2,1)}) custom-call(s32[4,16]{1,0:T(4,128)S(4)} %get-tuple-element.34.links, s32[64]{0:T(128)S(4)} %get-tuple-element.35.holder, f32[16]{0:T(128)S(4)} %get-tuple-element.47.scale, s32[64,128]{1,0:T(8,128)S(1)} %get-tuple-element.36.lanes, ...), custom_call_target="tpu_custom_call" | custom-call | tf_op jit(solution)/shard_map/base_sums/pallas_call | solution.py:422
  29.7 0.0 collective-permute-done.6.message.refs_2_
  29.7 0.1 add_drops.2.field_in
  29.8 0.2 add_drops.3.field_own
  30.0 1.7 %collective-permute-done.11.refs_0_ = bf16[12,16,128]{2,1,0:T(8,128)(2,1)S(1)} collective-permute-done((bf16[12,16,128]{2,1,0:T(8,128)(2,1)S(1)}, bf16[12,16,128]{2,1,0:T(8,128)(2,1)S(1)}, u32[]{:S(2)}, u32[]{:S(2)}) %collective-permute-start.11) | collective-permute-done | bytes 49184 | tf_op jit(solution)/shard_map/ppermute | solution.py:20
  31.7 0.6 %collective-permute-done.12.refs_3_ = bf16[32,16,128]{2,1,0:T(8,128)(2,1)S(1)} collective-permute-done((bf16[32,16,128]{2,1,0:T(8,128)(2,1)S(1)}, bf16[32,16,128]{2,1,0:T(8,128)(2,1)S(1)}, u32[]{:S(2)}, u32[]{:S(2)}) %collective-permute-start.12) | collective-permute-done | bytes 131104 | tf_op jit(solution)/shard_map/ppermute | solution.py:20
  32.3 0.8 %outputs.1 = (bf16[16,4096]{1,0:T(8,128)(2,1)}, bf16[16,512]{1,0:T(8,128)(2,1)}) custom-call(s32[4,16]{1,0:T(4,128)S(4)} %get-tuple-element.34.links, s32[64]{0:T(128)S(4)} %get-tuple-element.35.holder, s32[64,128]{1,0:T(8,128)S(1)} %get-tuple-element.36.lanes, f32[32,16,128]{2,1,0:T(8,128)S(1)} %add_drops.3.field_own, ...), custom_call_target="tpu_custom_call" | custom-call | flops 1000000000 | bytes 1048576 | tf_op jit(solution)/shard_map/outputs/pallas_call | solution.py:441
  (11 shorter events, 0.1 us)
Async XLA Ops:
  0.6 4.9 %collective-permute-start = (bf16[16,512]{1,0:T(8,128)(2,1)}, bf16[16,512]{1,0:T(8,128)(2,1)S(1)}, u32[]{:S(2)}, u32[]{:S(2)}) collective-permute-start(bf16[16,512]{1,0:T(8,128)(2,1)} %charge.1), channel_id=1, source_target_pairs={{0,2},{2,0},{1,3},{3,1},{4,6},{6,4},{5,7},{7,5},{8,10},{10,8},{9,1... | collective-permute-start | bytes 49160 | tf_op jit(solution)/shard_map/ppermute | solution.py:20
  3.6 13.7 %collective-permute-start.7 = (bf16[16,4096]{1,0:T(8,128)(2,1)}, bf16[16,4096]{1,0:T(8,128)(2,1)S(1)}, u32[]{:S(2)}, u32[]{:S(2)}) collective-permute-start(bf16[16,4096]{1,0:T(8,128)(2,1)} %refs_0_.1), channel_id=1, source_target_pairs={{0,2},{2,0},{1,3},{3,1},{4,6},{6,4},{5,7},{7,5},{8,10},{10,8},{9,1... | collective-permute-start | bytes 393224 | tf_op jit(solution)/shard_map/ppermute | solution.py:20
  3.7 21.7 %slice-start = ((s8[6291456]{0:T(1024)(128)(4,1)}), s8[4194304]{0:T(1024)(128)(4,1)S(1)}, s32[]{:S(2)}) async-start(s8[6291456]{0:T(1024)(128)(4,1)} %bitcast.2), calls=%async_computation | async-start | bytes 8388608
  5.6 7.0 %collective-permute-start.1 = (bf16[9,16,128]{2,1,0:T(8,128)(2,1)S(1)}, bf16[9,16,128]{2,1,0:T(8,128)(2,1)S(1)}, u32[]{:S(2)}, u32[]{:S(2)}) collective-permute-start(bf16[9,16,128]{2,1,0:T(8,128)(2,1)S(1)} %join_charges.1.refs_3_.pack), channel_id=1, source_target_pairs={{0,12},{4,8},{8,4},{12,0},{1,13},{5,9},{9,5},{13,1},{2,14},{6,10},... | collective-permute-start | bytes 110600 | tf_op jit(solution)/shard_map/ppermute | solution.py:20
  9.9 4.9 %collective-permute-start.2 = (bf16[9,16,128]{2,1,0:T(8,128)(2,1)S(1)}, bf16[9,16,128]{2,1,0:T(8,128)(2,1)S(1)}, u32[]{:S(2)}, u32[]{:S(2)}) collective-permute-start(bf16[9,16,128]{2,1,0:T(8,128)(2,1)S(1)} %join_charges.1.refs_3_.pack), channel_id=1, source_target_pairs={{0,8},{4,12},{8,0},{12,4},{1,9},{5,13},{9,1},{13,5},{2,10},{6,14},... | collective-permute-start | bytes 110600 | tf_op jit(solution)/shard_map/ppermute | solution.py:20
  9.9 4.9 %collective-permute-start.3 = (bf16[9,16,128]{2,1,0:T(8,128)(2,1)S(1)}, bf16[9,16,128]{2,1,0:T(8,128)(2,1)S(1)}, u32[]{:S(2)}, u32[]{:S(2)}) collective-permute-start(bf16[9,16,128]{2,1,0:T(8,128)(2,1)S(1)} %join_charges.1.refs_3_.pack), channel_id=1, source_target_pairs={{0,4},{4,0},{8,12},{12,8},{1,5},{5,1},{9,13},{13,9},{2,6},{6,2},{1... | collective-permute-start | bytes 110600 | tf_op jit(solution)/shard_map/ppermute | solution.py:20
  14.7 10.7 %slice-start.1 = ((s8[6291456]{0:T(1024)(128)(4,1)}), s8[2097152]{0:T(1024)(128)(4,1)S(1)}, s32[]{:S(2)}) async-start(s8[6291456]{0:T(1024)(128)(4,1)} %bitcast.2), calls=%async_computation.1 | async-start | bytes 4194304
  15.7 6.4 %collective-permute-start.4 = (bf16[32,16,128]{2,1,0:T(8,128)(2,1)S(1)}, bf16[32,16,128]{2,1,0:T(8,128)(2,1)S(1)}, u32[]{:S(2)}, u32[]{:S(2)}) collective-permute-start(bf16[32,16,128]{2,1,0:T(8,128)(2,1)S(1)} %get-tuple-element.44), channel_id=1, source_target_pairs={{0,2},{2,0},{1,3},{3,1},{4,6},{6,4},{5,7},{7,5},{8,10},{10,8},{9,1... | collective-permute-start | bytes 393224 | tf_op jit(solution)/shard_map/ppermute | solution.py:20
  17.6 6.2 %collective-permute-start.10 = (bf16[8,16,128]{2,1,0:T(8,128)(2,1)S(1)}, bf16[8,16,128]{2,1,0:T(8,128)(2,1)S(1)}, u32[]{:S(2)}, u32[]{:S(2)}) collective-permute-start(bf16[8,16,128]{2,1,0:T(8,128)(2,1)S(1)} %get-tuple-element.55), channel_id=1, source_target_pairs={{0,12},{4,8},{8,4},{12,0},{1,13},{5,9},{9,5},{13,1},{2,14},{6,10},... | collective-permute-start | bytes 98312 | tf_op jit(solution)/shard_map/ppermute | solution.py:20
  19.3 6.1 %collective-permute-start.8 = (bf16[8,16,128]{2,1,0:T(8,128)(2,1)S(1)}, bf16[8,16,128]{2,1,0:T(8,128)(2,1)S(1)}, u32[]{:S(2)}, u32[]{:S(2)}) collective-permute-start(bf16[8,16,128]{2,1,0:T(8,128)(2,1)S(1)} %get-tuple-element.52), channel_id=1, source_target_pairs={{0,8},{4,12},{8,0},{12,4},{1,9},{5,13},{9,1},{13,5},{2,10},{6,14},... | collective-permute-start | bytes 98312 | tf_op jit(solution)/shard_map/ppermute | solution.py:20
  19.7 5.6 %collective-permute-start.9 = (bf16[8,16,128]{2,1,0:T(8,128)(2,1)S(1)}, bf16[8,16,128]{2,1,0:T(8,128)(2,1)S(1)}, u32[]{:S(2)}, u32[]{:S(2)}) collective-permute-start(bf16[8,16,128]{2,1,0:T(8,128)(2,1)S(1)} %get-tuple-element.53), channel_id=1, source_target_pairs={{0,4},{4,0},{8,12},{12,8},{1,5},{5,1},{9,13},{13,9},{2,6},{6,2},{1... | collective-permute-start | bytes 98312 | tf_op jit(solution)/shard_map/ppermute | solution.py:20
  22.1 7.6 %collective-permute-start.6 = (bf16[12,16,128]{2,1,0:T(8,128)(2,1)S(1)}, bf16[12,16,128]{2,1,0:T(8,128)(2,1)S(1)}, u32[]{:S(2)}, u32[]{:S(2)}) collective-permute-start(bf16[12,16,128]{2,1,0:T(8,128)(2,1)S(1)} %get-tuple-element.46), channel_id=1, source_target_pairs={{0,12},{4,8},{8,4},{12,0},{1,13},{5,9},{9,5},{13,1},{2,14},{6,10},... | collective-permute-start | bytes 147464 | tf_op jit(solution)/shard_map/ppermute | solution.py:20
  23.8 6.0 %collective-permute-start.5 = (bf16[12,16,128]{2,1,0:T(8,128)(2,1)S(1)}, bf16[12,16,128]{2,1,0:T(8,128)(2,1)S(1)}, u32[]{:S(2)}, u32[]{:S(2)}) collective-permute-start(bf16[12,16,128]{2,1,0:T(8,128)(2,1)S(1)} %get-tuple-element.45), channel_id=1, source_target_pairs={{0,8},{4,12},{8,0},{12,4},{1,9},{5,13},{9,1},{13,5},{2,10},{6,14},... | collective-permute-start | bytes 147464 | tf_op jit(solution)/shard_map/ppermute | solution.py:20
  27.3 5.0 %collective-permute-start.12 = (bf16[32,16,128]{2,1,0:T(8,128)(2,1)S(1)}, bf16[32,16,128]{2,1,0:T(8,128)(2,1)S(1)}, u32[]{:S(2)}, u32[]{:S(2)}) collective-permute-start(bf16[32,16,128]{2,1,0:T(8,128)(2,1)S(1)} %get-tuple-element.61), channel_id=1, source_target_pairs={{0,2},{2,0},{1,3},{3,1},{4,6},{6,4},{5,7},{7,5},{8,10},{10,8},{9,1... | collective-permute-start | bytes 393224 | tf_op jit(solution)/shard_map/ppermute | solution.py:20
  27.6 4.1 %collective-permute-start.11 = (bf16[12,16,128]{2,1,0:T(8,128)(2,1)S(1)}, bf16[12,16,128]{2,1,0:T(8,128)(2,1)S(1)}, u32[]{:S(2)}, u32[]{:S(2)}) collective-permute-start(bf16[12,16,128]{2,1,0:T(8,128)(2,1)S(1)} %hold_near.1), channel_id=1, source_target_pairs={{0,4},{4,0},{8,12},{12,8},{1,5},{5,1},{9,13},{13,9},{2,6},{6,2},{1... | collective-permute-start | bytes 147464 | tf_op jit(solution)/shard_map/ppermute | solution.py:20

commit v10 on v8

--- a/solution.py
+++ b/solution.py
@@ -143,22 +143,33 @@
 
 def multiply(tiles, src, source, rows, acc):
     rhs, width = src.shape[1:]
-    unroll = min(32, tiles.shape[0])
-
-    def step(i, carry):
-        start = i * unroll
+    count = tiles.shape[0]
+    run = max(d for d in range(8, 97, 8) if count % d == 0)
+
+    def products(start):
         got = []
-        for u in range(0, unroll, 2):
-            t = start + u
+        for t in (start, start + 2, start + 4, start + 6):
             left = jnp.concatenate([src[source(t)], src[source(t + 1)]], axis=0)
             right = jnp.concatenate([tiles[t], tiles[t + 1]], axis=1)
             both = jnp.dot(left, right, preferred_element_type=F32)
             got += [both[:rhs, :width], both[rhs:, width:]]
+        return got
+
+    def add(start, got):
         for u, value in enumerate(got):
             acc[rows[start + u]] += value
+
+    def step(i, carry):
+        start = i * run
+        waiting = products(start)
+        for first in range(8, run, 8):
+            ahead = products(start + first)
+            add(start + first - 8, waiting)
+            waiting = ahead
+        add(start + run - 8, waiting)
         return carry
 
-    lax.fori_loop(0, tiles.shape[0] // unroll, step, 0)
+    lax.fori_loop(0, count // run, step, 0)
 
 
 def coeff_body(n_row, n_col, pan_own, slots, rows, needs, *refs):

time: 33.3 us -> 33 us (level)
  Pallas kernels: 7.75 us -> 7.02 us
  waiting for transfers between devices: 5.32 us -> 5.72 us
    pallas_call x1, Pallas kernels: 1.84 us -> 1.36 us  [shards(): call(functools.partial(induct_body, n_row, n_col, seg_own), 'induct_tiles...]
    ppermute x13, waiting for transfers between devices: 5.32 us -> 5.72 us  [exchange(): lax.ppermute(x, axis, [(i, i ^ k) for i in range(lax.axis_size(axis))])]
  transfers between devices with their start and end apart: 13 -> 13, of which waited for: 4 -> 4; matrix products, arithmetic and copies ran while one was open for 0% -> 0% of each run, Pallas kernels for 21% -> 19%
where the time goes in v10:
time: 33 us; the launch traced here: 32.7 us
  starting transfers between devices  19.1 us (58%)
  Pallas kernels  7.02 us (21%)
  waiting for transfers between devices  5.72 us (17%)
  between operations  0.71 us (2%)
    ppermute x13, starting transfers between devices, exchange(): lax.ppermute(x, axis, [(i, i ^ k) for i in range(lax.axis_size(axis))])  19.1 us
    ppermute x13, waiting for transfers between devices, exchange(): lax.ppermute(x, axis, [(i, i ^ k) for i in range(lax.axis_size(axis))])  5.72 us
    pallas_call x1, Pallas kernels, shards(): call(functools.partial(ends_body, n_row, n_col, pan_own, cap_k, len(moved...  2.09 us
    pallas_call x1, Pallas kernels, shards(): call(functools.partial(induct_body, n_row, n_col, seg_own), 'induct_tiles...  1.36 us
    pallas_call x1, Pallas kernels, shards(): call(functools.partial(final_body, n_row, pan_own), 'outputs', [jax.Shape...  0.84 us
    pallas_call x1, Pallas kernels, shards(): call(functools.partial(pack_body, pan_own), 'pack_charges', [like(pan_own...  0.73 us
    pallas_call x1, Pallas kernels, shards(): call(functools.partial(base_body, n_col, pan_own), 'base_sums', [like(seg...  0.72 us
    pallas_call x1, Pallas kernels, shards(): call(functools.partial(coeff_body, n_row, n_col, pan_own), 'coeff_tiles',...  0.69 us
  transfers between devices with their start and end apart: 13, of which 4 were waited for; matrix products, arithmetic and copies ran while one was open for 0% of the time, Pallas kernels for 19%

profile of v10, /device:TPU:0, one launch (start us, length us, event | category | flops | bytes accessed | tf_op | source)
XLA Modules:
  0.0 32.7 jit_solution(1180605918431796468)
XLA Ops:
  0.6 3.0 %collective-permute-start.3 = (bf16[16,4096]{1,0:T(8,128)(2,1)}, bf16[16,4096]{1,0:T(8,128)(2,1)S(1)}, u32[]{:S(2)}, u32[]{:S(2)}) collective-permute-start(bf16[16,4096]{1,0:T(8,128)(2,1)} %refs_0_.1), channel_id=1, source_target_pairs={{0,2},{2,0},{1,3},{3,1},{4,6},{6,4},{5,7},{7,5},{8,10},{10,8},{9,1... | collective-permute-start | bytes 393224 | tf_op jit(solution)/shard_map/ppermute | solution.py:20
  3.6 0.7 %pack_charges.1.refs_0_.pack = bf16[5,16,128]{2,1,0:T(8,128)(2,1)S(1)} custom-call(bf16[16,512]{1,0:T(8,128)(2,1)} %charge.1, s32[4,8]{1,0:T(4,128)} %needs.1), custom_call_target="tpu_custom_call" | custom-call | bytes 65536 | tf_op jit(solution)/shard_map/pack_charges/pallas_call | solution.py:329
  4.4 3.6 %collective-permute-start.2 = (bf16[5,16,128]{2,1,0:T(8,128)(2,1)S(1)}, bf16[5,16,128]{2,1,0:T(8,128)(2,1)S(1)}, u32[]{:S(2)}, u32[]{:S(2)}) collective-permute-start(bf16[5,16,128]{2,1,0:T(8,128)(2,1)S(1)} %pack_charges.1.refs_0_.pack), channel_id=1, source_target_pairs={{0,12},{4,8},{8,4},{12,0},{1,13},{5,9},{9,5},{13,1},{2,14},{6,10},... | collective-permute-start | bytes 61448 | tf_op jit(solution)/shard_map/ppermute | solution.py:20
  8.0 0.0 collective-permute-start.1
  8.0 0.8 %collective-permute-start = (bf16[5,16,128]{2,1,0:T(8,128)(2,1)S(1)}, bf16[5,16,128]{2,1,0:T(8,128)(2,1)S(1)}, u32[]{:S(2)}, u32[]{:S(2)}) collective-permute-start(bf16[5,16,128]{2,1,0:T(8,128)(2,1)S(1)} %pack_charges.1.refs_0_.pack), channel_id=1, source_target_pairs={{0,4},{4,0},{8,12},{12,8},{1,5},{5,1},{9,13},{13,9},{2,6},{6,2},{1... | collective-permute-start | bytes 61448 | tf_op jit(solution)/shard_map/ppermute | solution.py:20
  8.8 2.1 %end_sums.1 = (s32[2,32]{1,0:T(2,128)S(4)}, s32[4,16]{1,0:T(4,128)S(4)}, s32[96]{0:T(128)S(4)}, s32[96]{0:T(128)S(4)}, s32[4,4]{1,0:T(4,128)S(4)}, /*index=5*/s3...) custom-call(bf16[16,4096]{1,0:T(8,128)(2,1)} %refs_0_.1, ...), custom_call_target="tpu_custom_call" | custom-call | flops 500000000 | bytes 262144 | tf_op jit(solution)/shard_map/end_sums/pallas_call | solution.py:342
  10.9 0.0 collective-permute-done.2.refs_3_
  10.9 1.8 %collective-permute-done.1.refs_2_ = bf16[5,16,128]{2,1,0:T(8,128)(2,1)S(1)} collective-permute-done((bf16[5,16,128]{2,1,0:T(8,128)(2,1)S(1)}, bf16[5,16,128]{2,1,0:T(8,128)(2,1)S(1)}, u32[]{:S(2)}, u32[]{:S(2)}) %collective-permute-start.1) | collective-permute-done | bytes 20512 | tf_op jit(solution)/shard_map/ppermute | solution.py:20
  12.6 0.0 collective-permute-done.refs_1_
  12.7 0.6 %collective-permute-start.4 = (bf16[32,16,128]{2,1,0:T(8,128)(2,1)S(1)}, bf16[32,16,128]{2,1,0:T(8,128)(2,1)S(1)}, u32[]{:S(2)}, u32[]{:S(2)}) collective-permute-start(bf16[32,16,128]{2,1,0:T(8,128)(2,1)S(1)} %get-tuple-element.43), channel_id=1, source_target_pairs={{0,2},{2,0},{1,3},{3,1},{4,6},{6,4},{5,7},{7,5},{8,10},{10,8},{9,1... | collective-permute-start | bytes 393224 | tf_op jit(solution)/shard_map/ppermute | solution.py:20
  13.3 0.3 pick_blocks.1
  13.6 1.9 %collective-permute-start.8 = (bf16[8,16,128]{2,1,0:T(8,128)(2,1)S(1)}, bf16[8,16,128]{2,1,0:T(8,128)(2,1)S(1)}, u32[]{:S(2)}, u32[]{:S(2)}) collective-permute-start(bf16[8,16,128]{2,1,0:T(8,128)(2,1)S(1)} %get-tuple-element.55), channel_id=1, source_target_pairs={{0,12},{4,8},{8,4},{12,0},{1,13},{5,9},{9,5},{13,1},{2,14},{6,10},... | collective-permute-start | bytes 98312 | tf_op jit(solution)/shard_map/ppermute | solution.py:20
  15.5 0.3 collective-permute-start.9
  15.7 2.3 %collective-permute-start.10 = (bf16[8,16,128]{2,1,0:T(8,128)(2,1)S(1)}, bf16[8,16,128]{2,1,0:T(8,128)(2,1)S(1)}, u32[]{:S(2)}, u32[]{:S(2)}) collective-permute-start(bf16[8,16,128]{2,1,0:T(8,128)(2,1)S(1)} %get-tuple-element.57), channel_id=1, source_target_pairs={{0,4},{4,0},{8,12},{12,8},{1,5},{5,1},{9,13},{13,9},{2,6},{6,2},{1... | collective-permute-start | bytes 98312 | tf_op jit(solution)/shard_map/ppermute | solution.py:20
  18.0 0.0 collective-permute-done.4.refs_4_.refs_1_
  18.0 0.7 %coeff_tiles.1 = (f32[8,16,128]{2,1,0:T(8,128)S(1)}, bf16[16,16,128]{2,1,0:T(8,128)(2,1)S(1)}) custom-call(s32[96]{0:T(128)S(4)} %get-tuple-element.39.slots, s32[96]{0:T(128)S(4)} %get-tuple-element.40.rows, s32[4,4]{1,0:T(4,128)S(4)} %get-tuple-element.41.needs, bf16[5,16,128]{2,1,0:T(8,128)(2,1)S(1)} %pack_charges.1.refs_0_.pack, ...), custom_call_target="tpu_custom_call" | custom-call | flops 2000000000 | bytes 3145728 | tf_op jit(solution)/shard_map/coeff_tiles/pallas_call | solution.py:382
  18.7 1.6 %collective-permute-start.5 = (bf16[16,16,128]{2,1,0:T(8,128)(2,1)S(1)}, bf16[16,16,128]{2,1,0:T(8,128)(2,1)S(1)}, u32[]{:S(2)}, u32[]{:S(2)}) collective-permute-start(bf16[16,16,128]{2,1,0:T(8,128)(2,1)S(1)} %get-tuple-element.47), channel_id=1, source_target_pairs={{0,2},{2,0},{1,3},{3,1},{4,6},{6,4},{5,7},{7,5},{8,10},{10,8},{9,1... | collective-permute-start | bytes 196616 | tf_op jit(solution)/shard_map/ppermute | solution.py:20
  20.3 0.0 collective-permute-done.8.refs_0_
  20.3 0.4 %collective-permute-done.9.refs_1_ = bf16[8,16,128]{2,1,0:T(8,128)(2,1)S(1)} collective-permute-done((bf16[8,16,128]{2,1,0:T(8,128)(2,1)S(1)}, bf16[8,16,128]{2,1,0:T(8,128)(2,1)S(1)}, u32[]{:S(2)}, u32[]{:S(2)}) %collective-permute-start.9) | collective-permute-done | bytes 32800 | tf_op jit(solution)/shard_map/ppermute | solution.py:20
  20.6 0.2 copy-done
  20.8 1.4 %induct_tiles.1 = (f32[32,16,128]{2,1,0:T(8,128)S(1)}, bf16[32,16,128]{2,1,0:T(8,128)(2,1)S(1)}) custom-call(s32[192]{0:T(256)S(4)} %get-tuple-element.51.slots, s32[192]{0:T(256)S(4)} %get-tuple-element.52.rows, f32[8,16,128]{2,1,0:T(8,128)S(1)} %get-tuple-element.45.part._after, bf16[8,16,128]{2,1,0:T(8,128)(2,1)S(1)} %collective-permute-done.8.refs_0_, ...), custom_call_target="tpu_custom_call" | custom-call | flops 4000000000 | bytes 6291456 | tf_op jit(solution)/shard_map/induct_tiles/pallas_call | solution.py:396
  22.2 1.6 %collective-permute-start.11 = (bf16[32,16,128]{2,1,0:T(8,128)(2,1)S(1)}, bf16[32,16,128]{2,1,0:T(8,128)(2,1)S(1)}, u32[]{:S(2)}, u32[]{:S(2)}) collective-permute-start(bf16[32,16,128]{2,1,0:T(8,128)(2,1)S(1)} %get-tuple-element.62), channel_id=1, source_target_pairs={{0,2},{2,0},{1,3},{3,1},{4,6},{6,4},{5,7},{7,5},{8,10},{10,8},{9,1... | collective-permute-start | bytes 393224 | tf_op jit(solution)/shard_map/ppermute | solution.py:20
  23.8 1.7 %collective-permute-start.6 = (bf16[12,16,128]{2,1,0:T(8,128)(2,1)S(1)}, bf16[12,16,128]{2,1,0:T(8,128)(2,1)S(1)}, u32[]{:S(2)}, u32[]{:S(2)}) collective-permute-start(bf16[12,16,128]{2,1,0:T(8,128)(2,1)S(1)} %get-tuple-element.48), channel_id=1, source_target_pairs={{0,8},{4,12},{8,0},{12,4},{1,9},{5,13},{9,1},{13,5},{2,10},{6,14},... | collective-permute-start | bytes 147464 | tf_op jit(solution)/shard_map/ppermute | solution.py:20
  25.5 1.8 %collective-permute-start.7 = (bf16[12,16,128]{2,1,0:T(8,128)(2,1)S(1)}, bf16[12,16,128]{2,1,0:T(8,128)(2,1)S(1)}, u32[]{:S(2)}, u32[]{:S(2)}) collective-permute-start(bf16[12,16,128]{2,1,0:T(8,128)(2,1)S(1)} %get-tuple-element.49), channel_id=1, source_target_pairs={{0,12},{4,8},{8,4},{12,0},{1,13},{5,9},{9,5},{13,1},{2,14},{6,10},... | collective-permute-start | bytes 147464 | tf_op jit(solution)/shard_map/ppermute | solution.py:20
  27.3 0.0 collective-permute-start.12
  27.3 0.0 collective-permute-done.11.refs_0_
  27.3 0.7 %base_sums.1 = (f32[32,16,128]{2,1,0:T(8,128)S(1)}, f32[4,16,128]{2,1,0:T(8,128)S(1)}, bf16[16,512]{1,0:T(8,128)(2,1)}) custom-call(s32[4,16]{1,0:T(4,128)S(4)} %get-tuple-element.36.links, s32[64]{0:T(128)S(4)} %get-tuple-element.37.holder, f32[16]{0:T(128)S(4)} %get-tuple-element.50.scale, s32[64,128]{1,0:T(8,128)S(1)} %get-tuple-element.38.lanes, ...), custom_call_target="tpu_custom_call" | custom-call | flops 1000000000 | bytes 1048576 | tf_op jit(solution)/shard_map/base_sums/pallas_call | solution.py:420
  28.0 3.4 %collective-permute-done.7.message.refs_2_ = bf16[12,16,128]{2,1,0:T(8,128)(2,1)S(1)} collective-permute-done((bf16[12,16,128]{2,1,0:T(8,128)(2,1)S(1)}, bf16[12,16,128]{2,1,0:T(8,128)(2,1)S(1)}, u32[]{:S(2)}, u32[]{:S(2)}) %collective-permute-start.7) | collective-permute-done | bytes 49184 | tf_op jit(solution)/shard_map/ppermute | solution.py:20
  31.4 0.1 add_drops.2.field_in
  31.6 0.1 add_drops.3.field_in
  31.7 0.2 collective-permute-done.12.refs_0_
  31.9 0.8 %outputs.1 = (bf16[16,4096]{1,0:T(8,128)(2,1)}, bf16[16,512]{1,0:T(8,128)(2,1)}) custom-call(s32[4,16]{1,0:T(4,128)S(4)} %get-tuple-element.36.links, s32[64]{0:T(128)S(4)} %get-tuple-element.37.holder, s32[64,128]{1,0:T(8,128)S(1)} %get-tuple-element.38.lanes, f32[32,16,128]{2,1,0:T(8,128)S(1)} %add_drops.3.field_in, ...), custom_call_target="tpu_custom_call" | custom-call | flops 1000000000 | bytes 1048576 | tf_op jit(solution)/shard_map/outputs/pallas_call | solution.py:439
  (7 shorter events, 0.1 us)
Async XLA Ops:
  0.6 12.0 %collective-permute-start.3 = (bf16[16,4096]{1,0:T(8,128)(2,1)}, bf16[16,4096]{1,0:T(8,128)(2,1)S(1)}, u32[]{:S(2)}, u32[]{:S(2)}) collective-permute-start(bf16[16,4096]{1,0:T(8,128)(2,1)} %refs_0_.1), channel_id=1, source_target_pairs={{0,2},{2,0},{1,3},{3,1},{4,6},{6,4},{5,7},{7,5},{8,10},{10,8},{9,1... | collective-permute-start | bytes 393224 | tf_op jit(solution)/shard_map/ppermute | solution.py:20
  4.4 6.5 %collective-permute-start.2 = (bf16[5,16,128]{2,1,0:T(8,128)(2,1)S(1)}, bf16[5,16,128]{2,1,0:T(8,128)(2,1)S(1)}, u32[]{:S(2)}, u32[]{:S(2)}) collective-permute-start(bf16[5,16,128]{2,1,0:T(8,128)(2,1)S(1)} %pack_charges.1.refs_0_.pack), channel_id=1, source_target_pairs={{0,12},{4,8},{8,4},{12,0},{1,13},{5,9},{9,5},{13,1},{2,14},{6,10},... | collective-permute-start | bytes 61448 | tf_op jit(solution)/shard_map/ppermute | solution.py:20
  8.0 4.7 %collective-permute-start.1 = (bf16[5,16,128]{2,1,0:T(8,128)(2,1)S(1)}, bf16[5,16,128]{2,1,0:T(8,128)(2,1)S(1)}, u32[]{:S(2)}, u32[]{:S(2)}) collective-permute-start(bf16[5,16,128]{2,1,0:T(8,128)(2,1)S(1)} %pack_charges.1.refs_0_.pack), channel_id=1, source_target_pairs={{0,8},{4,12},{8,0},{12,4},{1,9},{5,13},{9,1},{13,5},{2,10},{6,14},... | collective-permute-start | bytes 61448 | tf_op jit(solution)/shard_map/ppermute | solution.py:20
  8.0 4.7 %collective-permute-start = (bf16[5,16,128]{2,1,0:T(8,128)(2,1)S(1)}, bf16[5,16,128]{2,1,0:T(8,128)(2,1)S(1)}, u32[]{:S(2)}, u32[]{:S(2)}) collective-permute-start(bf16[5,16,128]{2,1,0:T(8,128)(2,1)S(1)} %pack_charges.1.refs_0_.pack), channel_id=1, source_target_pairs={{0,4},{4,0},{8,12},{12,8},{1,5},{5,1},{9,13},{13,9},{2,6},{6,2},{1... | collective-permute-start | bytes 61448 | tf_op jit(solution)/shard_map/ppermute | solution.py:20
  12.7 5.3 %collective-permute-start.4 = (bf16[32,16,128]{2,1,0:T(8,128)(2,1)S(1)}, bf16[32,16,128]{2,1,0:T(8,128)(2,1)S(1)}, u32[]{:S(2)}, u32[]{:S(2)}) collective-permute-start(bf16[32,16,128]{2,1,0:T(8,128)(2,1)S(1)} %get-tuple-element.43), channel_id=1, source_target_pairs={{0,2},{2,0},{1,3},{3,1},{4,6},{6,4},{5,7},{7,5},{8,10},{10,8},{9,1... | collective-permute-start | bytes 393224 | tf_op jit(solution)/shard_map/ppermute | solution.py:20
  13.6 6.7 %collective-permute-start.8 = (bf16[8,16,128]{2,1,0:T(8,128)(2,1)S(1)}, bf16[8,16,128]{2,1,0:T(8,128)(2,1)S(1)}, u32[]{:S(2)}, u32[]{:S(2)}) collective-permute-start(bf16[8,16,128]{2,1,0:T(8,128)(2,1)S(1)} %get-tuple-element.55), channel_id=1, source_target_pairs={{0,12},{4,8},{8,4},{12,0},{1,13},{5,9},{9,5},{13,1},{2,14},{6,10},... | collective-permute-start | bytes 98312 | tf_op jit(solution)/shard_map/ppermute | solution.py:20
  15.5 5.2 %collective-permute-start.9 = (bf16[8,16,128]{2,1,0:T(8,128)(2,1)S(1)}, bf16[8,16,128]{2,1,0:T(8,128)(2,1)S(1)}, u32[]{:S(2)}, u32[]{:S(2)}) collective-permute-start(bf16[8,16,128]{2,1,0:T(8,128)(2,1)S(1)} %get-tuple-element.56), channel_id=1, source_target_pairs={{0,8},{4,12},{8,0},{12,4},{1,9},{5,13},{9,1},{13,5},{2,10},{6,14},... | collective-permute-start | bytes 98312 | tf_op jit(solution)/shard_map/ppermute | solution.py:20
  15.7 4.9 %collective-permute-start.10 = (bf16[8,16,128]{2,1,0:T(8,128)(2,1)S(1)}, bf16[8,16,128]{2,1,0:T(8,128)(2,1)S(1)}, u32[]{:S(2)}, u32[]{:S(2)}) collective-permute-start(bf16[8,16,128]{2,1,0:T(8,128)(2,1)S(1)} %get-tuple-element.57), channel_id=1, source_target_pairs={{0,4},{4,0},{8,12},{12,8},{1,5},{5,1},{9,13},{13,9},{2,6},{6,2},{1... | collective-permute-start | bytes 98312 | tf_op jit(solution)/shard_map/ppermute | solution.py:20
  18.0 2.8 %copy-start = (bf16[192,128,128]{2,1,0:T(8,128)(2,1)S(1)}, bf16[192,128,128]{2,1,0:T(8,128)(2,1)}, u32[]{:S(2)}) copy-start(bf16[192,128,128]{2,1,0:T(8,128)(2,1)} %refs_4_.3) | copy-start | bytes 18874372
  18.7 5.0 %collective-permute-start.5 = (bf16[16,16,128]{2,1,0:T(8,128)(2,1)S(1)}, bf16[16,16,128]{2,1,0:T(8,128)(2,1)S(1)}, u32[]{:S(2)}, u32[]{:S(2)}) collective-permute-start(bf16[16,16,128]{2,1,0:T(8,128)(2,1)S(1)} %get-tuple-element.47), channel_id=1, source_target_pairs={{0,2},{2,0},{1,3},{3,1},{4,6},{6,4},{5,7},{7,5},{8,10},{10,8},{9,1... | collective-permute-start | bytes 196616 | tf_op jit(solution)/shard_map/ppermute | solution.py:20
  22.2 5.1 %collective-permute-start.11 = (bf16[32,16,128]{2,1,0:T(8,128)(2,1)S(1)}, bf16[32,16,128]{2,1,0:T(8,128)(2,1)S(1)}, u32[]{:S(2)}, u32[]{:S(2)}) collective-permute-start(bf16[32,16,128]{2,1,0:T(8,128)(2,1)S(1)} %get-tuple-element.62), channel_id=1, source_target_pairs={{0,2},{2,0},{1,3},{3,1},{4,6},{6,4},{5,7},{7,5},{8,10},{10,8},{9,1... | collective-permute-start | bytes 393224 | tf_op jit(solution)/shard_map/ppermute | solution.py:20
  23.8 7.8 %collective-permute-start.6 = (bf16[12,16,128]{2,1,0:T(8,128)(2,1)S(1)}, bf16[12,16,128]{2,1,0:T(8,128)(2,1)S(1)}, u32[]{:S(2)}, u32[]{:S(2)}) collective-permute-start(bf16[12,16,128]{2,1,0:T(8,128)(2,1)S(1)} %get-tuple-element.48), channel_id=1, source_target_pairs={{0,8},{4,12},{8,0},{12,4},{1,9},{5,13},{9,1},{13,5},{2,10},{6,14},... | collective-permute-start | bytes 147464 | tf_op jit(solution)/shard_map/ppermute | solution.py:20
  25.5 5.9 %collective-permute-start.7 = (bf16[12,16,128]{2,1,0:T(8,128)(2,1)S(1)}, bf16[12,16,128]{2,1,0:T(8,128)(2,1)S(1)}, u32[]{:S(2)}, u32[]{:S(2)}) collective-permute-start(bf16[12,16,128]{2,1,0:T(8,128)(2,1)S(1)} %get-tuple-element.49), channel_id=1, source_target_pairs={{0,12},{4,8},{8,4},{12,0},{1,13},{5,9},{9,5},{13,1},{2,14},{6,10},... | collective-permute-start | bytes 147464 | tf_op jit(solution)/shard_map/ppermute | solution.py:20
  27.3 4.6 %collective-permute-start.12 = (bf16[12,16,128]{2,1,0:T(8,128)(2,1)S(1)}, bf16[12,16,128]{2,1,0:T(8,128)(2,1)S(1)}, u32[]{:S(2)}, u32[]{:S(2)}) collective-permute-start(bf16[12,16,128]{2,1,0:T(8,128)(2,1)S(1)} %get-tuple-element.65), channel_id=1, source_target_pairs={{0,4},{4,0},{8,12},{12,8},{1,5},{5,1},{9,13},{13,9},{2,6},{6,2},{1... | collective-permute-start | bytes 147464 | tf_op jit(solution)/shard_map/ppermute | solution.py:20

commit v11 on v9

--- a/solution.py
+++ b/solution.py
@@ -144,22 +144,33 @@
 
 def multiply(tiles, src, source, rows, acc):
     rhs, width = src.shape[1:]
-    unroll = min(32, tiles.shape[0])
-
-    def step(i, carry):
-        start = i * unroll
+    count = tiles.shape[0]
+    run = max(d for d in range(8, 97, 8) if count % d == 0)
+
+    def products(start):
         got = []
-        for u in range(0, unroll, 2):
-            t = start + u
+        for t in (start, start + 2, start + 4, start + 6):
             left = jnp.concatenate([src[source(t)], src[source(t + 1)]], axis=0)
             right = jnp.concatenate([tiles[t], tiles[t + 1]], axis=1)
             both = jnp.dot(left, right, preferred_element_type=F32)
             got += [both[:rhs, :width], both[rhs:, width:]]
+        return got
+
+    def add(start, got):
         for u, value in enumerate(got):
             acc[rows[start + u]] += value
+
+    def step(i, carry):
+        start = i * run
+        waiting = products(start)
+        for first in range(8, run, 8):
+            ahead = products(start + first)
+            add(start + first - 8, waiting)
+            waiting = ahead
+        add(start + run - 8, waiting)
         return carry
 
-    lax.fori_loop(0, tiles.shape[0] // unroll, step, 0)
+    lax.fori_loop(0, count // run, step, 0)
 
 
 def coeff_body(n_row, n_col, pan_own, slots, rows, needs, *refs):

time: 33.3 us -> 32.6 us (0.979)
  Pallas kernels: 7.92 us -> 7.18 us
    pallas_call x1, Pallas kernels: 1.85 us -> 1.37 us  [shards(): call(functools.partial(induct_body, n_row, n_col, seg_own, order), 'induc...]
  transfers between devices with their start and end apart: 13 -> 13, of which waited for: 5 -> 5; matrix products, arithmetic and copies ran while one was open for 0% -> 0% of each run, Pallas kernels for 21% -> 20%
where the time goes in v11:
time: 32.6 us; the launch traced here: 32.4 us
  starting transfers between devices  17.5 us (54%)
  Pallas kernels  7.18 us (22%)
  waiting for transfers between devices  7.01 us (22%)
  between operations  0.72 us (2%)
    ppermute x13, starting transfers between devices, exchange(): lax.ppermute(x, axis, [(i, i ^ k) for i in range(lax.axis_size(axis))])  17.5 us
    ppermute x13, waiting for transfers between devices, exchange(): lax.ppermute(x, axis, [(i, i ^ k) for i in range(lax.axis_size(axis))])  7.01 us
    pallas_call x1, Pallas kernels, shards(): call(functools.partial(ends_body, n_row, n_col, pan_own, cap_k, len(moved...  2.09 us
    pallas_call x1, Pallas kernels, shards(): call(functools.partial(induct_body, n_row, n_col, seg_own, order), 'induc...  1.37 us
    pallas_call x1, Pallas kernels, shards(): call(functools.partial(pack_body, pan_own), 'pack_charges', [like(pan_own...  0.88 us
    pallas_call x1, Pallas kernels, shards(): call(functools.partial(final_body, n_row, n_col, pan_own), 'outputs', [ja...  0.83 us
    pallas_call x1, Pallas kernels, shards(): call(functools.partial(base_body, pan_own), 'base_sums', [like(seg_own, F...  0.72 us
    pallas_call x1, Pallas kernels, shards(): call(functools.partial(coeff_body, n_row, n_col, pan_own), 'coeff_tiles',...  0.68 us
  transfers between devices with their start and end apart: 13, of which 5 were waited for; matrix products, arithmetic and copies ran while one was open for 0% of the time, Pallas kernels for 20%

profile of v11, /device:TPU:0, one launch (start us, length us, event | category | flops | bytes accessed | tf_op | source)
XLA Modules:
  0.0 32.4 jit_solution(5074957072549643004)
XLA Ops:
  0.6 3.0 %collective-permute-start = (bf16[16,512]{1,0:T(8,128)(2,1)}, bf16[16,512]{1,0:T(8,128)(2,1)S(1)}, u32[]{:S(2)}, u32[]{:S(2)}) collective-permute-start(bf16[16,512]{1,0:T(8,128)(2,1)} %charge.1), channel_id=1, source_target_pairs={{0,2},{2,0},{1,3},{3,1},{4,6},{6,4},{5,7},{7,5},{8,10},{10,8},{9,1... | collective-permute-start | bytes 49160 | tf_op jit(solution)/shard_map/ppermute | solution.py:20
  3.6 0.1 collective-permute-start.7
  3.7 0.9 %pack_charges.1.own = bf16[5,16,128]{2,1,0:T(8,128)(2,1)S(1)} custom-call(bf16[16,512]{1,0:T(8,128)(2,1)} %charge.1, s32[4,8]{1,0:T(4,128)} %needs.1), custom_call_target="tpu_custom_call" | custom-call | bytes 65536 | tf_op jit(solution)/shard_map/pack_charges/pallas_call | solution.py:334
  4.6 1.0 %collective-permute-done.refs_0_ = bf16[16,512]{1,0:T(8,128)(2,1)S(1)} collective-permute-done((bf16[16,512]{1,0:T(8,128)(2,1)}, bf16[16,512]{1,0:T(8,128)(2,1)S(1)}, u32[]{:S(2)}, u32[]{:S(2)}) %collective-permute-start) | collective-permute-done | bytes 16416 | tf_op jit(solution)/shard_map/ppermute | solution.py:20
  5.6 4.3 %collective-permute-start.1 = (bf16[9,16,128]{2,1,0:T(8,128)(2,1)S(1)}, bf16[9,16,128]{2,1,0:T(8,128)(2,1)S(1)}, u32[]{:S(2)}, u32[]{:S(2)}) collective-permute-start(bf16[9,16,128]{2,1,0:T(8,128)(2,1)S(1)} %join_charges.1.refs_3_.pack), channel_id=1, source_target_pairs={{0,12},{4,8},{8,4},{12,0},{1,13},{5,9},{9,5},{13,1},{2,14},{6,10},... | collective-permute-start | bytes 110600 | tf_op jit(solution)/shard_map/ppermute | solution.py:20
  9.9 0.6 %collective-permute-start.3 = (bf16[9,16,128]{2,1,0:T(8,128)(2,1)S(1)}, bf16[9,16,128]{2,1,0:T(8,128)(2,1)S(1)}, u32[]{:S(2)}, u32[]{:S(2)}) collective-permute-start(bf16[9,16,128]{2,1,0:T(8,128)(2,1)S(1)} %join_charges.1.refs_3_.pack), channel_id=1, source_target_pairs={{0,4},{4,0},{8,12},{12,8},{1,5},{5,1},{9,13},{13,9},{2,6},{6,2},{1... | collective-permute-start | bytes 110600 | tf_op jit(solution)/shard_map/ppermute | solution.py:20
  10.5 2.1 %end_sums.1 = (s32[2,32]{1,0:T(2,128)S(4)}, s32[4,16]{1,0:T(4,128)S(4)}, s32[96]{0:T(128)S(4)}, s32[96]{0:T(128)S(4)}, s32[4,4]{1,0:T(4,128)S(4)}, /*index=5*/s3...) custom-call(bf16[16,4096]{1,0:T(8,128)(2,1)} %refs_0_.1, ...), custom_call_target="tpu_custom_call" | custom-call | flops 500000000 | bytes 262144 | tf_op jit(solution)/shard_map/end_sums/pallas_call | solution.py:354
  12.6 0.0 collective-permute-done.1.refs_0_
  12.6 2.1 %collective-permute-done.2.refs_1_ = bf16[9,16,128]{2,1,0:T(8,128)(2,1)S(1)} collective-permute-done((bf16[9,16,128]{2,1,0:T(8,128)(2,1)S(1)}, bf16[9,16,128]{2,1,0:T(8,128)(2,1)S(1)}, u32[]{:S(2)}, u32[]{:S(2)}) %collective-permute-start.2) | collective-permute-done | bytes 36896 | tf_op jit(solution)/shard_map/ppermute | solution.py:20
  14.7 0.0 collective-permute-done.3.refs_2_
  14.7 0.7 %coeff_tiles.1 = (f32[8,16,128]{2,1,0:T(8,128)S(1)}, bf16[32,16,128]{2,1,0:T(8,128)(2,1)S(1)}) custom-call(s32[96]{0:T(128)S(4)} %get-tuple-element.37.slots, s32[96]{0:T(128)S(4)} %get-tuple-element.38.rows, s32[4,4]{1,0:T(4,128)S(4)} %get-tuple-element.39.needs, bf16[9,16,128]{2,1,0:T(8,128)(2,1)S(1)} %collective-permute-done.1.refs_0_, ...), custom_call_target="tpu_custom_call" | custom-call | flops 1000000000 | bytes 3145728 | tf_op jit(solution)/shard_map/coeff_tiles/pallas_call | solution.py:376
  15.4 1.6 %collective-permute-start.4 = (bf16[32,16,128]{2,1,0:T(8,128)(2,1)S(1)}, bf16[32,16,128]{2,1,0:T(8,128)(2,1)S(1)}, u32[]{:S(2)}, u32[]{:S(2)}) collective-permute-start(bf16[32,16,128]{2,1,0:T(8,128)(2,1)S(1)} %get-tuple-element.44), channel_id=1, source_target_pairs={{0,2},{2,0},{1,3},{3,1},{4,6},{6,4},{5,7},{7,5},{8,10},{10,8},{9,1... | collective-permute-start | bytes 393224 | tf_op jit(solution)/shard_map/ppermute | solution.py:20
  17.0 0.3 pick_blocks.1
  17.3 1.7 %collective-permute-start.10 = (bf16[8,16,128]{2,1,0:T(8,128)(2,1)S(1)}, bf16[8,16,128]{2,1,0:T(8,128)(2,1)S(1)}, u32[]{:S(2)}, u32[]{:S(2)}) collective-permute-start(bf16[8,16,128]{2,1,0:T(8,128)(2,1)S(1)} %get-tuple-element.55), channel_id=1, source_target_pairs={{0,12},{4,8},{8,4},{12,0},{1,13},{5,9},{9,5},{13,1},{2,14},{6,10},... | collective-permute-start | bytes 98312 | tf_op jit(solution)/shard_map/ppermute | solution.py:20
  19.0 0.4 %collective-permute-start.8 = (bf16[8,16,128]{2,1,0:T(8,128)(2,1)S(1)}, bf16[8,16,128]{2,1,0:T(8,128)(2,1)S(1)}, u32[]{:S(2)}, u32[]{:S(2)}) collective-permute-start(bf16[8,16,128]{2,1,0:T(8,128)(2,1)S(1)} %get-tuple-element.52), channel_id=1, source_target_pairs={{0,8},{4,12},{8,0},{12,4},{1,9},{5,13},{9,1},{13,5},{2,10},{6,14},... | collective-permute-start | bytes 98312 | tf_op jit(solution)/shard_map/ppermute | solution.py:20
  19.5 2.3 %collective-permute-start.9 = (bf16[8,16,128]{2,1,0:T(8,128)(2,1)S(1)}, bf16[8,16,128]{2,1,0:T(8,128)(2,1)S(1)}, u32[]{:S(2)}, u32[]{:S(2)}) collective-permute-start(bf16[8,16,128]{2,1,0:T(8,128)(2,1)S(1)} %get-tuple-element.53), channel_id=1, source_target_pairs={{0,4},{4,0},{8,12},{12,8},{1,5},{5,1},{9,13},{13,9},{2,6},{6,2},{1... | collective-permute-start | bytes 98312 | tf_op jit(solution)/shard_map/ppermute | solution.py:20
  21.8 0.0 collective-permute-done.4.refs_0_
  21.8 1.7 %collective-permute-start.6 = (bf16[12,16,128]{2,1,0:T(8,128)(2,1)S(1)}, bf16[12,16,128]{2,1,0:T(8,128)(2,1)S(1)}, u32[]{:S(2)}, u32[]{:S(2)}) collective-permute-start(bf16[12,16,128]{2,1,0:T(8,128)(2,1)S(1)} %get-tuple-element.46), channel_id=1, source_target_pairs={{0,12},{4,8},{8,4},{12,0},{1,13},{5,9},{9,5},{13,1},{2,14},{6,10},... | collective-permute-start | bytes 147464 | tf_op jit(solution)/shard_map/ppermute | solution.py:20
  23.5 0.0 collective-permute-start.5
  23.5 0.0 collective-permute-done.10.refs_3_
  23.5 1.6 %collective-permute-done.8.refs_0_ = bf16[8,16,128]{2,1,0:T(8,128)(2,1)S(1)} collective-permute-done((bf16[8,16,128]{2,1,0:T(8,128)(2,1)S(1)}, bf16[8,16,128]{2,1,0:T(8,128)(2,1)S(1)}, u32[]{:S(2)}, u32[]{:S(2)}) %collective-permute-start.8) | collective-permute-done | bytes 32800 | tf_op jit(solution)/shard_map/ppermute | solution.py:20
  25.2 1.4 %induct_tiles.1 = (f32[32,16,128]{2,1,0:T(8,128)S(1)}, bf16[32,16,128]{2,1,0:T(8,128)(2,1)S(1)}) custom-call(s32[192]{0:T(256)S(4)} %get-tuple-element.48.slots, s32[192]{0:T(256)S(4)} %get-tuple-element.49.rows, bf16[8,16,128]{2,1,0:T(8,128)(2,1)S(1)} %get-tuple-element.50._after.pot, bf16[8,16,128]{2,1,0:T(8,128)(2,1)S(1)} %collective-permute-done.8.refs_0_, ...), custom_call_target="tpu_custom_call" | custom-call | flops 100000000 | bytes 65536 | tf_op jit(solution)/shard_map/induct_tiles/pallas_call | solution.py:410
  26.5 0.3 %collective-permute-start.12 = (bf16[32,16,128]{2,1,0:T(8,128)(2,1)S(1)}, bf16[32,16,128]{2,1,0:T(8,128)(2,1)S(1)}, u32[]{:S(2)}, u32[]{:S(2)}) collective-permute-start(bf16[32,16,128]{2,1,0:T(8,128)(2,1)S(1)} %get-tuple-element.61), channel_id=1, source_target_pairs={{0,2},{2,0},{1,3},{3,1},{4,6},{6,4},{5,7},{7,5},{8,10},{10,8},{9,1... | collective-permute-start | bytes 393224 | tf_op jit(solution)/shard_map/ppermute | solution.py:20
  26.9 1.3 %collective-permute-start.11 = (bf16[12,16,128]{2,1,0:T(8,128)(2,1)S(1)}, bf16[12,16,128]{2,1,0:T(8,128)(2,1)S(1)}, u32[]{:S(2)}, u32[]{:S(2)}) collective-permute-start(bf16[12,16,128]{2,1,0:T(8,128)(2,1)S(1)} %hold_near.1), channel_id=1, source_target_pairs={{0,4},{4,0},{8,12},{12,8},{1,5},{5,1},{9,13},{13,9},{2,6},{6,2},{1... | collective-permute-start | bytes 147464 | tf_op jit(solution)/shard_map/ppermute | solution.py:20
  28.2 0.7 %base_sums.1 = (f32[32,16,128]{2,1,0:T(8,128)S(1)}, f32[4,16,128]{2,1,0:T(8,128)S(1)}, bf16[16,512]{1,0:T(8,128)(2,1)}) custom-call(s32[4,16]{1,0:T(4,128)S(4)} %get-tuple-element.34.links, s32[64]{0:T(128)S(4)} %get-tuple-element.35.holder, f32[16]{0:T(128)S(4)} %get-tuple-element.47.scale, s32[64,128]{1,0:T(8,128)S(1)} %get-tuple-element.36.lanes, ...), custom_call_target="tpu_custom_call" | custom-call | tf_op jit(solution)/shard_map/base_sums/pallas_call | solution.py:433
  28.9 0.0 collective-permute-done.6.message.refs_2_
  29.0 0.1 add_drops.2.field_in
  29.1 0.0 collective-permute-done.5.message.refs_1_
  29.1 0.1 add_drops.3.field_own
  29.3 1.7 %collective-permute-done.11.refs_0_ = bf16[12,16,128]{2,1,0:T(8,128)(2,1)S(1)} collective-permute-done((bf16[12,16,128]{2,1,0:T(8,128)(2,1)S(1)}, bf16[12,16,128]{2,1,0:T(8,128)(2,1)S(1)}, u32[]{:S(2)}, u32[]{:S(2)}) %collective-permute-start.11) | collective-permute-done | bytes 49184 | tf_op jit(solution)/shard_map/ppermute | solution.py:20
  31.0 0.6 %collective-permute-done.12.refs_3_ = bf16[32,16,128]{2,1,0:T(8,128)(2,1)S(1)} collective-permute-done((bf16[32,16,128]{2,1,0:T(8,128)(2,1)S(1)}, bf16[32,16,128]{2,1,0:T(8,128)(2,1)S(1)}, u32[]{:S(2)}, u32[]{:S(2)}) %collective-permute-start.12) | collective-permute-done | bytes 131104 | tf_op jit(solution)/shard_map/ppermute | solution.py:20
  31.6 0.8 %outputs.1 = (bf16[16,4096]{1,0:T(8,128)(2,1)}, bf16[16,512]{1,0:T(8,128)(2,1)}) custom-call(s32[4,16]{1,0:T(4,128)S(4)} %get-tuple-element.34.links, s32[64]{0:T(128)S(4)} %get-tuple-element.35.holder, s32[64,128]{1,0:T(8,128)S(1)} %get-tuple-element.36.lanes, f32[32,16,128]{2,1,0:T(8,128)S(1)} %add_drops.3.field_own, ...), custom_call_target="tpu_custom_call" | custom-call | flops 1000000000 | bytes 1048576 | tf_op jit(solution)/shard_map/outputs/pallas_call | solution.py:452
  (11 shorter events, 0.1 us)
Async XLA Ops:
  0.6 4.9 %collective-permute-start = (bf16[16,512]{1,0:T(8,128)(2,1)}, bf16[16,512]{1,0:T(8,128)(2,1)S(1)}, u32[]{:S(2)}, u32[]{:S(2)}) collective-permute-start(bf16[16,512]{1,0:T(8,128)(2,1)} %charge.1), channel_id=1, source_target_pairs={{0,2},{2,0},{1,3},{3,1},{4,6},{6,4},{5,7},{7,5},{8,10},{10,8},{9,1... | collective-permute-start | bytes 49160 | tf_op jit(solution)/shard_map/ppermute | solution.py:20
  3.6 13.4 %collective-permute-start.7 = (bf16[16,4096]{1,0:T(8,128)(2,1)}, bf16[16,4096]{1,0:T(8,128)(2,1)S(1)}, u32[]{:S(2)}, u32[]{:S(2)}) collective-permute-start(bf16[16,4096]{1,0:T(8,128)(2,1)} %refs_0_.1), channel_id=1, source_target_pairs={{0,2},{2,0},{1,3},{3,1},{4,6},{6,4},{5,7},{7,5},{8,10},{10,8},{9,1... | collective-permute-start | bytes 393224 | tf_op jit(solution)/shard_map/ppermute | solution.py:20
  3.7 21.4 %slice-start = ((s8[6291456]{0:T(1024)(128)(4,1)}), s8[4194304]{0:T(1024)(128)(4,1)S(1)}, s32[]{:S(2)}) async-start(s8[6291456]{0:T(1024)(128)(4,1)} %bitcast.2), calls=%async_computation | async-start | bytes 8388608
  5.6 7.0 %collective-permute-start.1 = (bf16[9,16,128]{2,1,0:T(8,128)(2,1)S(1)}, bf16[9,16,128]{2,1,0:T(8,128)(2,1)S(1)}, u32[]{:S(2)}, u32[]{:S(2)}) collective-permute-start(bf16[9,16,128]{2,1,0:T(8,128)(2,1)S(1)} %join_charges.1.refs_3_.pack), channel_id=1, source_target_pairs={{0,12},{4,8},{8,4},{12,0},{1,13},{5,9},{9,5},{13,1},{2,14},{6,10},... | collective-permute-start | bytes 110600 | tf_op jit(solution)/shard_map/ppermute | solution.py:20
  9.9 4.9 %collective-permute-start.2 = (bf16[9,16,128]{2,1,0:T(8,128)(2,1)S(1)}, bf16[9,16,128]{2,1,0:T(8,128)(2,1)S(1)}, u32[]{:S(2)}, u32[]{:S(2)}) collective-permute-start(bf16[9,16,128]{2,1,0:T(8,128)(2,1)S(1)} %join_charges.1.refs_3_.pack), channel_id=1, source_target_pairs={{0,8},{4,12},{8,0},{12,4},{1,9},{5,13},{9,1},{13,5},{2,10},{6,14},... | collective-permute-start | bytes 110600 | tf_op jit(solution)/shard_map/ppermute | solution.py:20
  9.9 4.9 %collective-permute-start.3 = (bf16[9,16,128]{2,1,0:T(8,128)(2,1)S(1)}, bf16[9,16,128]{2,1,0:T(8,128)(2,1)S(1)}, u32[]{:S(2)}, u32[]{:S(2)}) collective-permute-start(bf16[9,16,128]{2,1,0:T(8,128)(2,1)S(1)} %join_charges.1.refs_3_.pack), channel_id=1, source_target_pairs={{0,4},{4,0},{8,12},{12,8},{1,5},{5,1},{9,13},{13,9},{2,6},{6,2},{1... | collective-permute-start | bytes 110600 | tf_op jit(solution)/shard_map/ppermute | solution.py:20
  14.7 10.4 %slice-start.1 = ((s8[6291456]{0:T(1024)(128)(4,1)}), s8[2097152]{0:T(1024)(128)(4,1)S(1)}, s32[]{:S(2)}) async-start(s8[6291456]{0:T(1024)(128)(4,1)} %bitcast.2), calls=%async_computation.1 | async-start | bytes 4194304
  15.4 6.4 %collective-permute-start.4 = (bf16[32,16,128]{2,1,0:T(8,128)(2,1)S(1)}, bf16[32,16,128]{2,1,0:T(8,128)(2,1)S(1)}, u32[]{:S(2)}, u32[]{:S(2)}) collective-permute-start(bf16[32,16,128]{2,1,0:T(8,128)(2,1)S(1)} %get-tuple-element.44), channel_id=1, source_target_pairs={{0,2},{2,0},{1,3},{3,1},{4,6},{6,4},{5,7},{7,5},{8,10},{10,8},{9,1... | collective-permute-start | bytes 393224 | tf_op jit(solution)/shard_map/ppermute | solution.py:20
  17.3 6.2 %collective-permute-start.10 = (bf16[8,16,128]{2,1,0:T(8,128)(2,1)S(1)}, bf16[8,16,128]{2,1,0:T(8,128)(2,1)S(1)}, u32[]{:S(2)}, u32[]{:S(2)}) collective-permute-start(bf16[8,16,128]{2,1,0:T(8,128)(2,1)S(1)} %get-tuple-element.55), channel_id=1, source_target_pairs={{0,12},{4,8},{8,4},{12,0},{1,13},{5,9},{9,5},{13,1},{2,14},{6,10},... | collective-permute-start | bytes 98312 | tf_op jit(solution)/shard_map/ppermute | solution.py:20
  19.0 6.1 %collective-permute-start.8 = (bf16[8,16,128]{2,1,0:T(8,128)(2,1)S(1)}, bf16[8,16,128]{2,1,0:T(8,128)(2,1)S(1)}, u32[]{:S(2)}, u32[]{:S(2)}) collective-permute-start(bf16[8,16,128]{2,1,0:T(8,128)(2,1)S(1)} %get-tuple-element.52), channel_id=1, source_target_pairs={{0,8},{4,12},{8,0},{12,4},{1,9},{5,13},{9,1},{13,5},{2,10},{6,14},... | collective-permute-start | bytes 98312 | tf_op jit(solution)/shard_map/ppermute | solution.py:20
  19.5 5.7 %collective-permute-start.9 = (bf16[8,16,128]{2,1,0:T(8,128)(2,1)S(1)}, bf16[8,16,128]{2,1,0:T(8,128)(2,1)S(1)}, u32[]{:S(2)}, u32[]{:S(2)}) collective-permute-start(bf16[8,16,128]{2,1,0:T(8,128)(2,1)S(1)} %get-tuple-element.53), channel_id=1, source_target_pairs={{0,4},{4,0},{8,12},{12,8},{1,5},{5,1},{9,13},{13,9},{2,6},{6,2},{1... | collective-permute-start | bytes 98312 | tf_op jit(solution)/shard_map/ppermute | solution.py:20
  21.8 7.2 %collective-permute-start.6 = (bf16[12,16,128]{2,1,0:T(8,128)(2,1)S(1)}, bf16[12,16,128]{2,1,0:T(8,128)(2,1)S(1)}, u32[]{:S(2)}, u32[]{:S(2)}) collective-permute-start(bf16[12,16,128]{2,1,0:T(8,128)(2,1)S(1)} %get-tuple-element.46), channel_id=1, source_target_pairs={{0,12},{4,8},{8,4},{12,0},{1,13},{5,9},{9,5},{13,1},{2,14},{6,10},... | collective-permute-start | bytes 147464 | tf_op jit(solution)/shard_map/ppermute | solution.py:20
  23.5 5.6 %collective-permute-start.5 = (bf16[12,16,128]{2,1,0:T(8,128)(2,1)S(1)}, bf16[12,16,128]{2,1,0:T(8,128)(2,1)S(1)}, u32[]{:S(2)}, u32[]{:S(2)}) collective-permute-start(bf16[12,16,128]{2,1,0:T(8,128)(2,1)S(1)} %get-tuple-element.45), channel_id=1, source_target_pairs={{0,8},{4,12},{8,0},{12,4},{1,9},{5,13},{9,1},{13,5},{2,10},{6,14},... | collective-permute-start | bytes 147464 | tf_op jit(solution)/shard_map/ppermute | solution.py:20
  26.5 5.0 %collective-permute-start.12 = (bf16[32,16,128]{2,1,0:T(8,128)(2,1)S(1)}, bf16[32,16,128]{2,1,0:T(8,128)(2,1)S(1)}, u32[]{:S(2)}, u32[]{:S(2)}) collective-permute-start(bf16[32,16,128]{2,1,0:T(8,128)(2,1)S(1)} %get-tuple-element.61), channel_id=1, source_target_pairs={{0,2},{2,0},{1,3},{3,1},{4,6},{6,4},{5,7},{7,5},{8,10},{10,8},{9,1... | collective-permute-start | bytes 393224 | tf_op jit(solution)/shard_map/ppermute | solution.py:20
  26.9 4.1 %collective-permute-start.11 = (bf16[12,16,128]{2,1,0:T(8,128)(2,1)S(1)}, bf16[12,16,128]{2,1,0:T(8,128)(2,1)S(1)}, u32[]{:S(2)}, u32[]{:S(2)}) collective-permute-start(bf16[12,16,128]{2,1,0:T(8,128)(2,1)S(1)} %hold_near.1), channel_id=1, source_target_pairs={{0,4},{4,0},{8,12},{12,8},{1,5},{5,1},{9,13},{13,9},{2,6},{6,2},{1... | collective-permute-start | bytes 147464 | tf_op jit(solution)/shard_map/ppermute | solution.py:20

commit v12 on v11

--- a/solution.py
+++ b/solution.py
@@ -142,19 +142,30 @@
             outs[n_row - 1 - k][s] = value
 
 
-def multiply(tiles, src, source, rows, acc):
+def products(tiles, src, source, start, side):
     rhs, width = src.shape[1:]
+    got = []
+    none = jnp.zeros((side * rhs, width), BF16)
+    for offset in range(0, 8, side * side):
+        first = start + offset
+        bands, lefts = [], []
+        for i in range(side):
+            row = [first + i * side + j for j in range(side)]
+            bands.append(jnp.concatenate([tiles[t] for t in row], axis=1))
+            own = jnp.concatenate([src[source(t)] for t in row], axis=0)
+            lefts.append(jnp.concatenate([own if j == i else none for j in range(side)], axis=1))
+        left, right = jnp.concatenate(lefts, axis=0), jnp.concatenate(bands, axis=0)
+        whole = jnp.dot(left, right, preferred_element_type=F32)
+        for i in range(side):
+            for j in range(side):
+                at = (i * side + j) * rhs
+                got.append(whole[at : at + rhs, j * width : (j + 1) * width])
+    return got
+
+
+def multiply(tiles, src, source, rows, acc, side):
     count = tiles.shape[0]
     run = max(d for d in range(8, 97, 8) if count % d == 0)
-
-    def products(start):
-        got = []
-        for t in (start, start + 2, start + 4, start + 6):
-            left = jnp.concatenate([src[source(t)], src[source(t + 1)]], axis=0)
-            right = jnp.concatenate([tiles[t], tiles[t + 1]], axis=1)
-            both = jnp.dot(left, right, preferred_element_type=F32)
-            got += [both[:rhs, :width], both[rhs:, width:]]
-        return got
 
     def add(start, got):
         for u, value in enumerate(got):
@@ -162,9 +173,9 @@
 
     def step(i, carry):
         start = i * run
-        waiting = products(start)
+        waiting = products(tiles, src, source, start, side)
         for first in range(8, run, 8):
-            ahead = products(start + first)
+            ahead = products(tiles, src, source, start + first, side)
             add(start + first - 8, waiting)
             waiting = ahead
         add(start + run - 8, waiting)
@@ -187,7 +198,7 @@
         for s in range(cap):
             named[p * cap + s] = p * pan_group + needs[p, s]
     part[...] = jnp.zeros_like(part)
-    multiply(tiles, src, lambda t: named[slots[t]], rows, part)
+    multiply(tiles, src, lambda t: named[slots[t]], rows, part, 1)
     high = part[...].astype(BF16)
     low = (part[...] - high.astype(F32)).astype(BF16)
     for message, sums in zip(messages, ends):
@@ -206,7 +217,7 @@
     for k in range(n_row):
         src[pl.ds(lax.bitwise_xor(r, k) * cap, cap)] = got[k][...]
     acc[...] = jnp.zeros_like(acc)
-    multiply(tiles, src, lambda t: slots[t], rows, acc)
+    multiply(tiles, src, lambda t: slots[t], rows, acc, 2)
     own[...] = acc[pl.ds(c * seg_own, seg_own)]
     for j in range(1, n_col):
         sends[j - 1][...] = acc[pl.ds(lax.bitwise_xor(c, j) * seg_own, seg_own)].astype(BF16)

time: 32.6 us -> 32.9 us (level)
  Pallas kernels: 7.18 us -> 7.55 us
where the time goes in v12:
time: 32.9 us; the launch traced here: 32.8 us
  starting transfers between devices  17.5 us (53%)
  Pallas kernels  7.55 us (23%)
  waiting for transfers between devices  7.02 us (21%)
  between operations  0.72 us (2%)
    ppermute x13, starting transfers between devices, exchange(): lax.ppermute(x, axis, [(i, i ^ k) for i in range(lax.axis_size(axis))])  17.5 us
    ppermute x13, waiting for transfers between devices, exchange(): lax.ppermute(x, axis, [(i, i ^ k) for i in range(lax.axis_size(axis))])  7.02 us
    pallas_call x1, Pallas kernels, shards(): call(functools.partial(ends_body, n_row, n_col, pan_own, cap_k, len(moved...  2.09 us
    pallas_call x1, Pallas kernels, shards(): call(functools.partial(induct_body, n_row, n_col, seg_own, order), 'induc...  1.44 us
    pallas_call x1, Pallas kernels, shards(): call(functools.partial(coeff_body, n_row, n_col, pan_own), 'coeff_tiles',...  0.98 us
    pallas_call x1, Pallas kernels, shards(): call(functools.partial(pack_body, pan_own), 'pack_charges', [like(pan_own...  0.88 us
    pallas_call x1, Pallas kernels, shards(): call(functools.partial(final_body, n_row, n_col, pan_own), 'outputs', [ja...  0.83 us
    pallas_call x1, Pallas kernels, shards(): call(functools.partial(base_body, pan_own), 'base_sums', [like(seg_own, F...  0.72 us
  transfers between devices with their start and end apart: 13, of which 5 were waited for; matrix products, arithmetic and copies ran while one was open for 0% of the time, Pallas kernels for 20%

profile of v12, /device:TPU:0, one launch (start us, length us, event | category | flops | bytes accessed | tf_op | source)
XLA Modules:
  0.0 32.8 jit_solution(13798518378069754626)
XLA Ops:
  0.6 3.0 %collective-permute-start = (bf16[16,512]{1,0:T(8,128)(2,1)}, bf16[16,512]{1,0:T(8,128)(2,1)S(1)}, u32[]{:S(2)}, u32[]{:S(2)}) collective-permute-start(bf16[16,512]{1,0:T(8,128)(2,1)} %charge.1), channel_id=1, source_target_pairs={{0,2},{2,0},{1,3},{3,1},{4,6},{6,4},{5,7},{7,5},{8,10},{10,8},{9,1... | collective-permute-start | bytes 49160 | tf_op jit(solution)/shard_map/ppermute | solution.py:20
  3.6 0.1 collective-permute-start.7
  3.7 0.9 %pack_charges.1.own = bf16[5,16,128]{2,1,0:T(8,128)(2,1)S(1)} custom-call(bf16[16,512]{1,0:T(8,128)(2,1)} %charge.1, s32[4,8]{1,0:T(4,128)} %needs.1), custom_call_target="tpu_custom_call" | custom-call | bytes 65536 | tf_op jit(solution)/shard_map/pack_charges/pallas_call | solution.py:345
  4.6 1.0 %collective-permute-done.refs_0_ = bf16[16,512]{1,0:T(8,128)(2,1)S(1)} collective-permute-done((bf16[16,512]{1,0:T(8,128)(2,1)}, bf16[16,512]{1,0:T(8,128)(2,1)S(1)}, u32[]{:S(2)}, u32[]{:S(2)}) %collective-permute-start) | collective-permute-done | bytes 16416 | tf_op jit(solution)/shard_map/ppermute | solution.py:20
  5.6 4.3 %collective-permute-start.1 = (bf16[9,16,128]{2,1,0:T(8,128)(2,1)S(1)}, bf16[9,16,128]{2,1,0:T(8,128)(2,1)S(1)}, u32[]{:S(2)}, u32[]{:S(2)}) collective-permute-start(bf16[9,16,128]{2,1,0:T(8,128)(2,1)S(1)} %join_charges.1.refs_3_.pack), channel_id=1, source_target_pairs={{0,12},{4,8},{8,4},{12,0},{1,13},{5,9},{9,5},{13,1},{2,14},{6,10},... | collective-permute-start | bytes 110600 | tf_op jit(solution)/shard_map/ppermute | solution.py:20
  9.9 0.0 collective-permute-start.2
  9.9 0.6 %collective-permute-start.3 = (bf16[9,16,128]{2,1,0:T(8,128)(2,1)S(1)}, bf16[9,16,128]{2,1,0:T(8,128)(2,1)S(1)}, u32[]{:S(2)}, u32[]{:S(2)}) collective-permute-start(bf16[9,16,128]{2,1,0:T(8,128)(2,1)S(1)} %join_charges.1.refs_3_.pack), channel_id=1, source_target_pairs={{0,4},{4,0},{8,12},{12,8},{1,5},{5,1},{9,13},{13,9},{2,6},{6,2},{1... | collective-permute-start | bytes 110600 | tf_op jit(solution)/shard_map/ppermute | solution.py:20
  10.5 2.1 %end_sums.1 = (s32[2,32]{1,0:T(2,128)S(4)}, s32[4,16]{1,0:T(4,128)S(4)}, s32[96]{0:T(128)S(4)}, s32[96]{0:T(128)S(4)}, s32[4,4]{1,0:T(4,128)S(4)}, /*index=5*/s3...) custom-call(bf16[16,4096]{1,0:T(8,128)(2,1)} %refs_0_.1, ...), custom_call_target="tpu_custom_call" | custom-call | flops 500000000 | bytes 262144 | tf_op jit(solution)/shard_map/end_sums/pallas_call | solution.py:365
  12.6 0.0 collective-permute-done.1.refs_0_
  12.6 2.1 %collective-permute-done.2.refs_1_ = bf16[9,16,128]{2,1,0:T(8,128)(2,1)S(1)} collective-permute-done((bf16[9,16,128]{2,1,0:T(8,128)(2,1)S(1)}, bf16[9,16,128]{2,1,0:T(8,128)(2,1)S(1)}, u32[]{:S(2)}, u32[]{:S(2)}) %collective-permute-start.2) | collective-permute-done | bytes 36896 | tf_op jit(solution)/shard_map/ppermute | solution.py:20
  14.7 0.0 collective-permute-done.3.refs_2_
  14.7 1.0 %coeff_tiles.1 = (f32[8,16,128]{2,1,0:T(8,128)S(1)}, bf16[32,16,128]{2,1,0:T(8,128)(2,1)S(1)}) custom-call(s32[96]{0:T(128)S(4)} %get-tuple-element.37.slots, s32[96]{0:T(128)S(4)} %get-tuple-element.38.rows, s32[4,4]{1,0:T(4,128)S(4)} %get-tuple-element.39.needs, bf16[9,16,128]{2,1,0:T(8,128)(2,1)S(1)} %collective-permute-done.1.refs_0_, ...), custom_call_target="tpu_custom_call" | custom-call | flops 1000000000 | bytes 3145728 | tf_op jit(solution)/shard_map/coeff_tiles/pallas_call | solution.py:387
  15.7 1.6 %collective-permute-start.4 = (bf16[32,16,128]{2,1,0:T(8,128)(2,1)S(1)}, bf16[32,16,128]{2,1,0:T(8,128)(2,1)S(1)}, u32[]{:S(2)}, u32[]{:S(2)}) collective-permute-start(bf16[32,16,128]{2,1,0:T(8,128)(2,1)S(1)} %get-tuple-element.44), channel_id=1, source_target_pairs={{0,2},{2,0},{1,3},{3,1},{4,6},{6,4},{5,7},{7,5},{8,10},{10,8},{9,1... | collective-permute-start | bytes 393224 | tf_op jit(solution)/shard_map/ppermute | solution.py:20
  17.3 0.0 collective-permute-done.7.refs_5_
  17.3 0.3 pick_blocks.1
  17.6 1.7 %collective-permute-start.10 = (bf16[8,16,128]{2,1,0:T(8,128)(2,1)S(1)}, bf16[8,16,128]{2,1,0:T(8,128)(2,1)S(1)}, u32[]{:S(2)}, u32[]{:S(2)}) collective-permute-start(bf16[8,16,128]{2,1,0:T(8,128)(2,1)S(1)} %get-tuple-element.55), channel_id=1, source_target_pairs={{0,12},{4,8},{8,4},{12,0},{1,13},{5,9},{9,5},{13,1},{2,14},{6,10},... | collective-permute-start | bytes 98312 | tf_op jit(solution)/shard_map/ppermute | solution.py:20
  19.4 0.4 %collective-permute-start.8 = (bf16[8,16,128]{2,1,0:T(8,128)(2,1)S(1)}, bf16[8,16,128]{2,1,0:T(8,128)(2,1)S(1)}, u32[]{:S(2)}, u32[]{:S(2)}) collective-permute-start(bf16[8,16,128]{2,1,0:T(8,128)(2,1)S(1)} %get-tuple-element.52), channel_id=1, source_target_pairs={{0,8},{4,12},{8,0},{12,4},{1,9},{5,13},{9,1},{13,5},{2,10},{6,14},... | collective-permute-start | bytes 98312 | tf_op jit(solution)/shard_map/ppermute | solution.py:20
  19.8 2.3 %collective-permute-start.9 = (bf16[8,16,128]{2,1,0:T(8,128)(2,1)S(1)}, bf16[8,16,128]{2,1,0:T(8,128)(2,1)S(1)}, u32[]{:S(2)}, u32[]{:S(2)}) collective-permute-start(bf16[8,16,128]{2,1,0:T(8,128)(2,1)S(1)} %get-tuple-element.53), channel_id=1, source_target_pairs={{0,4},{4,0},{8,12},{12,8},{1,5},{5,1},{9,13},{13,9},{2,6},{6,2},{1... | collective-permute-start | bytes 98312 | tf_op jit(solution)/shard_map/ppermute | solution.py:20
  22.1 0.0 collective-permute-done.4.refs_0_
  22.1 1.7 %collective-permute-start.6 = (bf16[12,16,128]{2,1,0:T(8,128)(2,1)S(1)}, bf16[12,16,128]{2,1,0:T(8,128)(2,1)S(1)}, u32[]{:S(2)}, u32[]{:S(2)}) collective-permute-start(bf16[12,16,128]{2,1,0:T(8,128)(2,1)S(1)} %get-tuple-element.46), channel_id=1, source_target_pairs={{0,12},{4,8},{8,4},{12,0},{1,13},{5,9},{9,5},{13,1},{2,14},{6,10},... | collective-permute-start | bytes 147464 | tf_op jit(solution)/shard_map/ppermute | solution.py:20
  23.8 1.6 %collective-permute-done.8.refs_0_ = bf16[8,16,128]{2,1,0:T(8,128)(2,1)S(1)} collective-permute-done((bf16[8,16,128]{2,1,0:T(8,128)(2,1)S(1)}, bf16[8,16,128]{2,1,0:T(8,128)(2,1)S(1)}, u32[]{:S(2)}, u32[]{:S(2)}) %collective-permute-start.8) | collective-permute-done | bytes 32800 | tf_op jit(solution)/shard_map/ppermute | solution.py:20
  25.5 1.4 %induct_tiles.1 = (f32[32,16,128]{2,1,0:T(8,128)S(1)}, bf16[32,16,128]{2,1,0:T(8,128)(2,1)S(1)}) custom-call(s32[192]{0:T(256)S(4)} %get-tuple-element.48.slots, s32[192]{0:T(256)S(4)} %get-tuple-element.49.rows, bf16[8,16,128]{2,1,0:T(8,128)(2,1)S(1)} %get-tuple-element.50._after.pot, bf16[8,16,128]{2,1,0:T(8,128)(2,1)S(1)} %collective-permute-done.8.refs_0_, ...), custom_call_target="tpu_custom_call" | custom-call | flops 100000000 | bytes 65536 | tf_op jit(solution)/shard_map/induct_tiles/pallas_call | solution.py:421
  26.9 0.3 collective-permute-start.12
  27.2 1.3 %collective-permute-start.11 = (bf16[12,16,128]{2,1,0:T(8,128)(2,1)S(1)}, bf16[12,16,128]{2,1,0:T(8,128)(2,1)S(1)}, u32[]{:S(2)}, u32[]{:S(2)}) collective-permute-start(bf16[12,16,128]{2,1,0:T(8,128)(2,1)S(1)} %hold_near.1), channel_id=1, source_target_pairs={{0,4},{4,0},{8,12},{12,8},{1,5},{5,1},{9,13},{13,9},{2,6},{6,2},{1... | collective-permute-start | bytes 147464 | tf_op jit(solution)/shard_map/ppermute | solution.py:20
  28.6 0.7 %base_sums.1 = (f32[32,16,128]{2,1,0:T(8,128)S(1)}, f32[4,16,128]{2,1,0:T(8,128)S(1)}, bf16[16,512]{1,0:T(8,128)(2,1)}) custom-call(s32[4,16]{1,0:T(4,128)S(4)} %get-tuple-element.34.links, s32[64]{0:T(128)S(4)} %get-tuple-element.35.holder, f32[16]{0:T(128)S(4)} %get-tuple-element.47.scale, s32[64,128]{1,0:T(8,128)S(1)} %get-tuple-element.36.lanes, ...), custom_call_target="tpu_custom_call" | custom-call | tf_op jit(solution)/shard_map/base_sums/pallas_call | solution.py:444
  29.3 0.0 collective-permute-done.6.message.refs_2_
  29.3 0.1 add_drops.2.field_in
  29.5 0.0 collective-permute-done.5.message.refs_1_
  29.5 0.1 add_drops.3.field_own
  29.6 1.7 %collective-permute-done.11.refs_0_ = bf16[12,16,128]{2,1,0:T(8,128)(2,1)S(1)} collective-permute-done((bf16[12,16,128]{2,1,0:T(8,128)(2,1)S(1)}, bf16[12,16,128]{2,1,0:T(8,128)(2,1)S(1)}, u32[]{:S(2)}, u32[]{:S(2)}) %collective-permute-start.11) | collective-permute-done | bytes 49184 | tf_op jit(solution)/shard_map/ppermute | solution.py:20
  31.3 0.6 %collective-permute-done.12.refs_3_ = bf16[32,16,128]{2,1,0:T(8,128)(2,1)S(1)} collective-permute-done((bf16[32,16,128]{2,1,0:T(8,128)(2,1)S(1)}, bf16[32,16,128]{2,1,0:T(8,128)(2,1)S(1)}, u32[]{:S(2)}, u32[]{:S(2)}) %collective-permute-start.12) | collective-permute-done | bytes 131104 | tf_op jit(solution)/shard_map/ppermute | solution.py:20
  31.9 0.8 %outputs.1 = (bf16[16,4096]{1,0:T(8,128)(2,1)}, bf16[16,512]{1,0:T(8,128)(2,1)}) custom-call(s32[4,16]{1,0:T(4,128)S(4)} %get-tuple-element.34.links, s32[64]{0:T(128)S(4)} %get-tuple-element.35.holder, s32[64,128]{1,0:T(8,128)S(1)} %get-tuple-element.36.lanes, f32[32,16,128]{2,1,0:T(8,128)S(1)} %add_drops.3.field_own, ...), custom_call_target="tpu_custom_call" | custom-call | flops 1000000000 | bytes 1048576 | tf_op jit(solution)/shard_map/outputs/pallas_call | solution.py:463
  (11 shorter events, 0.1 us)
Async XLA Ops:
  0.6 4.9 %collective-permute-start = (bf16[16,512]{1,0:T(8,128)(2,1)}, bf16[16,512]{1,0:T(8,128)(2,1)S(1)}, u32[]{:S(2)}, u32[]{:S(2)}) collective-permute-start(bf16[16,512]{1,0:T(8,128)(2,1)} %charge.1), channel_id=1, source_target_pairs={{0,2},{2,0},{1,3},{3,1},{4,6},{6,4},{5,7},{7,5},{8,10},{10,8},{9,1... | collective-permute-start | bytes 49160 | tf_op jit(solution)/shard_map/ppermute | solution.py:20
  3.6 13.7 %collective-permute-start.7 = (bf16[16,4096]{1,0:T(8,128)(2,1)}, bf16[16,4096]{1,0:T(8,128)(2,1)S(1)}, u32[]{:S(2)}, u32[]{:S(2)}) collective-permute-start(bf16[16,4096]{1,0:T(8,128)(2,1)} %refs_0_.1), channel_id=1, source_target_pairs={{0,2},{2,0},{1,3},{3,1},{4,6},{6,4},{5,7},{7,5},{8,10},{10,8},{9,1... | collective-permute-start | bytes 393224 | tf_op jit(solution)/shard_map/ppermute | solution.py:20
  3.7 21.7 %slice-start = ((s8[6291456]{0:T(1024)(128)(4,1)}), s8[4194304]{0:T(1024)(128)(4,1)S(1)}, s32[]{:S(2)}) async-start(s8[6291456]{0:T(1024)(128)(4,1)} %bitcast.2), calls=%async_computation | async-start | bytes 8388608
  5.6 7.0 %collective-permute-start.1 = (bf16[9,16,128]{2,1,0:T(8,128)(2,1)S(1)}, bf16[9,16,128]{2,1,0:T(8,128)(2,1)S(1)}, u32[]{:S(2)}, u32[]{:S(2)}) collective-permute-start(bf16[9,16,128]{2,1,0:T(8,128)(2,1)S(1)} %join_charges.1.refs_3_.pack), channel_id=1, source_target_pairs={{0,12},{4,8},{8,4},{12,0},{1,13},{5,9},{9,5},{13,1},{2,14},{6,10},... | collective-permute-start | bytes 110600 | tf_op jit(solution)/shard_map/ppermute | solution.py:20
  9.9 4.9 %collective-permute-start.2 = (bf16[9,16,128]{2,1,0:T(8,128)(2,1)S(1)}, bf16[9,16,128]{2,1,0:T(8,128)(2,1)S(1)}, u32[]{:S(2)}, u32[]{:S(2)}) collective-permute-start(bf16[9,16,128]{2,1,0:T(8,128)(2,1)S(1)} %join_charges.1.refs_3_.pack), channel_id=1, source_target_pairs={{0,8},{4,12},{8,0},{12,4},{1,9},{5,13},{9,1},{13,5},{2,10},{6,14},... | collective-permute-start | bytes 110600 | tf_op jit(solution)/shard_map/ppermute | solution.py:20
  9.9 4.9 %collective-permute-start.3 = (bf16[9,16,128]{2,1,0:T(8,128)(2,1)S(1)}, bf16[9,16,128]{2,1,0:T(8,128)(2,1)S(1)}, u32[]{:S(2)}, u32[]{:S(2)}) collective-permute-start(bf16[9,16,128]{2,1,0:T(8,128)(2,1)S(1)} %join_charges.1.refs_3_.pack), channel_id=1, source_target_pairs={{0,4},{4,0},{8,12},{12,8},{1,5},{5,1},{9,13},{13,9},{2,6},{6,2},{1... | collective-permute-start | bytes 110600 | tf_op jit(solution)/shard_map/ppermute | solution.py:20
  14.7 10.7 %slice-start.1 = ((s8[6291456]{0:T(1024)(128)(4,1)}), s8[2097152]{0:T(1024)(128)(4,1)S(1)}, s32[]{:S(2)}) async-start(s8[6291456]{0:T(1024)(128)(4,1)} %bitcast.2), calls=%async_computation.1 | async-start | bytes 4194304
  15.7 6.4 %collective-permute-start.4 = (bf16[32,16,128]{2,1,0:T(8,128)(2,1)S(1)}, bf16[32,16,128]{2,1,0:T(8,128)(2,1)S(1)}, u32[]{:S(2)}, u32[]{:S(2)}) collective-permute-start(bf16[32,16,128]{2,1,0:T(8,128)(2,1)S(1)} %get-tuple-element.44), channel_id=1, source_target_pairs={{0,2},{2,0},{1,3},{3,1},{4,6},{6,4},{5,7},{7,5},{8,10},{10,8},{9,1... | collective-permute-start | bytes 393224 | tf_op jit(solution)/shard_map/ppermute | solution.py:20
  17.6 6.2 %collective-permute-start.10 = (bf16[8,16,128]{2,1,0:T(8,128)(2,1)S(1)}, bf16[8,16,128]{2,1,0:T(8,128)(2,1)S(1)}, u32[]{:S(2)}, u32[]{:S(2)}) collective-permute-start(bf16[8,16,128]{2,1,0:T(8,128)(2,1)S(1)} %get-tuple-element.55), channel_id=1, source_target_pairs={{0,12},{4,8},{8,4},{12,0},{1,13},{5,9},{9,5},{13,1},{2,14},{6,10},... | collective-permute-start | bytes 98312 | tf_op jit(solution)/shard_map/ppermute | solution.py:20
  19.4 6.1 %collective-permute-start.8 = (bf16[8,16,128]{2,1,0:T(8,128)(2,1)S(1)}, bf16[8,16,128]{2,1,0:T(8,128)(2,1)S(1)}, u32[]{:S(2)}, u32[]{:S(2)}) collective-permute-start(bf16[8,16,128]{2,1,0:T(8,128)(2,1)S(1)} %get-tuple-element.52), channel_id=1, source_target_pairs={{0,8},{4,12},{8,0},{12,4},{1,9},{5,13},{9,1},{13,5},{2,10},{6,14},... | collective-permute-start | bytes 98312 | tf_op jit(solution)/shard_map/ppermute | solution.py:20
  19.8 5.7 %collective-permute-start.9 = (bf16[8,16,128]{2,1,0:T(8,128)(2,1)S(1)}, bf16[8,16,128]{2,1,0:T(8,128)(2,1)S(1)}, u32[]{:S(2)}, u32[]{:S(2)}) collective-permute-start(bf16[8,16,128]{2,1,0:T(8,128)(2,1)S(1)} %get-tuple-element.53), channel_id=1, source_target_pairs={{0,4},{4,0},{8,12},{12,8},{1,5},{5,1},{9,13},{13,9},{2,6},{6,2},{1... | collective-permute-start | bytes 98312 | tf_op jit(solution)/shard_map/ppermute | solution.py:20
  22.1 7.2 %collective-permute-start.6 = (bf16[12,16,128]{2,1,0:T(8,128)(2,1)S(1)}, bf16[12,16,128]{2,1,0:T(8,128)(2,1)S(1)}, u32[]{:S(2)}, u32[]{:S(2)}) collective-permute-start(bf16[12,16,128]{2,1,0:T(8,128)(2,1)S(1)} %get-tuple-element.46), channel_id=1, source_target_pairs={{0,12},{4,8},{8,4},{12,0},{1,13},{5,9},{9,5},{13,1},{2,14},{6,10},... | collective-permute-start | bytes 147464 | tf_op jit(solution)/shard_map/ppermute | solution.py:20
  23.8 5.6 %collective-permute-start.5 = (bf16[12,16,128]{2,1,0:T(8,128)(2,1)S(1)}, bf16[12,16,128]{2,1,0:T(8,128)(2,1)S(1)}, u32[]{:S(2)}, u32[]{:S(2)}) collective-permute-start(bf16[12,16,128]{2,1,0:T(8,128)(2,1)S(1)} %get-tuple-element.45), channel_id=1, source_target_pairs={{0,8},{4,12},{8,0},{12,4},{1,9},{5,13},{9,1},{13,5},{2,10},{6,14},... | collective-permute-start | bytes 147464 | tf_op jit(solution)/shard_map/ppermute | solution.py:20
  26.9 5.0 %collective-permute-start.12 = (bf16[32,16,128]{2,1,0:T(8,128)(2,1)S(1)}, bf16[32,16,128]{2,1,0:T(8,128)(2,1)S(1)}, u32[]{:S(2)}, u32[]{:S(2)}) collective-permute-start(bf16[32,16,128]{2,1,0:T(8,128)(2,1)S(1)} %get-tuple-element.61), channel_id=1, source_target_pairs={{0,2},{2,0},{1,3},{3,1},{4,6},{6,4},{5,7},{7,5},{8,10},{10,8},{9,1... | collective-permute-start | bytes 393224 | tf_op jit(solution)/shard_map/ppermute | solution.py:20
  27.2 4.1 %collective-permute-start.11 = (bf16[12,16,128]{2,1,0:T(8,128)(2,1)S(1)}, bf16[12,16,128]{2,1,0:T(8,128)(2,1)S(1)}, u32[]{:S(2)}, u32[]{:S(2)}) collective-permute-start(bf16[12,16,128]{2,1,0:T(8,128)(2,1)S(1)} %hold_near.1), channel_id=1, source_target_pairs={{0,4},{4,0},{8,12},{12,8},{1,5},{5,1},{9,13},{13,9},{2,6},{6,2},{1... | collective-permute-start | bytes 147464 | tf_op jit(solution)/shard_map/ppermute | solution.py:20

commit v13 on v11

--- a/solution.py
+++ b/solution.py
@@ -120,8 +120,9 @@
         copy.wait()
 
 
-def pick_body(n_row, n_col, cap, _after, *refs):
-    packs, own, peers = refs[:n_row][::-1], refs[n_row], refs[n_row + 1 : n_row + n_col]
+def pick_body(n_row, n_col, cap, partners, _after, *refs):
+    packs = {k: refs[i] for i, k in enumerate([*partners, 0])}
+    own, peers = refs[n_row], refs[n_row + 1 : n_row + n_col]
     outs, asked = refs[n_row + n_col : -1], refs[-1]
     seg_own, rhs, width = own.shape
     r, c = lax.axis_index("row"), lax.axis_index("col")
@@ -173,8 +174,8 @@
     lax.fori_loop(0, count // run, step, 0)
 
 
-def coeff_body(n_row, n_col, pan_own, slots, rows, needs, *refs):
-    packs = refs[:n_row][::-1]
+def coeff_body(n_row, n_col, pan_own, partners, slots, rows, needs, *refs):
+    packs = {k: refs[i] for i, k in enumerate([*partners, 0])}
     ends = refs[n_row : n_row + n_col - 1]
     tiles, part, *messages = refs[n_row + n_col - 1 : -2]
     src, named = refs[-2:]
@@ -326,6 +327,9 @@
     cap_l, cap_p, cap_k = induct_needs.shape[1], coeff_needs.shape[1], link_needs.shape[1]
     slots_t, off_t = end_slots.T, end_offsets.T
 
+    partners = [*reversed(range(1, n_row))]
+    partners[:2] = partners[1::-1]
+
     def like(blocks, dtype):
         return jax.ShapeDtypeStruct((blocks, rhs, width), dtype)
 
@@ -374,7 +378,7 @@
     holder, lanes, own_blocks, ends_own, *ends_out = outs[len(moved) :]
 
     part, *messages = call(
-        functools.partial(coeff_body, n_row, n_col, pan_own),
+        functools.partial(coeff_body, n_row, n_col, pan_own, partners),
         "coeff_tiles",
         [like(pan_group, F32)] + [like(2 * pan_group + rows_own, BF16)] * (n_col - 1),
         [SMEM] * 3 + [VMEM] * (n_row + n_col),
@@ -384,17 +388,17 @@
         ],
         flops=10**9,
         moved=coeff_tiles.size * 2,
-    )(coeff_slots, coeff_rows, coeff_needs, *packs[::-1], *ends_out, coeff_tiles)
+    )(coeff_slots, coeff_rows, coeff_needs, *[packs[k] for k in partners], packs[0], *ends_out, coeff_tiles)
     parts = exchange_all(None, messages, "col")[1:]
 
     *picks, own_picks = call(
-        functools.partial(pick_body, n_row, n_col, cap_l),
+        functools.partial(pick_body, n_row, n_col, cap_l, partners),
         "pick_blocks",
         [like(cap_l, BF16)] * n_row,
         [ANY] + [VMEM] * (n_row + n_col),
         [pltpu.VMEM((n_row, width), jnp.int32)],
         moved=2**18,
-    )(part, *packs[::-1], own_blocks, *cur[1:])
+    )(part, *[packs[k] for k in partners], packs[0], own_blocks, *cur[1:])
     got = exchange_all(own_picks, picks[::-1], "row")
 
     pot, end_keep, *row_messages = call(
@@ -406,7 +410,7 @@
         moved=2**18,
     )(part, ends_own, *parts)
 
-    order = [*range(n_row - 2, -1, -1), n_row - 1]
+    order = [*partners[1:], 0, partners[0]]
     field_own, *field_out = call(
         functools.partial(induct_body, n_row, n_col, seg_own, order),
         "induct_tiles",

time: 32.6 us -> 31.6 us (0.969)
  waiting for transfers between devices: 7.01 us -> 5.88 us
    ppermute x13, waiting for transfers between devices: 7.01 us -> 5.88 us  [exchange(): lax.ppermute(x, axis, [(i, i ^ k) for i in range(lax.axis_size(axis))])]
where the time goes in v13:
time: 31.6 us; the launch traced here: 31.5 us
  starting transfers between devices  17.7 us (56%)
  Pallas kernels  7.17 us (23%)
  waiting for transfers between devices  5.88 us (19%)
  between operations  0.72 us (2%)
    ppermute x13, starting transfers between devices, exchange(): lax.ppermute(x, axis, [(i, i ^ k) for i in range(lax.axis_size(axis))])  17.7 us
    ppermute x13, waiting for transfers between devices, exchange(): lax.ppermute(x, axis, [(i, i ^ k) for i in range(lax.axis_size(axis))])  5.88 us
    pallas_call x1, Pallas kernels, shards(): call(functools.partial(ends_body, n_row, n_col, pan_own, cap_k, len(moved...  2.09 us
    pallas_call x1, Pallas kernels, shards(): call(functools.partial(induct_body, n_row, n_col, seg_own, order), 'induc...  1.36 us
    pallas_call x1, Pallas kernels, shards(): call(functools.partial(pack_body, pan_own), 'pack_charges', [like(pan_own...  0.88 us
    pallas_call x1, Pallas kernels, shards(): call(functools.partial(final_body, n_row, n_col, pan_own), 'outputs', [ja...  0.84 us
    pallas_call x1, Pallas kernels, shards(): call(functools.partial(base_body, pan_own), 'base_sums', [like(seg_own, F...  0.72 us
    pallas_call x1, Pallas kernels, shards(): call(functools.partial(coeff_body, n_row, n_col, pan_own, partners), 'coe...  0.67 us
  transfers between devices with their start and end apart: 13, of which 5 were waited for; matrix products, arithmetic and copies ran while one was open for 0% of the time, Pallas kernels for 20%

profile of v13, /device:TPU:0, one launch (start us, length us, event | category | flops | bytes accessed | tf_op | source)
XLA Modules:
  0.0 31.5 jit_solution(6828225541951117280)
XLA Ops:
  0.6 3.0 %collective-permute-start = (bf16[16,512]{1,0:T(8,128)(2,1)}, bf16[16,512]{1,0:T(8,128)(2,1)S(1)}, u32[]{:S(2)}, u32[]{:S(2)}) collective-permute-start(bf16[16,512]{1,0:T(8,128)(2,1)} %charge.1), channel_id=1, source_target_pairs={{0,2},{2,0},{1,3},{3,1},{4,6},{6,4},{5,7},{7,5},{8,10},{10,8},{9,1... | collective-permute-start | bytes 49160 | tf_op jit(solution)/shard_map/ppermute | solution.py:20
  3.6 0.1 collective-permute-start.7
  3.7 0.9 %pack_charges.1.own = bf16[5,16,128]{2,1,0:T(8,128)(2,1)S(1)} custom-call(bf16[16,512]{1,0:T(8,128)(2,1)} %charge.1, s32[4,8]{1,0:T(4,128)} %needs.1), custom_call_target="tpu_custom_call" | custom-call | bytes 65536 | tf_op jit(solution)/shard_map/pack_charges/pallas_call | solution.py:338
  4.6 1.0 %collective-permute-done.refs_0_ = bf16[16,512]{1,0:T(8,128)(2,1)S(1)} collective-permute-done((bf16[16,512]{1,0:T(8,128)(2,1)}, bf16[16,512]{1,0:T(8,128)(2,1)S(1)}, u32[]{:S(2)}, u32[]{:S(2)}) %collective-permute-start) | collective-permute-done | bytes 16416 | tf_op jit(solution)/shard_map/ppermute | solution.py:20
  5.6 3.3 %collective-permute-start.1 = (bf16[9,16,128]{2,1,0:T(8,128)(2,1)S(1)}, bf16[9,16,128]{2,1,0:T(8,128)(2,1)S(1)}, u32[]{:S(2)}, u32[]{:S(2)}) collective-permute-start(bf16[9,16,128]{2,1,0:T(8,128)(2,1)S(1)} %join_charges.1.refs_3_.pack), channel_id=1, source_target_pairs={{0,8},{4,12},{8,0},{12,4},{1,9},{5,13},{9,1},{13,5},{2,10},{6,14},... | collective-permute-start | bytes 110600 | tf_op jit(solution)/shard_map/ppermute | solution.py:20
  8.8 1.3 %collective-permute-start.2 = (bf16[9,16,128]{2,1,0:T(8,128)(2,1)S(1)}, bf16[9,16,128]{2,1,0:T(8,128)(2,1)S(1)}, u32[]{:S(2)}, u32[]{:S(2)}) collective-permute-start(bf16[9,16,128]{2,1,0:T(8,128)(2,1)S(1)} %join_charges.1.refs_3_.pack), channel_id=1, source_target_pairs={{0,12},{4,8},{8,4},{12,0},{1,13},{5,9},{9,5},{13,1},{2,14},{6,10},... | collective-permute-start | bytes 110600 | tf_op jit(solution)/shard_map/ppermute | solution.py:20
  10.2 0.2 collective-permute-start.3
  10.4 2.1 %end_sums.1 = (s32[2,32]{1,0:T(2,128)S(4)}, s32[4,16]{1,0:T(4,128)S(4)}, s32[96]{0:T(128)S(4)}, s32[96]{0:T(128)S(4)}, s32[4,4]{1,0:T(4,128)S(4)}, /*index=5*/s3...) custom-call(bf16[16,4096]{1,0:T(8,128)(2,1)} %refs_0_.1, ...), custom_call_target="tpu_custom_call" | custom-call | flops 500000000 | bytes 262144 | tf_op jit(solution)/shard_map/end_sums/pallas_call | solution.py:358
  12.5 0.0 collective-permute-done.1.refs_0_
  12.5 2.1 %collective-permute-done.2.refs_1_ = bf16[9,16,128]{2,1,0:T(8,128)(2,1)S(1)} collective-permute-done((bf16[9,16,128]{2,1,0:T(8,128)(2,1)S(1)}, bf16[9,16,128]{2,1,0:T(8,128)(2,1)S(1)}, u32[]{:S(2)}, u32[]{:S(2)}) %collective-permute-start.2) | collective-permute-done | bytes 36896 | tf_op jit(solution)/shard_map/ppermute | solution.py:20
  14.6 0.7 %coeff_tiles.1 = (f32[8,16,128]{2,1,0:T(8,128)S(1)}, bf16[32,16,128]{2,1,0:T(8,128)(2,1)S(1)}) custom-call(s32[96]{0:T(128)S(4)} %get-tuple-element.37.slots, s32[96]{0:T(128)S(4)} %get-tuple-element.38.rows, s32[4,4]{1,0:T(4,128)S(4)} %get-tuple-element.39.needs, bf16[9,16,128]{2,1,0:T(8,128)(2,1)S(1)} %collective-permute-done.1.refs_0_, ...), custom_call_target="tpu_custom_call" | custom-call | flops 1000000000 | bytes 3145728 | tf_op jit(solution)/shard_map/coeff_tiles/pallas_call | solution.py:380
  15.3 1.6 %collective-permute-start.4 = (bf16[32,16,128]{2,1,0:T(8,128)(2,1)S(1)}, bf16[32,16,128]{2,1,0:T(8,128)(2,1)S(1)}, u32[]{:S(2)}, u32[]{:S(2)}) collective-permute-start(bf16[32,16,128]{2,1,0:T(8,128)(2,1)S(1)} %get-tuple-element.44), channel_id=1, source_target_pairs={{0,2},{2,0},{1,3},{3,1},{4,6},{6,4},{5,7},{7,5},{8,10},{10,8},{9,1... | collective-permute-start | bytes 393224 | tf_op jit(solution)/shard_map/ppermute | solution.py:20
  16.9 0.0 collective-permute-done.7.refs_5_
  16.9 0.3 pick_blocks.1
  17.2 1.3 %collective-permute-start.10 = (bf16[8,16,128]{2,1,0:T(8,128)(2,1)S(1)}, bf16[8,16,128]{2,1,0:T(8,128)(2,1)S(1)}, u32[]{:S(2)}, u32[]{:S(2)}) collective-permute-start(bf16[8,16,128]{2,1,0:T(8,128)(2,1)S(1)} %get-tuple-element.55), channel_id=1, source_target_pairs={{0,8},{4,12},{8,0},{12,4},{1,9},{5,13},{9,1},{13,5},{2,10},{6,14},... | collective-permute-start | bytes 98312 | tf_op jit(solution)/shard_map/ppermute | solution.py:20
  18.5 1.1 %collective-permute-start.8 = (bf16[8,16,128]{2,1,0:T(8,128)(2,1)S(1)}, bf16[8,16,128]{2,1,0:T(8,128)(2,1)S(1)}, u32[]{:S(2)}, u32[]{:S(2)}) collective-permute-start(bf16[8,16,128]{2,1,0:T(8,128)(2,1)S(1)} %get-tuple-element.52), channel_id=1, source_target_pairs={{0,12},{4,8},{8,4},{12,0},{1,13},{5,9},{9,5},{13,1},{2,14},{6,10},... | collective-permute-start | bytes 98312 | tf_op jit(solution)/shard_map/ppermute | solution.py:20
  19.6 1.2 %collective-permute-start.9 = (bf16[8,16,128]{2,1,0:T(8,128)(2,1)S(1)}, bf16[8,16,128]{2,1,0:T(8,128)(2,1)S(1)}, u32[]{:S(2)}, u32[]{:S(2)}) collective-permute-start(bf16[8,16,128]{2,1,0:T(8,128)(2,1)S(1)} %get-tuple-element.53), channel_id=1, source_target_pairs={{0,4},{4,0},{8,12},{12,8},{1,5},{5,1},{9,13},{13,9},{2,6},{6,2},{1... | collective-permute-start | bytes 98312 | tf_op jit(solution)/shard_map/ppermute | solution.py:20
  20.8 0.0 collective-permute-done.4.refs_0_
  20.8 2.1 %collective-permute-start.6 = (bf16[12,16,128]{2,1,0:T(8,128)(2,1)S(1)}, bf16[12,16,128]{2,1,0:T(8,128)(2,1)S(1)}, u32[]{:S(2)}, u32[]{:S(2)}) collective-permute-start(bf16[12,16,128]{2,1,0:T(8,128)(2,1)S(1)} %get-tuple-element.46), channel_id=1, source_target_pairs={{0,12},{4,8},{8,4},{12,0},{1,13},{5,9},{9,5},{13,1},{2,14},{6,10},... | collective-permute-start | bytes 147464 | tf_op jit(solution)/shard_map/ppermute | solution.py:20
  22.9 0.3 collective-permute-start.5
  23.1 0.0 collective-permute-done.10.refs_3_
  23.1 1.1 %collective-permute-done.8.refs_0_ = bf16[8,16,128]{2,1,0:T(8,128)(2,1)S(1)} collective-permute-done((bf16[8,16,128]{2,1,0:T(8,128)(2,1)S(1)}, bf16[8,16,128]{2,1,0:T(8,128)(2,1)S(1)}, u32[]{:S(2)}, u32[]{:S(2)}) %collective-permute-start.8) | collective-permute-done | bytes 32800 | tf_op jit(solution)/shard_map/ppermute | solution.py:20
  24.2 1.4 %induct_tiles.1 = (f32[32,16,128]{2,1,0:T(8,128)S(1)}, bf16[32,16,128]{2,1,0:T(8,128)(2,1)S(1)}) custom-call(s32[192]{0:T(256)S(4)} %get-tuple-element.48.slots, s32[192]{0:T(256)S(4)} %get-tuple-element.49.rows, bf16[8,16,128]{2,1,0:T(8,128)(2,1)S(1)} %get-tuple-element.50._after.pot, bf16[8,16,128]{2,1,0:T(8,128)(2,1)S(1)} %collective-permute-done.8.refs_0_, ...), custom_call_target="tpu_custom_call" | custom-call | flops 100000000 | bytes 65536 | tf_op jit(solution)/shard_map/induct_tiles/pallas_call | solution.py:414
  25.6 0.6 %collective-permute-start.12 = (bf16[32,16,128]{2,1,0:T(8,128)(2,1)S(1)}, bf16[32,16,128]{2,1,0:T(8,128)(2,1)S(1)}, u32[]{:S(2)}, u32[]{:S(2)}) collective-permute-start(bf16[32,16,128]{2,1,0:T(8,128)(2,1)S(1)} %get-tuple-element.61), channel_id=1, source_target_pairs={{0,2},{2,0},{1,3},{3,1},{4,6},{6,4},{5,7},{7,5},{8,10},{10,8},{9,1... | collective-permute-start | bytes 393224 | tf_op jit(solution)/shard_map/ppermute | solution.py:20
  26.3 1.6 %collective-permute-start.11 = (bf16[12,16,128]{2,1,0:T(8,128)(2,1)S(1)}, bf16[12,16,128]{2,1,0:T(8,128)(2,1)S(1)}, u32[]{:S(2)}, u32[]{:S(2)}) collective-permute-start(bf16[12,16,128]{2,1,0:T(8,128)(2,1)S(1)} %hold_near.1), channel_id=1, source_target_pairs={{0,4},{4,0},{8,12},{12,8},{1,5},{5,1},{9,13},{13,9},{2,6},{6,2},{1... | collective-permute-start | bytes 147464 | tf_op jit(solution)/shard_map/ppermute | solution.py:20
  27.8 0.7 %base_sums.1 = (f32[32,16,128]{2,1,0:T(8,128)S(1)}, f32[4,16,128]{2,1,0:T(8,128)S(1)}, bf16[16,512]{1,0:T(8,128)(2,1)}) custom-call(s32[4,16]{1,0:T(4,128)S(4)} %get-tuple-element.34.links, s32[64]{0:T(128)S(4)} %get-tuple-element.35.holder, f32[16]{0:T(128)S(4)} %get-tuple-element.47.scale, s32[64,128]{1,0:T(8,128)S(1)} %get-tuple-element.36.lanes, ...), custom_call_target="tpu_custom_call" | custom-call | tf_op jit(solution)/shard_map/base_sums/pallas_call | solution.py:437
  28.6 0.1 add_drops.2.field_in
  28.7 0.0 collective-permute-done.5.message.refs_1_
  28.7 0.1 add_drops.3.field_own
  28.9 1.5 %collective-permute-done.11.refs_0_ = bf16[12,16,128]{2,1,0:T(8,128)(2,1)S(1)} collective-permute-done((bf16[12,16,128]{2,1,0:T(8,128)(2,1)S(1)}, bf16[12,16,128]{2,1,0:T(8,128)(2,1)S(1)}, u32[]{:S(2)}, u32[]{:S(2)}) %collective-permute-start.11) | collective-permute-done | bytes 49184 | tf_op jit(solution)/shard_map/ppermute | solution.py:20
  30.3 0.3 collective-permute-done.12.refs_3_
  30.6 0.8 %outputs.1 = (bf16[16,4096]{1,0:T(8,128)(2,1)}, bf16[16,512]{1,0:T(8,128)(2,1)}) custom-call(s32[4,16]{1,0:T(4,128)S(4)} %get-tuple-element.34.links, s32[64]{0:T(128)S(4)} %get-tuple-element.35.holder, s32[64,128]{1,0:T(8,128)S(1)} %get-tuple-element.36.lanes, f32[32,16,128]{2,1,0:T(8,128)S(1)} %add_drops.3.field_own, ...), custom_call_target="tpu_custom_call" | custom-call | flops 1000000000 | bytes 1048576 | tf_op jit(solution)/shard_map/outputs/pallas_call | solution.py:456
  (11 shorter events, 0.1 us)
Async XLA Ops:
  0.6 4.9 %collective-permute-start = (bf16[16,512]{1,0:T(8,128)(2,1)}, bf16[16,512]{1,0:T(8,128)(2,1)S(1)}, u32[]{:S(2)}, u32[]{:S(2)}) collective-permute-start(bf16[16,512]{1,0:T(8,128)(2,1)} %charge.1), channel_id=1, source_target_pairs={{0,2},{2,0},{1,3},{3,1},{4,6},{6,4},{5,7},{7,5},{8,10},{10,8},{9,1... | collective-permute-start | bytes 49160 | tf_op jit(solution)/shard_map/ppermute | solution.py:20
  3.6 13.3 %collective-permute-start.7 = (bf16[16,4096]{1,0:T(8,128)(2,1)}, bf16[16,4096]{1,0:T(8,128)(2,1)S(1)}, u32[]{:S(2)}, u32[]{:S(2)}) collective-permute-start(bf16[16,4096]{1,0:T(8,128)(2,1)} %refs_0_.1), channel_id=1, source_target_pairs={{0,2},{2,0},{1,3},{3,1},{4,6},{6,4},{5,7},{7,5},{8,10},{10,8},{9,1... | collective-permute-start | bytes 393224 | tf_op jit(solution)/shard_map/ppermute | solution.py:20
  3.7 20.5 %slice-start = ((s8[6291456]{0:T(1024)(128)(4,1)}), s8[4194304]{0:T(1024)(128)(4,1)S(1)}, s32[]{:S(2)}) async-start(s8[6291456]{0:T(1024)(128)(4,1)} %bitcast.2), calls=%async_computation | async-start | bytes 8388608
  5.6 7.0 %collective-permute-start.1 = (bf16[9,16,128]{2,1,0:T(8,128)(2,1)S(1)}, bf16[9,16,128]{2,1,0:T(8,128)(2,1)S(1)}, u32[]{:S(2)}, u32[]{:S(2)}) collective-permute-start(bf16[9,16,128]{2,1,0:T(8,128)(2,1)S(1)} %join_charges.1.refs_3_.pack), channel_id=1, source_target_pairs={{0,8},{4,12},{8,0},{12,4},{1,9},{5,13},{9,1},{13,5},{2,10},{6,14},... | collective-permute-start | bytes 110600 | tf_op jit(solution)/shard_map/ppermute | solution.py:20
  8.8 5.8 %collective-permute-start.2 = (bf16[9,16,128]{2,1,0:T(8,128)(2,1)S(1)}, bf16[9,16,128]{2,1,0:T(8,128)(2,1)S(1)}, u32[]{:S(2)}, u32[]{:S(2)}) collective-permute-start(bf16[9,16,128]{2,1,0:T(8,128)(2,1)S(1)} %join_charges.1.refs_3_.pack), channel_id=1, source_target_pairs={{0,12},{4,8},{8,4},{12,0},{1,13},{5,9},{9,5},{13,1},{2,14},{6,10},... | collective-permute-start | bytes 110600 | tf_op jit(solution)/shard_map/ppermute | solution.py:20
  10.2 4.4 %collective-permute-start.3 = (bf16[9,16,128]{2,1,0:T(8,128)(2,1)S(1)}, bf16[9,16,128]{2,1,0:T(8,128)(2,1)S(1)}, u32[]{:S(2)}, u32[]{:S(2)}) collective-permute-start(bf16[9,16,128]{2,1,0:T(8,128)(2,1)S(1)} %join_charges.1.refs_3_.pack), channel_id=1, source_target_pairs={{0,4},{4,0},{8,12},{12,8},{1,5},{5,1},{9,13},{13,9},{2,6},{6,2},{1... | collective-permute-start | bytes 110600 | tf_op jit(solution)/shard_map/ppermute | solution.py:20
  14.6 9.6 %slice-start.1 = ((s8[6291456]{0:T(1024)(128)(4,1)}), s8[2097152]{0:T(1024)(128)(4,1)S(1)}, s32[]{:S(2)}) async-start(s8[6291456]{0:T(1024)(128)(4,1)} %bitcast.2), calls=%async_computation.1 | async-start | bytes 4194304
  15.3 5.5 %collective-permute-start.4 = (bf16[32,16,128]{2,1,0:T(8,128)(2,1)S(1)}, bf16[32,16,128]{2,1,0:T(8,128)(2,1)S(1)}, u32[]{:S(2)}, u32[]{:S(2)}) collective-permute-start(bf16[32,16,128]{2,1,0:T(8,128)(2,1)S(1)} %get-tuple-element.44), channel_id=1, source_target_pairs={{0,2},{2,0},{1,3},{3,1},{4,6},{6,4},{5,7},{7,5},{8,10},{10,8},{9,1... | collective-permute-start | bytes 393224 | tf_op jit(solution)/shard_map/ppermute | solution.py:20
  17.2 5.9 %collective-permute-start.10 = (bf16[8,16,128]{2,1,0:T(8,128)(2,1)S(1)}, bf16[8,16,128]{2,1,0:T(8,128)(2,1)S(1)}, u32[]{:S(2)}, u32[]{:S(2)}) collective-permute-start(bf16[8,16,128]{2,1,0:T(8,128)(2,1)S(1)} %get-tuple-element.55), channel_id=1, source_target_pairs={{0,8},{4,12},{8,0},{12,4},{1,9},{5,13},{9,1},{13,5},{2,10},{6,14},... | collective-permute-start | bytes 98312 | tf_op jit(solution)/shard_map/ppermute | solution.py:20
  18.5 5.7 %collective-permute-start.8 = (bf16[8,16,128]{2,1,0:T(8,128)(2,1)S(1)}, bf16[8,16,128]{2,1,0:T(8,128)(2,1)S(1)}, u32[]{:S(2)}, u32[]{:S(2)}) collective-permute-start(bf16[8,16,128]{2,1,0:T(8,128)(2,1)S(1)} %get-tuple-element.52), channel_id=1, source_target_pairs={{0,12},{4,8},{8,4},{12,0},{1,13},{5,9},{9,5},{13,1},{2,14},{6,10},... | collective-permute-start | bytes 98312 | tf_op jit(solution)/shard_map/ppermute | solution.py:20
  19.6 4.7 %collective-permute-start.9 = (bf16[8,16,128]{2,1,0:T(8,128)(2,1)S(1)}, bf16[8,16,128]{2,1,0:T(8,128)(2,1)S(1)}, u32[]{:S(2)}, u32[]{:S(2)}) collective-permute-start(bf16[8,16,128]{2,1,0:T(8,128)(2,1)S(1)} %get-tuple-element.53), channel_id=1, source_target_pairs={{0,4},{4,0},{8,12},{12,8},{1,5},{5,1},{9,13},{13,9},{2,6},{6,2},{1... | collective-permute-start | bytes 98312 | tf_op jit(solution)/shard_map/ppermute | solution.py:20
  20.8 7.8 %collective-permute-start.6 = (bf16[12,16,128]{2,1,0:T(8,128)(2,1)S(1)}, bf16[12,16,128]{2,1,0:T(8,128)(2,1)S(1)}, u32[]{:S(2)}, u32[]{:S(2)}) collective-permute-start(bf16[12,16,128]{2,1,0:T(8,128)(2,1)S(1)} %get-tuple-element.46), channel_id=1, source_target_pairs={{0,12},{4,8},{8,4},{12,0},{1,13},{5,9},{9,5},{13,1},{2,14},{6,10},... | collective-permute-start | bytes 147464 | tf_op jit(solution)/shard_map/ppermute | solution.py:20
  22.9 5.8 %collective-permute-start.5 = (bf16[12,16,128]{2,1,0:T(8,128)(2,1)S(1)}, bf16[12,16,128]{2,1,0:T(8,128)(2,1)S(1)}, u32[]{:S(2)}, u32[]{:S(2)}) collective-permute-start(bf16[12,16,128]{2,1,0:T(8,128)(2,1)S(1)} %get-tuple-element.45), channel_id=1, source_target_pairs={{0,8},{4,12},{8,0},{12,4},{1,9},{5,13},{9,1},{13,5},{2,10},{6,14},... | collective-permute-start | bytes 147464 | tf_op jit(solution)/shard_map/ppermute | solution.py:20
  25.6 5.0 %collective-permute-start.12 = (bf16[32,16,128]{2,1,0:T(8,128)(2,1)S(1)}, bf16[32,16,128]{2,1,0:T(8,128)(2,1)S(1)}, u32[]{:S(2)}, u32[]{:S(2)}) collective-permute-start(bf16[32,16,128]{2,1,0:T(8,128)(2,1)S(1)} %get-tuple-element.61), channel_id=1, source_target_pairs={{0,2},{2,0},{1,3},{3,1},{4,6},{6,4},{5,7},{7,5},{8,10},{10,8},{9,1... | collective-permute-start | bytes 393224 | tf_op jit(solution)/shard_map/ppermute | solution.py:20
  26.3 4.1 %collective-permute-start.11 = (bf16[12,16,128]{2,1,0:T(8,128)(2,1)S(1)}, bf16[12,16,128]{2,1,0:T(8,128)(2,1)S(1)}, u32[]{:S(2)}, u32[]{:S(2)}) collective-permute-start(bf16[12,16,128]{2,1,0:T(8,128)(2,1)S(1)} %hold_near.1), channel_id=1, source_target_pairs={{0,4},{4,0},{8,12},{12,8},{1,5},{5,1},{9,13},{13,9},{2,6},{6,2},{1... | collective-permute-start | bytes 147464 | tf_op jit(solution)/shard_map/ppermute | solution.py:20

commit v14 on v13

--- a/solution.py
+++ b/solution.py
@@ -443,13 +443,13 @@
         moved=0,
     )(links_s, holder, scale, lanes, pack, field_own, end_keep, pot)
 
-    for k in reversed(range(2, n_row)):
+    for k in partners[:-1]:
         (field,) = call(
             functools.partial(drops_body, k, pan_own),
             "add_drops",
             [like(seg_own, F32)],
             [SMEM] * 2 + [VMEM] * 3,
-            flops=11 * 10**8 if k == 2 else 0,
+            flops=11 * 10**8 if k == partners[-2] else 0,
             moved=0,
         )(links_s, holder, lanes, arrived[k - 1], field)
 

time: 31.6 us -> 31.8 us (level)
  transfers between devices with their start and end apart: 13 -> 13, of which waited for: 5 -> 7; matrix products, arithmetic and copies ran while one was open for 0% -> 0% of each run, Pallas kernels for 20% -> 20%
where the time goes in v14:
time: 31.8 us; the launch traced here: 31.6 us
  starting transfers between devices  17.6 us (55%)
  Pallas kernels  7.17 us (23%)
  waiting for transfers between devices  6.18 us (19%)
  between operations  0.69 us (2%)
    ppermute x13, starting transfers between devices, exchange(): lax.ppermute(x, axis, [(i, i ^ k) for i in range(lax.axis_size(axis))])  17.6 us
    ppermute x13, waiting for transfers between devices, exchange(): lax.ppermute(x, axis, [(i, i ^ k) for i in range(lax.axis_size(axis))])  6.18 us
    pallas_call x1, Pallas kernels, shards(): call(functools.partial(ends_body, n_row, n_col, pan_own, cap_k, len(moved...  2.09 us
    pallas_call x1, Pallas kernels, shards(): call(functools.partial(induct_body, n_row, n_col, seg_own, order), 'induc...  1.36 us
    pallas_call x1, Pallas kernels, shards(): call(functools.partial(pack_body, pan_own), 'pack_charges', [like(pan_own...  0.88 us
    pallas_call x1, Pallas kernels, shards(): call(functools.partial(final_body, n_row, n_col, pan_own), 'outputs', [ja...  0.83 us
    pallas_call x1, Pallas kernels, shards(): call(functools.partial(base_body, pan_own), 'base_sums', [like(seg_own, F...  0.72 us
    pallas_call x1, Pallas kernels, shards(): call(functools.partial(coeff_body, n_row, n_col, pan_own, partners), 'coe...  0.67 us
  transfers between devices with their start and end apart: 13, of which 7 were waited for; matrix products, arithmetic and copies ran while one was open for 0% of the time, Pallas kernels for 20%

profile of v14, /device:TPU:0, one launch (start us, length us, event | category | flops | bytes accessed | tf_op | source)
XLA Modules:
  0.0 31.6 jit_solution(7148659760714524778)
XLA Ops:
  0.6 3.0 %collective-permute-start = (bf16[16,512]{1,0:T(8,128)(2,1)}, bf16[16,512]{1,0:T(8,128)(2,1)S(1)}, u32[]{:S(2)}, u32[]{:S(2)}) collective-permute-start(bf16[16,512]{1,0:T(8,128)(2,1)} %charge.1), channel_id=1, source_target_pairs={{0,2},{2,0},{1,3},{3,1},{4,6},{6,4},{5,7},{7,5},{8,10},{10,8},{9,1... | collective-permute-start | bytes 49160 | tf_op jit(solution)/shard_map/ppermute | solution.py:20
  3.6 0.1 collective-permute-start.7
  3.7 0.9 %pack_charges.1.own = bf16[5,16,128]{2,1,0:T(8,128)(2,1)S(1)} custom-call(bf16[16,512]{1,0:T(8,128)(2,1)} %charge.1, s32[4,8]{1,0:T(4,128)} %needs.1), custom_call_target="tpu_custom_call" | custom-call | bytes 65536 | tf_op jit(solution)/shard_map/pack_charges/pallas_call | solution.py:338
  4.6 1.0 %collective-permute-done.refs_0_ = bf16[16,512]{1,0:T(8,128)(2,1)S(1)} collective-permute-done((bf16[16,512]{1,0:T(8,128)(2,1)}, bf16[16,512]{1,0:T(8,128)(2,1)S(1)}, u32[]{:S(2)}, u32[]{:S(2)}) %collective-permute-start) | collective-permute-done | bytes 16416 | tf_op jit(solution)/shard_map/ppermute | solution.py:20
  5.6 3.3 %collective-permute-start.1 = (bf16[9,16,128]{2,1,0:T(8,128)(2,1)S(1)}, bf16[9,16,128]{2,1,0:T(8,128)(2,1)S(1)}, u32[]{:S(2)}, u32[]{:S(2)}) collective-permute-start(bf16[9,16,128]{2,1,0:T(8,128)(2,1)S(1)} %join_charges.1.refs_3_.pack), channel_id=1, source_target_pairs={{0,8},{4,12},{8,0},{12,4},{1,9},{5,13},{9,1},{13,5},{2,10},{6,14},... | collective-permute-start | bytes 110600 | tf_op jit(solution)/shard_map/ppermute | solution.py:20
  8.8 1.3 %collective-permute-start.2 = (bf16[9,16,128]{2,1,0:T(8,128)(2,1)S(1)}, bf16[9,16,128]{2,1,0:T(8,128)(2,1)S(1)}, u32[]{:S(2)}, u32[]{:S(2)}) collective-permute-start(bf16[9,16,128]{2,1,0:T(8,128)(2,1)S(1)} %join_charges.1.refs_3_.pack), channel_id=1, source_target_pairs={{0,12},{4,8},{8,4},{12,0},{1,13},{5,9},{9,5},{13,1},{2,14},{6,10},... | collective-permute-start | bytes 110600 | tf_op jit(solution)/shard_map/ppermute | solution.py:20
  10.2 0.2 collective-permute-start.3
  10.4 2.1 %end_sums.1 = (s32[2,32]{1,0:T(2,128)S(4)}, s32[4,16]{1,0:T(4,128)S(4)}, s32[96]{0:T(128)S(4)}, s32[96]{0:T(128)S(4)}, s32[4,4]{1,0:T(4,128)S(4)}, /*index=5*/s3...) custom-call(bf16[16,4096]{1,0:T(8,128)(2,1)} %refs_0_.1, ...), custom_call_target="tpu_custom_call" | custom-call | flops 500000000 | bytes 262144 | tf_op jit(solution)/shard_map/end_sums/pallas_call | solution.py:358
  12.5 0.0 collective-permute-done.1.refs_0_
  12.5 2.1 %collective-permute-done.2.refs_1_ = bf16[9,16,128]{2,1,0:T(8,128)(2,1)S(1)} collective-permute-done((bf16[9,16,128]{2,1,0:T(8,128)(2,1)S(1)}, bf16[9,16,128]{2,1,0:T(8,128)(2,1)S(1)}, u32[]{:S(2)}, u32[]{:S(2)}) %collective-permute-start.2) | collective-permute-done | bytes 36896 | tf_op jit(solution)/shard_map/ppermute | solution.py:20
  14.6 0.7 %coeff_tiles.1 = (f32[8,16,128]{2,1,0:T(8,128)S(1)}, bf16[32,16,128]{2,1,0:T(8,128)(2,1)S(1)}) custom-call(s32[96]{0:T(128)S(4)} %get-tuple-element.37.slots, s32[96]{0:T(128)S(4)} %get-tuple-element.38.rows, s32[4,4]{1,0:T(4,128)S(4)} %get-tuple-element.39.needs, bf16[9,16,128]{2,1,0:T(8,128)(2,1)S(1)} %collective-permute-done.1.refs_0_, ...), custom_call_target="tpu_custom_call" | custom-call | flops 1000000000 | bytes 3145728 | tf_op jit(solution)/shard_map/coeff_tiles/pallas_call | solution.py:380
  15.3 1.6 %collective-permute-start.4 = (bf16[32,16,128]{2,1,0:T(8,128)(2,1)S(1)}, bf16[32,16,128]{2,1,0:T(8,128)(2,1)S(1)}, u32[]{:S(2)}, u32[]{:S(2)}) collective-permute-start(bf16[32,16,128]{2,1,0:T(8,128)(2,1)S(1)} %get-tuple-element.44), channel_id=1, source_target_pairs={{0,2},{2,0},{1,3},{3,1},{4,6},{6,4},{5,7},{7,5},{8,10},{10,8},{9,1... | collective-permute-start | bytes 393224 | tf_op jit(solution)/shard_map/ppermute | solution.py:20
  16.9 0.3 pick_blocks.1
  17.2 1.3 %collective-permute-start.10 = (bf16[8,16,128]{2,1,0:T(8,128)(2,1)S(1)}, bf16[8,16,128]{2,1,0:T(8,128)(2,1)S(1)}, u32[]{:S(2)}, u32[]{:S(2)}) collective-permute-start(bf16[8,16,128]{2,1,0:T(8,128)(2,1)S(1)} %get-tuple-element.55), channel_id=1, source_target_pairs={{0,8},{4,12},{8,0},{12,4},{1,9},{5,13},{9,1},{13,5},{2,10},{6,14},... | collective-permute-start | bytes 98312 | tf_op jit(solution)/shard_map/ppermute | solution.py:20
  18.5 1.1 %collective-permute-start.8 = (bf16[8,16,128]{2,1,0:T(8,128)(2,1)S(1)}, bf16[8,16,128]{2,1,0:T(8,128)(2,1)S(1)}, u32[]{:S(2)}, u32[]{:S(2)}) collective-permute-start(bf16[8,16,128]{2,1,0:T(8,128)(2,1)S(1)} %get-tuple-element.52), channel_id=1, source_target_pairs={{0,12},{4,8},{8,4},{12,0},{1,13},{5,9},{9,5},{13,1},{2,14},{6,10},... | collective-permute-start | bytes 98312 | tf_op jit(solution)/shard_map/ppermute | solution.py:20
  19.6 1.2 %collective-permute-start.9 = (bf16[8,16,128]{2,1,0:T(8,128)(2,1)S(1)}, bf16[8,16,128]{2,1,0:T(8,128)(2,1)S(1)}, u32[]{:S(2)}, u32[]{:S(2)}) collective-permute-start(bf16[8,16,128]{2,1,0:T(8,128)(2,1)S(1)} %get-tuple-element.53), channel_id=1, source_target_pairs={{0,4},{4,0},{8,12},{12,8},{1,5},{5,1},{9,13},{13,9},{2,6},{6,2},{1... | collective-permute-start | bytes 98312 | tf_op jit(solution)/shard_map/ppermute | solution.py:20
  20.8 2.2 %collective-permute-start.6 = (bf16[12,16,128]{2,1,0:T(8,128)(2,1)S(1)}, bf16[12,16,128]{2,1,0:T(8,128)(2,1)S(1)}, u32[]{:S(2)}, u32[]{:S(2)}) collective-permute-start(bf16[12,16,128]{2,1,0:T(8,128)(2,1)S(1)} %get-tuple-element.46), channel_id=1, source_target_pairs={{0,8},{4,12},{8,0},{12,4},{1,9},{5,13},{9,1},{13,5},{2,10},{6,14},... | collective-permute-start | bytes 147464 | tf_op jit(solution)/shard_map/ppermute | solution.py:20
  23.0 1.0 %collective-permute-start.5 = (bf16[12,16,128]{2,1,0:T(8,128)(2,1)S(1)}, bf16[12,16,128]{2,1,0:T(8,128)(2,1)S(1)}, u32[]{:S(2)}, u32[]{:S(2)}) collective-permute-start(bf16[12,16,128]{2,1,0:T(8,128)(2,1)S(1)} %get-tuple-element.45), channel_id=1, source_target_pairs={{0,12},{4,8},{8,4},{12,0},{1,13},{5,9},{9,5},{13,1},{2,14},{6,10},... | collective-permute-start | bytes 147464 | tf_op jit(solution)/shard_map/ppermute | solution.py:20
  24.0 0.0 collective-permute-done.10.refs_3_
  24.0 0.2 collective-permute-done.8.refs_0_
  24.3 0.1 collective-permute-done.9.refs_1_
  24.4 1.4 %induct_tiles.1 = (f32[32,16,128]{2,1,0:T(8,128)S(1)}, bf16[32,16,128]{2,1,0:T(8,128)(2,1)S(1)}) custom-call(s32[192]{0:T(256)S(4)} %get-tuple-element.48.slots, s32[192]{0:T(256)S(4)} %get-tuple-element.49.rows, bf16[8,16,128]{2,1,0:T(8,128)(2,1)S(1)} %get-tuple-element.50._after.pot, bf16[8,16,128]{2,1,0:T(8,128)(2,1)S(1)} %collective-permute-done.8.refs_0_, ...), custom_call_target="tpu_custom_call" | custom-call | flops 100000000 | bytes 65536 | tf_op jit(solution)/shard_map/induct_tiles/pallas_call | solution.py:414
  25.7 0.7 %collective-permute-start.12 = (bf16[32,16,128]{2,1,0:T(8,128)(2,1)S(1)}, bf16[32,16,128]{2,1,0:T(8,128)(2,1)S(1)}, u32[]{:S(2)}, u32[]{:S(2)}) collective-permute-start(bf16[32,16,128]{2,1,0:T(8,128)(2,1)S(1)} %get-tuple-element.61), channel_id=1, source_target_pairs={{0,2},{2,0},{1,3},{3,1},{4,6},{6,4},{5,7},{7,5},{8,10},{10,8},{9,1... | collective-permute-start | bytes 393224 | tf_op jit(solution)/shard_map/ppermute | solution.py:20
  26.5 0.5 %collective-permute-start.11 = (bf16[12,16,128]{2,1,0:T(8,128)(2,1)S(1)}, bf16[12,16,128]{2,1,0:T(8,128)(2,1)S(1)}, u32[]{:S(2)}, u32[]{:S(2)}) collective-permute-start(bf16[12,16,128]{2,1,0:T(8,128)(2,1)S(1)} %hold_near.1), channel_id=1, source_target_pairs={{0,4},{4,0},{8,12},{12,8},{1,5},{5,1},{9,13},{13,9},{2,6},{6,2},{1... | collective-permute-start | bytes 147464 | tf_op jit(solution)/shard_map/ppermute | solution.py:20
  26.9 0.7 %base_sums.1 = (f32[32,16,128]{2,1,0:T(8,128)S(1)}, f32[4,16,128]{2,1,0:T(8,128)S(1)}, bf16[16,512]{1,0:T(8,128)(2,1)}) custom-call(s32[4,16]{1,0:T(4,128)S(4)} %get-tuple-element.34.links, s32[64]{0:T(128)S(4)} %get-tuple-element.35.holder, f32[16]{0:T(128)S(4)} %get-tuple-element.47.scale, s32[64,128]{1,0:T(8,128)S(1)} %get-tuple-element.36.lanes, ...), custom_call_target="tpu_custom_call" | custom-call | tf_op jit(solution)/shard_map/base_sums/pallas_call | solution.py:437
  27.7 0.0 collective-permute-done.6.message.refs_1_
  27.7 0.1 add_drops.2.field_in
  27.8 1.1 %collective-permute-done.5.message.refs_2_ = bf16[12,16,128]{2,1,0:T(8,128)(2,1)S(1)} collective-permute-done((bf16[12,16,128]{2,1,0:T(8,128)(2,1)S(1)}, bf16[12,16,128]{2,1,0:T(8,128)(2,1)S(1)}, u32[]{:S(2)}, u32[]{:S(2)}) %collective-permute-start.5) | collective-permute-done | bytes 49184 | tf_op jit(solution)/shard_map/ppermute | solution.py:20
  28.9 0.1 add_drops.3.field_own
  29.0 1.5 %collective-permute-done.11.refs_0_ = bf16[12,16,128]{2,1,0:T(8,128)(2,1)S(1)} collective-permute-done((bf16[12,16,128]{2,1,0:T(8,128)(2,1)S(1)}, bf16[12,16,128]{2,1,0:T(8,128)(2,1)S(1)}, u32[]{:S(2)}, u32[]{:S(2)}) %collective-permute-start.11) | collective-permute-done | bytes 49184 | tf_op jit(solution)/shard_map/ppermute | solution.py:20
  30.6 0.2 collective-permute-done.12.refs_3_
  30.8 0.8 %outputs.1 = (bf16[16,4096]{1,0:T(8,128)(2,1)}, bf16[16,512]{1,0:T(8,128)(2,1)}) custom-call(s32[4,16]{1,0:T(4,128)S(4)} %get-tuple-element.34.links, s32[64]{0:T(128)S(4)} %get-tuple-element.35.holder, s32[64,128]{1,0:T(8,128)S(1)} %get-tuple-element.36.lanes, f32[32,16,128]{2,1,0:T(8,128)S(1)} %add_drops.3.field_own, ...), custom_call_target="tpu_custom_call" | custom-call | flops 1000000000 | bytes 1048576 | tf_op jit(solution)/shard_map/outputs/pallas_call | solution.py:456
  (11 shorter events, 0.1 us)
Async XLA Ops:
  0.6 4.9 %collective-permute-start = (bf16[16,512]{1,0:T(8,128)(2,1)}, bf16[16,512]{1,0:T(8,128)(2,1)S(1)}, u32[]{:S(2)}, u32[]{:S(2)}) collective-permute-start(bf16[16,512]{1,0:T(8,128)(2,1)} %charge.1), channel_id=1, source_target_pairs={{0,2},{2,0},{1,3},{3,1},{4,6},{6,4},{5,7},{7,5},{8,10},{10,8},{9,1... | collective-permute-start | bytes 49160 | tf_op jit(solution)/shard_map/ppermute | solution.py:20
  3.6 13.3 %collective-permute-start.7 = (bf16[16,4096]{1,0:T(8,128)(2,1)}, bf16[16,4096]{1,0:T(8,128)(2,1)S(1)}, u32[]{:S(2)}, u32[]{:S(2)}) collective-permute-start(bf16[16,4096]{1,0:T(8,128)(2,1)} %refs_0_.1), channel_id=1, source_target_pairs={{0,2},{2,0},{1,3},{3,1},{4,6},{6,4},{5,7},{7,5},{8,10},{10,8},{9,1... | collective-permute-start | bytes 393224 | tf_op jit(solution)/shard_map/ppermute | solution.py:20
  3.7 20.7 %slice-start = ((s8[6291456]{0:T(1024)(128)(4,1)}), s8[4194304]{0:T(1024)(128)(4,1)S(1)}, s32[]{:S(2)}) async-start(s8[6291456]{0:T(1024)(128)(4,1)} %bitcast.2), calls=%async_computation | async-start | bytes 8388608
  5.6 7.0 %collective-permute-start.1 = (bf16[9,16,128]{2,1,0:T(8,128)(2,1)S(1)}, bf16[9,16,128]{2,1,0:T(8,128)(2,1)S(1)}, u32[]{:S(2)}, u32[]{:S(2)}) collective-permute-start(bf16[9,16,128]{2,1,0:T(8,128)(2,1)S(1)} %join_charges.1.refs_3_.pack), channel_id=1, source_target_pairs={{0,8},{4,12},{8,0},{12,4},{1,9},{5,13},{9,1},{13,5},{2,10},{6,14},... | collective-permute-start | bytes 110600 | tf_op jit(solution)/shard_map/ppermute | solution.py:20
  8.8 5.8 %collective-permute-start.2 = (bf16[9,16,128]{2,1,0:T(8,128)(2,1)S(1)}, bf16[9,16,128]{2,1,0:T(8,128)(2,1)S(1)}, u32[]{:S(2)}, u32[]{:S(2)}) collective-permute-start(bf16[9,16,128]{2,1,0:T(8,128)(2,1)S(1)} %join_charges.1.refs_3_.pack), channel_id=1, source_target_pairs={{0,12},{4,8},{8,4},{12,0},{1,13},{5,9},{9,5},{13,1},{2,14},{6,10},... | collective-permute-start | bytes 110600 | tf_op jit(solution)/shard_map/ppermute | solution.py:20
  10.2 4.4 %collective-permute-start.3 = (bf16[9,16,128]{2,1,0:T(8,128)(2,1)S(1)}, bf16[9,16,128]{2,1,0:T(8,128)(2,1)S(1)}, u32[]{:S(2)}, u32[]{:S(2)}) collective-permute-start(bf16[9,16,128]{2,1,0:T(8,128)(2,1)S(1)} %join_charges.1.refs_3_.pack), channel_id=1, source_target_pairs={{0,4},{4,0},{8,12},{12,8},{1,5},{5,1},{9,13},{13,9},{2,6},{6,2},{1... | collective-permute-start | bytes 110600 | tf_op jit(solution)/shard_map/ppermute | solution.py:20
  14.6 9.8 %slice-start.1 = ((s8[6291456]{0:T(1024)(128)(4,1)}), s8[2097152]{0:T(1024)(128)(4,1)S(1)}, s32[]{:S(2)}) async-start(s8[6291456]{0:T(1024)(128)(4,1)} %bitcast.2), calls=%async_computation.1 | async-start | bytes 4194304
  15.3 5.5 %collective-permute-start.4 = (bf16[32,16,128]{2,1,0:T(8,128)(2,1)S(1)}, bf16[32,16,128]{2,1,0:T(8,128)(2,1)S(1)}, u32[]{:S(2)}, u32[]{:S(2)}) collective-permute-start(bf16[32,16,128]{2,1,0:T(8,128)(2,1)S(1)} %get-tuple-element.44), channel_id=1, source_target_pairs={{0,2},{2,0},{1,3},{3,1},{4,6},{6,4},{5,7},{7,5},{8,10},{10,8},{9,1... | collective-permute-start | bytes 393224 | tf_op jit(solution)/shard_map/ppermute | solution.py:20
  17.2 6.8 %collective-permute-start.10 = (bf16[8,16,128]{2,1,0:T(8,128)(2,1)S(1)}, bf16[8,16,128]{2,1,0:T(8,128)(2,1)S(1)}, u32[]{:S(2)}, u32[]{:S(2)}) collective-permute-start(bf16[8,16,128]{2,1,0:T(8,128)(2,1)S(1)} %get-tuple-element.55), channel_id=1, source_target_pairs={{0,8},{4,12},{8,0},{12,4},{1,9},{5,13},{9,1},{13,5},{2,10},{6,14},... | collective-permute-start | bytes 98312 | tf_op jit(solution)/shard_map/ppermute | solution.py:20
  18.5 5.8 %collective-permute-start.8 = (bf16[8,16,128]{2,1,0:T(8,128)(2,1)S(1)}, bf16[8,16,128]{2,1,0:T(8,128)(2,1)S(1)}, u32[]{:S(2)}, u32[]{:S(2)}) collective-permute-start(bf16[8,16,128]{2,1,0:T(8,128)(2,1)S(1)} %get-tuple-element.52), channel_id=1, source_target_pairs={{0,12},{4,8},{8,4},{12,0},{1,13},{5,9},{9,5},{13,1},{2,14},{6,10},... | collective-permute-start | bytes 98312 | tf_op jit(solution)/shard_map/ppermute | solution.py:20
  19.6 4.8 %collective-permute-start.9 = (bf16[8,16,128]{2,1,0:T(8,128)(2,1)S(1)}, bf16[8,16,128]{2,1,0:T(8,128)(2,1)S(1)}, u32[]{:S(2)}, u32[]{:S(2)}) collective-permute-start(bf16[8,16,128]{2,1,0:T(8,128)(2,1)S(1)} %get-tuple-element.53), channel_id=1, source_target_pairs={{0,4},{4,0},{8,12},{12,8},{1,5},{5,1},{9,13},{13,9},{2,6},{6,2},{1... | collective-permute-start | bytes 98312 | tf_op jit(solution)/shard_map/ppermute | solution.py:20
  20.8 6.9 %collective-permute-start.6 = (bf16[12,16,128]{2,1,0:T(8,128)(2,1)S(1)}, bf16[12,16,128]{2,1,0:T(8,128)(2,1)S(1)}, u32[]{:S(2)}, u32[]{:S(2)}) collective-permute-start(bf16[12,16,128]{2,1,0:T(8,128)(2,1)S(1)} %get-tuple-element.46), channel_id=1, source_target_pairs={{0,8},{4,12},{8,0},{12,4},{1,9},{5,13},{9,1},{13,5},{2,10},{6,14},... | collective-permute-start | bytes 147464 | tf_op jit(solution)/shard_map/ppermute | solution.py:20
  23.0 5.9 %collective-permute-start.5 = (bf16[12,16,128]{2,1,0:T(8,128)(2,1)S(1)}, bf16[12,16,128]{2,1,0:T(8,128)(2,1)S(1)}, u32[]{:S(2)}, u32[]{:S(2)}) collective-permute-start(bf16[12,16,128]{2,1,0:T(8,128)(2,1)S(1)} %get-tuple-element.45), channel_id=1, source_target_pairs={{0,12},{4,8},{8,4},{12,0},{1,13},{5,9},{9,5},{13,1},{2,14},{6,10},... | collective-permute-start | bytes 147464 | tf_op jit(solution)/shard_map/ppermute | solution.py:20
  25.7 5.0 %collective-permute-start.12 = (bf16[32,16,128]{2,1,0:T(8,128)(2,1)S(1)}, bf16[32,16,128]{2,1,0:T(8,128)(2,1)S(1)}, u32[]{:S(2)}, u32[]{:S(2)}) collective-permute-start(bf16[32,16,128]{2,1,0:T(8,128)(2,1)S(1)} %get-tuple-element.61), channel_id=1, source_target_pairs={{0,2},{2,0},{1,3},{3,1},{4,6},{6,4},{5,7},{7,5},{8,10},{10,8},{9,1... | collective-permute-start | bytes 393224 | tf_op jit(solution)/shard_map/ppermute | solution.py:20
  26.5 4.1 %collective-permute-start.11 = (bf16[12,16,128]{2,1,0:T(8,128)(2,1)S(1)}, bf16[12,16,128]{2,1,0:T(8,128)(2,1)S(1)}, u32[]{:S(2)}, u32[]{:S(2)}) collective-permute-start(bf16[12,16,128]{2,1,0:T(8,128)(2,1)S(1)} %hold_near.1), channel_id=1, source_target_pairs={{0,4},{4,0},{8,12},{12,8},{1,5},{5,1},{9,13},{13,9},{2,6},{6,2},{1... | collective-permute-start | bytes 147464 | tf_op jit(solution)/shard_map/ppermute | solution.py:20

commit v15 on v13

--- a/solution.py
+++ b/solution.py
@@ -66,9 +66,53 @@
     message[message.shape[0] - 1] = own[pan_own]
 
 
-def ends_body(n_row, n_col, pan_own, cap, n_moved, *refs):
+STEP = 16
+
+
+def list_size(count):
+    return count + STEP
+
+
+def first_run(count):
+    return count // 2 // STEP * STEP
+
+
+def sort_tiles(slots, rows, listed, seg_own, n_col, spare_slot):
+    count = slots.shape[0]
+    size, run = list_size(count), first_run(count)
+    c = lax.axis_index("col")
+
+    def put(at, tile, slot, row):
+        listed[at] = tile
+        listed[2 * size + at] = slot
+        listed[4 * size + at] = row
+
+    def step(i, found):
+        away, here = found
+        for u in range(8):
+            t = i * 8 + u
+            row = rows[t]
+            mine = (lax.div(row, seg_own) == c).astype(jnp.int32)
+            put(jnp.where(mine == 1, size + here, away), t, slots[t], row)
+            away, here = away + 1 - mine, here + mine
+        return away, here
+
+    found = lax.fori_loop(0, count // 8, step, (jnp.int32(0), jnp.int32(0)))
+    for half, n in enumerate(found):
+        steps = lax.max(lax.div(n - run + STEP - 1, STEP), 0)
+        spare_row = (lax.rem(c + 1 - half, n_col)) * seg_own
+
+        def fill(i, carry, half=half, spare_row=spare_row):
+            put(half * size + i, 0, spare_slot, spare_row)
+            return carry
+
+        lax.fori_loop(n, run + steps * STEP, fill, 0)
+        listed[6 * size + half] = steps
+
+
+def ends_body(n_row, n_col, pan_own, cap, n_moved, spare_slot, *refs):
     sources, targets = refs[: n_moved + 2], refs[n_moved + 2 : 2 * n_moved + 2]
-    (holder, lanes, blocks, own, *sends), (cur, off, acc, sems) = refs[2 * n_moved + 2 : -4], refs[-4:]
+    (holder, listed, lanes, blocks, own, *sends), (cur, off, acc, sems) = refs[2 * n_moved + 2 : -4], refs[-4:]
     copies = [
         pltpu.make_async_copy(source, target, sems.at[i])
         for i, (source, target) in enumerate(zip(sources, (cur, off, *targets)))
@@ -118,6 +162,7 @@
             sends[j - 1][here] = acc[pl.ds(k * pan_group + there * pan_own, pan_own)].astype(BF16)
     for copy in copies[4:]:
         copy.wait()
+    sort_tiles(targets[5], targets[6], listed, seg_own, n_col, spare_slot)
 
 
 def pick_body(n_row, n_col, cap, partners, _after, *refs):
@@ -143,35 +188,28 @@
             outs[n_row - 1 - k][s] = value
 
 
-def multiply(tiles, src, source, rows, acc):
+def multiply(tiles, src, tile, source, row, acc, start, count):
     rhs, width = src.shape[1:]
-    count = tiles.shape[0]
-    run = max(d for d in range(8, 97, 8) if count % d == 0)
-
-    def products(start):
+
+    def products(first):
         got = []
-        for t in (start, start + 2, start + 4, start + 6):
-            left = jnp.concatenate([src[source(t)], src[source(t + 1)]], axis=0)
-            right = jnp.concatenate([tiles[t], tiles[t + 1]], axis=1)
+        for i in (first, first + 2, first + 4, first + 6):
+            left = jnp.concatenate([src[source(i)], src[source(i + 1)]], axis=0)
+            right = jnp.concatenate([tiles[tile(i)], tiles[tile(i + 1)]], axis=1)
             both = jnp.dot(left, right, preferred_element_type=F32)
             got += [both[:rhs, :width], both[rhs:, width:]]
         return got
 
-    def add(start, got):
+    def add(first, got):
         for u, value in enumerate(got):
-            acc[rows[start + u]] += value
-
-    def step(i, carry):
-        start = i * run
-        waiting = products(start)
-        for first in range(8, run, 8):
-            ahead = products(start + first)
-            add(start + first - 8, waiting)
-            waiting = ahead
-        add(start + run - 8, waiting)
-        return carry
-
-    lax.fori_loop(0, count // run, step, 0)
+            acc[row(first + u)] += value
+
+    waiting = products(start)
+    for first in range(8, count, 8):
+        ahead = products(start + first)
+        add(start + first - 8, waiting)
+        waiting = ahead
+    add(start + count - 8, waiting)
 
 
 def coeff_body(n_row, n_col, pan_own, partners, slots, rows, needs, *refs):
@@ -188,7 +226,7 @@
         for s in range(cap):
             named[p * cap + s] = p * pan_group + needs[p, s]
     part[...] = jnp.zeros_like(part)
-    multiply(tiles, src, lambda t: named[slots[t]], rows, part)
+    multiply(tiles, src, lambda t: t, lambda t: named[slots[t]], lambda t: rows[t], part, 0, tiles.shape[0])
     high = part[...].astype(BF16)
     low = (part[...] - high.astype(F32)).astype(BF16)
     for message, sums in zip(messages, ends):
@@ -197,20 +235,30 @@
         message[pl.ds(2 * pan_group, sums.shape[0])] = sums[...]
 
 
-def induct_body(n_row, n_col, seg_own, order, slots, rows, _after, *refs):
+def induct_body(n_row, n_col, seg_own, order, half, listed, _after, *refs):
     got = {k: refs[i] for i, k in enumerate(order)}
     tiles = refs[n_row]
-    own, *sends = refs[n_row + 1 : -2]
-    src, acc = refs[-2:]
+    outs, (src, acc) = refs[n_row + 1 : -2], refs[-2:]
     cap = got[0].shape[0]
     r, c = lax.axis_index("row"), lax.axis_index("col")
     for k in range(n_row):
         src[pl.ds(lax.bitwise_xor(r, k) * cap, cap)] = got[k][...]
-    acc[...] = jnp.zeros_like(acc)
-    multiply(tiles, src, lambda t: slots[t], rows, acc)
-    own[...] = acc[pl.ds(c * seg_own, seg_own)]
-    for j in range(1, n_col):
-        sends[j - 1][...] = acc[pl.ds(lax.bitwise_xor(c, j) * seg_own, seg_own)].astype(BF16)
+    src[n_row * cap] = jnp.zeros(src.shape[1:], BF16)
+    columns = range(1, n_col) if half == 0 else range(1)
+    spans = [pl.ds(lax.bitwise_xor(c, j) * seg_own, seg_own) for j in columns]
+    for span in spans:
+        acc[span] = jnp.zeros((seg_own, *acc.shape[1:]), F32)
+    size, run = list_size(tiles.shape[0]), first_run(tiles.shape[0])
+    entry = [lambda i, at=kind * 2 * size + half * size: listed[at + i] for kind in range(3)]
+    multiply(tiles, src, *entry, acc, 0, run)
+
+    def step(i, carry):
+        multiply(tiles, src, *entry, acc, run + i * STEP, STEP)
+        return carry
+
+    lax.fori_loop(0, listed[6 * size + half], step, 0)
+    for out, span in zip(outs, spans):
+        out[...] = acc[span].astype(out.dtype)
 
 
 def panels_body(n_row, n_col, pan_own, part, ends_own, *refs):
@@ -356,11 +404,12 @@
     scalars = [slots_t, link_needs, coeff_slots, coeff_rows, coeff_needs, induct_slots, induct_rows, rhs_scale]
     moved = [*scalars, coeff_tiles]
     outs = call(
-        functools.partial(ends_body, n_row, n_col, pan_own, cap_k, len(moved)),
+        functools.partial(ends_body, n_row, n_col, pan_own, cap_k, len(moved), n_row * cap_l),
         "end_sums",
         [pltpu.SMEM(x.shape, x.dtype) for x in scalars]
         + [jax.ShapeDtypeStruct(coeff_tiles.shape, BF16)]
-        + [pltpu.SMEM((2 * seg_own,), jnp.int32), jax.ShapeDtypeStruct((2 * seg_own, width), jnp.int32)]
+        + [pltpu.SMEM((2 * seg_own,), jnp.int32), pltpu.SMEM((6 * list_size(induct_rows.shape[0]) + 2,), jnp.int32)]
+        + [jax.ShapeDtypeStruct((2 * seg_own, width), jnp.int32)]
         + [like(seg_own, BF16), like(rows_own, F32)]
         + [like(rows_own, BF16)] * (n_col - 1),
         [ANY] * (len(moved) + 2),
@@ -372,10 +421,10 @@
         ],
         flops=5 * 10**8,
         moved=2**18,
-        out_specs=[SMEM] * len(scalars) + [VMEM, SMEM] + [VMEM] * (2 + n_col),
+        out_specs=[SMEM] * len(scalars) + [VMEM, SMEM, SMEM] + [VMEM] * (2 + n_col),
     )(*in_hbm(current, off_t, *moved))
     _, links_s, coeff_slots, coeff_rows, coeff_needs, induct_slots, induct_rows, scale, coeff_tiles = outs[: len(moved)]
-    holder, lanes, own_blocks, ends_own, *ends_out = outs[len(moved) :]
+    holder, listed, lanes, own_blocks, ends_own, *ends_out = outs[len(moved) :]
 
     part, *messages = call(
         functools.partial(coeff_body, n_row, n_col, pan_own, partners),
@@ -411,18 +460,22 @@
     )(part, ends_own, *parts)
 
     order = [*partners[1:], 0, partners[0]]
-    field_own, *field_out = call(
-        functools.partial(induct_body, n_row, n_col, seg_own, order),
-        "induct_tiles",
-        [like(seg_own, F32)] + [like(seg_own, BF16)] * (n_col - 1),
-        [SMEM, SMEM, ANY] + [VMEM] * (n_row + 1),
-        [
-            pltpu.VMEM((n_row * cap_l, rhs, width), BF16),
-            pltpu.VMEM((seg_group, rhs, width), F32),
-        ],
-        flops=10**8,
-        moved=2**16,
-    )(induct_slots, induct_rows, pot, *[got[k] for k in order], induct_tiles)
+
+    def induct(name, half, outs, after):
+        return call(
+            functools.partial(induct_body, n_row, n_col, seg_own, order, half),
+            name,
+            outs,
+            [SMEM, ANY] + [VMEM] * (n_row + 1),
+            [
+                pltpu.VMEM((n_row * cap_l + 1, rhs, width), BF16),
+                pltpu.VMEM((seg_group, rhs, width), F32),
+            ],
+            flops=10**8,
+            moved=2**16,
+        )(listed, after, *[got[k] for k in order], induct_tiles)
+
+    field_out = induct("induct_away", 0, [like(seg_own, BF16)] * (n_col - 1), pot)
     field_in = exchange_all(None, field_out, "col")[1:]
 
     (row_messages[-1],) = call(
@@ -431,8 +484,9 @@
         [like(pan_own + pan_group, BF16)],
         [ANY, VMEM],
         moved=2**16,
-    )(field_own, row_messages[-1])
+    )(field_out[0], row_messages[-1])
     arrived = exchange_all(None, row_messages[::-1], "row")[1:]
+    (field_own,) = induct("induct_own", 1, [like(seg_own, F32)], row_messages[-1])
 
     field, panels, pot_out = call(
         functools.partial(base_body, pan_own),

time: 31.6 us -> 32.5 us (1.028)
  Pallas kernels: 7.17 us -> 8.95 us
  waiting for transfers between devices: 5.88 us -> 4.86 us
    pallas_call x1, Pallas kernels: 2.09 us -> 3.6 us  [shards(): call(functools.partial(ends_body, n_row, n_col, pan_own, cap_k, len(moved...]
    ppermute x13, waiting for transfers between devices: 5.88 us -> 4.86 us  [exchange(): lax.ppermute(x, axis, [(i, i ^ k) for i in range(lax.axis_size(axis))])]
    pallas_call x1 -> x2, Pallas kernels: 1.36 us -> 1.62 us  [induct(): call(functools.partial(induct_body, n_row, n_col, seg_own, order, half),...]
  transfers between devices with their start and end apart: 13 -> 13, of which waited for: 5 -> 6; matrix products, arithmetic and copies ran while one was open for 0% -> 0% of each run, Pallas kernels for 20% -> 25%
where the time goes in v15:
time: 32.5 us; the launch traced here: 32.3 us
  starting transfers between devices  17.8 us (55%)
  Pallas kernels  8.95 us (28%)
  waiting for transfers between devices  4.86 us (15%)
  between operations  0.72 us (2%)
    ppermute x13, starting transfers between devices, exchange(): lax.ppermute(x, axis, [(i, i ^ k) for i in range(lax.axis_size(axis))])  17.8 us
    ppermute x13, waiting for transfers between devices, exchange(): lax.ppermute(x, axis, [(i, i ^ k) for i in range(lax.axis_size(axis))])  4.86 us
    pallas_call x1, Pallas kernels, shards(): call(functools.partial(ends_body, n_row, n_col, pan_own, cap_k, len(moved...  3.6 us
    pallas_call x2, Pallas kernels, induct(): call(functools.partial(induct_body, n_row, n_col, seg_own, order, half),...  1.62 us
    pallas_call x1, Pallas kernels, shards(): call(functools.partial(pack_body, pan_own), 'pack_charges', [like(pan_own...  0.88 us
    pallas_call x1, Pallas kernels, shards(): call(functools.partial(final_body, n_row, n_col, pan_own), 'outputs', [ja...  0.83 us
    pallas_call x1, Pallas kernels, shards(): call(functools.partial(base_body, pan_own), 'base_sums', [like(seg_own, F...  0.73 us
    pallas_call x1, Pallas kernels, shards(): call(functools.partial(coeff_body, n_row, n_col, pan_own, partners), 'coe...  0.67 us
  transfers between devices with their start and end apart: 13, of which 6 were waited for; matrix products, arithmetic and copies ran while one was open for 0% of the time, Pallas kernels for 25%

profile of v15, /device:TPU:0, one launch (start us, length us, event | category | flops | bytes accessed | tf_op | source)
XLA Modules:
  0.0 32.3 jit_solution(13789362953222319129)
XLA Ops:
  0.6 3.0 %collective-permute-start = (bf16[16,512]{1,0:T(8,128)(2,1)}, bf16[16,512]{1,0:T(8,128)(2,1)S(1)}, u32[]{:S(2)}, u32[]{:S(2)}) collective-permute-start(bf16[16,512]{1,0:T(8,128)(2,1)} %charge.1), channel_id=1, source_target_pairs={{0,2},{2,0},{1,3},{3,1},{4,6},{6,4},{5,7},{7,5},{8,10},{10,8},{9,1... | collective-permute-start | bytes 49160 | tf_op jit(solution)/shard_map/ppermute | solution.py:20
  3.6 0.1 collective-permute-start.7
  3.7 0.9 %pack_charges.1.own = bf16[5,16,128]{2,1,0:T(8,128)(2,1)S(1)} custom-call(bf16[16,512]{1,0:T(8,128)(2,1)} %charge.1, s32[4,8]{1,0:T(4,128)} %needs.1), custom_call_target="tpu_custom_call" | custom-call | bytes 65536 | tf_op jit(solution)/shard_map/pack_charges/pallas_call | solution.py:386
  4.6 1.0 %collective-permute-done.refs_0_ = bf16[16,512]{1,0:T(8,128)(2,1)S(1)} collective-permute-done((bf16[16,512]{1,0:T(8,128)(2,1)}, bf16[16,512]{1,0:T(8,128)(2,1)S(1)}, u32[]{:S(2)}, u32[]{:S(2)}) %collective-permute-start) | collective-permute-done | bytes 16416 | tf_op jit(solution)/shard_map/ppermute | solution.py:20
  5.6 3.3 %collective-permute-start.1 = (bf16[9,16,128]{2,1,0:T(8,128)(2,1)S(1)}, bf16[9,16,128]{2,1,0:T(8,128)(2,1)S(1)}, u32[]{:S(2)}, u32[]{:S(2)}) collective-permute-start(bf16[9,16,128]{2,1,0:T(8,128)(2,1)S(1)} %join_charges.1.refs_3_.pack), channel_id=1, source_target_pairs={{0,8},{4,12},{8,0},{12,4},{1,9},{5,13},{9,1},{13,5},{2,10},{6,14},... | collective-permute-start | bytes 110600 | tf_op jit(solution)/shard_map/ppermute | solution.py:20
  8.8 1.3 %collective-permute-start.2 = (bf16[9,16,128]{2,1,0:T(8,128)(2,1)S(1)}, bf16[9,16,128]{2,1,0:T(8,128)(2,1)S(1)}, u32[]{:S(2)}, u32[]{:S(2)}) collective-permute-start(bf16[9,16,128]{2,1,0:T(8,128)(2,1)S(1)} %join_charges.1.refs_3_.pack), channel_id=1, source_target_pairs={{0,12},{4,8},{8,4},{12,0},{1,13},{5,9},{9,5},{13,1},{2,14},{6,10},... | collective-permute-start | bytes 110600 | tf_op jit(solution)/shard_map/ppermute | solution.py:20
  10.2 0.2 collective-permute-start.3
  10.4 3.6 %end_sums.1 = (s32[2,32]{1,0:T(2,128)S(4)}, s32[4,16]{1,0:T(4,128)S(4)}, s32[96]{0:T(128)S(4)}, s32[96]{0:T(128)S(4)}, s32[4,4]{1,0:T(4,128)S(4)}, /*index=5*/s3...) custom-call(bf16[16,4096]{1,0:T(8,128)(2,1)} %refs_0_.1, ...), custom_call_target="tpu_custom_call" | custom-call | flops 500000000 | bytes 262144 | tf_op jit(solution)/shard_map/end_sums/pallas_call | solution.py:406
  14.0 0.0 collective-permute-done.1.refs_0_
  14.1 0.6 %collective-permute-done.2.refs_1_ = bf16[9,16,128]{2,1,0:T(8,128)(2,1)S(1)} collective-permute-done((bf16[9,16,128]{2,1,0:T(8,128)(2,1)S(1)}, bf16[9,16,128]{2,1,0:T(8,128)(2,1)S(1)}, u32[]{:S(2)}, u32[]{:S(2)}) %collective-permute-start.2) | collective-permute-done | bytes 36896 | tf_op jit(solution)/shard_map/ppermute | solution.py:20
  14.6 0.7 %coeff_tiles.1 = (f32[8,16,128]{2,1,0:T(8,128)S(1)}, bf16[32,16,128]{2,1,0:T(8,128)(2,1)S(1)}) custom-call(s32[96]{0:T(128)S(4)} %get-tuple-element.34.slots, s32[96]{0:T(128)S(4)} %get-tuple-element.35.rows, s32[4,4]{1,0:T(4,128)S(4)} %get-tuple-element.36.needs, bf16[9,16,128]{2,1,0:T(8,128)(2,1)S(1)} %collective-permute-done.1.refs_0_, ...), custom_call_target="tpu_custom_call" | custom-call | flops 1000000000 | bytes 3145728 | tf_op jit(solution)/shard_map/coeff_tiles/pallas_call | solution.py:429
  15.3 1.6 %collective-permute-start.4 = (bf16[32,16,128]{2,1,0:T(8,128)(2,1)S(1)}, bf16[32,16,128]{2,1,0:T(8,128)(2,1)S(1)}, u32[]{:S(2)}, u32[]{:S(2)}) collective-permute-start(bf16[32,16,128]{2,1,0:T(8,128)(2,1)S(1)} %get-tuple-element.41), channel_id=1, source_target_pairs={{0,2},{2,0},{1,3},{3,1},{4,6},{6,4},{5,7},{7,5},{8,10},{10,8},{9,1... | collective-permute-start | bytes 393224 | tf_op jit(solution)/shard_map/ppermute | solution.py:20
  16.9 0.0 collective-permute-done.7.refs_5_
  16.9 0.3 pick_blocks.1
  17.2 2.4 %collective-permute-start.10 = (bf16[8,16,128]{2,1,0:T(8,128)(2,1)S(1)}, bf16[8,16,128]{2,1,0:T(8,128)(2,1)S(1)}, u32[]{:S(2)}, u32[]{:S(2)}) collective-permute-start(bf16[8,16,128]{2,1,0:T(8,128)(2,1)S(1)} %get-tuple-element.51), channel_id=1, source_target_pairs={{0,8},{4,12},{8,0},{12,4},{1,9},{5,13},{9,1},{13,5},{2,10},{6,14},... | collective-permute-start | bytes 98312 | tf_op jit(solution)/shard_map/ppermute | solution.py:20
  19.6 1.3 %collective-permute-start.8 = (bf16[8,16,128]{2,1,0:T(8,128)(2,1)S(1)}, bf16[8,16,128]{2,1,0:T(8,128)(2,1)S(1)}, u32[]{:S(2)}, u32[]{:S(2)}) collective-permute-start(bf16[8,16,128]{2,1,0:T(8,128)(2,1)S(1)} %get-tuple-element.48), channel_id=1, source_target_pairs={{0,12},{4,8},{8,4},{12,0},{1,13},{5,9},{9,5},{13,1},{2,14},{6,10},... | collective-permute-start | bytes 98312 | tf_op jit(solution)/shard_map/ppermute | solution.py:20
  20.9 2.6 %collective-permute-start.6 = (bf16[12,16,128]{2,1,0:T(8,128)(2,1)S(1)}, bf16[12,16,128]{2,1,0:T(8,128)(2,1)S(1)}, u32[]{:S(2)}, u32[]{:S(2)}) collective-permute-start(bf16[12,16,128]{2,1,0:T(8,128)(2,1)S(1)} %get-tuple-element.43), channel_id=1, source_target_pairs={{0,12},{4,8},{8,4},{12,0},{1,13},{5,9},{9,5},{13,1},{2,14},{6,10},... | collective-permute-start | bytes 147464 | tf_op jit(solution)/shard_map/ppermute | solution.py:20
  23.5 1.0 %collective-permute-start.5 = (bf16[12,16,128]{2,1,0:T(8,128)(2,1)S(1)}, bf16[12,16,128]{2,1,0:T(8,128)(2,1)S(1)}, u32[]{:S(2)}, u32[]{:S(2)}) collective-permute-start(bf16[12,16,128]{2,1,0:T(8,128)(2,1)S(1)} %get-tuple-element.42), channel_id=1, source_target_pairs={{0,8},{4,12},{8,0},{12,4},{1,9},{5,13},{9,1},{13,5},{2,10},{6,14},... | collective-permute-start | bytes 147464 | tf_op jit(solution)/shard_map/ppermute | solution.py:20
  24.5 0.8 %collective-permute-done.8.refs_0_ = bf16[8,16,128]{2,1,0:T(8,128)(2,1)S(1)} collective-permute-done((bf16[8,16,128]{2,1,0:T(8,128)(2,1)S(1)}, bf16[8,16,128]{2,1,0:T(8,128)(2,1)S(1)}, u32[]{:S(2)}, u32[]{:S(2)}) %collective-permute-start.8) | collective-permute-done | bytes 32800 | tf_op jit(solution)/shard_map/ppermute | solution.py:20
  25.3 0.4 %collective-permute-done.9.refs_1_ = bf16[8,16,128]{2,1,0:T(8,128)(2,1)S(1)} collective-permute-done((bf16[8,16,128]{2,1,0:T(8,128)(2,1)S(1)}, bf16[8,16,128]{2,1,0:T(8,128)(2,1)S(1)}, u32[]{:S(2)}, u32[]{:S(2)}) %collective-permute-start.9) | collective-permute-done | bytes 32800 | tf_op jit(solution)/shard_map/ppermute | solution.py:20
  25.7 0.7 %induct_away.1._after = bf16[32,16,128]{2,1,0:T(8,128)(2,1)S(1)} custom-call(s32[1250]{0:T(1024)S(4)} %get-tuple-element.45.listed, bf16[8,16,128]{2,1,0:T(8,128)(2,1)S(1)} %get-tuple-element.46._after.pot, bf16[8,16,128]{2,1,0:T(8,128)(2,1)S(1)} %collective-permute-done.8.refs_0_, bf16[8,16,128]{2,1,0:T(8,128)(2,1)S(1)} %collective-permute-done.9.refs_1_, ...), custom_call_target="tpu_custom_call" | custom-call | flops 100000000 | bytes 65536 | tf_op jit(solution)/shard_map/induct_away/pallas_call | solution.py:465
  26.4 0.6 %collective-permute-start.12 = (bf16[32,16,128]{2,1,0:T(8,128)(2,1)S(1)}, bf16[32,16,128]{2,1,0:T(8,128)(2,1)S(1)}, u32[]{:S(2)}, u32[]{:S(2)}) collective-permute-start(bf16[32,16,128]{2,1,0:T(8,128)(2,1)S(1)} %induct_away.1._after), channel_id=1, source_target_pairs={{0,2},{2,0},{1,3},{3,1},{4,6},{6,4},{5,7},{7,5},{8,10},{10,8},{9,1... | collective-permute-start | bytes 393224 | tf_op jit(solution)/shard_map/ppermute | solution.py:20
  27.0 0.4 %collective-permute-start.11 = (bf16[12,16,128]{2,1,0:T(8,128)(2,1)S(1)}, bf16[12,16,128]{2,1,0:T(8,128)(2,1)S(1)}, u32[]{:S(2)}, u32[]{:S(2)}) collective-permute-start(bf16[12,16,128]{2,1,0:T(8,128)(2,1)S(1)} %hold_near.1._after), channel_id=1, source_target_pairs={{0,4},{4,0},{8,12},{12,8},{1,5},{5,1},{9,13},{13,9},{2,6},{6,2},{1... | collective-permute-start | bytes 147464 | tf_op jit(solution)/shard_map/ppermute | solution.py:20
  27.4 0.9 %induct_own.1.field_own = f32[32,16,128]{2,1,0:T(8,128)S(1)} custom-call(s32[1250]{0:T(1024)S(4)} %get-tuple-element.45.listed, bf16[12,16,128]{2,1,0:T(8,128)(2,1)S(1)} %hold_near.1._after, bf16[8,16,128]{2,1,0:T(8,128)(2,1)S(1)} %collective-permute-done.8.refs_0_, bf16[8,16,128]{2,1,0:T(8,128)(2,1)S(1)} %collective-permute-done.9.refs_1_, ...), custom_call_target="tpu_custom_call" | custom-call | flops 100000000 | bytes 65536 | tf_op jit(solution)/shard_map/induct_own/pallas_call | solution.py:465
  28.3 0.7 %base_sums.1 = (f32[32,16,128]{2,1,0:T(8,128)S(1)}, f32[4,16,128]{2,1,0:T(8,128)S(1)}, bf16[16,512]{1,0:T(8,128)(2,1)}) custom-call(s32[4,16]{1,0:T(4,128)S(4)} %get-tuple-element.31.links, s32[64]{0:T(128)S(4)} %get-tuple-element.32.holder, f32[16]{0:T(128)S(4)} %get-tuple-element.44.scale, s32[64,128]{1,0:T(8,128)S(1)} %get-tuple-element.33.lanes, ...), custom_call_target="tpu_custom_call" | custom-call | tf_op jit(solution)/shard_map/base_sums/pallas_call | solution.py:491
  29.1 0.0 collective-permute-done.6.message.refs_2_
  29.1 0.1 add_drops.2.field_in
  29.2 0.0 collective-permute-done.5.message.refs_1_
  29.2 0.1 add_drops.3.field_own
  29.4 1.7 %collective-permute-done.11.refs_0_ = bf16[12,16,128]{2,1,0:T(8,128)(2,1)S(1)} collective-permute-done((bf16[12,16,128]{2,1,0:T(8,128)(2,1)S(1)}, bf16[12,16,128]{2,1,0:T(8,128)(2,1)S(1)}, u32[]{:S(2)}, u32[]{:S(2)}) %collective-permute-start.11) | collective-permute-done | bytes 49184 | tf_op jit(solution)/shard_map/ppermute | solution.py:20
  31.1 0.3 %collective-permute-done.12.refs_3_ = bf16[32,16,128]{2,1,0:T(8,128)(2,1)S(1)} collective-permute-done((bf16[32,16,128]{2,1,0:T(8,128)(2,1)S(1)}, bf16[32,16,128]{2,1,0:T(8,128)(2,1)S(1)}, u32[]{:S(2)}, u32[]{:S(2)}) %collective-permute-start.12) | collective-permute-done | bytes 131104 | tf_op jit(solution)/shard_map/ppermute | solution.py:20
  31.5 0.8 %outputs.1 = (bf16[16,4096]{1,0:T(8,128)(2,1)}, bf16[16,512]{1,0:T(8,128)(2,1)}) custom-call(s32[4,16]{1,0:T(4,128)S(4)} %get-tuple-element.31.links, s32[64]{0:T(128)S(4)} %get-tuple-element.32.holder, s32[64,128]{1,0:T(8,128)S(1)} %get-tuple-element.33.lanes, f32[32,16,128]{2,1,0:T(8,128)S(1)} %add_drops.3.field_own, ...), custom_call_target="tpu_custom_call" | custom-call | flops 1000000000 | bytes 1048576 | tf_op jit(solution)/shard_map/outputs/pallas_call | solution.py:510
  (12 shorter events, 0.1 us)
Async XLA Ops:
  0.6 4.9 %collective-permute-start = (bf16[16,512]{1,0:T(8,128)(2,1)}, bf16[16,512]{1,0:T(8,128)(2,1)S(1)}, u32[]{:S(2)}, u32[]{:S(2)}) collective-permute-start(bf16[16,512]{1,0:T(8,128)(2,1)} %charge.1), channel_id=1, source_target_pairs={{0,2},{2,0},{1,3},{3,1},{4,6},{6,4},{5,7},{7,5},{8,10},{10,8},{9,1... | collective-permute-start | bytes 49160 | tf_op jit(solution)/shard_map/ppermute | solution.py:20
  3.6 13.3 %collective-permute-start.7 = (bf16[16,4096]{1,0:T(8,128)(2,1)}, bf16[16,4096]{1,0:T(8,128)(2,1)S(1)}, u32[]{:S(2)}, u32[]{:S(2)}) collective-permute-start(bf16[16,4096]{1,0:T(8,128)(2,1)} %refs_0_.1), channel_id=1, source_target_pairs={{0,2},{2,0},{1,3},{3,1},{4,6},{6,4},{5,7},{7,5},{8,10},{10,8},{9,1... | collective-permute-start | bytes 393224 | tf_op jit(solution)/shard_map/ppermute | solution.py:20
  3.7 22.0 %slice-start = ((s8[6291456]{0:T(1024)(128)(4,1)}), s8[4194304]{0:T(1024)(128)(4,1)S(1)}, s32[]{:S(2)}) async-start(s8[6291456]{0:T(1024)(128)(4,1)} %bitcast.2), calls=%async_computation | async-start | bytes 8388608
  5.6 8.5 %collective-permute-start.1 = (bf16[9,16,128]{2,1,0:T(8,128)(2,1)S(1)}, bf16[9,16,128]{2,1,0:T(8,128)(2,1)S(1)}, u32[]{:S(2)}, u32[]{:S(2)}) collective-permute-start(bf16[9,16,128]{2,1,0:T(8,128)(2,1)S(1)} %join_charges.1.refs_3_.pack), channel_id=1, source_target_pairs={{0,8},{4,12},{8,0},{12,4},{1,9},{5,13},{9,1},{13,5},{2,10},{6,14},... | collective-permute-start | bytes 110600 | tf_op jit(solution)/shard_map/ppermute | solution.py:20
  8.8 5.8 %collective-permute-start.2 = (bf16[9,16,128]{2,1,0:T(8,128)(2,1)S(1)}, bf16[9,16,128]{2,1,0:T(8,128)(2,1)S(1)}, u32[]{:S(2)}, u32[]{:S(2)}) collective-permute-start(bf16[9,16,128]{2,1,0:T(8,128)(2,1)S(1)} %join_charges.1.refs_3_.pack), channel_id=1, source_target_pairs={{0,12},{4,8},{8,4},{12,0},{1,13},{5,9},{9,5},{13,1},{2,14},{6,10},... | collective-permute-start | bytes 110600 | tf_op jit(solution)/shard_map/ppermute | solution.py:20
  10.2 4.4 %collective-permute-start.3 = (bf16[9,16,128]{2,1,0:T(8,128)(2,1)S(1)}, bf16[9,16,128]{2,1,0:T(8,128)(2,1)S(1)}, u32[]{:S(2)}, u32[]{:S(2)}) collective-permute-start(bf16[9,16,128]{2,1,0:T(8,128)(2,1)S(1)} %join_charges.1.refs_3_.pack), channel_id=1, source_target_pairs={{0,4},{4,0},{8,12},{12,8},{1,5},{5,1},{9,13},{13,9},{2,6},{6,2},{1... | collective-permute-start | bytes 110600 | tf_op jit(solution)/shard_map/ppermute | solution.py:20
  14.6 11.1 %slice-start.1 = ((s8[6291456]{0:T(1024)(128)(4,1)}), s8[2097152]{0:T(1024)(128)(4,1)S(1)}, s32[]{:S(2)}) async-start(s8[6291456]{0:T(1024)(128)(4,1)} %bitcast.2), calls=%async_computation.1 | async-start | bytes 4194304
  15.3 5.6 %collective-permute-start.4 = (bf16[32,16,128]{2,1,0:T(8,128)(2,1)S(1)}, bf16[32,16,128]{2,1,0:T(8,128)(2,1)S(1)}, u32[]{:S(2)}, u32[]{:S(2)}) collective-permute-start(bf16[32,16,128]{2,1,0:T(8,128)(2,1)S(1)} %get-tuple-element.41), channel_id=1, source_target_pairs={{0,2},{2,0},{1,3},{3,1},{4,6},{6,4},{5,7},{7,5},{8,10},{10,8},{9,1... | collective-permute-start | bytes 393224 | tf_op jit(solution)/shard_map/ppermute | solution.py:20
  17.2 7.3 %collective-permute-start.10 = (bf16[8,16,128]{2,1,0:T(8,128)(2,1)S(1)}, bf16[8,16,128]{2,1,0:T(8,128)(2,1)S(1)}, u32[]{:S(2)}, u32[]{:S(2)}) collective-permute-start(bf16[8,16,128]{2,1,0:T(8,128)(2,1)S(1)} %get-tuple-element.51), channel_id=1, source_target_pairs={{0,8},{4,12},{8,0},{12,4},{1,9},{5,13},{9,1},{13,5},{2,10},{6,14},... | collective-permute-start | bytes 98312 | tf_op jit(solution)/shard_map/ppermute | solution.py:20
  19.6 5.8 %collective-permute-start.8 = (bf16[8,16,128]{2,1,0:T(8,128)(2,1)S(1)}, bf16[8,16,128]{2,1,0:T(8,128)(2,1)S(1)}, u32[]{:S(2)}, u32[]{:S(2)}) collective-permute-start(bf16[8,16,128]{2,1,0:T(8,128)(2,1)S(1)} %get-tuple-element.48), channel_id=1, source_target_pairs={{0,12},{4,8},{8,4},{12,0},{1,13},{5,9},{9,5},{13,1},{2,14},{6,10},... | collective-permute-start | bytes 98312 | tf_op jit(solution)/shard_map/ppermute | solution.py:20
  20.9 4.8 %collective-permute-start.9 = (bf16[8,16,128]{2,1,0:T(8,128)(2,1)S(1)}, bf16[8,16,128]{2,1,0:T(8,128)(2,1)S(1)}, u32[]{:S(2)}, u32[]{:S(2)}) collective-permute-start(bf16[8,16,128]{2,1,0:T(8,128)(2,1)S(1)} %get-tuple-element.49), channel_id=1, source_target_pairs={{0,4},{4,0},{8,12},{12,8},{1,5},{5,1},{9,13},{13,9},{2,6},{6,2},{1... | collective-permute-start | bytes 98312 | tf_op jit(solution)/shard_map/ppermute | solution.py:20
  20.9 8.1 %collective-permute-start.6 = (bf16[12,16,128]{2,1,0:T(8,128)(2,1)S(1)}, bf16[12,16,128]{2,1,0:T(8,128)(2,1)S(1)}, u32[]{:S(2)}, u32[]{:S(2)}) collective-permute-start(bf16[12,16,128]{2,1,0:T(8,128)(2,1)S(1)} %get-tuple-element.43), channel_id=1, source_target_pairs={{0,12},{4,8},{8,4},{12,0},{1,13},{5,9},{9,5},{13,1},{2,14},{6,10},... | collective-permute-start | bytes 147464 | tf_op jit(solution)/shard_map/ppermute | solution.py:20
  23.5 5.7 %collective-permute-start.5 = (bf16[12,16,128]{2,1,0:T(8,128)(2,1)S(1)}, bf16[12,16,128]{2,1,0:T(8,128)(2,1)S(1)}, u32[]{:S(2)}, u32[]{:S(2)}) collective-permute-start(bf16[12,16,128]{2,1,0:T(8,128)(2,1)S(1)} %get-tuple-element.42), channel_id=1, source_target_pairs={{0,8},{4,12},{8,0},{12,4},{1,9},{5,13},{9,1},{13,5},{2,10},{6,14},... | collective-permute-start | bytes 147464 | tf_op jit(solution)/shard_map/ppermute | solution.py:20
  26.4 5.0 %collective-permute-start.12 = (bf16[32,16,128]{2,1,0:T(8,128)(2,1)S(1)}, bf16[32,16,128]{2,1,0:T(8,128)(2,1)S(1)}, u32[]{:S(2)}, u32[]{:S(2)}) collective-permute-start(bf16[32,16,128]{2,1,0:T(8,128)(2,1)S(1)} %induct_away.1._after), channel_id=1, source_target_pairs={{0,2},{2,0},{1,3},{3,1},{4,6},{6,4},{5,7},{7,5},{8,10},{10,8},{9,1... | collective-permute-start | bytes 393224 | tf_op jit(solution)/shard_map/ppermute | solution.py:20
  27.0 4.1 %collective-permute-start.11 = (bf16[12,16,128]{2,1,0:T(8,128)(2,1)S(1)}, bf16[12,16,128]{2,1,0:T(8,128)(2,1)S(1)}, u32[]{:S(2)}, u32[]{:S(2)}) collective-permute-start(bf16[12,16,128]{2,1,0:T(8,128)(2,1)S(1)} %hold_near.1._after), channel_id=1, source_target_pairs={{0,4},{4,0},{8,12},{12,8},{1,5},{5,1},{9,13},{13,9},{2,6},{6,2},{1... | collective-permute-start | bytes 147464 | tf_op jit(solution)/shard_map/ppermute | solution.py:20

commit v16 on v15

--- a/solution.py
+++ b/solution.py
@@ -77,40 +77,34 @@
     return count // 2 // STEP * STEP
 
 
-def sort_tiles(slots, rows, listed, seg_own, n_col, spare_slot):
-    count = slots.shape[0]
+def sort_tiles(rows, listed, seg_own):
+    count = rows.shape[0]
     size, run = list_size(count), first_run(count)
-    c = lax.axis_index("col")
-
-    def put(at, tile, slot, row):
-        listed[at] = tile
-        listed[2 * size + at] = slot
-        listed[4 * size + at] = row
-
-    def step(i, found):
-        away, here = found
-        for u in range(8):
-            t = i * 8 + u
-            row = rows[t]
-            mine = (lax.div(row, seg_own) == c).astype(jnp.int32)
-            put(jnp.where(mine == 1, size + here, away), t, slots[t], row)
-            away, here = away + 1 - mine, here + mine
-        return away, here
-
-    found = lax.fori_loop(0, count // 8, step, (jnp.int32(0), jnp.int32(0)))
-    for half, n in enumerate(found):
+    base = lax.axis_index("col") * seg_own
+
+    def step(i, here):
+        for u in range(16):
+            t = i * 16 + u
+            inside = rows[t] - base
+            mine = jnp.logical_and(inside >= 0, inside < seg_own)
+            listed[jnp.where(mine, size + here, t - here)] = t
+            here = here + mine.astype(jnp.int32)
+        return here
+
+    here = lax.fori_loop(0, count // 16, step, jnp.int32(0))
+    for half, n in enumerate((count - here, here)):
         steps = lax.max(lax.div(n - run + STEP - 1, STEP), 0)
-        spare_row = (lax.rem(c + 1 - half, n_col)) * seg_own
-
-        def fill(i, carry, half=half, spare_row=spare_row):
-            put(half * size + i, 0, spare_slot, spare_row)
+
+        def fill(i, carry, half=half):
+            listed[half * size + i] = 0
             return carry
 
         lax.fori_loop(n, run + steps * STEP, fill, 0)
-        listed[6 * size + half] = steps
-
-
-def ends_body(n_row, n_col, pan_own, cap, n_moved, spare_slot, *refs):
+        listed[2 * size + half] = steps
+        listed[2 * size + 2 + half] = n
+
+
+def ends_body(n_row, n_col, pan_own, cap, n_moved, *refs):
     sources, targets = refs[: n_moved + 2], refs[n_moved + 2 : 2 * n_moved + 2]
     (holder, listed, lanes, blocks, own, *sends), (cur, off, acc, sems) = refs[2 * n_moved + 2 : -4], refs[-4:]
     copies = [
@@ -162,7 +156,7 @@
             sends[j - 1][here] = acc[pl.ds(k * pan_group + there * pan_own, pan_own)].astype(BF16)
     for copy in copies[4:]:
         copy.wait()
-    sort_tiles(targets[5], targets[6], listed, seg_own, n_col, spare_slot)
+    sort_tiles(targets[6], listed, seg_own)
 
 
 def pick_body(n_row, n_col, cap, partners, _after, *refs):
@@ -235,7 +229,7 @@
         message[pl.ds(2 * pan_group, sums.shape[0])] = sums[...]
 
 
-def induct_body(n_row, n_col, seg_own, order, half, listed, _after, *refs):
+def induct_body(n_row, n_col, seg_own, order, half, slots, rows, listed, _after, *refs):
     got = {k: refs[i] for i, k in enumerate(order)}
     tiles = refs[n_row]
     outs, (src, acc) = refs[n_row + 1 : -2], refs[-2:]
@@ -249,14 +243,24 @@
     for span in spans:
         acc[span] = jnp.zeros((seg_own, *acc.shape[1:]), F32)
     size, run = list_size(tiles.shape[0]), first_run(tiles.shape[0])
-    entry = [lambda i, at=kind * 2 * size + half * size: listed[at + i] for kind in range(3)]
-    multiply(tiles, src, *entry, acc, 0, run)
+    length = listed[2 * size + 2 + half]
+
+    def tile(i):
+        return listed[half * size + i]
+
+    def source(i):
+        return jnp.where(i < length, slots[tile(i)], n_row * cap)
+
+    def row(i):
+        return rows[tile(i)]
+
+    multiply(tiles, src, tile, source, row, acc, 0, run)
 
     def step(i, carry):
-        multiply(tiles, src, *entry, acc, run + i * STEP, STEP)
+        multiply(tiles, src, tile, source, row, acc, run + i * STEP, STEP)
         return carry
 
-    lax.fori_loop(0, listed[6 * size + half], step, 0)
+    lax.fori_loop(0, listed[2 * size + half], step, 0)
     for out, span in zip(outs, spans):
         out[...] = acc[span].astype(out.dtype)
 
@@ -404,11 +408,11 @@
     scalars = [slots_t, link_needs, coeff_slots, coeff_rows, coeff_needs, induct_slots, induct_rows, rhs_scale]
     moved = [*scalars, coeff_tiles]
     outs = call(
-        functools.partial(ends_body, n_row, n_col, pan_own, cap_k, len(moved), n_row * cap_l),
+        functools.partial(ends_body, n_row, n_col, pan_own, cap_k, len(moved)),
         "end_sums",
         [pltpu.SMEM(x.shape, x.dtype) for x in scalars]
         + [jax.ShapeDtypeStruct(coeff_tiles.shape, BF16)]
-        + [pltpu.SMEM((2 * seg_own,), jnp.int32), pltpu.SMEM((6 * list_size(induct_rows.shape[0]) + 2,), jnp.int32)]
+        + [pltpu.SMEM((2 * seg_own,), jnp.int32), pltpu.SMEM((2 * list_size(induct_rows.shape[0]) + 4,), jnp.int32)]
         + [jax.ShapeDtypeStruct((2 * seg_own, width), jnp.int32)]
         + [like(seg_own, BF16), like(rows_own, F32)]
         + [like(rows_own, BF16)] * (n_col - 1),
@@ -466,14 +470,14 @@
             functools.partial(induct_body, n_row, n_col, seg_own, order, half),
             name,
             outs,
-            [SMEM, ANY] + [VMEM] * (n_row + 1),
+            [SMEM] * 3 + [ANY] + [VMEM] * (n_row + 1),
             [
                 pltpu.VMEM((n_row * cap_l + 1, rhs, width), BF16),
                 pltpu.VMEM((seg_group, rhs, width), F32),
             ],
             flops=10**8,
             moved=2**16,
-        )(listed, after, *[got[k] for k in order], induct_tiles)
+        )(induct_slots, induct_rows, listed, after, *[got[k] for k in order], induct_tiles)
 
     field_out = induct("induct_away", 0, [like(seg_own, BF16)] * (n_col - 1), pot)
     field_in = exchange_all(None, field_out, "col")[1:]

time: 32.5 us -> 31.9 us (0.982)
  Pallas kernels: 8.95 us -> 8.27 us
  waiting for transfers between devices: 4.86 us -> 5.24 us
    pallas_call x1, Pallas kernels: 3.6 us -> 2.92 us  [shards(): call(functools.partial(ends_body, n_row, n_col, pan_own, cap_k, len(moved...]
    ppermute x13, waiting for transfers between devices: 4.86 us -> 5.24 us  [exchange(): lax.ppermute(x, axis, [(i, i ^ k) for i in range(lax.axis_size(axis))])]
  transfers between devices with their start and end apart: 13 -> 13, of which waited for: 6 -> 6; matrix products, arithmetic and copies ran while one was open for 0% -> 0% of each run, Pallas kernels for 25% -> 23%
where the time goes in v16:
time: 31.9 us; the launch traced here: 31.7 us
  starting transfers between devices  17.5 us (55%)
  Pallas kernels  8.27 us (26%)
  waiting for transfers between devices  5.24 us (16%)
  between operations  0.71 us (2%)
    ppermute x13, starting transfers between devices, exchange(): lax.ppermute(x, axis, [(i, i ^ k) for i in range(lax.axis_size(axis))])  17.5 us
    ppermute x13, waiting for transfers between devices, exchange(): lax.ppermute(x, axis, [(i, i ^ k) for i in range(lax.axis_size(axis))])  5.24 us
    pallas_call x1, Pallas kernels, shards(): call(functools.partial(ends_body, n_row, n_col, pan_own, cap_k, len(moved...  2.92 us
    pallas_call x2, Pallas kernels, induct(): call(functools.partial(induct_body, n_row, n_col, seg_own, order, half),...  1.62 us
    pallas_call x1, Pallas kernels, shards(): call(functools.partial(pack_body, pan_own), 'pack_charges', [like(pan_own...  0.88 us
    pallas_call x1, Pallas kernels, shards(): call(functools.partial(final_body, n_row, n_col, pan_own), 'outputs', [ja...  0.83 us
    pallas_call x1, Pallas kernels, shards(): call(functools.partial(base_body, pan_own), 'base_sums', [like(seg_own, F...  0.73 us
    pallas_call x1, Pallas kernels, shards(): call(functools.partial(coeff_body, n_row, n_col, pan_own, partners), 'coe...  0.67 us
  transfers between devices with their start and end apart: 13, of which 6 were waited for; matrix products, arithmetic and copies ran while one was open for 0% of the time, Pallas kernels for 23%

profile of v16, /device:TPU:0, one launch (start us, length us, event | category | flops | bytes accessed | tf_op | source)
XLA Modules:
  0.0 31.7 jit_solution(5700304048978248320)
XLA Ops:
  0.6 3.0 %collective-permute-start = (bf16[16,512]{1,0:T(8,128)(2,1)}, bf16[16,512]{1,0:T(8,128)(2,1)S(1)}, u32[]{:S(2)}, u32[]{:S(2)}) collective-permute-start(bf16[16,512]{1,0:T(8,128)(2,1)} %charge.1), channel_id=1, source_target_pairs={{0,2},{2,0},{1,3},{3,1},{4,6},{6,4},{5,7},{7,5},{8,10},{10,8},{9,1... | collective-permute-start | bytes 49160 | tf_op jit(solution)/shard_map/ppermute | solution.py:20
  3.6 0.1 collective-permute-start.7
  3.7 0.9 %pack_charges.1.own = bf16[5,16,128]{2,1,0:T(8,128)(2,1)S(1)} custom-call(bf16[16,512]{1,0:T(8,128)(2,1)} %charge.1, s32[4,8]{1,0:T(4,128)} %needs.1), custom_call_target="tpu_custom_call" | custom-call | bytes 65536 | tf_op jit(solution)/shard_map/pack_charges/pallas_call | solution.py:390
  4.6 1.0 %collective-permute-done.refs_0_ = bf16[16,512]{1,0:T(8,128)(2,1)S(1)} collective-permute-done((bf16[16,512]{1,0:T(8,128)(2,1)}, bf16[16,512]{1,0:T(8,128)(2,1)S(1)}, u32[]{:S(2)}, u32[]{:S(2)}) %collective-permute-start) | collective-permute-done | bytes 16416 | tf_op jit(solution)/shard_map/ppermute | solution.py:20
  5.6 3.3 %collective-permute-start.1 = (bf16[9,16,128]{2,1,0:T(8,128)(2,1)S(1)}, bf16[9,16,128]{2,1,0:T(8,128)(2,1)S(1)}, u32[]{:S(2)}, u32[]{:S(2)}) collective-permute-start(bf16[9,16,128]{2,1,0:T(8,128)(2,1)S(1)} %join_charges.1.refs_3_.pack), channel_id=1, source_target_pairs={{0,8},{4,12},{8,0},{12,4},{1,9},{5,13},{9,1},{13,5},{2,10},{6,14},... | collective-permute-start | bytes 110600 | tf_op jit(solution)/shard_map/ppermute | solution.py:20
  8.8 1.3 %collective-permute-start.2 = (bf16[9,16,128]{2,1,0:T(8,128)(2,1)S(1)}, bf16[9,16,128]{2,1,0:T(8,128)(2,1)S(1)}, u32[]{:S(2)}, u32[]{:S(2)}) collective-permute-start(bf16[9,16,128]{2,1,0:T(8,128)(2,1)S(1)} %join_charges.1.refs_3_.pack), channel_id=1, source_target_pairs={{0,12},{4,8},{8,4},{12,0},{1,13},{5,9},{9,5},{13,1},{2,14},{6,10},... | collective-permute-start | bytes 110600 | tf_op jit(solution)/shard_map/ppermute | solution.py:20
  10.2 0.2 collective-permute-start.3
  10.4 2.9 %end_sums.1 = (s32[2,32]{1,0:T(2,128)S(4)}, s32[4,16]{1,0:T(4,128)S(4)}, s32[96]{0:T(128)S(4)}, s32[96]{0:T(128)S(4)}, s32[4,4]{1,0:T(4,128)S(4)}, /*index=5*/s3...) custom-call(bf16[16,4096]{1,0:T(8,128)(2,1)} %refs_0_.1, ...), custom_call_target="tpu_custom_call" | custom-call | flops 500000000 | bytes 262144 | tf_op jit(solution)/shard_map/end_sums/pallas_call | solution.py:410
  13.4 0.0 collective-permute-done.1.refs_0_
  13.4 1.2 %collective-permute-done.2.refs_1_ = bf16[9,16,128]{2,1,0:T(8,128)(2,1)S(1)} collective-permute-done((bf16[9,16,128]{2,1,0:T(8,128)(2,1)S(1)}, bf16[9,16,128]{2,1,0:T(8,128)(2,1)S(1)}, u32[]{:S(2)}, u32[]{:S(2)}) %collective-permute-start.2) | collective-permute-done | bytes 36896 | tf_op jit(solution)/shard_map/ppermute | solution.py:20
  14.6 0.0 collective-permute-done.3.refs_2_
  14.6 0.7 %coeff_tiles.1 = (f32[8,16,128]{2,1,0:T(8,128)S(1)}, bf16[32,16,128]{2,1,0:T(8,128)(2,1)S(1)}) custom-call(s32[96]{0:T(128)S(4)} %get-tuple-element.36.slots, s32[96]{0:T(128)S(4)} %get-tuple-element.37.rows, s32[4,4]{1,0:T(4,128)S(4)} %get-tuple-element.38.needs, bf16[9,16,128]{2,1,0:T(8,128)(2,1)S(1)} %collective-permute-done.1.refs_0_, ...), custom_call_target="tpu_custom_call" | custom-call | flops 1000000000 | bytes 3145728 | tf_op jit(solution)/shard_map/coeff_tiles/pallas_call | solution.py:433
  15.3 1.6 %collective-permute-start.4 = (bf16[32,16,128]{2,1,0:T(8,128)(2,1)S(1)}, bf16[32,16,128]{2,1,0:T(8,128)(2,1)S(1)}, u32[]{:S(2)}, u32[]{:S(2)}) collective-permute-start(bf16[32,16,128]{2,1,0:T(8,128)(2,1)S(1)} %get-tuple-element.43), channel_id=1, source_target_pairs={{0,2},{2,0},{1,3},{3,1},{4,6},{6,4},{5,7},{7,5},{8,10},{10,8},{9,1... | collective-permute-start | bytes 393224 | tf_op jit(solution)/shard_map/ppermute | solution.py:20
  16.9 0.0 collective-permute-done.7.refs_5_
  16.9 0.3 pick_blocks.1
  17.2 1.7 %collective-permute-start.10 = (bf16[8,16,128]{2,1,0:T(8,128)(2,1)S(1)}, bf16[8,16,128]{2,1,0:T(8,128)(2,1)S(1)}, u32[]{:S(2)}, u32[]{:S(2)}) collective-permute-start(bf16[8,16,128]{2,1,0:T(8,128)(2,1)S(1)} %get-tuple-element.55), channel_id=1, source_target_pairs={{0,8},{4,12},{8,0},{12,4},{1,9},{5,13},{9,1},{13,5},{2,10},{6,14},... | collective-permute-start | bytes 98312 | tf_op jit(solution)/shard_map/ppermute | solution.py:20
  18.9 1.3 %collective-permute-start.8 = (bf16[8,16,128]{2,1,0:T(8,128)(2,1)S(1)}, bf16[8,16,128]{2,1,0:T(8,128)(2,1)S(1)}, u32[]{:S(2)}, u32[]{:S(2)}) collective-permute-start(bf16[8,16,128]{2,1,0:T(8,128)(2,1)S(1)} %get-tuple-element.52), channel_id=1, source_target_pairs={{0,12},{4,8},{8,4},{12,0},{1,13},{5,9},{9,5},{13,1},{2,14},{6,10},... | collective-permute-start | bytes 98312 | tf_op jit(solution)/shard_map/ppermute | solution.py:20
  20.2 0.6 %collective-permute-start.9 = (bf16[8,16,128]{2,1,0:T(8,128)(2,1)S(1)}, bf16[8,16,128]{2,1,0:T(8,128)(2,1)S(1)}, u32[]{:S(2)}, u32[]{:S(2)}) collective-permute-start(bf16[8,16,128]{2,1,0:T(8,128)(2,1)S(1)} %get-tuple-element.53), channel_id=1, source_target_pairs={{0,4},{4,0},{8,12},{12,8},{1,5},{5,1},{9,13},{13,9},{2,6},{6,2},{1... | collective-permute-start | bytes 98312 | tf_op jit(solution)/shard_map/ppermute | solution.py:20
  20.8 2.1 %collective-permute-start.6 = (bf16[12,16,128]{2,1,0:T(8,128)(2,1)S(1)}, bf16[12,16,128]{2,1,0:T(8,128)(2,1)S(1)}, u32[]{:S(2)}, u32[]{:S(2)}) collective-permute-start(bf16[12,16,128]{2,1,0:T(8,128)(2,1)S(1)} %get-tuple-element.45), channel_id=1, source_target_pairs={{0,12},{4,8},{8,4},{12,0},{1,13},{5,9},{9,5},{13,1},{2,14},{6,10},... | collective-permute-start | bytes 147464 | tf_op jit(solution)/shard_map/ppermute | solution.py:20
  22.9 0.9 %collective-permute-start.5 = (bf16[12,16,128]{2,1,0:T(8,128)(2,1)S(1)}, bf16[12,16,128]{2,1,0:T(8,128)(2,1)S(1)}, u32[]{:S(2)}, u32[]{:S(2)}) collective-permute-start(bf16[12,16,128]{2,1,0:T(8,128)(2,1)S(1)} %get-tuple-element.44), channel_id=1, source_target_pairs={{0,8},{4,12},{8,0},{12,4},{1,9},{5,13},{9,1},{13,5},{2,10},{6,14},... | collective-permute-start | bytes 147464 | tf_op jit(solution)/shard_map/ppermute | solution.py:20
  23.8 0.9 %collective-permute-done.8.refs_0_ = bf16[8,16,128]{2,1,0:T(8,128)(2,1)S(1)} collective-permute-done((bf16[8,16,128]{2,1,0:T(8,128)(2,1)S(1)}, bf16[8,16,128]{2,1,0:T(8,128)(2,1)S(1)}, u32[]{:S(2)}, u32[]{:S(2)}) %collective-permute-start.8) | collective-permute-done | bytes 32800 | tf_op jit(solution)/shard_map/ppermute | solution.py:20
  24.7 0.2 collective-permute-done.9.refs_1_
  24.9 0.9 %induct_away.1._after = bf16[32,16,128]{2,1,0:T(8,128)(2,1)S(1)} custom-call(s32[192]{0:T(256)S(4)} %get-tuple-element.47.slots, s32[192]{0:T(256)S(4)} %get-tuple-element.48.rows, s32[420]{0:T(512)S(4)} %get-tuple-element.49.listed, bf16[8,16,128]{2,1,0:T(8,128)(2,1)S(1)} %get-tuple-element.50._after.pot, ...), custom_call_target="tpu_custom_call" | custom-call | flops 100000000 | bytes 65536 | tf_op jit(solution)/shard_map/induct_away/pallas_call | solution.py:469
  25.8 0.5 %collective-permute-start.12 = (bf16[32,16,128]{2,1,0:T(8,128)(2,1)S(1)}, bf16[32,16,128]{2,1,0:T(8,128)(2,1)S(1)}, u32[]{:S(2)}, u32[]{:S(2)}) collective-permute-start(bf16[32,16,128]{2,1,0:T(8,128)(2,1)S(1)} %induct_away.1._after), channel_id=1, source_target_pairs={{0,2},{2,0},{1,3},{3,1},{4,6},{6,4},{5,7},{7,5},{8,10},{10,8},{9,1... | collective-permute-start | bytes 393224 | tf_op jit(solution)/shard_map/ppermute | solution.py:20
  26.4 0.8 %collective-permute-start.11 = (bf16[12,16,128]{2,1,0:T(8,128)(2,1)S(1)}, bf16[12,16,128]{2,1,0:T(8,128)(2,1)S(1)}, u32[]{:S(2)}, u32[]{:S(2)}) collective-permute-start(bf16[12,16,128]{2,1,0:T(8,128)(2,1)S(1)} %hold_near.1._after), channel_id=1, source_target_pairs={{0,4},{4,0},{8,12},{12,8},{1,5},{5,1},{9,13},{13,9},{2,6},{6,2},{1... | collective-permute-start | bytes 147464 | tf_op jit(solution)/shard_map/ppermute | solution.py:20
  27.2 0.7 %induct_own.1.field_own = f32[32,16,128]{2,1,0:T(8,128)S(1)} custom-call(s32[192]{0:T(256)S(4)} %get-tuple-element.47.slots, s32[192]{0:T(256)S(4)} %get-tuple-element.48.rows, s32[420]{0:T(512)S(4)} %get-tuple-element.49.listed, bf16[12,16,128]{2,1,0:T(8,128)(2,1)S(1)} %hold_near.1._after, bf16[8,16,128]{2,1,0:T(8,128)(2,1)S(1)} %collective-permute-done.8.refs_0_, ...), custom_call_target="tpu_custom_call" | custom-call | flops 100000000 | bytes 65536 | tf_op jit(solution)/shard_map/induct_own/pallas_call | solution.py:469
  27.9 0.7 %base_sums.1 = (f32[32,16,128]{2,1,0:T(8,128)S(1)}, f32[4,16,128]{2,1,0:T(8,128)S(1)}, bf16[16,512]{1,0:T(8,128)(2,1)}) custom-call(s32[4,16]{1,0:T(4,128)S(4)} %get-tuple-element.33.links, s32[64]{0:T(128)S(4)} %get-tuple-element.34.holder, f32[16]{0:T(128)S(4)} %get-tuple-element.46.scale, s32[64,128]{1,0:T(8,128)S(1)} %get-tuple-element.35.lanes, ...), custom_call_target="tpu_custom_call" | custom-call | tf_op jit(solution)/shard_map/base_sums/pallas_call | solution.py:495
  28.6 0.1 add_drops.2.field_in
  28.8 0.2 add_drops.3.field_own
  29.0 1.5 %collective-permute-done.11.refs_0_ = bf16[12,16,128]{2,1,0:T(8,128)(2,1)S(1)} collective-permute-done((bf16[12,16,128]{2,1,0:T(8,128)(2,1)S(1)}, bf16[12,16,128]{2,1,0:T(8,128)(2,1)S(1)}, u32[]{:S(2)}, u32[]{:S(2)}) %collective-permute-start.11) | collective-permute-done | bytes 49184 | tf_op jit(solution)/shard_map/ppermute | solution.py:20
  30.5 0.4 %collective-permute-done.12.refs_3_ = bf16[32,16,128]{2,1,0:T(8,128)(2,1)S(1)} collective-permute-done((bf16[32,16,128]{2,1,0:T(8,128)(2,1)S(1)}, bf16[32,16,128]{2,1,0:T(8,128)(2,1)S(1)}, u32[]{:S(2)}, u32[]{:S(2)}) %collective-permute-start.12) | collective-permute-done | bytes 131104 | tf_op jit(solution)/shard_map/ppermute | solution.py:20
  30.9 0.8 %outputs.1 = (bf16[16,4096]{1,0:T(8,128)(2,1)}, bf16[16,512]{1,0:T(8,128)(2,1)}) custom-call(s32[4,16]{1,0:T(4,128)S(4)} %get-tuple-element.33.links, s32[64]{0:T(128)S(4)} %get-tuple-element.34.holder, s32[64,128]{1,0:T(8,128)S(1)} %get-tuple-element.35.lanes, f32[32,16,128]{2,1,0:T(8,128)S(1)} %add_drops.3.field_own, ...), custom_call_target="tpu_custom_call" | custom-call | flops 1000000000 | bytes 1048576 | tf_op jit(solution)/shard_map/outputs/pallas_call | solution.py:514
  (12 shorter events, 0.1 us)
Async XLA Ops:
  0.6 4.9 %collective-permute-start = (bf16[16,512]{1,0:T(8,128)(2,1)}, bf16[16,512]{1,0:T(8,128)(2,1)S(1)}, u32[]{:S(2)}, u32[]{:S(2)}) collective-permute-start(bf16[16,512]{1,0:T(8,128)(2,1)} %charge.1), channel_id=1, source_target_pairs={{0,2},{2,0},{1,3},{3,1},{4,6},{6,4},{5,7},{7,5},{8,10},{10,8},{9,1... | collective-permute-start | bytes 49160 | tf_op jit(solution)/shard_map/ppermute | solution.py:20
  3.6 13.3 %collective-permute-start.7 = (bf16[16,4096]{1,0:T(8,128)(2,1)}, bf16[16,4096]{1,0:T(8,128)(2,1)S(1)}, u32[]{:S(2)}, u32[]{:S(2)}) collective-permute-start(bf16[16,4096]{1,0:T(8,128)(2,1)} %refs_0_.1), channel_id=1, source_target_pairs={{0,2},{2,0},{1,3},{3,1},{4,6},{6,4},{5,7},{7,5},{8,10},{10,8},{9,1... | collective-permute-start | bytes 393224 | tf_op jit(solution)/shard_map/ppermute | solution.py:20
  3.7 21.2 %slice-start = ((s8[6291456]{0:T(1024)(128)(4,1)}), s8[4194304]{0:T(1024)(128)(4,1)S(1)}, s32[]{:S(2)}) async-start(s8[6291456]{0:T(1024)(128)(4,1)} %bitcast.2), calls=%async_computation | async-start | bytes 8388608
  5.6 7.8 %collective-permute-start.1 = (bf16[9,16,128]{2,1,0:T(8,128)(2,1)S(1)}, bf16[9,16,128]{2,1,0:T(8,128)(2,1)S(1)}, u32[]{:S(2)}, u32[]{:S(2)}) collective-permute-start(bf16[9,16,128]{2,1,0:T(8,128)(2,1)S(1)} %join_charges.1.refs_3_.pack), channel_id=1, source_target_pairs={{0,8},{4,12},{8,0},{12,4},{1,9},{5,13},{9,1},{13,5},{2,10},{6,14},... | collective-permute-start | bytes 110600 | tf_op jit(solution)/shard_map/ppermute | solution.py:20
  8.8 5.8 %collective-permute-start.2 = (bf16[9,16,128]{2,1,0:T(8,128)(2,1)S(1)}, bf16[9,16,128]{2,1,0:T(8,128)(2,1)S(1)}, u32[]{:S(2)}, u32[]{:S(2)}) collective-permute-start(bf16[9,16,128]{2,1,0:T(8,128)(2,1)S(1)} %join_charges.1.refs_3_.pack), channel_id=1, source_target_pairs={{0,12},{4,8},{8,4},{12,0},{1,13},{5,9},{9,5},{13,1},{2,14},{6,10},... | collective-permute-start | bytes 110600 | tf_op jit(solution)/shard_map/ppermute | solution.py:20
  10.2 4.4 %collective-permute-start.3 = (bf16[9,16,128]{2,1,0:T(8,128)(2,1)S(1)}, bf16[9,16,128]{2,1,0:T(8,128)(2,1)S(1)}, u32[]{:S(2)}, u32[]{:S(2)}) collective-permute-start(bf16[9,16,128]{2,1,0:T(8,128)(2,1)S(1)} %join_charges.1.refs_3_.pack), channel_id=1, source_target_pairs={{0,4},{4,0},{8,12},{12,8},{1,5},{5,1},{9,13},{13,9},{2,6},{6,2},{1... | collective-permute-start | bytes 110600 | tf_op jit(solution)/shard_map/ppermute | solution.py:20
  14.6 10.3 %slice-start.1 = ((s8[6291456]{0:T(1024)(128)(4,1)}), s8[2097152]{0:T(1024)(128)(4,1)S(1)}, s32[]{:S(2)}) async-start(s8[6291456]{0:T(1024)(128)(4,1)} %bitcast.2), calls=%async_computation.1 | async-start | bytes 4194304
  15.3 5.5 %collective-permute-start.4 = (bf16[32,16,128]{2,1,0:T(8,128)(2,1)S(1)}, bf16[32,16,128]{2,1,0:T(8,128)(2,1)S(1)}, u32[]{:S(2)}, u32[]{:S(2)}) collective-permute-start(bf16[32,16,128]{2,1,0:T(8,128)(2,1)S(1)} %get-tuple-element.43), channel_id=1, source_target_pairs={{0,2},{2,0},{1,3},{3,1},{4,6},{6,4},{5,7},{7,5},{8,10},{10,8},{9,1... | collective-permute-start | bytes 393224 | tf_op jit(solution)/shard_map/ppermute | solution.py:20
  17.2 6.6 %collective-permute-start.10 = (bf16[8,16,128]{2,1,0:T(8,128)(2,1)S(1)}, bf16[8,16,128]{2,1,0:T(8,128)(2,1)S(1)}, u32[]{:S(2)}, u32[]{:S(2)}) collective-permute-start(bf16[8,16,128]{2,1,0:T(8,128)(2,1)S(1)} %get-tuple-element.55), channel_id=1, source_target_pairs={{0,8},{4,12},{8,0},{12,4},{1,9},{5,13},{9,1},{13,5},{2,10},{6,14},... | collective-permute-start | bytes 98312 | tf_op jit(solution)/shard_map/ppermute | solution.py:20
  18.9 5.8 %collective-permute-start.8 = (bf16[8,16,128]{2,1,0:T(8,128)(2,1)S(1)}, bf16[8,16,128]{2,1,0:T(8,128)(2,1)S(1)}, u32[]{:S(2)}, u32[]{:S(2)}) collective-permute-start(bf16[8,16,128]{2,1,0:T(8,128)(2,1)S(1)} %get-tuple-element.52), channel_id=1, source_target_pairs={{0,12},{4,8},{8,4},{12,0},{1,13},{5,9},{9,5},{13,1},{2,14},{6,10},... | collective-permute-start | bytes 98312 | tf_op jit(solution)/shard_map/ppermute | solution.py:20
  20.2 4.7 %collective-permute-start.9 = (bf16[8,16,128]{2,1,0:T(8,128)(2,1)S(1)}, bf16[8,16,128]{2,1,0:T(8,128)(2,1)S(1)}, u32[]{:S(2)}, u32[]{:S(2)}) collective-permute-start(bf16[8,16,128]{2,1,0:T(8,128)(2,1)S(1)} %get-tuple-element.53), channel_id=1, source_target_pairs={{0,4},{4,0},{8,12},{12,8},{1,5},{5,1},{9,13},{13,9},{2,6},{6,2},{1... | collective-permute-start | bytes 98312 | tf_op jit(solution)/shard_map/ppermute | solution.py:20
  20.8 7.8 %collective-permute-start.6 = (bf16[12,16,128]{2,1,0:T(8,128)(2,1)S(1)}, bf16[12,16,128]{2,1,0:T(8,128)(2,1)S(1)}, u32[]{:S(2)}, u32[]{:S(2)}) collective-permute-start(bf16[12,16,128]{2,1,0:T(8,128)(2,1)S(1)} %get-tuple-element.45), channel_id=1, source_target_pairs={{0,12},{4,8},{8,4},{12,0},{1,13},{5,9},{9,5},{13,1},{2,14},{6,10},... | collective-permute-start | bytes 147464 | tf_op jit(solution)/shard_map/ppermute | solution.py:20
  22.9 5.9 %collective-permute-start.5 = (bf16[12,16,128]{2,1,0:T(8,128)(2,1)S(1)}, bf16[12,16,128]{2,1,0:T(8,128)(2,1)S(1)}, u32[]{:S(2)}, u32[]{:S(2)}) collective-permute-start(bf16[12,16,128]{2,1,0:T(8,128)(2,1)S(1)} %get-tuple-element.44), channel_id=1, source_target_pairs={{0,8},{4,12},{8,0},{12,4},{1,9},{5,13},{9,1},{13,5},{2,10},{6,14},... | collective-permute-start | bytes 147464 | tf_op jit(solution)/shard_map/ppermute | solution.py:20
  25.8 5.0 %collective-permute-start.12 = (bf16[32,16,128]{2,1,0:T(8,128)(2,1)S(1)}, bf16[32,16,128]{2,1,0:T(8,128)(2,1)S(1)}, u32[]{:S(2)}, u32[]{:S(2)}) collective-permute-start(bf16[32,16,128]{2,1,0:T(8,128)(2,1)S(1)} %induct_away.1._after), channel_id=1, source_target_pairs={{0,2},{2,0},{1,3},{3,1},{4,6},{6,4},{5,7},{7,5},{8,10},{10,8},{9,1... | collective-permute-start | bytes 393224 | tf_op jit(solution)/shard_map/ppermute | solution.py:20
  26.4 4.1 %collective-permute-start.11 = (bf16[12,16,128]{2,1,0:T(8,128)(2,1)S(1)}, bf16[12,16,128]{2,1,0:T(8,128)(2,1)S(1)}, u32[]{:S(2)}, u32[]{:S(2)}) collective-permute-start(bf16[12,16,128]{2,1,0:T(8,128)(2,1)S(1)} %hold_near.1._after), channel_id=1, source_target_pairs={{0,4},{4,0},{8,12},{12,8},{1,5},{5,1},{9,13},{13,9},{2,6},{6,2},{1... | collective-permute-start | bytes 147464 | tf_op jit(solution)/shard_map/ppermute | solution.py:20

commit v17 on v16

--- a/solution.py
+++ b/solution.py
@@ -45,13 +45,14 @@
     return [pltpu.with_memory_space_constraint(x, pltpu.HBM) for x in arrays]
 
 
-def pack_body(pan_own, charge, needs, message, wide):
+def pack_body(pan_own, seg_own, charge, needs, rows, message, listed, wide):
     width = charge.shape[1] // pan_own
     for q in range(pan_own):
         message[q] = charge[:, q * width : (q + 1) * width]
     wide[...] = jnp.zeros_like(wide)
     wide[: needs.shape[0], : needs.shape[1]] = needs[...]
     message[pan_own] = wide[...].astype(F32).astype(BF16)
+    sort_tiles(rows, listed, seg_own)
 
 
 def join_body(pan_own, own, *refs):
@@ -106,7 +107,7 @@
 
 def ends_body(n_row, n_col, pan_own, cap, n_moved, *refs):
     sources, targets = refs[: n_moved + 2], refs[n_moved + 2 : 2 * n_moved + 2]
-    (holder, listed, lanes, blocks, own, *sends), (cur, off, acc, sems) = refs[2 * n_moved + 2 : -4], refs[-4:]
+    (holder, lanes, blocks, own, *sends), (cur, off, acc, sems) = refs[2 * n_moved + 2 : -4], refs[-4:]
     copies = [
         pltpu.make_async_copy(source, target, sems.at[i])
         for i, (source, target) in enumerate(zip(sources, (cur, off, *targets)))
@@ -156,7 +157,6 @@
             sends[j - 1][here] = acc[pl.ds(k * pan_group + there * pan_own, pan_own)].astype(BF16)
     for copy in copies[4:]:
         copy.wait()
-    sort_tiles(targets[6], listed, seg_own)
 
 
 def pick_body(n_row, n_col, cap, partners, _after, *refs):
@@ -387,14 +387,15 @@
 
     charges = exchange_all(charge, [charge] * (n_col - 1), "col")
     cur = exchange_all(current, [current] * (n_col - 1), "col")
-    (pack,) = call(
-        functools.partial(pack_body, pan_own),
+    pack, listed = call(
+        functools.partial(pack_body, pan_own, seg_own),
         "pack_charges",
-        [like(pan_own + 1, BF16)],
-        [VMEM] * 2,
+        [like(pan_own + 1, BF16), pltpu.SMEM((2 * list_size(induct_rows.shape[0]) + 4,), jnp.int32)],
+        [VMEM, VMEM, SMEM],
         [pltpu.VMEM((rhs, width), jnp.int32)],
         moved=2**16,
-    )(*in_hbm(charge, induct_needs))
+        out_specs=[VMEM, SMEM],
+    )(*in_hbm(charge, induct_needs, induct_rows))
     (pack,) = call(
         functools.partial(join_body, pan_own),
         "join_charges",
@@ -412,7 +413,7 @@
         "end_sums",
         [pltpu.SMEM(x.shape, x.dtype) for x in scalars]
         + [jax.ShapeDtypeStruct(coeff_tiles.shape, BF16)]
-        + [pltpu.SMEM((2 * seg_own,), jnp.int32), pltpu.SMEM((2 * list_size(induct_rows.shape[0]) + 4,), jnp.int32)]
+        + [pltpu.SMEM((2 * seg_own,), jnp.int32)]
         + [jax.ShapeDtypeStruct((2 * seg_own, width), jnp.int32)]
         + [like(seg_own, BF16), like(rows_own, F32)]
         + [like(rows_own, BF16)] * (n_col - 1),
@@ -425,10 +426,10 @@
         ],
         flops=5 * 10**8,
         moved=2**18,
-        out_specs=[SMEM] * len(scalars) + [VMEM, SMEM, SMEM] + [VMEM] * (2 + n_col),
+        out_specs=[SMEM] * len(scalars) + [VMEM, SMEM] + [VMEM] * (2 + n_col),
     )(*in_hbm(current, off_t, *moved))
     _, links_s, coeff_slots, coeff_rows, coeff_needs, induct_slots, induct_rows, scale, coeff_tiles = outs[: len(moved)]
-    holder, listed, lanes, own_blocks, ends_own, *ends_out = outs[len(moved) :]
+    holder, lanes, own_blocks, ends_own, *ends_out = outs[len(moved) :]
 
     part, *messages = call(
         functools.partial(coeff_body, n_row, n_col, pan_own, partners),

time: 31.9 us -> 31.1 us (0.975)
  waiting for transfers between devices: 5.24 us -> 4.35 us
    ppermute x13, waiting for transfers between devices: 5.24 us -> 4.35 us  [exchange(): lax.ppermute(x, axis, [(i, i ^ k) for i in range(lax.axis_size(axis))])]
    pallas_call x1, Pallas kernels: 0.88 us -> 1.74 us  [shards(): call(functools.partial(pack_body, pan_own, seg_own), 'pack_charges', [lik...]
    pallas_call x1, Pallas kernels: 2.92 us -> 2.09 us  [shards(): call(functools.partial(ends_body, n_row, n_col, pan_own, cap_k, len(moved...]
  transfers between devices with their start and end apart: 13 -> 13, of which waited for: 6 -> 5; matrix products, arithmetic and copies ran while one was open for 0% -> 0% of each run, Pallas kernels for 23% -> 24%
where the time goes in v17:
time: 31.1 us; the launch traced here: 30.9 us
  starting transfers between devices  17.6 us (57%)
  Pallas kernels  8.3 us (27%)
  waiting for transfers between devices  4.35 us (14%)
  between operations  0.73 us (2%)
    ppermute x13, starting transfers between devices, exchange(): lax.ppermute(x, axis, [(i, i ^ k) for i in range(lax.axis_size(axis))])  17.6 us
    ppermute x13, waiting for transfers between devices, exchange(): lax.ppermute(x, axis, [(i, i ^ k) for i in range(lax.axis_size(axis))])  4.35 us
    pallas_call x1, Pallas kernels, shards(): call(functools.partial(ends_body, n_row, n_col, pan_own, cap_k, len(moved...  2.09 us
    pallas_call x1, Pallas kernels, shards(): call(functools.partial(pack_body, pan_own, seg_own), 'pack_charges', [lik...  1.74 us
    pallas_call x2, Pallas kernels, induct(): call(functools.partial(induct_body, n_row, n_col, seg_own, order, half),...  1.62 us
    pallas_call x1, Pallas kernels, shards(): call(functools.partial(final_body, n_row, n_col, pan_own), 'outputs', [ja...  0.83 us
    pallas_call x1, Pallas kernels, shards(): call(functools.partial(base_body, pan_own), 'base_sums', [like(seg_own, F...  0.73 us
    pallas_call x1, Pallas kernels, shards(): call(functools.partial(coeff_body, n_row, n_col, pan_own, partners), 'coe...  0.67 us
  transfers between devices with their start and end apart: 13, of which 5 were waited for; matrix products, arithmetic and copies ran while one was open for 0% of the time, Pallas kernels for 24%

profile of v17, /device:TPU:0, one launch (start us, length us, event | category | flops | bytes accessed | tf_op | source)
XLA Modules:
  0.0 30.9 jit_solution(3641478901363150028)
XLA Ops:
  0.6 3.0 %collective-permute-start = (bf16[16,512]{1,0:T(8,128)(2,1)}, bf16[16,512]{1,0:T(8,128)(2,1)S(1)}, u32[]{:S(2)}, u32[]{:S(2)}) collective-permute-start(bf16[16,512]{1,0:T(8,128)(2,1)} %charge.1), channel_id=1, source_target_pairs={{0,2},{2,0},{1,3},{3,1},{4,6},{6,4},{5,7},{7,5},{8,10},{10,8},{9,1... | collective-permute-start | bytes 49160 | tf_op jit(solution)/shard_map/ppermute | solution.py:20
  3.6 0.1 collective-permute-start.7
  3.7 1.7 %pack_charges.1 = (bf16[5,16,128]{2,1,0:T(8,128)(2,1)S(1)}, s32[420]{0:T(512)S(4)}) custom-call(bf16[16,512]{1,0:T(8,128)(2,1)} %charge.1, s32[4,8]{1,0:T(4,128)} %needs.1, s32[192]{0:T(256)} %rows.1), custom_call_target="tpu_custom_call" | custom-call | bytes 65536 | tf_op jit(solution)/shard_map/pack_charges/pallas_call | solution.py:390
  5.5 0.1 collective-permute-done.refs_0_
  5.6 3.3 %collective-permute-start.1 = (bf16[9,16,128]{2,1,0:T(8,128)(2,1)S(1)}, bf16[9,16,128]{2,1,0:T(8,128)(2,1)S(1)}, u32[]{:S(2)}, u32[]{:S(2)}) collective-permute-start(bf16[9,16,128]{2,1,0:T(8,128)(2,1)S(1)} %join_charges.1.refs_3_.pack), channel_id=1, source_target_pairs={{0,8},{4,12},{8,0},{12,4},{1,9},{5,13},{9,1},{13,5},{2,10},{6,14},... | collective-permute-start | bytes 110600 | tf_op jit(solution)/shard_map/ppermute | solution.py:20
  8.8 1.3 %collective-permute-start.2 = (bf16[9,16,128]{2,1,0:T(8,128)(2,1)S(1)}, bf16[9,16,128]{2,1,0:T(8,128)(2,1)S(1)}, u32[]{:S(2)}, u32[]{:S(2)}) collective-permute-start(bf16[9,16,128]{2,1,0:T(8,128)(2,1)S(1)} %join_charges.1.refs_3_.pack), channel_id=1, source_target_pairs={{0,12},{4,8},{8,4},{12,0},{1,13},{5,9},{9,5},{13,1},{2,14},{6,10},... | collective-permute-start | bytes 110600 | tf_op jit(solution)/shard_map/ppermute | solution.py:20
  10.2 0.2 collective-permute-start.3
  10.4 2.1 %end_sums.1 = (s32[2,32]{1,0:T(2,128)S(4)}, s32[4,16]{1,0:T(4,128)S(4)}, s32[96]{0:T(128)S(4)}, s32[96]{0:T(128)S(4)}, s32[4,4]{1,0:T(4,128)S(4)}, /*index=5*/s3...) custom-call(bf16[16,4096]{1,0:T(8,128)(2,1)} %refs_0_.1, ...), custom_call_target="tpu_custom_call" | custom-call | flops 500000000 | bytes 262144 | tf_op jit(solution)/shard_map/end_sums/pallas_call | solution.py:411
  12.5 0.0 collective-permute-done.1.refs_0_
  12.5 2.1 %collective-permute-done.2.refs_1_ = bf16[9,16,128]{2,1,0:T(8,128)(2,1)S(1)} collective-permute-done((bf16[9,16,128]{2,1,0:T(8,128)(2,1)S(1)}, bf16[9,16,128]{2,1,0:T(8,128)(2,1)S(1)}, u32[]{:S(2)}, u32[]{:S(2)}) %collective-permute-start.2) | collective-permute-done | bytes 36896 | tf_op jit(solution)/shard_map/ppermute | solution.py:20
  14.6 0.0 collective-permute-done.3.refs_2_
  14.6 0.7 %coeff_tiles.1 = (f32[8,16,128]{2,1,0:T(8,128)S(1)}, bf16[32,16,128]{2,1,0:T(8,128)(2,1)S(1)}) custom-call(s32[96]{0:T(128)S(4)} %get-tuple-element.37.slots, s32[96]{0:T(128)S(4)} %get-tuple-element.38.rows, s32[4,4]{1,0:T(4,128)S(4)} %get-tuple-element.39.needs, bf16[9,16,128]{2,1,0:T(8,128)(2,1)S(1)} %collective-permute-done.1.refs_0_, ...), custom_call_target="tpu_custom_call" | custom-call | flops 1000000000 | bytes 3145728 | tf_op jit(solution)/shard_map/coeff_tiles/pallas_call | solution.py:434
  15.3 1.6 %collective-permute-start.4 = (bf16[32,16,128]{2,1,0:T(8,128)(2,1)S(1)}, bf16[32,16,128]{2,1,0:T(8,128)(2,1)S(1)}, u32[]{:S(2)}, u32[]{:S(2)}) collective-permute-start(bf16[32,16,128]{2,1,0:T(8,128)(2,1)S(1)} %get-tuple-element.45), channel_id=1, source_target_pairs={{0,2},{2,0},{1,3},{3,1},{4,6},{6,4},{5,7},{7,5},{8,10},{10,8},{9,1... | collective-permute-start | bytes 393224 | tf_op jit(solution)/shard_map/ppermute | solution.py:20
  16.9 0.0 collective-permute-done.7.refs_5_
  16.9 0.3 pick_blocks.1
  17.2 1.3 %collective-permute-start.10 = (bf16[8,16,128]{2,1,0:T(8,128)(2,1)S(1)}, bf16[8,16,128]{2,1,0:T(8,128)(2,1)S(1)}, u32[]{:S(2)}, u32[]{:S(2)}) collective-permute-start(bf16[8,16,128]{2,1,0:T(8,128)(2,1)S(1)} %get-tuple-element.57), channel_id=1, source_target_pairs={{0,8},{4,12},{8,0},{12,4},{1,9},{5,13},{9,1},{13,5},{2,10},{6,14},... | collective-permute-start | bytes 98312 | tf_op jit(solution)/shard_map/ppermute | solution.py:20
  18.5 1.1 %collective-permute-start.8 = (bf16[8,16,128]{2,1,0:T(8,128)(2,1)S(1)}, bf16[8,16,128]{2,1,0:T(8,128)(2,1)S(1)}, u32[]{:S(2)}, u32[]{:S(2)}) collective-permute-start(bf16[8,16,128]{2,1,0:T(8,128)(2,1)S(1)} %get-tuple-element.54), channel_id=1, source_target_pairs={{0,12},{4,8},{8,4},{12,0},{1,13},{5,9},{9,5},{13,1},{2,14},{6,10},... | collective-permute-start | bytes 98312 | tf_op jit(solution)/shard_map/ppermute | solution.py:20
  19.6 1.2 %collective-permute-start.9 = (bf16[8,16,128]{2,1,0:T(8,128)(2,1)S(1)}, bf16[8,16,128]{2,1,0:T(8,128)(2,1)S(1)}, u32[]{:S(2)}, u32[]{:S(2)}) collective-permute-start(bf16[8,16,128]{2,1,0:T(8,128)(2,1)S(1)} %get-tuple-element.55), channel_id=1, source_target_pairs={{0,4},{4,0},{8,12},{12,8},{1,5},{5,1},{9,13},{13,9},{2,6},{6,2},{1... | collective-permute-start | bytes 98312 | tf_op jit(solution)/shard_map/ppermute | solution.py:20
  20.8 0.0 collective-permute-done.4.refs_0_
  20.8 2.1 %collective-permute-start.6 = (bf16[12,16,128]{2,1,0:T(8,128)(2,1)S(1)}, bf16[12,16,128]{2,1,0:T(8,128)(2,1)S(1)}, u32[]{:S(2)}, u32[]{:S(2)}) collective-permute-start(bf16[12,16,128]{2,1,0:T(8,128)(2,1)S(1)} %get-tuple-element.47), channel_id=1, source_target_pairs={{0,12},{4,8},{8,4},{12,0},{1,13},{5,9},{9,5},{13,1},{2,14},{6,10},... | collective-permute-start | bytes 147464 | tf_op jit(solution)/shard_map/ppermute | solution.py:20
  22.9 0.3 collective-permute-start.5
  23.1 1.2 %collective-permute-done.8.refs_0_ = bf16[8,16,128]{2,1,0:T(8,128)(2,1)S(1)} collective-permute-done((bf16[8,16,128]{2,1,0:T(8,128)(2,1)S(1)}, bf16[8,16,128]{2,1,0:T(8,128)(2,1)S(1)}, u32[]{:S(2)}, u32[]{:S(2)}) %collective-permute-start.8) | collective-permute-done | bytes 32800 | tf_op jit(solution)/shard_map/ppermute | solution.py:20
  24.4 0.7 %induct_away.1._after = bf16[32,16,128]{2,1,0:T(8,128)(2,1)S(1)} custom-call(s32[192]{0:T(256)S(4)} %get-tuple-element.49.slots, s32[192]{0:T(256)S(4)} %get-tuple-element.50.rows, s32[420]{0:T(512)S(4)} %get-tuple-element.51.listed, bf16[8,16,128]{2,1,0:T(8,128)(2,1)S(1)} %get-tuple-element.52._after.pot, ...), custom_call_target="tpu_custom_call" | custom-call | flops 100000000 | bytes 65536 | tf_op jit(solution)/shard_map/induct_away/pallas_call | solution.py:470
  25.1 0.6 %collective-permute-start.12 = (bf16[32,16,128]{2,1,0:T(8,128)(2,1)S(1)}, bf16[32,16,128]{2,1,0:T(8,128)(2,1)S(1)}, u32[]{:S(2)}, u32[]{:S(2)}) collective-permute-start(bf16[32,16,128]{2,1,0:T(8,128)(2,1)S(1)} %induct_away.1._after), channel_id=1, source_target_pairs={{0,2},{2,0},{1,3},{3,1},{4,6},{6,4},{5,7},{7,5},{8,10},{10,8},{9,1... | collective-permute-start | bytes 393224 | tf_op jit(solution)/shard_map/ppermute | solution.py:20
  25.7 1.5 %collective-permute-start.11 = (bf16[12,16,128]{2,1,0:T(8,128)(2,1)S(1)}, bf16[12,16,128]{2,1,0:T(8,128)(2,1)S(1)}, u32[]{:S(2)}, u32[]{:S(2)}) collective-permute-start(bf16[12,16,128]{2,1,0:T(8,128)(2,1)S(1)} %hold_near.1._after), channel_id=1, source_target_pairs={{0,4},{4,0},{8,12},{12,8},{1,5},{5,1},{9,13},{13,9},{2,6},{6,2},{1... | collective-permute-start | bytes 147464 | tf_op jit(solution)/shard_map/ppermute | solution.py:20
  27.2 0.9 %induct_own.1.field_own = f32[32,16,128]{2,1,0:T(8,128)S(1)} custom-call(s32[192]{0:T(256)S(4)} %get-tuple-element.49.slots, s32[192]{0:T(256)S(4)} %get-tuple-element.50.rows, s32[420]{0:T(512)S(4)} %get-tuple-element.51.listed, bf16[12,16,128]{2,1,0:T(8,128)(2,1)S(1)} %hold_near.1._after, bf16[8,16,128]{2,1,0:T(8,128)(2,1)S(1)} %collective-permute-done.8.refs_0_, ...), custom_call_target="tpu_custom_call" | custom-call | flops 100000000 | bytes 65536 | tf_op jit(solution)/shard_map/induct_own/pallas_call | solution.py:470
  28.1 0.7 %base_sums.1 = (f32[32,16,128]{2,1,0:T(8,128)S(1)}, f32[4,16,128]{2,1,0:T(8,128)S(1)}, bf16[16,512]{1,0:T(8,128)(2,1)}) custom-call(s32[4,16]{1,0:T(4,128)S(4)} %get-tuple-element.34.links, s32[64]{0:T(128)S(4)} %get-tuple-element.35.holder, f32[16]{0:T(128)S(4)} %get-tuple-element.48.scale, s32[64,128]{1,0:T(8,128)S(1)} %get-tuple-element.36.lanes, ...), custom_call_target="tpu_custom_call" | custom-call | tf_op jit(solution)/shard_map/base_sums/pallas_call | solution.py:496
  28.8 0.2 add_drops.2.field_in
  29.0 0.2 add_drops.3.field_own
  29.1 0.7 %collective-permute-done.11.refs_0_ = bf16[12,16,128]{2,1,0:T(8,128)(2,1)S(1)} collective-permute-done((bf16[12,16,128]{2,1,0:T(8,128)(2,1)S(1)}, bf16[12,16,128]{2,1,0:T(8,128)(2,1)S(1)}, u32[]{:S(2)}, u32[]{:S(2)}) %collective-permute-start.11) | collective-permute-done | bytes 49184 | tf_op jit(solution)/shard_map/ppermute | solution.py:20
  29.8 0.3 collective-permute-done.12.refs_3_
  30.1 0.8 %outputs.1 = (bf16[16,4096]{1,0:T(8,128)(2,1)}, bf16[16,512]{1,0:T(8,128)(2,1)}) custom-call(s32[4,16]{1,0:T(4,128)S(4)} %get-tuple-element.34.links, s32[64]{0:T(128)S(4)} %get-tuple-element.35.holder, s32[64,128]{1,0:T(8,128)S(1)} %get-tuple-element.36.lanes, f32[32,16,128]{2,1,0:T(8,128)S(1)} %add_drops.3.field_own, ...), custom_call_target="tpu_custom_call" | custom-call | flops 1000000000 | bytes 1048576 | tf_op jit(solution)/shard_map/outputs/pallas_call | solution.py:515
  (12 shorter events, 0.1 us)
Async XLA Ops:
  0.6 4.9 %collective-permute-start = (bf16[16,512]{1,0:T(8,128)(2,1)}, bf16[16,512]{1,0:T(8,128)(2,1)S(1)}, u32[]{:S(2)}, u32[]{:S(2)}) collective-permute-start(bf16[16,512]{1,0:T(8,128)(2,1)} %charge.1), channel_id=1, source_target_pairs={{0,2},{2,0},{1,3},{3,1},{4,6},{6,4},{5,7},{7,5},{8,10},{10,8},{9,1... | collective-permute-start | bytes 49160 | tf_op jit(solution)/shard_map/ppermute | solution.py:20
  3.6 13.3 %collective-permute-start.7 = (bf16[16,4096]{1,0:T(8,128)(2,1)}, bf16[16,4096]{1,0:T(8,128)(2,1)S(1)}, u32[]{:S(2)}, u32[]{:S(2)}) collective-permute-start(bf16[16,4096]{1,0:T(8,128)(2,1)} %refs_0_.1), channel_id=1, source_target_pairs={{0,2},{2,0},{1,3},{3,1},{4,6},{6,4},{5,7},{7,5},{8,10},{10,8},{9,1... | collective-permute-start | bytes 393224 | tf_op jit(solution)/shard_map/ppermute | solution.py:20
  3.7 20.6 %slice-start = ((s8[6291456]{0:T(1024)(128)(4,1)}), s8[4194304]{0:T(1024)(128)(4,1)S(1)}, s32[]{:S(2)}) async-start(s8[6291456]{0:T(1024)(128)(4,1)} %bitcast.2), calls=%async_computation | async-start | bytes 8388608
  5.6 7.0 %collective-permute-start.1 = (bf16[9,16,128]{2,1,0:T(8,128)(2,1)S(1)}, bf16[9,16,128]{2,1,0:T(8,128)(2,1)S(1)}, u32[]{:S(2)}, u32[]{:S(2)}) collective-permute-start(bf16[9,16,128]{2,1,0:T(8,128)(2,1)S(1)} %join_charges.1.refs_3_.pack), channel_id=1, source_target_pairs={{0,8},{4,12},{8,0},{12,4},{1,9},{5,13},{9,1},{13,5},{2,10},{6,14},... | collective-permute-start | bytes 110600 | tf_op jit(solution)/shard_map/ppermute | solution.py:20
  8.8 5.8 %collective-permute-start.2 = (bf16[9,16,128]{2,1,0:T(8,128)(2,1)S(1)}, bf16[9,16,128]{2,1,0:T(8,128)(2,1)S(1)}, u32[]{:S(2)}, u32[]{:S(2)}) collective-permute-start(bf16[9,16,128]{2,1,0:T(8,128)(2,1)S(1)} %join_charges.1.refs_3_.pack), channel_id=1, source_target_pairs={{0,12},{4,8},{8,4},{12,0},{1,13},{5,9},{9,5},{13,1},{2,14},{6,10},... | collective-permute-start | bytes 110600 | tf_op jit(solution)/shard_map/ppermute | solution.py:20
  10.2 4.4 %collective-permute-start.3 = (bf16[9,16,128]{2,1,0:T(8,128)(2,1)S(1)}, bf16[9,16,128]{2,1,0:T(8,128)(2,1)S(1)}, u32[]{:S(2)}, u32[]{:S(2)}) collective-permute-start(bf16[9,16,128]{2,1,0:T(8,128)(2,1)S(1)} %join_charges.1.refs_3_.pack), channel_id=1, source_target_pairs={{0,4},{4,0},{8,12},{12,8},{1,5},{5,1},{9,13},{13,9},{2,6},{6,2},{1... | collective-permute-start | bytes 110600 | tf_op jit(solution)/shard_map/ppermute | solution.py:20
  14.6 9.7 %slice-start.1 = ((s8[6291456]{0:T(1024)(128)(4,1)}), s8[2097152]{0:T(1024)(128)(4,1)S(1)}, s32[]{:S(2)}) async-start(s8[6291456]{0:T(1024)(128)(4,1)} %bitcast.2), calls=%async_computation.1 | async-start | bytes 4194304
  15.3 5.5 %collective-permute-start.4 = (bf16[32,16,128]{2,1,0:T(8,128)(2,1)S(1)}, bf16[32,16,128]{2,1,0:T(8,128)(2,1)S(1)}, u32[]{:S(2)}, u32[]{:S(2)}) collective-permute-start(bf16[32,16,128]{2,1,0:T(8,128)(2,1)S(1)} %get-tuple-element.45), channel_id=1, source_target_pairs={{0,2},{2,0},{1,3},{3,1},{4,6},{6,4},{5,7},{7,5},{8,10},{10,8},{9,1... | collective-permute-start | bytes 393224 | tf_op jit(solution)/shard_map/ppermute | solution.py:20
  17.2 5.9 %collective-permute-start.10 = (bf16[8,16,128]{2,1,0:T(8,128)(2,1)S(1)}, bf16[8,16,128]{2,1,0:T(8,128)(2,1)S(1)}, u32[]{:S(2)}, u32[]{:S(2)}) collective-permute-start(bf16[8,16,128]{2,1,0:T(8,128)(2,1)S(1)} %get-tuple-element.57), channel_id=1, source_target_pairs={{0,8},{4,12},{8,0},{12,4},{1,9},{5,13},{9,1},{13,5},{2,10},{6,14},... | collective-permute-start | bytes 98312 | tf_op jit(solution)/shard_map/ppermute | solution.py:20
  18.5 5.8 %collective-permute-start.8 = (bf16[8,16,128]{2,1,0:T(8,128)(2,1)S(1)}, bf16[8,16,128]{2,1,0:T(8,128)(2,1)S(1)}, u32[]{:S(2)}, u32[]{:S(2)}) collective-permute-start(bf16[8,16,128]{2,1,0:T(8,128)(2,1)S(1)} %get-tuple-element.54), channel_id=1, source_target_pairs={{0,12},{4,8},{8,4},{12,0},{1,13},{5,9},{9,5},{13,1},{2,14},{6,10},... | collective-permute-start | bytes 98312 | tf_op jit(solution)/shard_map/ppermute | solution.py:20
  19.6 4.8 %collective-permute-start.9 = (bf16[8,16,128]{2,1,0:T(8,128)(2,1)S(1)}, bf16[8,16,128]{2,1,0:T(8,128)(2,1)S(1)}, u32[]{:S(2)}, u32[]{:S(2)}) collective-permute-start(bf16[8,16,128]{2,1,0:T(8,128)(2,1)S(1)} %get-tuple-element.55), channel_id=1, source_target_pairs={{0,4},{4,0},{8,12},{12,8},{1,5},{5,1},{9,13},{13,9},{2,6},{6,2},{1... | collective-permute-start | bytes 98312 | tf_op jit(solution)/shard_map/ppermute | solution.py:20
  20.8 8.0 %collective-permute-start.6 = (bf16[12,16,128]{2,1,0:T(8,128)(2,1)S(1)}, bf16[12,16,128]{2,1,0:T(8,128)(2,1)S(1)}, u32[]{:S(2)}, u32[]{:S(2)}) collective-permute-start(bf16[12,16,128]{2,1,0:T(8,128)(2,1)S(1)} %get-tuple-element.47), channel_id=1, source_target_pairs={{0,12},{4,8},{8,4},{12,0},{1,13},{5,9},{9,5},{13,1},{2,14},{6,10},... | collective-permute-start | bytes 147464 | tf_op jit(solution)/shard_map/ppermute | solution.py:20
  22.9 6.1 %collective-permute-start.5 = (bf16[12,16,128]{2,1,0:T(8,128)(2,1)S(1)}, bf16[12,16,128]{2,1,0:T(8,128)(2,1)S(1)}, u32[]{:S(2)}, u32[]{:S(2)}) collective-permute-start(bf16[12,16,128]{2,1,0:T(8,128)(2,1)S(1)} %get-tuple-element.46), channel_id=1, source_target_pairs={{0,8},{4,12},{8,0},{12,4},{1,9},{5,13},{9,1},{13,5},{2,10},{6,14},... | collective-permute-start | bytes 147464 | tf_op jit(solution)/shard_map/ppermute | solution.py:20
  25.1 5.0 %collective-permute-start.12 = (bf16[32,16,128]{2,1,0:T(8,128)(2,1)S(1)}, bf16[32,16,128]{2,1,0:T(8,128)(2,1)S(1)}, u32[]{:S(2)}, u32[]{:S(2)}) collective-permute-start(bf16[32,16,128]{2,1,0:T(8,128)(2,1)S(1)} %induct_away.1._after), channel_id=1, source_target_pairs={{0,2},{2,0},{1,3},{3,1},{4,6},{6,4},{5,7},{7,5},{8,10},{10,8},{9,1... | collective-permute-start | bytes 393224 | tf_op jit(solution)/shard_map/ppermute | solution.py:20
  25.7 4.1 %collective-permute-start.11 = (bf16[12,16,128]{2,1,0:T(8,128)(2,1)S(1)}, bf16[12,16,128]{2,1,0:T(8,128)(2,1)S(1)}, u32[]{:S(2)}, u32[]{:S(2)}) collective-permute-start(bf16[12,16,128]{2,1,0:T(8,128)(2,1)S(1)} %hold_near.1._after), channel_id=1, source_target_pairs={{0,4},{4,0},{8,12},{12,8},{1,5},{5,1},{9,13},{13,9},{2,6},{6,2},{1... | collective-permute-start | bytes 147464 | tf_op jit(solution)/shard_map/ppermute | solution.py:20

commit v18 on v17

--- a/solution.py
+++ b/solution.py
@@ -75,7 +75,7 @@
 
 
 def first_run(count):
-    return count // 2 // STEP * STEP
+    return count * 7 // 12 // STEP * STEP
 
 
 def sort_tiles(rows, listed, seg_own):
@@ -107,7 +107,7 @@
 
 def ends_body(n_row, n_col, pan_own, cap, n_moved, *refs):
     sources, targets = refs[: n_moved + 2], refs[n_moved + 2 : 2 * n_moved + 2]
-    (holder, lanes, blocks, own, *sends), (cur, off, acc, sems) = refs[2 * n_moved + 2 : -4], refs[-4:]
+    (holder, named, lanes, blocks, own, *sends), (cur, off, acc, sems) = refs[2 * n_moved + 2 : -4], refs[-4:]
     copies = [
         pltpu.make_async_copy(source, target, sems.at[i])
         for i, (source, target) in enumerate(zip(sources, (cur, off, *targets)))
@@ -157,6 +157,10 @@
             sends[j - 1][here] = acc[pl.ds(k * pan_group + there * pan_own, pan_own)].astype(BF16)
     for copy in copies[4:]:
         copy.wait()
+    needs = targets[4]
+    for p in range(n_row):
+        for s in range(needs.shape[1]):
+            named[p * needs.shape[1] + s] = p * pan_group + needs[p, s]
 
 
 def pick_body(n_row, n_col, cap, partners, _after, *refs):
@@ -206,19 +210,15 @@
     add(start + count - 8, waiting)
 
 
-def coeff_body(n_row, n_col, pan_own, partners, slots, rows, needs, *refs):
+def coeff_body(n_row, n_col, pan_own, partners, slots, rows, named, *refs):
     packs = {k: refs[i] for i, k in enumerate([*partners, 0])}
     ends = refs[n_row : n_row + n_col - 1]
-    tiles, part, *messages = refs[n_row + n_col - 1 : -2]
-    src, named = refs[-2:]
+    tiles, part, *messages = refs[n_row + n_col - 1 : -1]
+    src = refs[-1]
     r = lax.axis_index("row")
     pan_group = pan_own * n_col
-    cap = needs.shape[1]
     for k in range(n_row):
         src[pl.ds(lax.bitwise_xor(r, k) * pan_group, pan_group)] = packs[k][pl.ds(0, pan_group)]
-    for p in range(n_row):
-        for s in range(cap):
-            named[p * cap + s] = p * pan_group + needs[p, s]
     part[...] = jnp.zeros_like(part)
     multiply(tiles, src, lambda t: t, lambda t: named[slots[t]], lambda t: rows[t], part, 0, tiles.shape[0])
     high = part[...].astype(BF16)
@@ -413,7 +413,7 @@
         "end_sums",
         [pltpu.SMEM(x.shape, x.dtype) for x in scalars]
         + [jax.ShapeDtypeStruct(coeff_tiles.shape, BF16)]
-        + [pltpu.SMEM((2 * seg_own,), jnp.int32)]
+        + [pltpu.SMEM((2 * seg_own,), jnp.int32), pltpu.SMEM((n_row * cap_p,), jnp.int32)]
         + [jax.ShapeDtypeStruct((2 * seg_own, width), jnp.int32)]
         + [like(seg_own, BF16), like(rows_own, F32)]
         + [like(rows_own, BF16)] * (n_col - 1),
@@ -426,23 +426,20 @@
         ],
         flops=5 * 10**8,
         moved=2**18,
-        out_specs=[SMEM] * len(scalars) + [VMEM, SMEM] + [VMEM] * (2 + n_col),
+        out_specs=[SMEM] * len(scalars) + [VMEM, SMEM, SMEM] + [VMEM] * (2 + n_col),
     )(*in_hbm(current, off_t, *moved))
     _, links_s, coeff_slots, coeff_rows, coeff_needs, induct_slots, induct_rows, scale, coeff_tiles = outs[: len(moved)]
-    holder, lanes, own_blocks, ends_own, *ends_out = outs[len(moved) :]
+    holder, named, lanes, own_blocks, ends_own, *ends_out = outs[len(moved) :]
 
     part, *messages = call(
         functools.partial(coeff_body, n_row, n_col, pan_own, partners),
         "coeff_tiles",
         [like(pan_group, F32)] + [like(2 * pan_group + rows_own, BF16)] * (n_col - 1),
         [SMEM] * 3 + [VMEM] * (n_row + n_col),
-        [
-            pltpu.VMEM((n_row * pan_group, rhs, width), BF16),
-            pltpu.SMEM((n_row * cap_p,), jnp.int32),
-        ],
+        [pltpu.VMEM((n_row * pan_group, rhs, width), BF16)],
         flops=10**9,
         moved=coeff_tiles.size * 2,
-    )(coeff_slots, coeff_rows, coeff_needs, *[packs[k] for k in partners], packs[0], *ends_out, coeff_tiles)
+    )(coeff_slots, coeff_rows, named, *[packs[k] for k in partners], packs[0], *ends_out, coeff_tiles)
     parts = exchange_all(None, messages, "col")[1:]
 
     *picks, own_picks = call(

time: 31.1 us -> 31.1 us (level)
  transfers between devices with their start and end apart: 13 -> 13, of which waited for: 5 -> 4; matrix products, arithmetic and copies ran while one was open for 0% -> 0% of each run, Pallas kernels for 24% -> 24%
where the time goes in v18:
time: 31.1 us; the launch traced here: 30.9 us
  starting transfers between devices  17.6 us (57%)
  Pallas kernels  8.38 us (27%)
  waiting for transfers between devices  4.15 us (13%)
  between operations  0.74 us (2%)
    ppermute x13, starting transfers between devices, exchange(): lax.ppermute(x, axis, [(i, i ^ k) for i in range(lax.axis_size(axis))])  17.6 us
    ppermute x13, waiting for transfers between devices, exchange(): lax.ppermute(x, axis, [(i, i ^ k) for i in range(lax.axis_size(axis))])  4.15 us
    pallas_call x1, Pallas kernels, shards(): call(functools.partial(ends_body, n_row, n_col, pan_own, cap_k, len(moved...  2.09 us
    pallas_call x1, Pallas kernels, shards(): call(functools.partial(pack_body, pan_own, seg_own), 'pack_charges', [lik...  1.83 us
    pallas_call x2, Pallas kernels, induct(): call(functools.partial(induct_body, n_row, n_col, seg_own, order, half),...  1.59 us
    pallas_call x1, Pallas kernels, shards(): call(functools.partial(final_body, n_row, n_col, pan_own), 'outputs', [ja...  0.83 us
    pallas_call x1, Pallas kernels, shards(): call(functools.partial(base_body, pan_own), 'base_sums', [like(seg_own, F...  0.73 us
    pallas_call x1, Pallas kernels, shards(): call(functools.partial(coeff_body, n_row, n_col, pan_own, partners), 'coe...  0.68 us
  transfers between devices with their start and end apart: 13, of which 4 were waited for; matrix products, arithmetic and copies ran while one was open for 0% of the time, Pallas kernels for 24%

profile of v18, /device:TPU:0, one launch (start us, length us, event | category | flops | bytes accessed | tf_op | source)
XLA Modules:
  0.0 30.9 jit_solution(17074577595412324638)
XLA Ops:
  0.6 3.0 %collective-permute-start = (bf16[16,512]{1,0:T(8,128)(2,1)}, bf16[16,512]{1,0:T(8,128)(2,1)S(1)}, u32[]{:S(2)}, u32[]{:S(2)}) collective-permute-start(bf16[16,512]{1,0:T(8,128)(2,1)} %charge.1), channel_id=1, source_target_pairs={{0,2},{2,0},{1,3},{3,1},{4,6},{6,4},{5,7},{7,5},{8,10},{10,8},{9,1... | collective-permute-start | bytes 49160 | tf_op jit(solution)/shard_map/ppermute | solution.py:20
  3.6 0.1 collective-permute-start.7
  3.7 1.8 %pack_charges.1 = (bf16[5,16,128]{2,1,0:T(8,128)(2,1)S(1)}, s32[420]{0:T(512)S(4)}) custom-call(bf16[16,512]{1,0:T(8,128)(2,1)} %charge.1, s32[4,8]{1,0:T(4,128)} %needs.1, s32[192]{0:T(256)} %rows.1), custom_call_target="tpu_custom_call" | custom-call | bytes 65536 | tf_op jit(solution)/shard_map/pack_charges/pallas_call | solution.py:390
  5.6 0.0 collective-permute-done.refs_0_
  5.6 3.3 %collective-permute-start.1 = (bf16[9,16,128]{2,1,0:T(8,128)(2,1)S(1)}, bf16[9,16,128]{2,1,0:T(8,128)(2,1)S(1)}, u32[]{:S(2)}, u32[]{:S(2)}) collective-permute-start(bf16[9,16,128]{2,1,0:T(8,128)(2,1)S(1)} %join_charges.1.refs_3_.pack), channel_id=1, source_target_pairs={{0,8},{4,12},{8,0},{12,4},{1,9},{5,13},{9,1},{13,5},{2,10},{6,14},... | collective-permute-start | bytes 110600 | tf_op jit(solution)/shard_map/ppermute | solution.py:20
  8.8 1.3 %collective-permute-start.2 = (bf16[9,16,128]{2,1,0:T(8,128)(2,1)S(1)}, bf16[9,16,128]{2,1,0:T(8,128)(2,1)S(1)}, u32[]{:S(2)}, u32[]{:S(2)}) collective-permute-start(bf16[9,16,128]{2,1,0:T(8,128)(2,1)S(1)} %join_charges.1.refs_3_.pack), channel_id=1, source_target_pairs={{0,12},{4,8},{8,4},{12,0},{1,13},{5,9},{9,5},{13,1},{2,14},{6,10},... | collective-permute-start | bytes 110600 | tf_op jit(solution)/shard_map/ppermute | solution.py:20
  10.2 0.2 collective-permute-start.3
  10.4 2.1 %end_sums.1 = (s32[2,32]{1,0:T(2,128)S(4)}, s32[4,16]{1,0:T(4,128)S(4)}, s32[96]{0:T(128)S(4)}, s32[96]{0:T(128)S(4)}, s32[4,4]{1,0:T(4,128)S(4)}, /*index=5*/s3...) custom-call(bf16[16,4096]{1,0:T(8,128)(2,1)} %refs_0_.1, ...), custom_call_target="tpu_custom_call" | custom-call | flops 500000000 | bytes 262144 | tf_op jit(solution)/shard_map/end_sums/pallas_call | solution.py:411
  12.5 0.0 collective-permute-done.1.refs_0_
  12.5 2.1 %collective-permute-done.2.refs_1_ = bf16[9,16,128]{2,1,0:T(8,128)(2,1)S(1)} collective-permute-done((bf16[9,16,128]{2,1,0:T(8,128)(2,1)S(1)}, bf16[9,16,128]{2,1,0:T(8,128)(2,1)S(1)}, u32[]{:S(2)}, u32[]{:S(2)}) %collective-permute-start.2) | collective-permute-done | bytes 36896 | tf_op jit(solution)/shard_map/ppermute | solution.py:20
  14.6 0.0 collective-permute-done.3.refs_2_
  14.6 0.7 %coeff_tiles.1 = (f32[8,16,128]{2,1,0:T(8,128)S(1)}, bf16[32,16,128]{2,1,0:T(8,128)(2,1)S(1)}) custom-call(s32[96]{0:T(128)S(4)} %get-tuple-element.37.slots, s32[96]{0:T(128)S(4)} %get-tuple-element.38.rows, s32[16]{0:T(128)S(4)} %get-tuple-element.39.named, bf16[9,16,128]{2,1,0:T(8,128)(2,1)S(1)} %collective-permute-done.1.refs_0_, ...), custom_call_target="tpu_custom_call" | custom-call | flops 1000000000 | bytes 3145728 | tf_op jit(solution)/shard_map/coeff_tiles/pallas_call | solution.py:434
  15.3 1.6 %collective-permute-start.4 = (bf16[32,16,128]{2,1,0:T(8,128)(2,1)S(1)}, bf16[32,16,128]{2,1,0:T(8,128)(2,1)S(1)}, u32[]{:S(2)}, u32[]{:S(2)}) collective-permute-start(bf16[32,16,128]{2,1,0:T(8,128)(2,1)S(1)} %get-tuple-element.45), channel_id=1, source_target_pairs={{0,2},{2,0},{1,3},{3,1},{4,6},{6,4},{5,7},{7,5},{8,10},{10,8},{9,1... | collective-permute-start | bytes 393224 | tf_op jit(solution)/shard_map/ppermute | solution.py:20
  16.9 0.0 collective-permute-done.7.refs_5_
  16.9 0.3 pick_blocks.1
  17.2 1.3 %collective-permute-start.10 = (bf16[8,16,128]{2,1,0:T(8,128)(2,1)S(1)}, bf16[8,16,128]{2,1,0:T(8,128)(2,1)S(1)}, u32[]{:S(2)}, u32[]{:S(2)}) collective-permute-start(bf16[8,16,128]{2,1,0:T(8,128)(2,1)S(1)} %get-tuple-element.57), channel_id=1, source_target_pairs={{0,8},{4,12},{8,0},{12,4},{1,9},{5,13},{9,1},{13,5},{2,10},{6,14},... | collective-permute-start | bytes 98312 | tf_op jit(solution)/shard_map/ppermute | solution.py:20
  18.5 1.1 %collective-permute-start.8 = (bf16[8,16,128]{2,1,0:T(8,128)(2,1)S(1)}, bf16[8,16,128]{2,1,0:T(8,128)(2,1)S(1)}, u32[]{:S(2)}, u32[]{:S(2)}) collective-permute-start(bf16[8,16,128]{2,1,0:T(8,128)(2,1)S(1)} %get-tuple-element.54), channel_id=1, source_target_pairs={{0,12},{4,8},{8,4},{12,0},{1,13},{5,9},{9,5},{13,1},{2,14},{6,10},... | collective-permute-start | bytes 98312 | tf_op jit(solution)/shard_map/ppermute | solution.py:20
  19.6 1.2 %collective-permute-start.9 = (bf16[8,16,128]{2,1,0:T(8,128)(2,1)S(1)}, bf16[8,16,128]{2,1,0:T(8,128)(2,1)S(1)}, u32[]{:S(2)}, u32[]{:S(2)}) collective-permute-start(bf16[8,16,128]{2,1,0:T(8,128)(2,1)S(1)} %get-tuple-element.55), channel_id=1, source_target_pairs={{0,4},{4,0},{8,12},{12,8},{1,5},{5,1},{9,13},{13,9},{2,6},{6,2},{1... | collective-permute-start | bytes 98312 | tf_op jit(solution)/shard_map/ppermute | solution.py:20
  20.8 2.1 %collective-permute-start.6 = (bf16[12,16,128]{2,1,0:T(8,128)(2,1)S(1)}, bf16[12,16,128]{2,1,0:T(8,128)(2,1)S(1)}, u32[]{:S(2)}, u32[]{:S(2)}) collective-permute-start(bf16[12,16,128]{2,1,0:T(8,128)(2,1)S(1)} %get-tuple-element.47), channel_id=1, source_target_pairs={{0,12},{4,8},{8,4},{12,0},{1,13},{5,9},{9,5},{13,1},{2,14},{6,10},... | collective-permute-start | bytes 147464 | tf_op jit(solution)/shard_map/ppermute | solution.py:20
  22.9 0.3 collective-permute-start.5
  23.1 1.1 %collective-permute-done.8.refs_0_ = bf16[8,16,128]{2,1,0:T(8,128)(2,1)S(1)} collective-permute-done((bf16[8,16,128]{2,1,0:T(8,128)(2,1)S(1)}, bf16[8,16,128]{2,1,0:T(8,128)(2,1)S(1)}, u32[]{:S(2)}, u32[]{:S(2)}) %collective-permute-start.8) | collective-permute-done | bytes 32800 | tf_op jit(solution)/shard_map/ppermute | solution.py:20
  24.2 0.8 %induct_away.1._after = bf16[32,16,128]{2,1,0:T(8,128)(2,1)S(1)} custom-call(s32[192]{0:T(256)S(4)} %get-tuple-element.49.slots, s32[192]{0:T(256)S(4)} %get-tuple-element.50.rows, s32[420]{0:T(512)S(4)} %get-tuple-element.51.listed, bf16[8,16,128]{2,1,0:T(8,128)(2,1)S(1)} %get-tuple-element.52._after.pot, ...), custom_call_target="tpu_custom_call" | custom-call | flops 100000000 | bytes 65536 | tf_op jit(solution)/shard_map/induct_away/pallas_call | solution.py:467
  25.1 0.5 %collective-permute-start.12 = (bf16[32,16,128]{2,1,0:T(8,128)(2,1)S(1)}, bf16[32,16,128]{2,1,0:T(8,128)(2,1)S(1)}, u32[]{:S(2)}, u32[]{:S(2)}) collective-permute-start(bf16[32,16,128]{2,1,0:T(8,128)(2,1)S(1)} %induct_away.1._after), channel_id=1, source_target_pairs={{0,2},{2,0},{1,3},{3,1},{4,6},{6,4},{5,7},{7,5},{8,10},{10,8},{9,1... | collective-permute-start | bytes 393224 | tf_op jit(solution)/shard_map/ppermute | solution.py:20
  25.6 1.7 %collective-permute-start.11 = (bf16[12,16,128]{2,1,0:T(8,128)(2,1)S(1)}, bf16[12,16,128]{2,1,0:T(8,128)(2,1)S(1)}, u32[]{:S(2)}, u32[]{:S(2)}) collective-permute-start(bf16[12,16,128]{2,1,0:T(8,128)(2,1)S(1)} %hold_near.1._after), channel_id=1, source_target_pairs={{0,4},{4,0},{8,12},{12,8},{1,5},{5,1},{9,13},{13,9},{2,6},{6,2},{1... | collective-permute-start | bytes 147464 | tf_op jit(solution)/shard_map/ppermute | solution.py:20
  27.3 0.8 %induct_own.1.field_own = f32[32,16,128]{2,1,0:T(8,128)S(1)} custom-call(s32[192]{0:T(256)S(4)} %get-tuple-element.49.slots, s32[192]{0:T(256)S(4)} %get-tuple-element.50.rows, s32[420]{0:T(512)S(4)} %get-tuple-element.51.listed, bf16[12,16,128]{2,1,0:T(8,128)(2,1)S(1)} %hold_near.1._after, bf16[8,16,128]{2,1,0:T(8,128)(2,1)S(1)} %collective-permute-done.8.refs_0_, ...), custom_call_target="tpu_custom_call" | custom-call | flops 100000000 | bytes 65536 | tf_op jit(solution)/shard_map/induct_own/pallas_call | solution.py:467
  28.1 0.7 %base_sums.1 = (f32[32,16,128]{2,1,0:T(8,128)S(1)}, f32[4,16,128]{2,1,0:T(8,128)S(1)}, bf16[16,512]{1,0:T(8,128)(2,1)}) custom-call(s32[4,16]{1,0:T(4,128)S(4)} %get-tuple-element.34.links, s32[64]{0:T(128)S(4)} %get-tuple-element.35.holder, f32[16]{0:T(128)S(4)} %get-tuple-element.48.scale, s32[64,128]{1,0:T(8,128)S(1)} %get-tuple-element.36.lanes, ...), custom_call_target="tpu_custom_call" | custom-call | tf_op jit(solution)/shard_map/base_sums/pallas_call | solution.py:493
  28.8 0.0 collective-permute-done.6.message.refs_2_
  28.8 0.1 add_drops.2.field_in
  29.0 0.1 add_drops.3.field_own
  29.1 0.6 %collective-permute-done.11.refs_0_ = bf16[12,16,128]{2,1,0:T(8,128)(2,1)S(1)} collective-permute-done((bf16[12,16,128]{2,1,0:T(8,128)(2,1)S(1)}, bf16[12,16,128]{2,1,0:T(8,128)(2,1)S(1)}, u32[]{:S(2)}, u32[]{:S(2)}) %collective-permute-start.11) | collective-permute-done | bytes 49184 | tf_op jit(solution)/shard_map/ppermute | solution.py:20
  29.7 0.4 %collective-permute-done.12.refs_3_ = bf16[32,16,128]{2,1,0:T(8,128)(2,1)S(1)} collective-permute-done((bf16[32,16,128]{2,1,0:T(8,128)(2,1)S(1)}, bf16[32,16,128]{2,1,0:T(8,128)(2,1)S(1)}, u32[]{:S(2)}, u32[]{:S(2)}) %collective-permute-start.12) | collective-permute-done | bytes 131104 | tf_op jit(solution)/shard_map/ppermute | solution.py:20
  30.1 0.8 %outputs.1 = (bf16[16,4096]{1,0:T(8,128)(2,1)}, bf16[16,512]{1,0:T(8,128)(2,1)}) custom-call(s32[4,16]{1,0:T(4,128)S(4)} %get-tuple-element.34.links, s32[64]{0:T(128)S(4)} %get-tuple-element.35.holder, s32[64,128]{1,0:T(8,128)S(1)} %get-tuple-element.36.lanes, f32[32,16,128]{2,1,0:T(8,128)S(1)} %add_drops.3.field_own, ...), custom_call_target="tpu_custom_call" | custom-call | flops 1000000000 | bytes 1048576 | tf_op jit(solution)/shard_map/outputs/pallas_call | solution.py:512
  (12 shorter events, 0.1 us)
Async XLA Ops:
  0.6 4.9 %collective-permute-start = (bf16[16,512]{1,0:T(8,128)(2,1)}, bf16[16,512]{1,0:T(8,128)(2,1)S(1)}, u32[]{:S(2)}, u32[]{:S(2)}) collective-permute-start(bf16[16,512]{1,0:T(8,128)(2,1)} %charge.1), channel_id=1, source_target_pairs={{0,2},{2,0},{1,3},{3,1},{4,6},{6,4},{5,7},{7,5},{8,10},{10,8},{9,1... | collective-permute-start | bytes 49160 | tf_op jit(solution)/shard_map/ppermute | solution.py:20
  3.6 13.3 %collective-permute-start.7 = (bf16[16,4096]{1,0:T(8,128)(2,1)}, bf16[16,4096]{1,0:T(8,128)(2,1)S(1)}, u32[]{:S(2)}, u32[]{:S(2)}) collective-permute-start(bf16[16,4096]{1,0:T(8,128)(2,1)} %refs_0_.1), channel_id=1, source_target_pairs={{0,2},{2,0},{1,3},{3,1},{4,6},{6,4},{5,7},{7,5},{8,10},{10,8},{9,1... | collective-permute-start | bytes 393224 | tf_op jit(solution)/shard_map/ppermute | solution.py:20
  3.7 20.5 %slice-start = ((s8[6291456]{0:T(1024)(128)(4,1)}), s8[4194304]{0:T(1024)(128)(4,1)S(1)}, s32[]{:S(2)}) async-start(s8[6291456]{0:T(1024)(128)(4,1)} %bitcast.2), calls=%async_computation | async-start | bytes 8388608
  5.6 6.9 %collective-permute-start.1 = (bf16[9,16,128]{2,1,0:T(8,128)(2,1)S(1)}, bf16[9,16,128]{2,1,0:T(8,128)(2,1)S(1)}, u32[]{:S(2)}, u32[]{:S(2)}) collective-permute-start(bf16[9,16,128]{2,1,0:T(8,128)(2,1)S(1)} %join_charges.1.refs_3_.pack), channel_id=1, source_target_pairs={{0,8},{4,12},{8,0},{12,4},{1,9},{5,13},{9,1},{13,5},{2,10},{6,14},... | collective-permute-start | bytes 110600 | tf_op jit(solution)/shard_map/ppermute | solution.py:20
  8.8 5.8 %collective-permute-start.2 = (bf16[9,16,128]{2,1,0:T(8,128)(2,1)S(1)}, bf16[9,16,128]{2,1,0:T(8,128)(2,1)S(1)}, u32[]{:S(2)}, u32[]{:S(2)}) collective-permute-start(bf16[9,16,128]{2,1,0:T(8,128)(2,1)S(1)} %join_charges.1.refs_3_.pack), channel_id=1, source_target_pairs={{0,12},{4,8},{8,4},{12,0},{1,13},{5,9},{9,5},{13,1},{2,14},{6,10},... | collective-permute-start | bytes 110600 | tf_op jit(solution)/shard_map/ppermute | solution.py:20
  10.2 4.4 %collective-permute-start.3 = (bf16[9,16,128]{2,1,0:T(8,128)(2,1)S(1)}, bf16[9,16,128]{2,1,0:T(8,128)(2,1)S(1)}, u32[]{:S(2)}, u32[]{:S(2)}) collective-permute-start(bf16[9,16,128]{2,1,0:T(8,128)(2,1)S(1)} %join_charges.1.refs_3_.pack), channel_id=1, source_target_pairs={{0,4},{4,0},{8,12},{12,8},{1,5},{5,1},{9,13},{13,9},{2,6},{6,2},{1... | collective-permute-start | bytes 110600 | tf_op jit(solution)/shard_map/ppermute | solution.py:20
  14.6 9.6 %slice-start.1 = ((s8[6291456]{0:T(1024)(128)(4,1)}), s8[2097152]{0:T(1024)(128)(4,1)S(1)}, s32[]{:S(2)}) async-start(s8[6291456]{0:T(1024)(128)(4,1)} %bitcast.2), calls=%async_computation.1 | async-start | bytes 4194304
  15.3 5.5 %collective-permute-start.4 = (bf16[32,16,128]{2,1,0:T(8,128)(2,1)S(1)}, bf16[32,16,128]{2,1,0:T(8,128)(2,1)S(1)}, u32[]{:S(2)}, u32[]{:S(2)}) collective-permute-start(bf16[32,16,128]{2,1,0:T(8,128)(2,1)S(1)} %get-tuple-element.45), channel_id=1, source_target_pairs={{0,2},{2,0},{1,3},{3,1},{4,6},{6,4},{5,7},{7,5},{8,10},{10,8},{9,1... | collective-permute-start | bytes 393224 | tf_op jit(solution)/shard_map/ppermute | solution.py:20
  17.2 6.0 %collective-permute-start.10 = (bf16[8,16,128]{2,1,0:T(8,128)(2,1)S(1)}, bf16[8,16,128]{2,1,0:T(8,128)(2,1)S(1)}, u32[]{:S(2)}, u32[]{:S(2)}) collective-permute-start(bf16[8,16,128]{2,1,0:T(8,128)(2,1)S(1)} %get-tuple-element.57), channel_id=1, source_target_pairs={{0,8},{4,12},{8,0},{12,4},{1,9},{5,13},{9,1},{13,5},{2,10},{6,14},... | collective-permute-start | bytes 98312 | tf_op jit(solution)/shard_map/ppermute | solution.py:20
  18.5 5.7 %collective-permute-start.8 = (bf16[8,16,128]{2,1,0:T(8,128)(2,1)S(1)}, bf16[8,16,128]{2,1,0:T(8,128)(2,1)S(1)}, u32[]{:S(2)}, u32[]{:S(2)}) collective-permute-start(bf16[8,16,128]{2,1,0:T(8,128)(2,1)S(1)} %get-tuple-element.54), channel_id=1, source_target_pairs={{0,12},{4,8},{8,4},{12,0},{1,13},{5,9},{9,5},{13,1},{2,14},{6,10},... | collective-permute-start | bytes 98312 | tf_op jit(solution)/shard_map/ppermute | solution.py:20
  19.6 4.7 %collective-permute-start.9 = (bf16[8,16,128]{2,1,0:T(8,128)(2,1)S(1)}, bf16[8,16,128]{2,1,0:T(8,128)(2,1)S(1)}, u32[]{:S(2)}, u32[]{:S(2)}) collective-permute-start(bf16[8,16,128]{2,1,0:T(8,128)(2,1)S(1)} %get-tuple-element.55), channel_id=1, source_target_pairs={{0,4},{4,0},{8,12},{12,8},{1,5},{5,1},{9,13},{13,9},{2,6},{6,2},{1... | collective-permute-start | bytes 98312 | tf_op jit(solution)/shard_map/ppermute | solution.py:20
  20.8 8.0 %collective-permute-start.6 = (bf16[12,16,128]{2,1,0:T(8,128)(2,1)S(1)}, bf16[12,16,128]{2,1,0:T(8,128)(2,1)S(1)}, u32[]{:S(2)}, u32[]{:S(2)}) collective-permute-start(bf16[12,16,128]{2,1,0:T(8,128)(2,1)S(1)} %get-tuple-element.47), channel_id=1, source_target_pairs={{0,12},{4,8},{8,4},{12,0},{1,13},{5,9},{9,5},{13,1},{2,14},{6,10},... | collective-permute-start | bytes 147464 | tf_op jit(solution)/shard_map/ppermute | solution.py:20
  22.9 6.1 %collective-permute-start.5 = (bf16[12,16,128]{2,1,0:T(8,128)(2,1)S(1)}, bf16[12,16,128]{2,1,0:T(8,128)(2,1)S(1)}, u32[]{:S(2)}, u32[]{:S(2)}) collective-permute-start(bf16[12,16,128]{2,1,0:T(8,128)(2,1)S(1)} %get-tuple-element.46), channel_id=1, source_target_pairs={{0,8},{4,12},{8,0},{12,4},{1,9},{5,13},{9,1},{13,5},{2,10},{6,14},... | collective-permute-start | bytes 147464 | tf_op jit(solution)/shard_map/ppermute | solution.py:20
  25.1 5.0 %collective-permute-start.12 = (bf16[32,16,128]{2,1,0:T(8,128)(2,1)S(1)}, bf16[32,16,128]{2,1,0:T(8,128)(2,1)S(1)}, u32[]{:S(2)}, u32[]{:S(2)}) collective-permute-start(bf16[32,16,128]{2,1,0:T(8,128)(2,1)S(1)} %induct_away.1._after), channel_id=1, source_target_pairs={{0,2},{2,0},{1,3},{3,1},{4,6},{6,4},{5,7},{7,5},{8,10},{10,8},{9,1... | collective-permute-start | bytes 393224 | tf_op jit(solution)/shard_map/ppermute | solution.py:20
  25.6 4.1 %collective-permute-start.11 = (bf16[12,16,128]{2,1,0:T(8,128)(2,1)S(1)}, bf16[12,16,128]{2,1,0:T(8,128)(2,1)S(1)}, u32[]{:S(2)}, u32[]{:S(2)}) collective-permute-start(bf16[12,16,128]{2,1,0:T(8,128)(2,1)S(1)} %hold_near.1._after), channel_id=1, source_target_pairs={{0,4},{4,0},{8,12},{12,8},{1,5},{5,1},{9,13},{13,9},{2,6},{6,2},{1... | collective-permute-start | bytes 147464 | tf_op jit(solution)/shard_map/ppermute | solution.py:20

commit v19 on v18

--- a/solution.py
+++ b/solution.py
@@ -461,7 +461,7 @@
         moved=2**18,
     )(part, ends_own, *parts)
 
-    order = [*partners[1:], 0, partners[0]]
+    order = [*range(n_row - 2, -1, -1), n_row - 1]
 
     def induct(name, half, outs, after):
         return call(
@@ -499,13 +499,13 @@
         moved=0,
     )(links_s, holder, scale, lanes, pack, field_own, end_keep, pot)
 
-    for k in reversed(range(2, n_row)):
+    for k in partners[:-1]:
         (field,) = call(
             functools.partial(drops_body, k, pan_own),
             "add_drops",
             [like(seg_own, F32)],
             [SMEM] * 2 + [VMEM] * 3,
-            flops=11 * 10**8 if k == 2 else 0,
+            flops=11 * 10**8 if k == partners[-2] else 0,
             moved=0,
         )(links_s, holder, lanes, arrived[k - 1], field)
 

time: 31.1 us -> 31.6 us (1.016)
  waiting for transfers between devices: 4.15 us -> 4.52 us
    ppermute x13, waiting for transfers between devices: 4.15 us -> 4.52 us  [exchange(): lax.ppermute(x, axis, [(i, i ^ k) for i in range(lax.axis_size(axis))])]
where the time goes in v19:
time: 31.6 us; the launch traced here: 31.4 us
  starting transfers between devices  17.8 us (56%)
  Pallas kernels  8.36 us (26%)
  waiting for transfers between devices  4.52 us (14%)
  between operations  0.74 us (2%)
    ppermute x13, starting transfers between devices, exchange(): lax.ppermute(x, axis, [(i, i ^ k) for i in range(lax.axis_size(axis))])  17.8 us
    ppermute x13, waiting for transfers between devices, exchange(): lax.ppermute(x, axis, [(i, i ^ k) for i in range(lax.axis_size(axis))])  4.52 us
    pallas_call x1, Pallas kernels, shards(): call(functools.partial(ends_body, n_row, n_col, pan_own, cap_k, len(moved...  2.09 us
    pallas_call x1, Pallas kernels, shards(): call(functools.partial(pack_body, pan_own, seg_own), 'pack_charges', [lik...  1.83 us
    pallas_call x2, Pallas kernels, induct(): call(functools.partial(induct_body, n_row, n_col, seg_own, order, half),...  1.59 us
    pallas_call x1, Pallas kernels, shards(): call(functools.partial(final_body, n_row, n_col, pan_own), 'outputs', [ja...  0.83 us
    pallas_call x1, Pallas kernels, shards(): call(functools.partial(base_body, pan_own), 'base_sums', [like(seg_own, F...  0.73 us
    pallas_call x1, Pallas kernels, shards(): call(functools.partial(coeff_body, n_row, n_col, pan_own, partners), 'coe...  0.67 us
  transfers between devices with their start and end apart: 13, of which 4 were waited for; matrix products, arithmetic and copies ran while one was open for 0% of the time, Pallas kernels for 24%

profile of v19, /device:TPU:0, one launch (start us, length us, event | category | flops | bytes accessed | tf_op | source)
XLA Modules:
  0.0 31.4 jit_solution(8075325241090369062)
XLA Ops:
  0.6 3.0 %collective-permute-start = (bf16[16,512]{1,0:T(8,128)(2,1)}, bf16[16,512]{1,0:T(8,128)(2,1)S(1)}, u32[]{:S(2)}, u32[]{:S(2)}) collective-permute-start(bf16[16,512]{1,0:T(8,128)(2,1)} %charge.1), channel_id=1, source_target_pairs={{0,2},{2,0},{1,3},{3,1},{4,6},{6,4},{5,7},{7,5},{8,10},{10,8},{9,1... | collective-permute-start | bytes 49160 | tf_op jit(solution)/shard_map/ppermute | solution.py:20
  3.6 0.1 collective-permute-start.7
  3.7 1.8 %pack_charges.1 = (bf16[5,16,128]{2,1,0:T(8,128)(2,1)S(1)}, s32[420]{0:T(512)S(4)}) custom-call(bf16[16,512]{1,0:T(8,128)(2,1)} %charge.1, s32[4,8]{1,0:T(4,128)} %needs.1, s32[192]{0:T(256)} %rows.1), custom_call_target="tpu_custom_call" | custom-call | bytes 65536 | tf_op jit(solution)/shard_map/pack_charges/pallas_call | solution.py:390
  5.6 0.0 collective-permute-done.refs_0_
  5.6 3.3 %collective-permute-start.1 = (bf16[9,16,128]{2,1,0:T(8,128)(2,1)S(1)}, bf16[9,16,128]{2,1,0:T(8,128)(2,1)S(1)}, u32[]{:S(2)}, u32[]{:S(2)}) collective-permute-start(bf16[9,16,128]{2,1,0:T(8,128)(2,1)S(1)} %join_charges.1.refs_3_.pack), channel_id=1, source_target_pairs={{0,8},{4,12},{8,0},{12,4},{1,9},{5,13},{9,1},{13,5},{2,10},{6,14},... | collective-permute-start | bytes 110600 | tf_op jit(solution)/shard_map/ppermute | solution.py:20
  8.8 1.3 %collective-permute-start.2 = (bf16[9,16,128]{2,1,0:T(8,128)(2,1)S(1)}, bf16[9,16,128]{2,1,0:T(8,128)(2,1)S(1)}, u32[]{:S(2)}, u32[]{:S(2)}) collective-permute-start(bf16[9,16,128]{2,1,0:T(8,128)(2,1)S(1)} %join_charges.1.refs_3_.pack), channel_id=1, source_target_pairs={{0,12},{4,8},{8,4},{12,0},{1,13},{5,9},{9,5},{13,1},{2,14},{6,10},... | collective-permute-start | bytes 110600 | tf_op jit(solution)/shard_map/ppermute | solution.py:20
  10.2 0.2 collective-permute-start.3
  10.4 2.1 %end_sums.1 = (s32[2,32]{1,0:T(2,128)S(4)}, s32[4,16]{1,0:T(4,128)S(4)}, s32[96]{0:T(128)S(4)}, s32[96]{0:T(128)S(4)}, s32[4,4]{1,0:T(4,128)S(4)}, /*index=5*/s3...) custom-call(bf16[16,4096]{1,0:T(8,128)(2,1)} %refs_0_.1, ...), custom_call_target="tpu_custom_call" | custom-call | flops 500000000 | bytes 262144 | tf_op jit(solution)/shard_map/end_sums/pallas_call | solution.py:411
  12.5 0.0 collective-permute-done.1.refs_0_
  12.5 2.1 %collective-permute-done.2.refs_1_ = bf16[9,16,128]{2,1,0:T(8,128)(2,1)S(1)} collective-permute-done((bf16[9,16,128]{2,1,0:T(8,128)(2,1)S(1)}, bf16[9,16,128]{2,1,0:T(8,128)(2,1)S(1)}, u32[]{:S(2)}, u32[]{:S(2)}) %collective-permute-start.2) | collective-permute-done | bytes 36896 | tf_op jit(solution)/shard_map/ppermute | solution.py:20
  14.6 0.0 collective-permute-done.3.refs_2_
  14.6 0.7 %coeff_tiles.1 = (f32[8,16,128]{2,1,0:T(8,128)S(1)}, bf16[32,16,128]{2,1,0:T(8,128)(2,1)S(1)}) custom-call(s32[96]{0:T(128)S(4)} %get-tuple-element.37.slots, s32[96]{0:T(128)S(4)} %get-tuple-element.38.rows, s32[16]{0:T(128)S(4)} %get-tuple-element.39.named, bf16[9,16,128]{2,1,0:T(8,128)(2,1)S(1)} %collective-permute-done.1.refs_0_, ...), custom_call_target="tpu_custom_call" | custom-call | flops 1000000000 | bytes 3145728 | tf_op jit(solution)/shard_map/coeff_tiles/pallas_call | solution.py:434
  15.3 1.6 %collective-permute-start.4 = (bf16[32,16,128]{2,1,0:T(8,128)(2,1)S(1)}, bf16[32,16,128]{2,1,0:T(8,128)(2,1)S(1)}, u32[]{:S(2)}, u32[]{:S(2)}) collective-permute-start(bf16[32,16,128]{2,1,0:T(8,128)(2,1)S(1)} %get-tuple-element.45), channel_id=1, source_target_pairs={{0,2},{2,0},{1,3},{3,1},{4,6},{6,4},{5,7},{7,5},{8,10},{10,8},{9,1... | collective-permute-start | bytes 393224 | tf_op jit(solution)/shard_map/ppermute | solution.py:20
  16.9 0.0 collective-permute-done.7.refs_5_
  16.9 0.3 pick_blocks.1
  17.2 2.1 %collective-permute-start.10 = (bf16[8,16,128]{2,1,0:T(8,128)(2,1)S(1)}, bf16[8,16,128]{2,1,0:T(8,128)(2,1)S(1)}, u32[]{:S(2)}, u32[]{:S(2)}) collective-permute-start(bf16[8,16,128]{2,1,0:T(8,128)(2,1)S(1)} %get-tuple-element.57), channel_id=1, source_target_pairs={{0,12},{4,8},{8,4},{12,0},{1,13},{5,9},{9,5},{13,1},{2,14},{6,10},... | collective-permute-start | bytes 98312 | tf_op jit(solution)/shard_map/ppermute | solution.py:20
  19.3 0.0 collective-permute-start.8
  19.3 2.4 %collective-permute-start.9 = (bf16[8,16,128]{2,1,0:T(8,128)(2,1)S(1)}, bf16[8,16,128]{2,1,0:T(8,128)(2,1)S(1)}, u32[]{:S(2)}, u32[]{:S(2)}) collective-permute-start(bf16[8,16,128]{2,1,0:T(8,128)(2,1)S(1)} %get-tuple-element.55), channel_id=1, source_target_pairs={{0,4},{4,0},{8,12},{12,8},{1,5},{5,1},{9,13},{13,9},{2,6},{6,2},{1... | collective-permute-start | bytes 98312 | tf_op jit(solution)/shard_map/ppermute | solution.py:20
  21.7 0.6 %collective-permute-start.6 = (bf16[12,16,128]{2,1,0:T(8,128)(2,1)S(1)}, bf16[12,16,128]{2,1,0:T(8,128)(2,1)S(1)}, u32[]{:S(2)}, u32[]{:S(2)}) collective-permute-start(bf16[12,16,128]{2,1,0:T(8,128)(2,1)S(1)} %get-tuple-element.47), channel_id=1, source_target_pairs={{0,8},{4,12},{8,0},{12,4},{1,9},{5,13},{9,1},{13,5},{2,10},{6,14},... | collective-permute-start | bytes 147464 | tf_op jit(solution)/shard_map/ppermute | solution.py:20
  22.3 1.8 %collective-permute-start.5 = (bf16[12,16,128]{2,1,0:T(8,128)(2,1)S(1)}, bf16[12,16,128]{2,1,0:T(8,128)(2,1)S(1)}, u32[]{:S(2)}, u32[]{:S(2)}) collective-permute-start(bf16[12,16,128]{2,1,0:T(8,128)(2,1)S(1)} %get-tuple-element.46), channel_id=1, source_target_pairs={{0,12},{4,8},{8,4},{12,0},{1,13},{5,9},{9,5},{13,1},{2,14},{6,10},... | collective-permute-start | bytes 147464 | tf_op jit(solution)/shard_map/ppermute | solution.py:20
  24.1 0.0 collective-permute-done.10.refs_3_
  24.1 0.6 %collective-permute-done.8.refs_0_ = bf16[8,16,128]{2,1,0:T(8,128)(2,1)S(1)} collective-permute-done((bf16[8,16,128]{2,1,0:T(8,128)(2,1)S(1)}, bf16[8,16,128]{2,1,0:T(8,128)(2,1)S(1)}, u32[]{:S(2)}, u32[]{:S(2)}) %collective-permute-start.8) | collective-permute-done | bytes 32800 | tf_op jit(solution)/shard_map/ppermute | solution.py:20
  24.7 0.8 %induct_away.1._after = bf16[32,16,128]{2,1,0:T(8,128)(2,1)S(1)} custom-call(s32[192]{0:T(256)S(4)} %get-tuple-element.49.slots, s32[192]{0:T(256)S(4)} %get-tuple-element.50.rows, s32[420]{0:T(512)S(4)} %get-tuple-element.51.listed, bf16[8,16,128]{2,1,0:T(8,128)(2,1)S(1)} %get-tuple-element.52._after.pot, ...), custom_call_target="tpu_custom_call" | custom-call | flops 100000000 | bytes 65536 | tf_op jit(solution)/shard_map/induct_away/pallas_call | solution.py:467
  25.5 0.6 %collective-permute-start.12 = (bf16[32,16,128]{2,1,0:T(8,128)(2,1)S(1)}, bf16[32,16,128]{2,1,0:T(8,128)(2,1)S(1)}, u32[]{:S(2)}, u32[]{:S(2)}) collective-permute-start(bf16[32,16,128]{2,1,0:T(8,128)(2,1)S(1)} %induct_away.1._after), channel_id=1, source_target_pairs={{0,2},{2,0},{1,3},{3,1},{4,6},{6,4},{5,7},{7,5},{8,10},{10,8},{9,1... | collective-permute-start | bytes 393224 | tf_op jit(solution)/shard_map/ppermute | solution.py:20
  26.1 0.8 %collective-permute-start.11 = (bf16[12,16,128]{2,1,0:T(8,128)(2,1)S(1)}, bf16[12,16,128]{2,1,0:T(8,128)(2,1)S(1)}, u32[]{:S(2)}, u32[]{:S(2)}) collective-permute-start(bf16[12,16,128]{2,1,0:T(8,128)(2,1)S(1)} %hold_near.1._after), channel_id=1, source_target_pairs={{0,4},{4,0},{8,12},{12,8},{1,5},{5,1},{9,13},{13,9},{2,6},{6,2},{1... | collective-permute-start | bytes 147464 | tf_op jit(solution)/shard_map/ppermute | solution.py:20
  26.9 0.8 %induct_own.1.field_own = f32[32,16,128]{2,1,0:T(8,128)S(1)} custom-call(s32[192]{0:T(256)S(4)} %get-tuple-element.49.slots, s32[192]{0:T(256)S(4)} %get-tuple-element.50.rows, s32[420]{0:T(512)S(4)} %get-tuple-element.51.listed, bf16[12,16,128]{2,1,0:T(8,128)(2,1)S(1)} %hold_near.1._after, bf16[8,16,128]{2,1,0:T(8,128)(2,1)S(1)} %collective-permute-done.8.refs_0_, ...), custom_call_target="tpu_custom_call" | custom-call | flops 100000000 | bytes 65536 | tf_op jit(solution)/shard_map/induct_own/pallas_call | solution.py:467
  27.7 0.7 %base_sums.1 = (f32[32,16,128]{2,1,0:T(8,128)S(1)}, f32[4,16,128]{2,1,0:T(8,128)S(1)}, bf16[16,512]{1,0:T(8,128)(2,1)}) custom-call(s32[4,16]{1,0:T(4,128)S(4)} %get-tuple-element.34.links, s32[64]{0:T(128)S(4)} %get-tuple-element.35.holder, f32[16]{0:T(128)S(4)} %get-tuple-element.48.scale, s32[64,128]{1,0:T(8,128)S(1)} %get-tuple-element.36.lanes, ...), custom_call_target="tpu_custom_call" | custom-call | tf_op jit(solution)/shard_map/base_sums/pallas_call | solution.py:493
  28.4 0.1 add_drops.2.field_in
  28.6 0.1 add_drops.3.field_own
  28.8 1.4 %collective-permute-done.11.refs_0_ = bf16[12,16,128]{2,1,0:T(8,128)(2,1)S(1)} collective-permute-done((bf16[12,16,128]{2,1,0:T(8,128)(2,1)S(1)}, bf16[12,16,128]{2,1,0:T(8,128)(2,1)S(1)}, u32[]{:S(2)}, u32[]{:S(2)}) %collective-permute-start.11) | collective-permute-done | bytes 49184 | tf_op jit(solution)/shard_map/ppermute | solution.py:20
  30.2 0.4 %collective-permute-done.12.refs_3_ = bf16[32,16,128]{2,1,0:T(8,128)(2,1)S(1)} collective-permute-done((bf16[32,16,128]{2,1,0:T(8,128)(2,1)S(1)}, bf16[32,16,128]{2,1,0:T(8,128)(2,1)S(1)}, u32[]{:S(2)}, u32[]{:S(2)}) %collective-permute-start.12) | collective-permute-done | bytes 131104 | tf_op jit(solution)/shard_map/ppermute | solution.py:20
  30.6 0.8 %outputs.1 = (bf16[16,4096]{1,0:T(8,128)(2,1)}, bf16[16,512]{1,0:T(8,128)(2,1)}) custom-call(s32[4,16]{1,0:T(4,128)S(4)} %get-tuple-element.34.links, s32[64]{0:T(128)S(4)} %get-tuple-element.35.holder, s32[64,128]{1,0:T(8,128)S(1)} %get-tuple-element.36.lanes, f32[32,16,128]{2,1,0:T(8,128)S(1)} %add_drops.3.field_own, ...), custom_call_target="tpu_custom_call" | custom-call | flops 1000000000 | bytes 1048576 | tf_op jit(solution)/shard_map/outputs/pallas_call | solution.py:512
  (12 shorter events, 0.1 us)
Async XLA Ops:
  0.6 4.9 %collective-permute-start = (bf16[16,512]{1,0:T(8,128)(2,1)}, bf16[16,512]{1,0:T(8,128)(2,1)S(1)}, u32[]{:S(2)}, u32[]{:S(2)}) collective-permute-start(bf16[16,512]{1,0:T(8,128)(2,1)} %charge.1), channel_id=1, source_target_pairs={{0,2},{2,0},{1,3},{3,1},{4,6},{6,4},{5,7},{7,5},{8,10},{10,8},{9,1... | collective-permute-start | bytes 49160 | tf_op jit(solution)/shard_map/ppermute | solution.py:20
  3.6 13.3 %collective-permute-start.7 = (bf16[16,4096]{1,0:T(8,128)(2,1)}, bf16[16,4096]{1,0:T(8,128)(2,1)S(1)}, u32[]{:S(2)}, u32[]{:S(2)}) collective-permute-start(bf16[16,4096]{1,0:T(8,128)(2,1)} %refs_0_.1), channel_id=1, source_target_pairs={{0,2},{2,0},{1,3},{3,1},{4,6},{6,4},{5,7},{7,5},{8,10},{10,8},{9,1... | collective-permute-start | bytes 393224 | tf_op jit(solution)/shard_map/ppermute | solution.py:20
  3.7 21.0 %slice-start = ((s8[6291456]{0:T(1024)(128)(4,1)}), s8[4194304]{0:T(1024)(128)(4,1)S(1)}, s32[]{:S(2)}) async-start(s8[6291456]{0:T(1024)(128)(4,1)} %bitcast.2), calls=%async_computation | async-start | bytes 8388608
  5.6 6.9 %collective-permute-start.1 = (bf16[9,16,128]{2,1,0:T(8,128)(2,1)S(1)}, bf16[9,16,128]{2,1,0:T(8,128)(2,1)S(1)}, u32[]{:S(2)}, u32[]{:S(2)}) collective-permute-start(bf16[9,16,128]{2,1,0:T(8,128)(2,1)S(1)} %join_charges.1.refs_3_.pack), channel_id=1, source_target_pairs={{0,8},{4,12},{8,0},{12,4},{1,9},{5,13},{9,1},{13,5},{2,10},{6,14},... | collective-permute-start | bytes 110600 | tf_op jit(solution)/shard_map/ppermute | solution.py:20
  8.8 5.8 %collective-permute-start.2 = (bf16[9,16,128]{2,1,0:T(8,128)(2,1)S(1)}, bf16[9,16,128]{2,1,0:T(8,128)(2,1)S(1)}, u32[]{:S(2)}, u32[]{:S(2)}) collective-permute-start(bf16[9,16,128]{2,1,0:T(8,128)(2,1)S(1)} %join_charges.1.refs_3_.pack), channel_id=1, source_target_pairs={{0,12},{4,8},{8,4},{12,0},{1,13},{5,9},{9,5},{13,1},{2,14},{6,10},... | collective-permute-start | bytes 110600 | tf_op jit(solution)/shard_map/ppermute | solution.py:20
  10.2 4.4 %collective-permute-start.3 = (bf16[9,16,128]{2,1,0:T(8,128)(2,1)S(1)}, bf16[9,16,128]{2,1,0:T(8,128)(2,1)S(1)}, u32[]{:S(2)}, u32[]{:S(2)}) collective-permute-start(bf16[9,16,128]{2,1,0:T(8,128)(2,1)S(1)} %join_charges.1.refs_3_.pack), channel_id=1, source_target_pairs={{0,4},{4,0},{8,12},{12,8},{1,5},{5,1},{9,13},{13,9},{2,6},{6,2},{1... | collective-permute-start | bytes 110600 | tf_op jit(solution)/shard_map/ppermute | solution.py:20
  14.6 10.1 %slice-start.1 = ((s8[6291456]{0:T(1024)(128)(4,1)}), s8[2097152]{0:T(1024)(128)(4,1)S(1)}, s32[]{:S(2)}) async-start(s8[6291456]{0:T(1024)(128)(4,1)} %bitcast.2), calls=%async_computation.1 | async-start | bytes 4194304
  15.3 6.4 %collective-permute-start.4 = (bf16[32,16,128]{2,1,0:T(8,128)(2,1)S(1)}, bf16[32,16,128]{2,1,0:T(8,128)(2,1)S(1)}, u32[]{:S(2)}, u32[]{:S(2)}) collective-permute-start(bf16[32,16,128]{2,1,0:T(8,128)(2,1)S(1)} %get-tuple-element.45), channel_id=1, source_target_pairs={{0,2},{2,0},{1,3},{3,1},{4,6},{6,4},{5,7},{7,5},{8,10},{10,8},{9,1... | collective-permute-start | bytes 393224 | tf_op jit(solution)/shard_map/ppermute | solution.py:20
  17.2 6.9 %collective-permute-start.10 = (bf16[8,16,128]{2,1,0:T(8,128)(2,1)S(1)}, bf16[8,16,128]{2,1,0:T(8,128)(2,1)S(1)}, u32[]{:S(2)}, u32[]{:S(2)}) collective-permute-start(bf16[8,16,128]{2,1,0:T(8,128)(2,1)S(1)} %get-tuple-element.57), channel_id=1, source_target_pairs={{0,12},{4,8},{8,4},{12,0},{1,13},{5,9},{9,5},{13,1},{2,14},{6,10},... | collective-permute-start | bytes 98312 | tf_op jit(solution)/shard_map/ppermute | solution.py:20
  19.3 5.4 %collective-permute-start.8 = (bf16[8,16,128]{2,1,0:T(8,128)(2,1)S(1)}, bf16[8,16,128]{2,1,0:T(8,128)(2,1)S(1)}, u32[]{:S(2)}, u32[]{:S(2)}) collective-permute-start(bf16[8,16,128]{2,1,0:T(8,128)(2,1)S(1)} %get-tuple-element.54), channel_id=1, source_target_pairs={{0,8},{4,12},{8,0},{12,4},{1,9},{5,13},{9,1},{13,5},{2,10},{6,14},... | collective-permute-start | bytes 98312 | tf_op jit(solution)/shard_map/ppermute | solution.py:20
  19.3 5.4 %collective-permute-start.9 = (bf16[8,16,128]{2,1,0:T(8,128)(2,1)S(1)}, bf16[8,16,128]{2,1,0:T(8,128)(2,1)S(1)}, u32[]{:S(2)}, u32[]{:S(2)}) collective-permute-start(bf16[8,16,128]{2,1,0:T(8,128)(2,1)S(1)} %get-tuple-element.55), channel_id=1, source_target_pairs={{0,4},{4,0},{8,12},{12,8},{1,5},{5,1},{9,13},{13,9},{2,6},{6,2},{1... | collective-permute-start | bytes 98312 | tf_op jit(solution)/shard_map/ppermute | solution.py:20
  21.7 6.8 %collective-permute-start.6 = (bf16[12,16,128]{2,1,0:T(8,128)(2,1)S(1)}, bf16[12,16,128]{2,1,0:T(8,128)(2,1)S(1)}, u32[]{:S(2)}, u32[]{:S(2)}) collective-permute-start(bf16[12,16,128]{2,1,0:T(8,128)(2,1)S(1)} %get-tuple-element.47), channel_id=1, source_target_pairs={{0,8},{4,12},{8,0},{12,4},{1,9},{5,13},{9,1},{13,5},{2,10},{6,14},... | collective-permute-start | bytes 147464 | tf_op jit(solution)/shard_map/ppermute | solution.py:20
  22.3 6.3 %collective-permute-start.5 = (bf16[12,16,128]{2,1,0:T(8,128)(2,1)S(1)}, bf16[12,16,128]{2,1,0:T(8,128)(2,1)S(1)}, u32[]{:S(2)}, u32[]{:S(2)}) collective-permute-start(bf16[12,16,128]{2,1,0:T(8,128)(2,1)S(1)} %get-tuple-element.46), channel_id=1, source_target_pairs={{0,12},{4,8},{8,4},{12,0},{1,13},{5,9},{9,5},{13,1},{2,14},{6,10},... | collective-permute-start | bytes 147464 | tf_op jit(solution)/shard_map/ppermute | solution.py:20
  25.5 5.0 %collective-permute-start.12 = (bf16[32,16,128]{2,1,0:T(8,128)(2,1)S(1)}, bf16[32,16,128]{2,1,0:T(8,128)(2,1)S(1)}, u32[]{:S(2)}, u32[]{:S(2)}) collective-permute-start(bf16[32,16,128]{2,1,0:T(8,128)(2,1)S(1)} %induct_away.1._after), channel_id=1, source_target_pairs={{0,2},{2,0},{1,3},{3,1},{4,6},{6,4},{5,7},{7,5},{8,10},{10,8},{9,1... | collective-permute-start | bytes 393224 | tf_op jit(solution)/shard_map/ppermute | solution.py:20
  26.1 4.1 %collective-permute-start.11 = (bf16[12,16,128]{2,1,0:T(8,128)(2,1)S(1)}, bf16[12,16,128]{2,1,0:T(8,128)(2,1)S(1)}, u32[]{:S(2)}, u32[]{:S(2)}) collective-permute-start(bf16[12,16,128]{2,1,0:T(8,128)(2,1)S(1)} %hold_near.1._after), channel_id=1, source_target_pairs={{0,4},{4,0},{8,12},{12,8},{1,5},{5,1},{9,13},{13,9},{2,6},{6,2},{1... | collective-permute-start | bytes 147464 | tf_op jit(solution)/shard_map/ppermute | solution.py:20

commit v20 on v18

--- a/solution.py
+++ b/solution.py
@@ -518,7 +518,7 @@
             pltpu.VMEM((seg_own, rhs, width), F32),
             pltpu.VMEM(current.shape, BF16),
             pltpu.VMEM(charge.shape, BF16),
-            pltpu.SemaphoreType.DMA((3,)),
+            pltpu.SemaphoreType.DMA((5,)),
         ],
         flops=10**9,
         moved=2**20,

time: 31.1 us -> 31.1 us (level)
  no operation moved by 1% of the time
where the time goes in v20:
time: 31.1 us; the launch traced here: 31 us
  starting transfers between devices  17.6 us (57%)
  Pallas kernels  8.38 us (27%)
  waiting for transfers between devices  4.35 us (14%)
  between operations  0.74 us (2%)
    ppermute x13, starting transfers between devices, exchange(): lax.ppermute(x, axis, [(i, i ^ k) for i in range(lax.axis_size(axis))])  17.6 us
    ppermute x13, waiting for transfers between devices, exchange(): lax.ppermute(x, axis, [(i, i ^ k) for i in range(lax.axis_size(axis))])  4.35 us
    pallas_call x1, Pallas kernels, shards(): call(functools.partial(ends_body, n_row, n_col, pan_own, cap_k, len(moved...  2.09 us
    pallas_call x1, Pallas kernels, shards(): call(functools.partial(pack_body, pan_own, seg_own), 'pack_charges', [lik...  1.83 us
    pallas_call x2, Pallas kernels, induct(): call(functools.partial(induct_body, n_row, n_col, seg_own, order, half),...  1.6 us
    pallas_call x1, Pallas kernels, shards(): call(functools.partial(final_body, n_row, n_col, pan_own), 'outputs', [ja...  0.84 us
    pallas_call x1, Pallas kernels, shards(): call(functools.partial(base_body, pan_own), 'base_sums', [like(seg_own, F...  0.73 us
    pallas_call x1, Pallas kernels, shards(): call(functools.partial(coeff_body, n_row, n_col, pan_own, partners), 'coe...  0.67 us
  transfers between devices with their start and end apart: 13, of which 4 were waited for; matrix products, arithmetic and copies ran while one was open for 0% of the time, Pallas kernels for 24%

profile of v20, /device:TPU:0, one launch (start us, length us, event | category | flops | bytes accessed | tf_op | source)
XLA Modules:
  0.0 31.0 jit_solution(1725197570031936072)
XLA Ops:
  0.6 3.0 %collective-permute-start = (bf16[16,512]{1,0:T(8,128)(2,1)}, bf16[16,512]{1,0:T(8,128)(2,1)S(1)}, u32[]{:S(2)}, u32[]{:S(2)}) collective-permute-start(bf16[16,512]{1,0:T(8,128)(2,1)} %charge.1), channel_id=1, source_target_pairs={{0,2},{2,0},{1,3},{3,1},{4,6},{6,4},{5,7},{7,5},{8,10},{10,8},{9,1... | collective-permute-start | bytes 49160 | tf_op jit(solution)/shard_map/ppermute | solution.py:20
  3.6 0.1 collective-permute-start.7
  3.7 1.8 %pack_charges.1 = (bf16[5,16,128]{2,1,0:T(8,128)(2,1)S(1)}, s32[420]{0:T(512)S(4)}) custom-call(bf16[16,512]{1,0:T(8,128)(2,1)} %charge.1, s32[4,8]{1,0:T(4,128)} %needs.1, s32[192]{0:T(256)} %rows.1), custom_call_target="tpu_custom_call" | custom-call | bytes 65536 | tf_op jit(solution)/shard_map/pack_charges/pallas_call | solution.py:390
  5.6 0.0 collective-permute-done.refs_0_
  5.6 3.3 %collective-permute-start.1 = (bf16[9,16,128]{2,1,0:T(8,128)(2,1)S(1)}, bf16[9,16,128]{2,1,0:T(8,128)(2,1)S(1)}, u32[]{:S(2)}, u32[]{:S(2)}) collective-permute-start(bf16[9,16,128]{2,1,0:T(8,128)(2,1)S(1)} %join_charges.1.refs_3_.pack), channel_id=1, source_target_pairs={{0,8},{4,12},{8,0},{12,4},{1,9},{5,13},{9,1},{13,5},{2,10},{6,14},... | collective-permute-start | bytes 110600 | tf_op jit(solution)/shard_map/ppermute | solution.py:20
  8.8 1.3 %collective-permute-start.2 = (bf16[9,16,128]{2,1,0:T(8,128)(2,1)S(1)}, bf16[9,16,128]{2,1,0:T(8,128)(2,1)S(1)}, u32[]{:S(2)}, u32[]{:S(2)}) collective-permute-start(bf16[9,16,128]{2,1,0:T(8,128)(2,1)S(1)} %join_charges.1.refs_3_.pack), channel_id=1, source_target_pairs={{0,12},{4,8},{8,4},{12,0},{1,13},{5,9},{9,5},{13,1},{2,14},{6,10},... | collective-permute-start | bytes 110600 | tf_op jit(solution)/shard_map/ppermute | solution.py:20
  10.2 0.2 collective-permute-start.3
  10.4 2.1 %end_sums.1 = (s32[2,32]{1,0:T(2,128)S(4)}, s32[4,16]{1,0:T(4,128)S(4)}, s32[96]{0:T(128)S(4)}, s32[96]{0:T(128)S(4)}, s32[4,4]{1,0:T(4,128)S(4)}, /*index=5*/s3...) custom-call(bf16[16,4096]{1,0:T(8,128)(2,1)} %refs_0_.1, ...), custom_call_target="tpu_custom_call" | custom-call | flops 500000000 | bytes 262144 | tf_op jit(solution)/shard_map/end_sums/pallas_call | solution.py:411
  12.5 0.0 collective-permute-done.1.refs_0_
  12.5 2.1 %collective-permute-done.2.refs_1_ = bf16[9,16,128]{2,1,0:T(8,128)(2,1)S(1)} collective-permute-done((bf16[9,16,128]{2,1,0:T(8,128)(2,1)S(1)}, bf16[9,16,128]{2,1,0:T(8,128)(2,1)S(1)}, u32[]{:S(2)}, u32[]{:S(2)}) %collective-permute-start.2) | collective-permute-done | bytes 36896 | tf_op jit(solution)/shard_map/ppermute | solution.py:20
  14.6 0.7 %coeff_tiles.1 = (f32[8,16,128]{2,1,0:T(8,128)S(1)}, bf16[32,16,128]{2,1,0:T(8,128)(2,1)S(1)}) custom-call(s32[96]{0:T(128)S(4)} %get-tuple-element.37.slots, s32[96]{0:T(128)S(4)} %get-tuple-element.38.rows, s32[16]{0:T(128)S(4)} %get-tuple-element.39.named, bf16[9,16,128]{2,1,0:T(8,128)(2,1)S(1)} %collective-permute-done.1.refs_0_, ...), custom_call_target="tpu_custom_call" | custom-call | flops 1000000000 | bytes 3145728 | tf_op jit(solution)/shard_map/coeff_tiles/pallas_call | solution.py:434
  15.3 1.6 %collective-permute-start.4 = (bf16[32,16,128]{2,1,0:T(8,128)(2,1)S(1)}, bf16[32,16,128]{2,1,0:T(8,128)(2,1)S(1)}, u32[]{:S(2)}, u32[]{:S(2)}) collective-permute-start(bf16[32,16,128]{2,1,0:T(8,128)(2,1)S(1)} %get-tuple-element.45), channel_id=1, source_target_pairs={{0,2},{2,0},{1,3},{3,1},{4,6},{6,4},{5,7},{7,5},{8,10},{10,8},{9,1... | collective-permute-start | bytes 393224 | tf_op jit(solution)/shard_map/ppermute | solution.py:20
  16.9 0.3 pick_blocks.1
  17.2 1.3 %collective-permute-start.10 = (bf16[8,16,128]{2,1,0:T(8,128)(2,1)S(1)}, bf16[8,16,128]{2,1,0:T(8,128)(2,1)S(1)}, u32[]{:S(2)}, u32[]{:S(2)}) collective-permute-start(bf16[8,16,128]{2,1,0:T(8,128)(2,1)S(1)} %get-tuple-element.57), channel_id=1, source_target_pairs={{0,8},{4,12},{8,0},{12,4},{1,9},{5,13},{9,1},{13,5},{2,10},{6,14},... | collective-permute-start | bytes 98312 | tf_op jit(solution)/shard_map/ppermute | solution.py:20
  18.5 1.1 %collective-permute-start.8 = (bf16[8,16,128]{2,1,0:T(8,128)(2,1)S(1)}, bf16[8,16,128]{2,1,0:T(8,128)(2,1)S(1)}, u32[]{:S(2)}, u32[]{:S(2)}) collective-permute-start(bf16[8,16,128]{2,1,0:T(8,128)(2,1)S(1)} %get-tuple-element.54), channel_id=1, source_target_pairs={{0,12},{4,8},{8,4},{12,0},{1,13},{5,9},{9,5},{13,1},{2,14},{6,10},... | collective-permute-start | bytes 98312 | tf_op jit(solution)/shard_map/ppermute | solution.py:20
  19.6 1.2 %collective-permute-start.9 = (bf16[8,16,128]{2,1,0:T(8,128)(2,1)S(1)}, bf16[8,16,128]{2,1,0:T(8,128)(2,1)S(1)}, u32[]{:S(2)}, u32[]{:S(2)}) collective-permute-start(bf16[8,16,128]{2,1,0:T(8,128)(2,1)S(1)} %get-tuple-element.55), channel_id=1, source_target_pairs={{0,4},{4,0},{8,12},{12,8},{1,5},{5,1},{9,13},{13,9},{2,6},{6,2},{1... | collective-permute-start | bytes 98312 | tf_op jit(solution)/shard_map/ppermute | solution.py:20
  20.8 2.1 %collective-permute-start.6 = (bf16[12,16,128]{2,1,0:T(8,128)(2,1)S(1)}, bf16[12,16,128]{2,1,0:T(8,128)(2,1)S(1)}, u32[]{:S(2)}, u32[]{:S(2)}) collective-permute-start(bf16[12,16,128]{2,1,0:T(8,128)(2,1)S(1)} %get-tuple-element.47), channel_id=1, source_target_pairs={{0,12},{4,8},{8,4},{12,0},{1,13},{5,9},{9,5},{13,1},{2,14},{6,10},... | collective-permute-start | bytes 147464 | tf_op jit(solution)/shard_map/ppermute | solution.py:20
  22.9 0.3 collective-permute-start.5
  23.2 0.0 collective-permute-done.10.refs_3_
  23.2 1.2 %collective-permute-done.8.refs_0_ = bf16[8,16,128]{2,1,0:T(8,128)(2,1)S(1)} collective-permute-done((bf16[8,16,128]{2,1,0:T(8,128)(2,1)S(1)}, bf16[8,16,128]{2,1,0:T(8,128)(2,1)S(1)}, u32[]{:S(2)}, u32[]{:S(2)}) %collective-permute-start.8) | collective-permute-done | bytes 32800 | tf_op jit(solution)/shard_map/ppermute | solution.py:20
  24.3 0.0 collective-permute-done.9.refs_1_
  24.4 0.8 %induct_away.1._after = bf16[32,16,128]{2,1,0:T(8,128)(2,1)S(1)} custom-call(s32[192]{0:T(256)S(4)} %get-tuple-element.49.slots, s32[192]{0:T(256)S(4)} %get-tuple-element.50.rows, s32[420]{0:T(512)S(4)} %get-tuple-element.51.listed, bf16[8,16,128]{2,1,0:T(8,128)(2,1)S(1)} %get-tuple-element.52._after.pot, ...), custom_call_target="tpu_custom_call" | custom-call | flops 100000000 | bytes 65536 | tf_op jit(solution)/shard_map/induct_away/pallas_call | solution.py:467
  25.2 0.4 %collective-permute-start.12 = (bf16[32,16,128]{2,1,0:T(8,128)(2,1)S(1)}, bf16[32,16,128]{2,1,0:T(8,128)(2,1)S(1)}, u32[]{:S(2)}, u32[]{:S(2)}) collective-permute-start(bf16[32,16,128]{2,1,0:T(8,128)(2,1)S(1)} %induct_away.1._after), channel_id=1, source_target_pairs={{0,2},{2,0},{1,3},{3,1},{4,6},{6,4},{5,7},{7,5},{8,10},{10,8},{9,1... | collective-permute-start | bytes 393224 | tf_op jit(solution)/shard_map/ppermute | solution.py:20
  25.6 1.7 %collective-permute-start.11 = (bf16[12,16,128]{2,1,0:T(8,128)(2,1)S(1)}, bf16[12,16,128]{2,1,0:T(8,128)(2,1)S(1)}, u32[]{:S(2)}, u32[]{:S(2)}) collective-permute-start(bf16[12,16,128]{2,1,0:T(8,128)(2,1)S(1)} %hold_near.1._after), channel_id=1, source_target_pairs={{0,4},{4,0},{8,12},{12,8},{1,5},{5,1},{9,13},{13,9},{2,6},{6,2},{1... | collective-permute-start | bytes 147464 | tf_op jit(solution)/shard_map/ppermute | solution.py:20
  27.3 0.8 %induct_own.1.field_own = f32[32,16,128]{2,1,0:T(8,128)S(1)} custom-call(s32[192]{0:T(256)S(4)} %get-tuple-element.49.slots, s32[192]{0:T(256)S(4)} %get-tuple-element.50.rows, s32[420]{0:T(512)S(4)} %get-tuple-element.51.listed, bf16[12,16,128]{2,1,0:T(8,128)(2,1)S(1)} %hold_near.1._after, bf16[8,16,128]{2,1,0:T(8,128)(2,1)S(1)} %collective-permute-done.8.refs_0_, ...), custom_call_target="tpu_custom_call" | custom-call | flops 100000000 | bytes 65536 | tf_op jit(solution)/shard_map/induct_own/pallas_call | solution.py:467
  28.1 0.7 %base_sums.1 = (f32[32,16,128]{2,1,0:T(8,128)S(1)}, f32[4,16,128]{2,1,0:T(8,128)S(1)}, bf16[16,512]{1,0:T(8,128)(2,1)}) custom-call(s32[4,16]{1,0:T(4,128)S(4)} %get-tuple-element.34.links, s32[64]{0:T(128)S(4)} %get-tuple-element.35.holder, f32[16]{0:T(128)S(4)} %get-tuple-element.48.scale, s32[64,128]{1,0:T(8,128)S(1)} %get-tuple-element.36.lanes, ...), custom_call_target="tpu_custom_call" | custom-call | tf_op jit(solution)/shard_map/base_sums/pallas_call | solution.py:493
  28.8 0.0 collective-permute-done.6.message.refs_2_
  28.8 0.1 add_drops.2.field_in
  29.0 0.1 add_drops.3.field_own
  29.1 0.5 %collective-permute-done.11.refs_0_ = bf16[12,16,128]{2,1,0:T(8,128)(2,1)S(1)} collective-permute-done((bf16[12,16,128]{2,1,0:T(8,128)(2,1)S(1)}, bf16[12,16,128]{2,1,0:T(8,128)(2,1)S(1)}, u32[]{:S(2)}, u32[]{:S(2)}) %collective-permute-start.11) | collective-permute-done | bytes 49184 | tf_op jit(solution)/shard_map/ppermute | solution.py:20
  29.7 0.5 %collective-permute-done.12.refs_3_ = bf16[32,16,128]{2,1,0:T(8,128)(2,1)S(1)} collective-permute-done((bf16[32,16,128]{2,1,0:T(8,128)(2,1)S(1)}, bf16[32,16,128]{2,1,0:T(8,128)(2,1)S(1)}, u32[]{:S(2)}, u32[]{:S(2)}) %collective-permute-start.12) | collective-permute-done | bytes 131104 | tf_op jit(solution)/shard_map/ppermute | solution.py:20
  30.2 0.8 %outputs.1 = (bf16[16,4096]{1,0:T(8,128)(2,1)}, bf16[16,512]{1,0:T(8,128)(2,1)}) custom-call(s32[4,16]{1,0:T(4,128)S(4)} %get-tuple-element.34.links, s32[64]{0:T(128)S(4)} %get-tuple-element.35.holder, s32[64,128]{1,0:T(8,128)S(1)} %get-tuple-element.36.lanes, f32[32,16,128]{2,1,0:T(8,128)S(1)} %add_drops.3.field_own, ...), custom_call_target="tpu_custom_call" | custom-call | flops 1000000000 | bytes 1048576 | tf_op jit(solution)/shard_map/outputs/pallas_call | solution.py:512
  (12 shorter events, 0.1 us)
Async XLA Ops:
  0.6 4.9 %collective-permute-start = (bf16[16,512]{1,0:T(8,128)(2,1)}, bf16[16,512]{1,0:T(8,128)(2,1)S(1)}, u32[]{:S(2)}, u32[]{:S(2)}) collective-permute-start(bf16[16,512]{1,0:T(8,128)(2,1)} %charge.1), channel_id=1, source_target_pairs={{0,2},{2,0},{1,3},{3,1},{4,6},{6,4},{5,7},{7,5},{8,10},{10,8},{9,1... | collective-permute-start | bytes 49160 | tf_op jit(solution)/shard_map/ppermute | solution.py:20
  3.6 13.3 %collective-permute-start.7 = (bf16[16,4096]{1,0:T(8,128)(2,1)}, bf16[16,4096]{1,0:T(8,128)(2,1)S(1)}, u32[]{:S(2)}, u32[]{:S(2)}) collective-permute-start(bf16[16,4096]{1,0:T(8,128)(2,1)} %refs_0_.1), channel_id=1, source_target_pairs={{0,2},{2,0},{1,3},{3,1},{4,6},{6,4},{5,7},{7,5},{8,10},{10,8},{9,1... | collective-permute-start | bytes 393224 | tf_op jit(solution)/shard_map/ppermute | solution.py:20
  3.7 20.6 %slice-start = ((s8[6291456]{0:T(1024)(128)(4,1)}), s8[4194304]{0:T(1024)(128)(4,1)S(1)}, s32[]{:S(2)}) async-start(s8[6291456]{0:T(1024)(128)(4,1)} %bitcast.2), calls=%async_computation | async-start | bytes 8388608
  5.6 6.9 %collective-permute-start.1 = (bf16[9,16,128]{2,1,0:T(8,128)(2,1)S(1)}, bf16[9,16,128]{2,1,0:T(8,128)(2,1)S(1)}, u32[]{:S(2)}, u32[]{:S(2)}) collective-permute-start(bf16[9,16,128]{2,1,0:T(8,128)(2,1)S(1)} %join_charges.1.refs_3_.pack), channel_id=1, source_target_pairs={{0,8},{4,12},{8,0},{12,4},{1,9},{5,13},{9,1},{13,5},{2,10},{6,14},... | collective-permute-start | bytes 110600 | tf_op jit(solution)/shard_map/ppermute | solution.py:20
  8.8 5.8 %collective-permute-start.2 = (bf16[9,16,128]{2,1,0:T(8,128)(2,1)S(1)}, bf16[9,16,128]{2,1,0:T(8,128)(2,1)S(1)}, u32[]{:S(2)}, u32[]{:S(2)}) collective-permute-start(bf16[9,16,128]{2,1,0:T(8,128)(2,1)S(1)} %join_charges.1.refs_3_.pack), channel_id=1, source_target_pairs={{0,12},{4,8},{8,4},{12,0},{1,13},{5,9},{9,5},{13,1},{2,14},{6,10},... | collective-permute-start | bytes 110600 | tf_op jit(solution)/shard_map/ppermute | solution.py:20
  10.2 4.4 %collective-permute-start.3 = (bf16[9,16,128]{2,1,0:T(8,128)(2,1)S(1)}, bf16[9,16,128]{2,1,0:T(8,128)(2,1)S(1)}, u32[]{:S(2)}, u32[]{:S(2)}) collective-permute-start(bf16[9,16,128]{2,1,0:T(8,128)(2,1)S(1)} %join_charges.1.refs_3_.pack), channel_id=1, source_target_pairs={{0,4},{4,0},{8,12},{12,8},{1,5},{5,1},{9,13},{13,9},{2,6},{6,2},{1... | collective-permute-start | bytes 110600 | tf_op jit(solution)/shard_map/ppermute | solution.py:20
  14.6 9.7 %slice-start.1 = ((s8[6291456]{0:T(1024)(128)(4,1)}), s8[2097152]{0:T(1024)(128)(4,1)S(1)}, s32[]{:S(2)}) async-start(s8[6291456]{0:T(1024)(128)(4,1)} %bitcast.2), calls=%async_computation.1 | async-start | bytes 4194304
  15.3 5.5 %collective-permute-start.4 = (bf16[32,16,128]{2,1,0:T(8,128)(2,1)S(1)}, bf16[32,16,128]{2,1,0:T(8,128)(2,1)S(1)}, u32[]{:S(2)}, u32[]{:S(2)}) collective-permute-start(bf16[32,16,128]{2,1,0:T(8,128)(2,1)S(1)} %get-tuple-element.45), channel_id=1, source_target_pairs={{0,2},{2,0},{1,3},{3,1},{4,6},{6,4},{5,7},{7,5},{8,10},{10,8},{9,1... | collective-permute-start | bytes 393224 | tf_op jit(solution)/shard_map/ppermute | solution.py:20
  17.2 6.0 %collective-permute-start.10 = (bf16[8,16,128]{2,1,0:T(8,128)(2,1)S(1)}, bf16[8,16,128]{2,1,0:T(8,128)(2,1)S(1)}, u32[]{:S(2)}, u32[]{:S(2)}) collective-permute-start(bf16[8,16,128]{2,1,0:T(8,128)(2,1)S(1)} %get-tuple-element.57), channel_id=1, source_target_pairs={{0,8},{4,12},{8,0},{12,4},{1,9},{5,13},{9,1},{13,5},{2,10},{6,14},... | collective-permute-start | bytes 98312 | tf_op jit(solution)/shard_map/ppermute | solution.py:20
  18.5 5.8 %collective-permute-start.8 = (bf16[8,16,128]{2,1,0:T(8,128)(2,1)S(1)}, bf16[8,16,128]{2,1,0:T(8,128)(2,1)S(1)}, u32[]{:S(2)}, u32[]{:S(2)}) collective-permute-start(bf16[8,16,128]{2,1,0:T(8,128)(2,1)S(1)} %get-tuple-element.54), channel_id=1, source_target_pairs={{0,12},{4,8},{8,4},{12,0},{1,13},{5,9},{9,5},{13,1},{2,14},{6,10},... | collective-permute-start | bytes 98312 | tf_op jit(solution)/shard_map/ppermute | solution.py:20
  19.6 4.8 %collective-permute-start.9 = (bf16[8,16,128]{2,1,0:T(8,128)(2,1)S(1)}, bf16[8,16,128]{2,1,0:T(8,128)(2,1)S(1)}, u32[]{:S(2)}, u32[]{:S(2)}) collective-permute-start(bf16[8,16,128]{2,1,0:T(8,128)(2,1)S(1)} %get-tuple-element.55), channel_id=1, source_target_pairs={{0,4},{4,0},{8,12},{12,8},{1,5},{5,1},{9,13},{13,9},{2,6},{6,2},{1... | collective-permute-start | bytes 98312 | tf_op jit(solution)/shard_map/ppermute | solution.py:20
  20.8 8.0 %collective-permute-start.6 = (bf16[12,16,128]{2,1,0:T(8,128)(2,1)S(1)}, bf16[12,16,128]{2,1,0:T(8,128)(2,1)S(1)}, u32[]{:S(2)}, u32[]{:S(2)}) collective-permute-start(bf16[12,16,128]{2,1,0:T(8,128)(2,1)S(1)} %get-tuple-element.47), channel_id=1, source_target_pairs={{0,12},{4,8},{8,4},{12,0},{1,13},{5,9},{9,5},{13,1},{2,14},{6,10},... | collective-permute-start | bytes 147464 | tf_op jit(solution)/shard_map/ppermute | solution.py:20
  22.9 6.1 %collective-permute-start.5 = (bf16[12,16,128]{2,1,0:T(8,128)(2,1)S(1)}, bf16[12,16,128]{2,1,0:T(8,128)(2,1)S(1)}, u32[]{:S(2)}, u32[]{:S(2)}) collective-permute-start(bf16[12,16,128]{2,1,0:T(8,128)(2,1)S(1)} %get-tuple-element.46), channel_id=1, source_target_pairs={{0,8},{4,12},{8,0},{12,4},{1,9},{5,13},{9,1},{13,5},{2,10},{6,14},... | collective-permute-start | bytes 147464 | tf_op jit(solution)/shard_map/ppermute | solution.py:20
  25.2 5.0 %collective-permute-start.12 = (bf16[32,16,128]{2,1,0:T(8,128)(2,1)S(1)}, bf16[32,16,128]{2,1,0:T(8,128)(2,1)S(1)}, u32[]{:S(2)}, u32[]{:S(2)}) collective-permute-start(bf16[32,16,128]{2,1,0:T(8,128)(2,1)S(1)} %induct_away.1._after), channel_id=1, source_target_pairs={{0,2},{2,0},{1,3},{3,1},{4,6},{6,4},{5,7},{7,5},{8,10},{10,8},{9,1... | collective-permute-start | bytes 393224 | tf_op jit(solution)/shard_map/ppermute | solution.py:20
  25.6 4.1 %collective-permute-start.11 = (bf16[12,16,128]{2,1,0:T(8,128)(2,1)S(1)}, bf16[12,16,128]{2,1,0:T(8,128)(2,1)S(1)}, u32[]{:S(2)}, u32[]{:S(2)}) collective-permute-start(bf16[12,16,128]{2,1,0:T(8,128)(2,1)S(1)} %hold_near.1._after), channel_id=1, source_target_pairs={{0,4},{4,0},{8,12},{12,8},{1,5},{5,1},{9,13},{13,9},{2,6},{6,2},{1... | collective-permute-start | bytes 147464 | tf_op jit(solution)/shard_map/ppermute | solution.py:20
